TPU v7x, 32 devices: a whole 2x2x4 slice. The times are simulated.
32 devices in a mesh: clip: 16 (over z, y, x), tm: 2 (over core).
Axes of the slice: x: 2, y: 2, z: 4, core: 2. Of those that a mesh axis runs over, the one named last changes fastest.
Arguments:
- audio_feats: bfloat16 [64, 512, 256], P('clip', 'tm'), may hold values from -6 to 6
- lip_feats: bfloat16 [64, 512, 256], P('clip', 'tm'), may hold values from -6 to 6
- lengths: int32 [64], P('clip'), may hold values from 256 to 512
- labels: int32 [64], P('clip'), may hold values from -15 to 15
- w_audio_conv: bfloat16 [3, 256, 512], replicated, may hold values from -0.21875 to 0.21875
- w_audio_proj: bfloat16 [512, 512], replicated, may hold values from -0.25 to 0.25
- w_lip_conv: bfloat16 [3, 256, 512], replicated, may hold values from -0.21875 to 0.21875
- w_lip_proj: bfloat16 [512, 512], replicated, may hold values from -0.25 to 0.25
Outputs:
- loss: float32 [], replicated
- grad_audio_conv: float32 [3, 256, 512], replicated
- grad_audio_proj: float32 [512, 512], replicated
- grad_lip_conv: float32 [3, 256, 512], replicated
- grad_lip_proj: float32 [512, 512], replicated
All inputs are finite; a program needn't handle non-finite values.
Results may differ from a plain program's by a relative error of at most 0.0075.
Values may be sent and summed in bfloat16 or wider, within the bound.
No kernel may reach another device: no remote copies, remote signals or barrier semaphores. Data moves between devices by JAX's collectives and lax.ppermute only.
A program may use at most 64 MiB of HBM per device.

v0:
```python
import jax
import jax.numpy as jnp
from jax import lax
from jax.sharding import PartitionSpec as P

SPAN = 15


logit_sharpening_divisor = 10.0
loss_scale = 1024.0
epsilon = 1e-06


def padded_2(cells, sides, width):
    for axis, dim in sides:
        count = lax.axis_size(axis)
        ends = count - 1
        head = lax.slice_in_dim(cells, 0, width, axis=dim)
        tail = lax.slice_in_dim(cells, cells.shape[dim] - width, cells.shape[dim], axis=dim)
        cells = jnp.concatenate(
            [
                lax.ppermute(tail, axis, [(i, (i + 1) % count) for i in range(ends)]),
                cells,
                lax.ppermute(head, axis, [((i + 1) % count, i) for i in range(ends)]),
            ],
            axis=dim,
        )
    return cells


def from_behind(value, axis, steps):
    count = lax.axis_size(axis)
    initial, last = (max(0, -steps), min(count, count - steps))
    return lax.ppermute(value, axis, [(source, source + steps) for source in range(initial, last)])


def silu_slope(values):
    sigma = jax.nn.sigmoid(values)
    return sigma * (1.0 + values * (1.0 - sigma))


def encoder(padded, w_conv, w_proj):
    clip_num, frame_pad, chan_num = padded.shape
    frame_num = frame_pad - 2
    columns = jnp.concatenate(
        [padded[:, 0:frame_num], padded[:, 1 : frame_num + 1], padded[:, 2 : frame_num + 2]], axis=2
    )
    before = jnp.einsum(
        "cfk,ke->cfe",
        columns,
        w_conv.reshape(3 * chan_num, w_conv.shape[2]),
        preferred_element_type=jnp.float32,
    )
    hidden = jax.nn.silu(before).astype(jnp.bfloat16)
    embedded = jnp.einsum("cfe,eg->cfg", hidden, w_proj, preferred_element_type=jnp.float32).astype(
        jnp.bfloat16
    )
    return (columns, before, hidden, embedded)


def inverse_norm(embedded):
    values = embedded.astype(jnp.float32)
    return lax.rsqrt(jnp.sum(values * values, axis=-1) + epsilon)


def spread_band(band, wide_len):
    clip_num, row_num, band_len = band.shape
    full_band = jnp.pad(band, ((0, 0), (0, 0), (0, wide_len + 1 - band_len)))
    flat_band = full_band.reshape(clip_num, row_num * (wide_len + 1))[:, : row_num * wide_len]
    return flat_band.reshape(clip_num, row_num, wide_len)


def narrow_band(matrix, band_len):
    clip_num, row_num, wide_len = matrix.shape
    flat_mat = jnp.pad(matrix.reshape(clip_num, row_num * wide_len), ((0, 0), (0, row_num)))
    return flat_mat.reshape(clip_num, row_num, wide_len + 1)[:, :, :band_len]


def flatten_rows(values):
    return values.reshape(values.shape[0] * values.shape[1], values.shape[2])


def proj_grad(hidden, grad_emb):
    return jnp.einsum("re,rf->ef", hidden, grad_emb, preferred_element_type=jnp.float32)


def conv_grad(columns, before, grad_emb, w_proj, w_conv):
    grad_hidden = jnp.einsum("rf,ef->re", grad_emb, w_proj, preferred_element_type=jnp.float32)
    grad_before = (grad_hidden * silu_slope(before)).astype(jnp.bfloat16)
    grad_conv = jnp.einsum("rk,re->ke", columns, grad_before, preferred_element_type=jnp.float32)
    return grad_conv.reshape(w_conv.shape)


def shards(
    audio_feats, lip_feats, lengths, labels, w_audio_conv, w_audio_proj, w_lip_conv, w_lip_proj
):
    clip_num, frame_num, chan_num = audio_feats.shape
    width = w_audio_proj.shape[1]
    offsets = 2 * SPAN + 1
    wide_len = frame_num + 2 * SPAN
    first_frame = lax.axis_index("tm") * frame_num
    stacked = jnp.stack([audio_feats, lip_feats])
    padded = padded_2(stacked, (("tm", 2),), 1)
    cols_a, pre_a, hid_a, emb_a = encoder(padded[0], w_audio_conv, w_audio_proj)
    cols_v, pre_v, hid_v, emb_v = encoder(padded[1], w_lip_conv, w_lip_proj)
    window = padded_2(emb_a, (("tm", 1),), SPAN)
    cols_a, pre_a, hid_a = (flatten_rows(cols_a), flatten_rows(pre_a), flatten_rows(hid_a))
    cols_v, pre_v, hid_v = (flatten_rows(cols_v), flatten_rows(pre_v), flatten_rows(hid_v))
    count = lax.psum(jnp.sum((lengths - jnp.abs(labels)).astype(jnp.float32)), "clip")
    matrix = jnp.einsum("cfe,cwe->cfw", emb_v, window, preferred_element_type=jnp.float32)
    lagged_inner_terms = narrow_band(matrix, offsets)
    inv_win = inverse_norm(window)
    reciprocal_visual_length = inverse_norm(emb_v)
    reciprocal_lag_strip = jnp.stack(
        [inv_win[:, offset : offset + frame_num] for offset in range(offsets)], axis=2
    )
    frame_ids = first_frame + jnp.arange(frame_num, dtype=jnp.int32)
    shifts = jnp.arange(offsets, dtype=jnp.int32) - SPAN
    positions = frame_ids[:, None] + shifts[None, :]
    inside = frame_ids[None, :] < lengths[:, None]
    valid = inside[:, :, None] & (positions[None] >= 0) & (positions[None] < lengths[:, None, None])
    target_pos = frame_ids[None, :] + labels[:, None]
    counted = inside & (target_pos >= 0) & (target_pos < lengths[:, None])
    correct_lag_position = (shifts[None, :] == labels[:, None]).astype(jnp.float32)
    lag_similarity_logits = (
        logit_sharpening_divisor
        * lagged_inner_terms
        * reciprocal_visual_length[:, :, None]
        * reciprocal_lag_strip
    )
    exponentiated_logits = jnp.where(valid, jnp.exp(lag_similarity_logits), 0.0)
    partition_sums = jnp.where(inside, jnp.sum(exponentiated_logits, axis=2), 1.0)
    picked = jnp.sum(lag_similarity_logits * correct_lag_position[:, None, :], axis=2)
    loss_local = jnp.sum(jnp.where(counted, jnp.log(partition_sums) - picked, 0.0))
    normalized_probabilities = jnp.where(counted, loss_scale / count, 0.0)
    logit_derivative = (
        logit_sharpening_divisor
        * normalized_probabilities[:, :, None]
        * (exponentiated_logits / partition_sums[:, :, None] - correct_lag_position[:, None, :])
    )
    grad_dots = (
        logit_derivative * reciprocal_visual_length[:, :, None] * reciprocal_lag_strip
    ).astype(jnp.bfloat16)
    grad_inv_v = jnp.sum(logit_derivative * lagged_inner_terms * reciprocal_lag_strip, axis=2)
    grad_inv_win = jnp.sum(
        spread_band(
            logit_derivative * lagged_inner_terms * reciprocal_visual_length[:, :, None], wide_len
        ),
        axis=1,
    )
    band_full = spread_band(grad_dots, wide_len)
    lip_sum = jnp.einsum("cfw,cwe->cfe", band_full, window, preferred_element_type=jnp.float32)
    lip_vals = emb_v.astype(jnp.float32)
    grad_lip = (
        lip_sum
        - (
            reciprocal_visual_length
            * reciprocal_visual_length
            * reciprocal_visual_length
            * grad_inv_v
        )[:, :, None]
        * lip_vals
    ).astype(jnp.bfloat16)
    win_sum = jnp.einsum("cfw,cfe->cwe", band_full, emb_v, preferred_element_type=jnp.float32)
    win_sum = win_sum - (inv_win * inv_win * inv_win * grad_inv_win)[:, :, None] * window.astype(
        jnp.float32
    )
    own_grad = win_sum[:, SPAN : SPAN + frame_num]
    from_after = from_behind(win_sum[:, :SPAN], "tm", -1)
    from_before = from_behind(win_sum[:, frame_num + SPAN :], "tm", 1)
    own_grad = own_grad.at[:, frame_num - SPAN :].add(from_after)
    own_grad = own_grad.at[:, :SPAN].add(from_before)
    grad_audio = own_grad.astype(jnp.bfloat16).reshape(clip_num * frame_num, width)
    grad_lip = grad_lip.reshape(clip_num * frame_num, width)
    grad_ap = proj_grad(hid_a, grad_audio)
    grad_vp = proj_grad(hid_v, grad_lip)
    grad_ac = conv_grad(cols_a, pre_a, grad_audio, w_audio_proj, w_audio_conv)
    grad_vc = conv_grad(cols_v, pre_v, grad_lip, w_lip_proj, w_lip_conv)
    grad_ac, grad_vc, grad_ap, grad_vp, loss_sum = lax.psum(
        (grad_ac, grad_vc, grad_ap, grad_vp, loss_local), ("clip", "tm")
    )
    return (loss_sum / count, grad_ac, grad_ap, grad_vc, grad_vp)


def solution(mesh):
    placed = (
        P("clip", "tm", None),
        P("clip", "tm", None),
        P("clip"),
        P("clip"),
        P(),
        P(),
        P(),
        P(),
    )
    return jax.shard_map(
        shards, mesh=mesh, in_specs=placed, out_specs=(P(), P(), P(), P(), P()), check_vma=False
    )
```

profile of v0, /device:TPU:0, one launch (start us, length us, event | category | flops | bytes accessed | tf_op | source)
XLA Modules:
  0.0 289.7 jit_solution(14646147873143938988)
XLA Ops:
  8.1 2.4 collective-permute-start
  16.4 43.5 %psum.43 = f32[]{:T(128)} all-reduce(f32[]{:T(128)} %convert_reduce_fusion), channel_id=1, replica_groups=mesh['clip'=16,'tm'=2] {'clip'}, use_global_device_ids=true, to_apply=%region_7.8 | all-reduce | flops 1 | bytes 8 | tf_op jit(solution)/shard_map/psum | solution.py:109
  63.9 1.8 fusion.2
  69.4 1.9 collective-permute-start.2
  73.8 1.7 copy.1171
  75.5 2.6 copy.1167
  82.1 2.3 fusion.28
  84.4 2.5 reshape.357
  88.5 2.6 reshape.358
  91.1 1.6 fusion.23
  92.8 2.8 multiply_reduce_fusion
  97.1 1.7 reshape.361
  98.8 2.7 fusion.4
  101.5 1.7 convolution_bitcast_fusion
  103.3 2.2 fusion.20
  108.1 3.1 %reshape.363 = f32[4,256,286]{2,1,0:T(8,128)S(1)} reshape(f32[4,73216]{1,0:T(4,128)} %slice.290) | data formatting | bytes 2342912 | tf_op jit(solution)/shard_map/reshape | solution.py:70
  111.3 2.4 fusion.1
  113.7 3.7 %collective-permute-start.5 = (f32[4,15,512]{2,1,0:T(8,128)S(1)}, f32[4,15,512]{2,1,0:T(8,128)S(1)}, u32[]{:S(2)}, u32[]{:S(2)}) collective-permute-start(f32[4,15,512]{2,1,0:T(8,128)S(1)} %get-tuple-element.37), channel_id=1, source_target_pairs={{0,1},{2,3},{4,5},{6,7},{8,9},{10,11},{12,13},{14,15},{16,17},{18,... | collective-permute-start | bytes 368648 | tf_op jit(solution)/shard_map/ppermute | solution.py:34
  118.7 2.2 fusion.36
  123.7 1.8 convolution_bitcast_fusion.1
  126.9 2.1 fusion.35
  130.3 38.2 %psum.42 = f32[]{:T(128)} all-reduce(f32[]{:T(128)} %select_reduce_fusion), channel_id=1, replica_groups=mesh['clip'=16,'tm'=2] {'clip','tm'}, use_global_device_ids=true, to_apply=%region_5.6 | all-reduce | flops 1 | bytes 8 | tf_op jit(solution)/shard_map/psum | solution.py:179
  169.9 105.3 %all-reduce.6.cloned.1.call-done = (f32[3,256,512]{2,1,0:T(8,128)}, f32[512,512]{1,0:T(8,128)}, f32[3,256,512]{2,1,0:T(8,128)}, f32[512,512]{1,0:T(8,128)}) async-done(((f32[3,256,512]{2,1,0:T(8,128)}, f32[512,512]{1,0:T(8,128)}, f32[3,256,512]{2,1,0:T(8,128)}, f32[512,512]{1,0:T(8,128)}), (f32[3,256,512]{2,1,0:T(8,128)}, f32[512,512]{1,0:T(8,128)}, f32[3,256,512]{2,1,0:T(8,128)}, ...) | async-done | bytes 5242896 | tf_op jit(solution)/shard_map/psum | solution.py:179
  275.2 2.8 copy.1216
  (148 shorter events, 36.7 us)
Async XLA Ops:
  7.2 55.7 %copy-start = (bf16[3,256,512]{2,1,0:T(8,128)(2,1)S(1)}, bf16[3,256,512]{2,1,0:T(8,128)(2,1)}, u32[]{:S(2)}) copy-start(bf16[3,256,512]{2,1,0:T(8,128)(2,1)} %param.18) | copy-start | bytes 2359300
  7.2 268.0 %all-reduce.6.cloned.1.call-start = ((), (), s32[]{:S(2)}) async-start(), calls=%async_computation | async-start | bytes 10485760 | tf_op jit(solution)/shard_map/psum | solution.py:179
  8.1 52.5 %collective-permute-start = (bf16[2,4,1,256]{3,2,1,0:T(2,128)(2,1)S(1)}, bf16[2,4,1,256]{3,2,1,0:T(2,128)(2,1)S(1)}, u32[]{:S(2)}, u32[]{:S(2)}) collective-permute-start(bf16[2,4,1,256]{3,2,1,0:T(2,128)(2,1)S(1)} %get-tuple-element.45), channel_id=1, source_target_pairs={{0,1},{2,3},{4,5},{6,7},{8,9},{10,11},{12,13},{14,15},{16,17},{18,... | collective-permute-start | bytes 12296 | tf_op jit(solution)/shard_map/ppermute | solution.py:22
  10.4 50.2 %collective-permute-start.1 = (bf16[2,4,1,256]{3,2,1,0:T(2,128)(2,1)S(1)}, bf16[2,4,1,256]{3,2,1,0:T(2,128)(2,1)S(1)}, u32[]{:S(2)}, u32[]{:S(2)}) collective-permute-start(bf16[2,4,1,256]{3,2,1,0:T(2,128)(2,1)S(1)} %get-tuple-element.46), channel_id=1, source_target_pairs={{1,0},{3,2},{5,4},{7,6},{9,8},{11,10},{13,12},{15,14},{17,16},{19,... | collective-permute-start | bytes 12296 | tf_op jit(solution)/shard_map/ppermute | solution.py:24
  68.7 9.4 %copy-start.4 = (bf16[4,256,512]{2,1,0:T(8,128)(2,1)}, bf16[4,256,512]{2,1,0:T(8,128)(2,1)S(1)}, u32[]{:S(2)}) copy-start(bf16[4,256,512]{2,1,0:T(8,128)(2,1)S(1)} %convolution_convert_fusion) | copy-start | bytes 3145732
  69.4 8.7 %collective-permute-start.2 = (bf16[4,15,512]{2,1,0:T(8,128)(2,1)}, bf16[4,15,512]{2,1,0:T(8,128)(2,1)}, u32[]{:S(2)}, u32[]{:S(2)}) collective-permute-start(bf16[4,15,512]{2,1,0:T(8,128)(2,1)} %get-tuple-element.43), channel_id=1, source_target_pairs={{0,1},{2,3},{4,5},{6,7},{8,9},{10,11},{12,13},{14,15},{16,17},{18,... | collective-permute-start | bytes 184328 | tf_op jit(solution)/shard_map/ppermute | solution.py:22
  71.3 6.8 %collective-permute-start.3 = (bf16[4,15,512]{2,1,0:T(8,128)(2,1)}, bf16[4,15,512]{2,1,0:T(8,128)(2,1)}, u32[]{:S(2)}, u32[]{:S(2)}) collective-permute-start(bf16[4,15,512]{2,1,0:T(8,128)(2,1)} %get-tuple-element.44), channel_id=1, source_target_pairs={{1,0},{3,2},{5,4},{7,6},{9,8},{11,10},{13,12},{15,14},{17,16},{19,... | collective-permute-start | bytes 184328 | tf_op jit(solution)/shard_map/ppermute | solution.py:24
  86.9 4.2 %copy-start.9 = (pred[256,31]{1,0:T(8,128)(4,1)S(1)}, pred[256,31]{1,0:T(8,128)(4,1)}, u32[]{:S(2)}) copy-start(pred[256,31]{1,0:T(8,128)(4,1)} %broadcast_compare_fusion) | copy-start | bytes 23812
  86.9 4.2 %copy-start.11 = (f32[4,256]{1,0:T(4,128)S(1)}, f32[4,256]{1,0:T(4,128)}, u32[]{:S(2)}) copy-start(f32[4,256]{1,0:T(4,128)} %get-tuple-element.54) | copy-start | bytes 12292
  86.9 4.2 %copy-start.15 = (s32[4]{0:T(128)S(1)}, s32[4]{0:T(128)}, u32[]{:S(2)}) copy-start(s32[4]{0:T(128)} %param.14) | copy-start | bytes 52
  86.9 4.2 %copy-start.17 = (pred[4,256]{1,0:T(4,128)(4,1)S(1)}, pred[4,256]{1,0:T(4,128)(4,1)}, u32[]{:S(2)}) copy-start(pred[4,256]{1,0:T(4,128)(4,1)} %broadcast_compare_fusion.1) | copy-start | bytes 3076
  88.4 4.3 %copy-start.19 = (s32[4]{0:T(128)S(1)}, s32[4]{0:T(128)}, u32[]{:S(2)}) copy-start(s32[4]{0:T(128)} %param.15) | copy-start | bytes 52
  88.4 4.3 %copy-start.10 = (f32[4,256]{1,0:T(4,128)S(1)}, f32[4,256]{1,0:T(4,128)}, u32[]{:S(2)}) copy-start(f32[4,256]{1,0:T(4,128)} %get-tuple-element.53) | copy-start | bytes 12292
  88.5 4.3 %copy-start.18 = (f32[4,31]{1,0:T(4,128)S(1)}, f32[4,31]{1,0:T(4,128)}, u32[]{:S(2)}) copy-start(f32[4,31]{1,0:T(4,128)} %compare_convert_fusion) | copy-start | bytes 1492
  91.1 4.5 %copy-start.14 = (f32[4,256]{1,0:T(4,128)S(1)}, f32[4,256]{1,0:T(4,128)}, u32[]{:S(2)}) copy-start(f32[4,256]{1,0:T(4,128)} %copy-done.13) | copy-start | bytes 12292
  98.8 2.7 copy-start.8
  98.8 2.7 copy-start.30
  108.1 3.2 %copy-start.5 = (bf16[4,256,512]{2,1,0:T(8,128)(2,1)S(1)}, bf16[4,256,512]{2,1,0:T(8,128)(2,1)}, u32[]{:S(2)}) copy-start(bf16[4,256,512]{2,1,0:T(8,128)(2,1)} %copy-done.4) | copy-start | bytes 3145732
  111.3 7.4 %copy-start.2 = (bf16[768,1024]{1,0:T(8,128)(2,1)S(1)}, bf16[768,1024]{1,0:T(8,128)(2,1)}, u32[]{:S(2)}) copy-start(bf16[768,1024]{1,0:T(8,128)(2,1)} %copy.1171) | copy-start | bytes 4718596
  111.3 7.4 %copy-start.26 = (bf16[1024,512,1]{1,0,2:T(8,128)(2,1)S(1)}, bf16[1024,512,1]{1,0,2:T(8,128)(2,1)}, u32[]{:S(2)}) copy-start(bf16[1024,512,1]{1,0,2:T(8,128)(2,1)} %fusion.20) | copy-start | bytes 3145732
  113.7 8.0 %collective-permute-start.5 = (f32[4,15,512]{2,1,0:T(8,128)S(1)}, f32[4,15,512]{2,1,0:T(8,128)S(1)}, u32[]{:S(2)}, u32[]{:S(2)}) collective-permute-start(f32[4,15,512]{2,1,0:T(8,128)S(1)} %get-tuple-element.37), channel_id=1, source_target_pairs={{0,1},{2,3},{4,5},{6,7},{8,9},{10,11},{12,13},{14,15},{16,17},{18,... | collective-permute-start | bytes 368648 | tf_op jit(solution)/shard_map/ppermute | solution.py:34
  117.4 3.8 %collective-permute-start.4 = (f32[4,15,512]{2,1,0:T(8,128)S(1)}, f32[4,15,512]{2,1,0:T(8,128)S(1)}, u32[]{:S(2)}, u32[]{:S(2)}) collective-permute-start(f32[4,15,512]{2,1,0:T(8,128)S(1)} %get-tuple-element.38), channel_id=1, source_target_pairs={{1,0},{3,2},{5,4},{7,6},{9,8},{11,10},{13,12},{15,14},{17,16},{19,... | collective-permute-start | bytes 368648 | tf_op jit(solution)/shard_map/ppermute | solution.py:34
  275.2 2.8 copy-start.7
  275.2 3.8 %copy-start.3 = (f32[3,256,512]{2,1,0:T(8,128)S(1)}, f32[3,256,512]{2,1,0:T(8,128)}, u32[]{:S(2)}) copy-start(f32[3,256,512]{2,1,0:T(8,128)} %get-tuple-element.65) | copy-start | bytes 4718596
  (14 other events, 19.5 us)
Sparse Core Ops, SparseCore 0:
  129.1 146.0 all-reduce.5
where the time goes:
time: 291 us; the launch traced here: 290 us
  waiting for transfers between devices  105 us (36%)
  blocking collectives  81.7 us (28%)
  local copies, waits for them, and re-layouts  34.6 us (12%)
  matrix products  22.9 us (8%)
  between operations  17.7 us (6%)
  other arithmetic  15.7 us (5%)
  starting transfers between devices  11.8 us (4%)
    psum x1, waiting for transfers between devices, shards(): lax.psum((grad_ac, grad_vc, grad_ap, grad_vp, loss_local), ('clip', 'tm'))  105 us
    psum x1, blocking collectives, shards(): lax.psum(jnp.sum((lengths - jnp.abs(labels)).astype(jnp.float32)), 'clip')  43.5 us
    psum x1, blocking collectives, shards(): lax.psum((grad_ac, grad_vc, grad_ap, grad_vp, loss_local), ('clip', 'tm'))  38.2 us
    unnamed x96, local copies, waits for them, and re-layouts  12 us
  transfers between devices with their start and end apart: 7, of which 1 were waited for; matrix products, arithmetic and copies ran while one was open for 5% of the time, Pallas kernels for 0%

commit v1 on v0

v1 whole, which is shorter than its diff:
```python
import functools

import jax
import jax.numpy as jnp
from jax import lax
from jax.experimental import pallas as pl
from jax.experimental.pallas import tpu as pltpu
from jax.sharding import PartitionSpec as P

SPAN = 15
PAD = 16
TILE = 128
WIN = TILE + 2 * PAD
HALO = 64
LANES = 128
DIGITS = 48
FRACTION = 20

logit_sharpening_divisor = 10.0
loss_scale = 1024.0
epsilon = 1e-06

BF16 = jnp.bfloat16
F32 = jnp.float32


def dot(a, b, dims):
    return lax.dot_general(a, b, (dims, ((), ())), preferred_element_type=F32)


NN = ((1,), (0,))
NT = ((1,), (1,))
TN = ((0,), (0,))


def digit_weights(shape):
    lane = lax.broadcasted_iota(jnp.int32, shape, len(shape) - 1)
    return lane, jnp.exp2((lane - FRACTION).astype(F32))


def digits_of(value):
    lane, weight = digit_weights((1, LANES))
    size = jnp.abs(value)
    bits = jnp.floor(size / weight) - 2.0 * jnp.floor(size / (2.0 * weight))
    return jnp.where(lane < DIGITS, jnp.where(value < 0, -bits, bits), 0.0)


def value_of(digits):
    lane, weight = digit_weights(digits.shape)
    return jnp.sum(jnp.where(lane < DIGITS, digits * weight, 0.0))


def forward(feats, m, w_conv, w_proj, cols, slope, hid, clips, frames, block, put):
    chan = feats.shape[-1]
    for c in range(clips):
        x = feats[m, c].astype(F32)
        row = lax.broadcasted_iota(jnp.int32, x.shape, 0)
        base = c * frames
        cols[m, base : base + frames, 0:chan] = jnp.where(row == 0, 0.0, pltpu.roll(x, 1, 0)).astype(BF16)
        cols[m, base : base + frames, chan : 2 * chan] = feats[m, c]
        cols[m, base : base + frames, 2 * chan : 3 * chan] = jnp.where(
            row == frames - 1, 0.0, pltpu.roll(x, frames - 1, 0)
        ).astype(BF16)

    def step(i, _):
        rows = pl.ds(pl.multiple_of(i * block, block), block)
        pre = dot(cols[m, rows, :], w_conv[...], NN)
        sigma = jax.nn.sigmoid(pre)
        hidden = (pre * sigma).astype(BF16)
        hid[m, rows, :] = hidden
        slope[m, rows, :] = sigma * (1.0 + pre * (1.0 - sigma))
        emb = dot(hidden, w_proj[...], NN).astype(BF16)
        values = emb.astype(F32)
        inv = lax.rsqrt(jnp.sum(values * values, axis=1, keepdims=True) + epsilon)
        put(i, emb, jnp.broadcast_to(inv, (block, LANES)))
        return 0

    lax.fori_loop(0, clips * frames // block, step, 0)


def backward(m, w_proj, cols, slope, hid, gemb, gpre, total, block, rows_total):
    def step(i, _):
        rows = pl.ds(pl.multiple_of(i * block, block), block)
        grad = dot(gemb[m, rows, :], w_proj[...], NT) * slope[m, rows, :]
        gpre[m, rows, :] = grad.astype(BF16)
        return 0

    lax.fori_loop(0, rows_total // block, step, 0)
    conv_rows = cols.shape[-1]

    def conv_step(i, _):
        at = pl.multiple_of(i * 256, 256)
        total[pl.ds(at, 256), :] = dot(cols[m, :, pl.ds(at, 256)], gpre[m], TN)
        return 0

    lax.fori_loop(0, conv_rows // 256, conv_step, 0)

    def proj_step(i, _):
        at = pl.multiple_of(i * 256, 256)
        total[pl.ds(conv_rows + at, 256), :] = dot(hid[m, :, pl.ds(at, 256)], gemb[m], TN)
        return 0

    lax.fori_loop(0, hid.shape[-1] // 256, proj_step, 0)


def hand_over(total, keep, send, m, half):
    width = total.shape[1] // 2
    for j in range(width // LANES):
        mine = pl.ds(pl.multiple_of(half * width + j * LANES, LANES), LANES)
        other = pl.ds(pl.multiple_of((1 - half) * width + j * LANES, LANES), LANES)
        keep[m, j] = total[:, mine]
        send[m, j] = total[:, other].astype(BF16)


def kernel(
    frames, clips, halo, lengths, labels, feats, wac, wap, wvc, wvp, keep, send, stats,
    cols, slope, hid, gemb, gpre, total, emb_a, emb_v, inv_a, inv_v, gacc, giacc,
):
    me = lax.axis_index("tm")
    half = lax.rem(me, 2)
    rows_total = clips * frames
    start = me * (frames - 2 * halo) - halo if halo else 0
    first_clip = 0 if halo else me * clips
    block = 256 if frames % 256 == 0 else TILE
    per_clip = frames // block

    for c in range(clips):
        for lo in (0, PAD + frames):
            emb_a[c, lo : lo + PAD, :] = jnp.zeros((PAD, emb_a.shape[2]), BF16)
            inv_a[c, lo : lo + PAD, :] = jnp.zeros((PAD, LANES), F32)

    def put_a(i, emb, inv):
        c = i // per_clip
        at = pl.multiple_of(PAD + lax.rem(i, per_clip) * block, PAD)
        emb_a[c, pl.ds(at, block), :] = emb
        inv_a[c, pl.ds(at, block), :] = inv

    def put_v(i, emb, inv):
        at = pl.multiple_of(i * block, block)
        emb_v[pl.ds(at, block), :] = emb
        inv_v[pl.ds(at, block), :] = inv

    forward(feats, 1, wvc, wvp, cols, slope, hid, clips, frames, block, put_v)
    forward(feats, 0, wac, wap, cols, slope, hid, clips, frames, block, put_a)

    gacc[...] = jnp.zeros(gacc.shape, F32)
    giacc[...] = jnp.zeros(giacc.shape, F32)
    tiles = frames // TILE
    row = lax.broadcasted_iota(jnp.int32, (TILE, WIN), 0)
    col = lax.broadcasted_iota(jnp.int32, (TILE, WIN), 1)
    shift = col - row - PAD
    in_band = (shift >= -SPAN) & (shift <= SPAN)
    row_1 = lax.broadcasted_iota(jnp.int32, (TILE, 1), 0)

    def tile_step(i, loss):
        c = i // tiles
        first = pl.multiple_of(lax.rem(i, tiles) * TILE, TILE)
        length = lengths[first_clip + c]
        label = labels[first_clip + c]
        here = pl.ds(pl.multiple_of(i * TILE, TILE), TILE)
        window = pl.ds(first, WIN)
        ev = emb_v[here, :]
        wa = emb_a[c, window, :]
        iv = inv_v[here, 0:1]
        ia = inv_a[c, window, :].T
        dots = dot(ev, wa, NT)
        scores = logit_sharpening_divisor * dots * iv * ia
        t = start + first + row_1
        u = start + first - PAD + col
        inside = t < length
        valid = in_band & inside & (u >= 0) & (u < length)
        target = t + label
        counted = inside & (target >= 0) & (target < length)
        hit = shift == label
        weights = jnp.where(valid, jnp.exp(scores), 0.0)
        sums = jnp.where(inside, jnp.sum(weights, axis=1, keepdims=True), 1.0)
        picked = jnp.sum(jnp.where(hit, scores, 0.0), axis=1, keepdims=True)
        own = (first + row_1 >= halo) & (first + row_1 < frames - halo)
        loss = loss + jnp.sum(jnp.where(counted & own, jnp.log(sums) - picked, 0.0))
        scale = jnp.where(counted, logit_sharpening_divisor * loss_scale, 0.0)
        grad = scale * (weights / sums - jnp.where(hit, 1.0, 0.0))
        gd = (grad * iv * ia).astype(BF16)
        by_dots = grad * dots
        giv = jnp.sum(by_dots * ia, axis=1, keepdims=True)
        gia = jnp.sum((by_dots * iv).T, axis=1, keepdims=True)
        glip = dot(gd, wa, NN) - (iv * iv * iv * giv) * ev.astype(F32)
        gemb[1, here, :] = jnp.where(own, glip, 0.0).astype(BF16)
        gacc[c, window, :] += dot(gd, ev, TN)
        giacc[c, window, :] += jnp.broadcast_to(gia, (WIN, LANES))
        return loss

    loss = lax.fori_loop(0, clips * tiles, tile_step, jnp.zeros((), F32))

    def audio_step(i, _):
        c = i // per_clip
        at = pl.ds(pl.multiple_of(PAD + lax.rem(i, per_clip) * block, PAD), block)
        inv = inv_a[c, at, 0:1]
        grad = gacc[c, at, :] - (inv * inv * inv * giacc[c, at, 0:1]) * emb_a[c, at, :].astype(F32)
        if halo:
            at_row = lax.rem(i, per_clip) * block + lax.broadcasted_iota(jnp.int32, (block, 1), 0)
            grad = jnp.where((at_row >= halo) & (at_row < frames - halo), grad, 0.0)
        gemb[0, pl.ds(pl.multiple_of(i * block, block), block), :] = grad.astype(BF16)
        return 0

    lax.fori_loop(0, rows_total // block, audio_step, 0)

    count = jnp.zeros((), F32)
    for c in range(clips):
        count = count + (lengths[first_clip + c] - jnp.abs(labels[first_clip + c])).astype(F32)
    if halo:
        count = jnp.where(me == 0, count, 0.0)
    stats[...] = jnp.zeros(stats.shape, BF16)
    stats[0:1, :] = digits_of(loss).astype(BF16)
    stats[16:17, :] = digits_of(count).astype(BF16)

    backward(1, wvp, cols, slope, hid, gemb, gpre, total, block, rows_total)
    hand_over(total, keep, send, 1, half)
    backward(0, wap, cols, slope, hid, gemb, gpre, total, block, rows_total)
    hand_over(total, keep, send, 0, half)


def local_grads(halo, lengths, labels, feats, wac, wap, wvc, wvp):
    _, clips, frames, chan = feats.shape
    width = wap.shape[0]
    rows = clips * frames
    taps = wac.shape[0]
    grad_rows = taps * chan + width
    wac = wac.reshape(taps * chan, width)
    wvc = wvc.reshape(taps * chan, width)
    blocks = width // 2 // LANES
    smem = pl.BlockSpec(memory_space=pltpu.SMEM)
    vmem = pl.BlockSpec(memory_space=pltpu.VMEM)
    return pl.pallas_call(
        functools.partial(kernel, frames, clips, halo),
        out_shape=(
            jax.ShapeDtypeStruct((2, blocks, grad_rows, LANES), F32),
            jax.ShapeDtypeStruct((2, blocks, grad_rows, LANES), BF16),
            jax.ShapeDtypeStruct((32, LANES), BF16),
        ),
        in_specs=[smem, smem] + [vmem] * 5,
        out_specs=(vmem, vmem, vmem),
        scratch_shapes=[
            pltpu.VMEM((2, rows, taps * chan), BF16),
            pltpu.VMEM((2, rows, width), F32),
            pltpu.VMEM((2, rows, width), BF16),
            pltpu.VMEM((2, rows, width), BF16),
            pltpu.VMEM((2, rows, width), BF16),
            pltpu.VMEM((grad_rows, width), F32),
            pltpu.VMEM((clips, frames + 2 * PAD, width), BF16),
            pltpu.VMEM((rows, width), BF16),
            pltpu.VMEM((clips, frames + 2 * PAD, LANES), F32),
            pltpu.VMEM((rows, LANES), F32),
            pltpu.VMEM((clips, frames + 2 * PAD, width), F32),
            pltpu.VMEM((clips, frames + 2 * PAD, LANES), F32),
        ],
        compiler_params=pltpu.CompilerParams(vmem_limit_bytes=60 * 1024 * 1024),
    )(lengths, labels, feats, wac, wap, wvc, wvp)


def swap(value, axis, bit):
    return lax.ppermute(value, axis, [(i, i ^ bit) for i in range(lax.axis_size(axis))])


def pick(value, index):
    return lax.dynamic_index_in_dim(value, index, 0, keepdims=False)


def halve(value, axis, bit, tile=None):
    me = (lax.axis_index(axis) // bit) % 2
    parts = value.reshape(2, -1, LANES)
    out = pick(parts, 1 - me).astype(BF16)
    if tile is not None:
        out = jnp.concatenate([out, tile])
    got = swap(out, axis, bit)
    rows = parts.shape[1]
    mine = pick(parts, me).astype(F32) + got[:rows].astype(F32)
    return mine if tile is None else (mine, (tile.astype(F32) + got[rows:].astype(F32)).astype(BF16))


def double(value, axis, bit):
    me = (lax.axis_index(axis) // bit) % 2
    got = swap(value, axis, bit)
    return jnp.stack([jnp.where(me == 0, value, got), jnp.where(me == 0, got, value)]).reshape(-1, LANES)


def quarter(parts, axis, bit, tile):
    me = (lax.axis_index(axis) // bit) % 4
    rows = parts.shape[1]
    mine = pick(parts, me).astype(F32)
    whole = tile.astype(F32)
    for k in (1, 2, 3):
        got = swap(jnp.concatenate([pick(parts, me ^ k).astype(BF16), tile]), axis, k * bit).astype(F32)
        mine = mine + got[:rows]
        whole = whole + got[rows:]
    return mine, whole


def quadruple(value, axis, bit):
    me = (lax.axis_index(axis) // bit) % 4
    got = [value] + [swap(value, axis, k * bit) for k in (1, 2, 3)]
    out = []
    for j in range(4):
        k = me ^ j
        out.append(jnp.where(k == 0, got[0], jnp.where(k == 1, got[1], jnp.where(k == 2, got[2], got[3]))))
    return jnp.stack(out)


def bits_of(axis):
    size, bits = lax.axis_size(axis), []
    bit = 1
    while bit < size:
        bits.append(bit)
        bit *= 2
    return bits


def reduce_all(keep, send, stats):
    shape = keep.shape
    tm_bits, clip_bits = bits_of("tm"), bits_of("clip")
    got = swap(jnp.concatenate([send.reshape(-1, LANES), stats]), "tm", 1)
    rows = shape[0] * shape[1] * shape[2]
    total = keep.reshape(rows, LANES) + got[:rows].astype(F32)
    tile = (stats.astype(F32) + got[rows:].astype(F32)).astype(BF16)
    first, second = total.reshape(2, -1, LANES)
    for bit in tm_bits[1:]:
        first, tile = halve(first, "tm", bit, tile)
        second = halve(second, "tm", bit)
    singles, last = clip_bits[:-2], clip_bits[-2]
    order_1 = singles
    order_2 = singles[1::-1] + singles[2:]
    for bit_1, bit_2 in zip(order_1, order_2):
        first, tile = halve(first, "clip", bit_1, tile)
        second = halve(second, "clip", bit_2)
    parts = jnp.concatenate([first.reshape(4, -1, LANES), second.reshape(4, -1, LANES)], axis=1)
    mine, tile = quarter(parts, "clip", last, tile)
    parts = quadruple(mine.astype(BF16), "clip", last)
    n = parts.shape[1] // 2
    first, second = parts[:, :n].reshape(-1, LANES), parts[:, n:].reshape(-1, LANES)
    for bit_1, bit_2 in zip(order_1[::-1], order_2[::-1]):
        first = double(first, "clip", bit_1)
        second = double(second, "clip", bit_2)
    for bit in tm_bits[:0:-1]:
        first = double(first, "tm", bit)
        second = double(second, "tm", bit)
    whole = double(jnp.concatenate([first, second]), "tm", 1)
    halves = whole.reshape(2, shape[0], shape[1], shape[2], LANES)
    return halves, tile


def shards(
    audio_feats, lip_feats, lengths, labels, w_audio_conv, w_audio_proj, w_lip_conv, w_lip_proj
):
    both = jnp.stack([audio_feats, lip_feats])
    peers = lax.axis_size("tm")
    halo = 0
    if peers == 2 and both.shape[1] % 2 == 0:
        me = lax.axis_index("tm")
        parts = both.reshape(2, 2, both.shape[1] // 2, *both.shape[2:])
        mine = lax.dynamic_index_in_dim(parts, me, 1, keepdims=False)
        got = swap(lax.dynamic_index_in_dim(parts, 1 - me, 1, keepdims=False), "tm", 1)
        feats = jnp.concatenate(
            [jnp.where(me == 0, mine, got), jnp.where(me == 0, got, mine)], axis=2
        )
    else:
        halo = HALO
        after = [(i, i + 1) for i in range(peers - 1)]
        before = [(i + 1, i) for i in range(peers - 1)]
        feats = jnp.concatenate(
            [
                lax.ppermute(both[:, :, -HALO:], "tm", after),
                both,
                lax.ppermute(both[:, :, :HALO], "tm", before),
            ],
            axis=2,
        )
    keep, send, stats = local_grads(
        halo, lengths, labels, feats, w_audio_conv, w_audio_proj, w_lip_conv, w_lip_proj
    )
    halves, tile = reduce_all(keep, send, stats)
    loss_sum, count = value_of(tile[0:1].astype(F32)), value_of(tile[16:17].astype(F32))
    scale = 1.0 / count
    taps, chan, width = w_audio_conv.shape
    full = halves.transpose(1, 3, 0, 2, 4).reshape(2, -1, width).astype(F32) * scale
    conv = full[:, : taps * chan].reshape(2, taps, chan, width)
    proj = full[:, taps * chan :]
    return (loss_sum * scale, conv[0], proj[0], conv[1], proj[1])


def solution(mesh):
    placed = (
        P("clip", "tm", None),
        P("clip", "tm", None),
        P("clip"),
        P("clip"),
        P(),
        P(),
        P(),
        P(),
    )
    return jax.shard_map(
        shards, mesh=mesh, in_specs=placed, out_specs=(P(), P(), P(), P(), P()), check_vma=False
    )
```

time: 291 us -> 122 us (0.42)
  blocking collectives: 81.7 us -> 0 us
  waiting for transfers between devices: 105 us -> 38 us
  Pallas kernels: 0 us -> 25.8 us
  matrix products: 22.9 us -> 0 us
  local copies, waits for them, and re-layouts: 34.6 us -> 18.6 us
  between operations: 17.7 us -> 3.38 us
  starting transfers between devices: 11.8 us -> 22.1 us
    psum x1 -> x0, waiting for transfers between devices: 105 us -> none  [shards(): lax.psum((grad_ac, grad_vc, grad_ap, grad_vp, loss_local), ('clip', 'tm'))]
    psum x2 -> x0, blocking collectives: 81.7 us -> none  [the longest x1 43.5 us: shards(): lax.psum(jnp.sum((lengths - jnp.abs(labels)).astype(jnp.float32)), 'clip')]
    ppermute x6 -> x17, waiting for transfers between devices: 0.02 us -> 38 us  [swap(): lax.ppermute(value, axis, [(i, i ^ bit) for i in range(lax.axis_size(axis...]
    pallas_call x0 -> x1, Pallas kernels: none -> 25.8 us  [local_grads(): pl.pallas_call(functools.partial(kernel, frames, clips, halo), out_shape=...]
    dot_general x13 -> x0, matrix products: 22.9 us -> none  [the longest x2 4.29 us: conv_grad(): jnp.einsum('rk,re->ke', columns, grad_before, preferred_element_type=jnp....]
    reshape x6 -> x0, local copies, waits for them, and re-layouts: 12.5 us -> none  [the longest x2 4.77 us: spread_band(): return flat_band.reshape(clip_num, row_num, wide_len)]
    ppermute x6 -> x17, starting transfers between devices: 11.8 us -> 22.1 us  [swap(): lax.ppermute(value, axis, [(i, i ^ bit) for i in range(lax.axis_size(axis...]
    unnamed x96 -> x12, local copies, waits for them, and re-layouts: 12 us -> 3.95 us
  transfers between devices with their start and end apart: 7 -> 17, of which waited for: 1 -> 16; matrix products, arithmetic and copies ran while one was open for 5% -> 2% of each run, Pallas kernels for 0% -> 0%
where the time goes in v1:
time: 122 us; the launch traced here: 121 us
  waiting for transfers between devices  38 us (31%)
  Pallas kernels  25.8 us (21%)
  starting transfers between devices  22.1 us (18%)
  local copies, waits for them, and re-layouts  18.6 us (15%)
  other arithmetic  13.6 us (11%)
  between operations  3.38 us (3%)
    ppermute x17, waiting for transfers between devices, swap(): lax.ppermute(value, axis, [(i, i ^ bit) for i in range(lax.axis_size(axis...  38 us
    pallas_call x1, Pallas kernels, local_grads(): pl.pallas_call(functools.partial(kernel, frames, clips, halo), out_shape=...  25.8 us
    ppermute x17, starting transfers between devices, swap(): lax.ppermute(value, axis, [(i, i ^ bit) for i in range(lax.axis_size(axis...  22.1 us
    mul x1, local copies, waits for them, and re-layouts, shards(): halves.transpose(1, 3, 0, 2, 4).reshape(2, -1, width).astype(F32) * scale  5.97 us
    slice x3, local copies, waits for them, and re-layouts, shards(): return (loss_sum * scale, conv[0], proj[0], conv[1], proj[1])  5.31 us
    unnamed x12, local copies, waits for them, and re-layouts  3.95 us
    squeeze x1, local copies, waits for them, and re-layouts, shards(): return (loss_sum * scale, conv[0], proj[0], conv[1], proj[1])  3.05 us
    mul x1, other arithmetic, shards(): halves.transpose(1, 3, 0, 2, 4).reshape(2, -1, width).astype(F32) * scale  2.75 us
  transfers between devices with their start and end apart: 17, of which 16 were waited for; matrix products, arithmetic and copies ran while one was open for 2% of the time, Pallas kernels for 0%

profile of v1, /device:TPU:0, one launch (start us, length us, event | category | flops | bytes accessed | tf_op | source)
XLA Modules:
  0.0 121.4 jit_solution(5104549355540739815)
XLA Ops:
  5.0 25.8 %shard_map.119 = (f32[2,2,1280,128]{3,2,1,0:T(8,128)}, bf16[2,2,1280,128]{3,2,1,0:T(8,128)(2,1)}, bf16[32,128]{1,0:T(8,128)(2,1)}) custom-call(s32[4]{0:T(128)} %lengths.1, s32[4]{0:T(128)} %labels.1, bf16[2,2,512,256]{3,2,1,0:T(8,128)(2,1)} %pad_maximum_fusion.2.feats, bf16[768,512]{1,0:T(8,128)(2,1)} %bitcast.135, bf16[512,512]{1,0:T(8,128)(2,1)} %wap.1, ...), custom_call_target="tpu_custom_call" | custom-call | tf_op jit(solution)/shard_map/pallas_call | solution.py:233
  30.8 2.6 %pad_maximum_fusion = bf16[5152,128]{1,0:T(8,128)(2,1)} fusion(bf16[32,128]{1,0:T(8,128)(2,1)} %get-tuple-element.8, bf16[5120,128]{1,0:T(8,128)(2,1)} %bitcast.132), kind=kLoop, calls=%fused_computation.2 | loop fusion | flops 2637824 | bytes 2637824 | tf_op jit(solution)/shard_map/concatenate | solution.py:320
  33.8 3.0 %collective-permute-done.1 = bf16[5152,128]{1,0:T(8,128)(2,1)} collective-permute-done((bf16[5152,128]{1,0:T(8,128)(2,1)}, bf16[5152,128]{1,0:T(8,128)(2,1)}, u32[]{:S(2)}, u32[]{:S(2)}) %collective-permute-start.1) | collective-permute-done | bytes 1318944 | tf_op jit(solution)/shard_map/ppermute | solution.py:261
  36.8 1.8 %bitcast_add_fusion = f32[5120,128]{1,0:T(8,128)S(1)} fusion(f32[2,2,1280,128]{3,2,1,0:T(8,128)S(1)} %copy-done.1, bf16[5152,128]{1,0:T(8,128)(2,1)} %collective-permute-done.1), kind=kLoop, calls=%fused_computation.1 | loop fusion | flops 1310720 | bytes 6553600 | tf_op jit(solution)/shard_map/add | solution.py:322
  38.9 3.0 %collective-permute-start.4 = (bf16[1280,128]{1,0:T(8,128)(2,1)S(1)}, bf16[1280,128]{1,0:T(8,128)(2,1)S(1)}, u32[]{:S(2)}, u32[]{:S(2)}) collective-permute-start(bf16[1280,128]{1,0:T(8,128)(2,1)S(1)} %fusion.5), channel_id=1, source_target_pairs={{0,4},{2,6},{4,0},{6,2},{8,12},{10,14},{12,8},{14,10},{16,20},{18,... | collective-permute-start | bytes 983048 | tf_op jit(solution)/shard_map/ppermute | solution.py:261
  44.2 5.7 %collective-permute-done.4 = bf16[1280,128]{1,0:T(8,128)(2,1)S(1)} collective-permute-done((bf16[1280,128]{1,0:T(8,128)(2,1)S(1)}, bf16[1280,128]{1,0:T(8,128)(2,1)S(1)}, u32[]{:S(2)}, u32[]{:S(2)}) %collective-permute-start.4) | collective-permute-done | bytes 327712 | tf_op jit(solution)/shard_map/ppermute | solution.py:261
  50.0 1.8 %collective-permute-start.5 = (bf16[640,128]{1,0:T(8,128)(2,1)S(1)}, bf16[640,128]{1,0:T(8,128)(2,1)S(1)}, u32[]{:S(2)}, u32[]{:S(2)}) collective-permute-start(bf16[640,128]{1,0:T(8,128)(2,1)S(1)} %fusion.7), channel_id=1, source_target_pairs={{0,2},{2,0},{4,6},{6,4},{8,10},{10,8},{12,14},{14,12},{16,18},{18,... | collective-permute-start | bytes 491528 | tf_op jit(solution)/shard_map/ppermute | solution.py:261
  53.5 2.4 %collective-permute-done.5 = bf16[640,128]{1,0:T(8,128)(2,1)S(1)} collective-permute-done((bf16[640,128]{1,0:T(8,128)(2,1)S(1)}, bf16[640,128]{1,0:T(8,128)(2,1)S(1)}, u32[]{:S(2)}, u32[]{:S(2)}) %collective-permute-start.5) | collective-permute-done | bytes 163872 | tf_op jit(solution)/shard_map/ppermute | solution.py:261
  55.9 2.1 %collective-permute-done.3 = bf16[672,128]{1,0:T(8,128)(2,1)S(1)} collective-permute-done((bf16[672,128]{1,0:T(8,128)(2,1)S(1)}, bf16[672,128]{1,0:T(8,128)(2,1)S(1)}, u32[]{:S(2)}, u32[]{:S(2)}) %collective-permute-start.3) | collective-permute-done | bytes 172064 | tf_op jit(solution)/shard_map/ppermute | solution.py:261
  58.1 1.7 %collective-permute-start.6 = (bf16[352,128]{1,0:T(8,128)(2,1)S(1)}, bf16[352,128]{1,0:T(8,128)(2,1)S(1)}, u32[]{:S(2)}, u32[]{:S(2)}) collective-permute-start(bf16[352,128]{1,0:T(8,128)(2,1)S(1)} %get-tuple-element.50), channel_id=1, source_target_pairs={{0,8},{2,10},{4,12},{6,14},{8,0},{10,2},{12,4},{14,6},{16,24},{18,... | collective-permute-start | bytes 270344 | tf_op jit(solution)/shard_map/ppermute | solution.py:261
  59.8 2.6 %collective-permute-start.7 = (bf16[352,128]{1,0:T(8,128)(2,1)S(1)}, bf16[352,128]{1,0:T(8,128)(2,1)S(1)}, u32[]{:S(2)}, u32[]{:S(2)}) collective-permute-start(bf16[352,128]{1,0:T(8,128)(2,1)S(1)} %get-tuple-element.51), channel_id=1, source_target_pairs={{0,16},{2,18},{4,20},{6,22},{8,24},{10,26},{12,28},{14,30},{16,0},... | collective-permute-start | bytes 270344 | tf_op jit(solution)/shard_map/ppermute | solution.py:261
  62.8 4.3 %collective-permute-done.7 = bf16[352,128]{1,0:T(8,128)(2,1)S(1)} collective-permute-done((bf16[352,128]{1,0:T(8,128)(2,1)S(1)}, bf16[352,128]{1,0:T(8,128)(2,1)S(1)}, u32[]{:S(2)}, u32[]{:S(2)}) %collective-permute-start.7) | collective-permute-done | bytes 90144 | tf_op jit(solution)/shard_map/ppermute | solution.py:261
  67.1 1.7 %collective-permute-done.8 = bf16[352,128]{1,0:T(8,128)(2,1)S(1)} collective-permute-done((bf16[352,128]{1,0:T(8,128)(2,1)S(1)}, bf16[352,128]{1,0:T(8,128)(2,1)S(1)}, u32[]{:S(2)}, u32[]{:S(2)}) %collective-permute-start.8) | collective-permute-done | bytes 90144 | tf_op jit(solution)/shard_map/ppermute | solution.py:261
  68.9 1.7 %collective-permute-start.11 = (bf16[320,128]{1,0:T(8,128)(2,1)S(1)}, bf16[320,128]{1,0:T(8,128)(2,1)S(1)}, u32[]{:S(2)}, u32[]{:S(2)}) collective-permute-start(bf16[320,128]{1,0:T(8,128)(2,1)S(1)} %fusion.13), channel_id=1, source_target_pairs={{0,24},{2,26},{4,28},{6,30},{8,16},{10,18},{12,20},{14,22},{16,8},... | collective-permute-start | bytes 245768 | tf_op jit(solution)/shard_map/ppermute | solution.py:261
  70.6 2.6 %collective-permute-start.10 = (bf16[320,128]{1,0:T(8,128)(2,1)S(1)}, bf16[320,128]{1,0:T(8,128)(2,1)S(1)}, u32[]{:S(2)}, u32[]{:S(2)}) collective-permute-start(bf16[320,128]{1,0:T(8,128)(2,1)S(1)} %fusion.13), channel_id=1, source_target_pairs={{0,16},{2,18},{4,20},{6,22},{8,24},{10,26},{12,28},{14,30},{16,0},... | collective-permute-start | bytes 245768 | tf_op jit(solution)/shard_map/ppermute | solution.py:261
  75.3 1.7 %collective-permute-done.10 = bf16[320,128]{1,0:T(8,128)(2,1)S(1)} collective-permute-done((bf16[320,128]{1,0:T(8,128)(2,1)S(1)}, bf16[320,128]{1,0:T(8,128)(2,1)S(1)}, u32[]{:S(2)}, u32[]{:S(2)}) %collective-permute-start.10) | collective-permute-done | bytes 81952 | tf_op jit(solution)/shard_map/ppermute | solution.py:261
  80.3 4.8 %collective-permute-done.12 = bf16[640,128]{1,0:T(8,128)(2,1)S(1)} collective-permute-done((bf16[640,128]{1,0:T(8,128)(2,1)S(1)}, bf16[640,128]{1,0:T(8,128)(2,1)S(1)}, u32[]{:S(2)}, u32[]{:S(2)}) %collective-permute-start.12) | collective-permute-done | bytes 163872 | tf_op jit(solution)/shard_map/ppermute | solution.py:261
  87.6 4.7 %collective-permute-done.13 = bf16[1280,128]{1,0:T(8,128)(2,1)S(1)} collective-permute-done((bf16[1280,128]{1,0:T(8,128)(2,1)S(1)}, bf16[1280,128]{1,0:T(8,128)(2,1)S(1)}, u32[]{:S(2)}, u32[]{:S(2)}) %collective-permute-start.13) | collective-permute-done | bytes 327712 | tf_op jit(solution)/shard_map/ppermute | solution.py:261
  97.4 1.8 %broadcast_select_fusion.1 = (bf16[5120,128]{1,0:T(8,128)(2,1)S(1)}, bf16[5120,128]{1,0:T(8,128)(2,1)S(1)}) fusion(bf16[5120,128]{1,0:T(8,128)(2,1)} %collective-permute-done.16, pred[]{:T(512)S(6)} %eq.69, bf16[2560,128]{1,0:T(8,128)(2,1)S(1)} %bitcast.111, bf16[2560,128]{1,0:T(8,128)(2,1)S(1)} %bitcast.109), kind=kLoop, calls=%fused_computation.5 | loop fusion | flops 3932160 | bytes 5242881 | tf_op jit(solution)/shard_map/jit(_where)/select_n | solution.py:283
  99.3 2.7 %multiply_bitcast_fusion = f32[2,1280,2,2,128]{4,1,3,0,2:T(8,128)} fusion(bf16[1,2,2,1280,128]{4,3,2,1,0:T(8,128)(2,1)S(1)} %bitcast.113, bf16[1,2,2,1280,128]{4,3,2,1,0:T(8,128)(2,1)S(1)} %bitcast.112, f32[]{:T(128)S(6)} %div.33), kind=kLoop, calls=%fused_computation | loop fusion | flops 3932160 | bytes 7864324 | tf_op jit(solution)/shard_map/mul | solution.py:383
  102.0 6.0 %copy.26 = f32[2,1280,2,2,128]{1,4,3,2,0:T(8,128)} copy(f32[2,1280,2,2,128]{4,1,3,0,2:T(8,128)} %multiply_bitcast_fusion) | data formatting | bytes 10485760 | tf_op jit(solution)/shard_map/mul | solution.py:383
  108.0 3.0 %slice_bitcast_fusion = (f32[512,512]{0,1:T(8,128)}, f32[512,512]{0,1:T(8,128)}) fusion(f32[2,1280,512]{1,2,0:T(8,128)} %bitcast.106), kind=kLoop, calls=%fused_computation.10 | loop fusion | bytes 4194304 | tf_op jit(solution)/shard_map/squeeze | solution.py:386
  111.0 2.1 %fusion.25 = (f32[1,768,512]{1,2,0:T(8,128)S(1)}, f32[1,768,512]{1,2,0:T(8,128)S(1)}) fusion(f32[2,1280,512]{1,2,0:T(8,128)} %bitcast.107), kind=kLoop, calls=%fused_computation.89 | loop fusion | bytes 6291456 | tf_op jit(solution)/shard_map/slice | solution.py:386
  114.7 2.6 %copy.30 = f32[512,512]{1,0:T(8,128)} copy(f32[512,512]{0,1:T(8,128)} %get-tuple-element.23) | data formatting | bytes 2097152
  (69 shorter events, 25.8 us)
Async XLA Ops:
  0.6 3.3 %copy-start.3 = (bf16[4,256,256]{2,1,0:T(8,128)(2,1)S(1)}, bf16[4,256,256]{2,1,0:T(8,128)(2,1)}, u32[]{:S(2)}) copy-start(bf16[4,256,256]{2,1,0:T(8,128)(2,1)} %param.9) | copy-start | bytes 1572868
  0.6 3.2 %copy-start.2 = (bf16[4,256,256]{2,1,0:T(8,128)(2,1)S(1)}, bf16[4,256,256]{2,1,0:T(8,128)(2,1)}, u32[]{:S(2)}) copy-start(bf16[4,256,256]{2,1,0:T(8,128)(2,1)} %param.8) | copy-start | bytes 1572868
  1.8 2.1 %collective-permute-start = (bf16[2,2,256,256]{3,2,1,0:T(8,128)(2,1)S(1)}, bf16[2,2,256,256]{3,2,1,0:T(8,128)(2,1)S(1)}, u32[]{:S(2)}, u32[]{:S(2)}) collective-permute-start(bf16[2,2,256,256]{3,2,1,0:T(8,128)(2,1)S(1)} %fusion.1), channel_id=1, source_target_pairs={{0,1},{1,0},{2,3},{3,2},{4,5},{5,4},{6,7},{7,6},{8,9},{9,8},{10,11... | collective-permute-start | bytes 1572872 | tf_op jit(solution)/shard_map/ppermute | solution.py:261
  30.8 6.0 %copy-start.1 = (f32[2,2,1280,128]{3,2,1,0:T(8,128)S(1)}, f32[2,2,1280,128]{3,2,1,0:T(8,128)}, u32[]{:S(2)}) copy-start(f32[2,2,1280,128]{3,2,1,0:T(8,128)} %get-tuple-element.10) | copy-start | bytes 7864324
  33.4 3.4 %collective-permute-start.1 = (bf16[5152,128]{1,0:T(8,128)(2,1)}, bf16[5152,128]{1,0:T(8,128)(2,1)}, u32[]{:S(2)}, u32[]{:S(2)}) collective-permute-start(bf16[5152,128]{1,0:T(8,128)(2,1)} %pad_maximum_fusion), channel_id=1, source_target_pairs={{0,1},{1,0},{2,3},{3,2},{4,5},{5,4},{6,7},{7,6},{8,9},{9,8},{10,11... | collective-permute-start | bytes 3956744 | tf_op jit(solution)/shard_map/ppermute | solution.py:261
  38.6 3.2 %copy-start.4 = (bf16[32,128]{1,0:T(8,128)(2,1)S(1)}, bf16[32,128]{1,0:T(8,128)(2,1)}, u32[]{:S(2)}) copy-start(bf16[32,128]{1,0:T(8,128)(2,1)} %get-tuple-element.8) | copy-start | bytes 24580
  38.9 11.0 %collective-permute-start.4 = (bf16[1280,128]{1,0:T(8,128)(2,1)S(1)}, bf16[1280,128]{1,0:T(8,128)(2,1)S(1)}, u32[]{:S(2)}, u32[]{:S(2)}) collective-permute-start(bf16[1280,128]{1,0:T(8,128)(2,1)S(1)} %fusion.5), channel_id=1, source_target_pairs={{0,4},{2,6},{4,0},{6,2},{8,12},{10,14},{12,8},{14,10},{16,20},{18,... | collective-permute-start | bytes 983048 | tf_op jit(solution)/shard_map/ppermute | solution.py:261
  42.6 9.7 %collective-permute-start.2 = (bf16[1312,128]{1,0:T(8,128)(2,1)S(1)}, bf16[1312,128]{1,0:T(8,128)(2,1)S(1)}, u32[]{:S(2)}, u32[]{:S(2)}) collective-permute-start(bf16[1312,128]{1,0:T(8,128)(2,1)S(1)} %pad_maximum_fusion.5), channel_id=1, source_target_pairs={{0,2},{2,0},{4,6},{6,4},{8,10},{10,8},{12,14},{14,12},{16,18},{18,... | collective-permute-start | bytes 1007624 | tf_op jit(solution)/shard_map/ppermute | solution.py:261
  50.0 5.9 %collective-permute-start.5 = (bf16[640,128]{1,0:T(8,128)(2,1)S(1)}, bf16[640,128]{1,0:T(8,128)(2,1)S(1)}, u32[]{:S(2)}, u32[]{:S(2)}) collective-permute-start(bf16[640,128]{1,0:T(8,128)(2,1)S(1)} %fusion.7), channel_id=1, source_target_pairs={{0,2},{2,0},{4,6},{6,4},{8,10},{10,8},{12,14},{14,12},{16,18},{18,... | collective-permute-start | bytes 491528 | tf_op jit(solution)/shard_map/ppermute | solution.py:261
  52.5 5.5 %collective-permute-start.3 = (bf16[672,128]{1,0:T(8,128)(2,1)S(1)}, bf16[672,128]{1,0:T(8,128)(2,1)S(1)}, u32[]{:S(2)}, u32[]{:S(2)}) collective-permute-start(bf16[672,128]{1,0:T(8,128)(2,1)S(1)} %pad_maximum_fusion.9), channel_id=1, source_target_pairs={{0,4},{2,6},{4,0},{6,2},{8,12},{10,14},{12,8},{14,10},{16,20},{18,... | collective-permute-start | bytes 516104 | tf_op jit(solution)/shard_map/ppermute | solution.py:261
  58.1 4.7 %collective-permute-start.6 = (bf16[352,128]{1,0:T(8,128)(2,1)S(1)}, bf16[352,128]{1,0:T(8,128)(2,1)S(1)}, u32[]{:S(2)}, u32[]{:S(2)}) collective-permute-start(bf16[352,128]{1,0:T(8,128)(2,1)S(1)} %get-tuple-element.50), channel_id=1, source_target_pairs={{0,8},{2,10},{4,12},{6,14},{8,0},{10,2},{12,4},{14,6},{16,24},{18,... | collective-permute-start | bytes 270344 | tf_op jit(solution)/shard_map/ppermute | solution.py:261
  59.8 7.3 %collective-permute-start.7 = (bf16[352,128]{1,0:T(8,128)(2,1)S(1)}, bf16[352,128]{1,0:T(8,128)(2,1)S(1)}, u32[]{:S(2)}, u32[]{:S(2)}) collective-permute-start(bf16[352,128]{1,0:T(8,128)(2,1)S(1)} %get-tuple-element.51), channel_id=1, source_target_pairs={{0,16},{2,18},{4,20},{6,22},{8,24},{10,26},{12,28},{14,30},{16,0},... | collective-permute-start | bytes 270344 | tf_op jit(solution)/shard_map/ppermute | solution.py:261
  62.4 6.4 %collective-permute-start.8 = (bf16[352,128]{1,0:T(8,128)(2,1)S(1)}, bf16[352,128]{1,0:T(8,128)(2,1)S(1)}, u32[]{:S(2)}, u32[]{:S(2)}) collective-permute-start(bf16[352,128]{1,0:T(8,128)(2,1)S(1)} %get-tuple-element.52), channel_id=1, source_target_pairs={{0,24},{2,26},{4,28},{6,30},{8,16},{10,18},{12,20},{14,22},{16,8},... | collective-permute-start | bytes 270344 | tf_op jit(solution)/shard_map/ppermute | solution.py:261
  68.9 6.4 %collective-permute-start.11 = (bf16[320,128]{1,0:T(8,128)(2,1)S(1)}, bf16[320,128]{1,0:T(8,128)(2,1)S(1)}, u32[]{:S(2)}, u32[]{:S(2)}) collective-permute-start(bf16[320,128]{1,0:T(8,128)(2,1)S(1)} %fusion.13), channel_id=1, source_target_pairs={{0,24},{2,26},{4,28},{6,30},{8,16},{10,18},{12,20},{14,22},{16,8},... | collective-permute-start | bytes 245768 | tf_op jit(solution)/shard_map/ppermute | solution.py:261
  70.6 6.4 %collective-permute-start.10 = (bf16[320,128]{1,0:T(8,128)(2,1)S(1)}, bf16[320,128]{1,0:T(8,128)(2,1)S(1)}, u32[]{:S(2)}, u32[]{:S(2)}) collective-permute-start(bf16[320,128]{1,0:T(8,128)(2,1)S(1)} %fusion.13), channel_id=1, source_target_pairs={{0,16},{2,18},{4,20},{6,22},{8,24},{10,26},{12,28},{14,30},{16,0},... | collective-permute-start | bytes 245768 | tf_op jit(solution)/shard_map/ppermute | solution.py:261
  73.2 4.7 %collective-permute-start.9 = (bf16[320,128]{1,0:T(8,128)(2,1)S(1)}, bf16[320,128]{1,0:T(8,128)(2,1)S(1)}, u32[]{:S(2)}, u32[]{:S(2)}) collective-permute-start(bf16[320,128]{1,0:T(8,128)(2,1)S(1)} %fusion.13), channel_id=1, source_target_pairs={{0,8},{2,10},{4,12},{6,14},{8,0},{10,2},{12,4},{14,6},{16,24},{18,... | collective-permute-start | bytes 245768 | tf_op jit(solution)/shard_map/ppermute | solution.py:261
  78.0 7.0 %collective-permute-start.12 = (bf16[640,128]{1,0:T(8,128)(2,1)S(1)}, bf16[640,128]{1,0:T(8,128)(2,1)S(1)}, u32[]{:S(2)}, u32[]{:S(2)}) collective-permute-start(bf16[640,128]{1,0:T(8,128)(2,1)S(1)} %bitcast.138), channel_id=1, source_target_pairs={{0,4},{2,6},{4,0},{6,2},{8,12},{10,14},{12,8},{14,10},{16,20},{18,... | collective-permute-start | bytes 491528 | tf_op jit(solution)/shard_map/ppermute | solution.py:261
  79.0 7.8 %collective-permute-start.14 = (bf16[640,128]{1,0:T(8,128)(2,1)S(1)}, bf16[640,128]{1,0:T(8,128)(2,1)S(1)}, u32[]{:S(2)}, u32[]{:S(2)}) collective-permute-start(bf16[640,128]{1,0:T(8,128)(2,1)S(1)} %bitcast.137), channel_id=1, source_target_pairs={{0,2},{2,0},{4,6},{6,4},{8,10},{10,8},{12,14},{14,12},{16,18},{18,... | collective-permute-start | bytes 491528 | tf_op jit(solution)/shard_map/ppermute | solution.py:261
  85.1 7.1 %collective-permute-start.13 = (bf16[1280,128]{1,0:T(8,128)(2,1)S(1)}, bf16[1280,128]{1,0:T(8,128)(2,1)S(1)}, u32[]{:S(2)}, u32[]{:S(2)}) collective-permute-start(bf16[1280,128]{1,0:T(8,128)(2,1)S(1)} %bitcast.133), channel_id=1, source_target_pairs={{0,2},{2,0},{4,6},{6,4},{8,10},{10,8},{12,14},{14,12},{16,18},{18,... | collective-permute-start | bytes 983048 | tf_op jit(solution)/shard_map/ppermute | solution.py:261
  86.8 7.1 %collective-permute-start.15 = (bf16[1280,128]{1,0:T(8,128)(2,1)S(1)}, bf16[1280,128]{1,0:T(8,128)(2,1)S(1)}, u32[]{:S(2)}, u32[]{:S(2)}) collective-permute-start(bf16[1280,128]{1,0:T(8,128)(2,1)S(1)} %bitcast.134), channel_id=1, source_target_pairs={{0,4},{2,6},{4,0},{6,2},{8,12},{10,14},{12,8},{14,10},{16,20},{18,... | collective-permute-start | bytes 983048 | tf_op jit(solution)/shard_map/ppermute | solution.py:261
  94.2 3.2 %collective-permute-start.16 = (bf16[5120,128]{1,0:T(8,128)(2,1)S(1)}, bf16[5120,128]{1,0:T(8,128)(2,1)}, u32[]{:S(2)}, u32[]{:S(2)}) collective-permute-start(bf16[5120,128]{1,0:T(8,128)(2,1)S(1)} %pad_maximum_fusion.1), channel_id=1, source_target_pairs={{0,1},{1,0},{2,3},{3,2},{4,5},{5,4},{6,7},{7,6},{8,9},{9,8},{10,11... | collective-permute-start | bytes 3932168 | tf_op jit(solution)/shard_map/ppermute | solution.py:261
  114.7 2.6 %copy-start = (f32[512,512]{0,1:T(8,128)S(1)}, f32[512,512]{0,1:T(8,128)}, u32[]{:S(2)}) copy-start(f32[512,512]{0,1:T(8,128)} %get-tuple-element.24) | copy-start | bytes 3145732

commit v2 on v1

--- a/solution.py
+++ b/solution.py
@@ -65,7 +65,7 @@
     def step(i, _):
         rows = pl.ds(pl.multiple_of(i * block, block), block)
         pre = dot(cols[m, rows, :], w_conv[...], NN)
-        sigma = jax.nn.sigmoid(pre)
+        sigma = 0.5 * jnp.tanh(0.5 * pre) + 0.5
         hidden = (pre * sigma).astype(BF16)
         hid[m, rows, :] = hidden
         slope[m, rows, :] = sigma * (1.0 + pre * (1.0 - sigma))
@@ -75,7 +75,7 @@
         put(i, emb, jnp.broadcast_to(inv, (block, LANES)))
         return 0
 
-    lax.fori_loop(0, clips * frames // block, step, 0)
+    lax.fori_loop(0, clips * frames // block, step, 0, unroll=True)
 
 
 def backward(m, w_proj, cols, slope, hid, gemb, gpre, total, block, rows_total):
@@ -85,7 +85,7 @@
         gpre[m, rows, :] = grad.astype(BF16)
         return 0
 
-    lax.fori_loop(0, rows_total // block, step, 0)
+    lax.fori_loop(0, rows_total // block, step, 0, unroll=True)
     conv_rows = cols.shape[-1]
 
     def conv_step(i, _):
@@ -108,12 +108,13 @@
     for j in range(width // LANES):
         mine = pl.ds(pl.multiple_of(half * width + j * LANES, LANES), LANES)
         other = pl.ds(pl.multiple_of((1 - half) * width + j * LANES, LANES), LANES)
-        keep[m, j] = total[:, mine]
-        send[m, j] = total[:, other].astype(BF16)
+        at = (m * (width // LANES) + j) * total.shape[0]
+        keep[at : at + total.shape[0], :] = total[:, mine]
+        send[at : at + total.shape[0], :] = total[:, other].astype(BF16)
 
 
 def kernel(
-    frames, clips, halo, lengths, labels, feats, wac, wap, wvc, wvp, keep, send, stats,
+    frames, clips, halo, lengths, labels, feats, wac, wap, wvc, wvp, keep, send,
     cols, slope, hid, gemb, gpre, total, emb_a, emb_v, inv_a, inv_v, gacc, giacc,
 ):
     me = lax.axis_index("tm")
@@ -189,7 +190,7 @@
         giacc[c, window, :] += jnp.broadcast_to(gia, (WIN, LANES))
         return loss
 
-    loss = lax.fori_loop(0, clips * tiles, tile_step, jnp.zeros((), F32))
+    loss = lax.fori_loop(0, clips * tiles, tile_step, jnp.zeros((), F32), unroll=clips * tiles <= 8)
 
     def audio_step(i, _):
         c = i // per_clip
@@ -209,9 +210,9 @@
         count = count + (lengths[first_clip + c] - jnp.abs(labels[first_clip + c])).astype(F32)
     if halo:
         count = jnp.where(me == 0, count, 0.0)
-    stats[...] = jnp.zeros(stats.shape, BF16)
-    stats[0:1, :] = digits_of(loss).astype(BF16)
-    stats[16:17, :] = digits_of(count).astype(BF16)
+    send_rows = send.shape[0] - 2 * PAD
+    send[send_rows : send_rows + PAD, :] = jnp.broadcast_to(digits_of(loss), (PAD, LANES)).astype(BF16)
+    send[send_rows + PAD :, :] = jnp.broadcast_to(digits_of(count), (PAD, LANES)).astype(BF16)
 
     backward(1, wvp, cols, slope, hid, gemb, gpre, total, block, rows_total)
     hand_over(total, keep, send, 1, half)
@@ -233,12 +234,11 @@
     return pl.pallas_call(
         functools.partial(kernel, frames, clips, halo),
         out_shape=(
-            jax.ShapeDtypeStruct((2, blocks, grad_rows, LANES), F32),
-            jax.ShapeDtypeStruct((2, blocks, grad_rows, LANES), BF16),
-            jax.ShapeDtypeStruct((32, LANES), BF16),
+            jax.ShapeDtypeStruct((2 * blocks * grad_rows, LANES), F32),
+            jax.ShapeDtypeStruct((2 * blocks * grad_rows + 2 * PAD, LANES), BF16),
         ),
         in_specs=[smem, smem] + [vmem] * 5,
-        out_specs=(vmem, vmem, vmem),
+        out_specs=(vmem, vmem),
         scratch_shapes=[
             pltpu.VMEM((2, rows, taps * chan), BF16),
             pltpu.VMEM((2, rows, width), F32),
@@ -314,13 +314,12 @@
     return bits
 
 
-def reduce_all(keep, send, stats):
-    shape = keep.shape
+def reduce_all(keep, send):
     tm_bits, clip_bits = bits_of("tm"), bits_of("clip")
-    got = swap(jnp.concatenate([send.reshape(-1, LANES), stats]), "tm", 1)
-    rows = shape[0] * shape[1] * shape[2]
-    total = keep.reshape(rows, LANES) + got[:rows].astype(F32)
-    tile = (stats.astype(F32) + got[rows:].astype(F32)).astype(BF16)
+    got = swap(send, "tm", 1)
+    rows = keep.shape[0]
+    total = keep + got[:rows].astype(F32)
+    tile = (send[rows:].astype(F32) + got[rows:].astype(F32)).astype(BF16)
     first, second = total.reshape(2, -1, LANES)
     for bit in tm_bits[1:]:
         first, tile = halve(first, "tm", bit, tile)
@@ -342,9 +341,53 @@
     for bit in tm_bits[:0:-1]:
         first = double(first, "tm", bit)
         second = double(second, "tm", bit)
-    whole = double(jnp.concatenate([first, second]), "tm", 1)
-    halves = whole.reshape(2, shape[0], shape[1], shape[2], LANES)
-    return halves, tile
+    mine = jnp.concatenate([first, second])
+    return mine, swap(mine, "tm", 1), tile
+
+
+def finish_kernel(mine_c, got_c, mine_p, got_p, tile, loss, ac, ap, vc, vp):
+    half = lax.rem(lax.axis_index("tm"), 2)
+    digits = tile[...].astype(F32)
+    count = value_of(digits[PAD : PAD + 1])
+    scale = 1.0 / count
+    loss[...] = jnp.broadcast_to(value_of(digits[0:1]) / count, loss.shape)
+    for mine, got, outs in ((mine_c, got_c, (ac, vc)), (mine_p, got_p, (ap, vp))):
+        for m, out in enumerate(outs):
+            blocks = mine.shape[1]
+            for j in range(blocks):
+                at = pl.multiple_of((half * blocks + j) * LANES, LANES)
+                out[:, pl.ds(at, LANES)] = mine[m, j].astype(F32) * scale
+                at = pl.multiple_of(((1 - half) * blocks + j) * LANES, LANES)
+                out[:, pl.ds(at, LANES)] = got[m, j].astype(F32) * scale
+
+
+def finish(mine, got, tile, conv_rows, width):
+    blocks = width // 2 // LANES
+    rows = conv_rows + width
+    mine = mine.reshape(2, blocks, rows, LANES)
+    got = got.reshape(2, blocks, rows, LANES)
+    steps = 4
+    conv, proj = conv_rows // steps, width // steps
+    skip = conv_rows // proj
+    conv_spec = pl.BlockSpec((2, blocks, conv, LANES), lambda i: (0, 0, i, 0))
+    proj_spec = pl.BlockSpec((2, blocks, proj, LANES), lambda i: (0, 0, skip + i, 0))
+    conv_out = pl.BlockSpec((conv, width), lambda i: (i, 0))
+    proj_out = pl.BlockSpec((proj, width), lambda i: (i, 0))
+    one = pl.BlockSpec((8, LANES), lambda i: (0, 0))
+    return pl.pallas_call(
+        finish_kernel,
+        grid=(steps,),
+        out_shape=(
+            jax.ShapeDtypeStruct((8, LANES), F32),
+            jax.ShapeDtypeStruct((conv_rows, width), F32),
+            jax.ShapeDtypeStruct((width, width), F32),
+            jax.ShapeDtypeStruct((conv_rows, width), F32),
+            jax.ShapeDtypeStruct((width, width), F32),
+        ),
+        in_specs=[conv_spec, conv_spec, proj_spec, proj_spec, pl.BlockSpec((2 * PAD, LANES), lambda i: (0, 0))],
+        out_specs=(one, conv_out, proj_out, conv_out, proj_out),
+        compiler_params=pltpu.CompilerParams(vmem_limit_bytes=32 * 1024 * 1024),
+    )(mine, got, mine, got, tile)
 
 
 def shards(
@@ -373,17 +416,13 @@
             ],
             axis=2,
         )
-    keep, send, stats = local_grads(
+    keep, send = local_grads(
         halo, lengths, labels, feats, w_audio_conv, w_audio_proj, w_lip_conv, w_lip_proj
     )
-    halves, tile = reduce_all(keep, send, stats)
-    loss_sum, count = value_of(tile[0:1].astype(F32)), value_of(tile[16:17].astype(F32))
-    scale = 1.0 / count
+    mine, got, tile = reduce_all(keep, send)
     taps, chan, width = w_audio_conv.shape
-    full = halves.transpose(1, 3, 0, 2, 4).reshape(2, -1, width).astype(F32) * scale
-    conv = full[:, : taps * chan].reshape(2, taps, chan, width)
-    proj = full[:, taps * chan :]
-    return (loss_sum * scale, conv[0], proj[0], conv[1], proj[1])
+    loss, ac, ap, vc, vp = finish(mine, got, tile.astype(BF16), taps * chan, width)
+    return (loss[0, 0], ac.reshape(w_audio_conv.shape), ap, vc.reshape(w_lip_conv.shape), vp)
 
 
 def solution(mesh):

time: 122 us -> 93 us (0.76)
  local copies, waits for them, and re-layouts: 18.6 us -> 0.84 us
  other arithmetic: 13.6 us -> 5.91 us
  between operations: 3.38 us -> 0.87 us
  Pallas kernels: 25.8 us -> 23.3 us
  waiting for transfers between devices: 38 us -> 40 us
    pallas_call x1, Pallas kernels: 25.8 us -> 19.8 us  [local_grads(): pl.pallas_call(functools.partial(kernel, frames, clips, halo), out_shape=...]
    mul x1 -> x0, local copies, waits for them, and re-layouts: 5.97 us -> none  [shards(): halves.transpose(1, 3, 0, 2, 4).reshape(2, -1, width).astype(F32) * scale]
    slice x3 -> x1, local copies, waits for them, and re-layouts: 5.31 us -> 0.51 us  [shards(): loss[0, 0]]
    unnamed x12 -> x4, local copies, waits for them, and re-layouts: 3.95 us -> 0.01 us
    pallas_call x0 -> x1, Pallas kernels: none -> 3.47 us  [finish(): pl.pallas_call(finish_kernel, grid=(steps,), out_shape=(jax.ShapeDtypeStr...]
    squeeze x1 -> x0, local copies, waits for them, and re-layouts: 3.05 us -> none  [shards(): return (loss_sum * scale, conv[0], proj[0], conv[1], proj[1])]
    mul x1 -> x0, other arithmetic: 2.75 us -> none  [shards(): halves.transpose(1, 3, 0, 2, 4).reshape(2, -1, width).astype(F32) * scale]
    concatenate x2 -> x1, other arithmetic: 2.71 us -> 0.09 us  [reduce_all(): mine = jnp.concatenate([first, second])]
  transfers between devices with their start and end apart: 17 -> 17, of which waited for: 16 -> 16; matrix products, arithmetic and copies ran while one was open for 2% -> 1% of each run, Pallas kernels for 0% -> 0%
where the time goes in v2:
time: 93 us; the launch traced here: 92.7 us
  waiting for transfers between devices  40 us (43%)
  Pallas kernels  23.3 us (25%)
  starting transfers between devices  21.8 us (23%)
  other arithmetic  5.91 us (6%)
    ppermute x17, waiting for transfers between devices, swap(): lax.ppermute(value, axis, [(i, i ^ bit) for i in range(lax.axis_size(axis...  40 us
    ppermute x17, starting transfers between devices, swap(): lax.ppermute(value, axis, [(i, i ^ bit) for i in range(lax.axis_size(axis...  21.8 us
    pallas_call x1, Pallas kernels, local_grads(): pl.pallas_call(functools.partial(kernel, frames, clips, halo), out_shape=...  19.8 us
    pallas_call x1, Pallas kernels, finish(): pl.pallas_call(finish_kernel, grid=(steps,), out_shape=(jax.ShapeDtypeStr...  3.47 us
    add x1, other arithmetic, reduce_all(): total = keep + got[:rows].astype(F32)  1.95 us
  transfers between devices with their start and end apart: 17, of which 16 were waited for; matrix products, arithmetic and copies ran while one was open for 1% of the time, Pallas kernels for 0%

profile of v2, /device:TPU:0, one launch (start us, length us, event | category | flops | bytes accessed | tf_op | source)
XLA Modules:
  0.0 92.7 jit_solution(1946413541355434637)
XLA Ops:
  2.3 1.5 %collective-permute-done = bf16[2,2,256,256]{3,2,1,0:T(8,128)(2,1)S(1)} collective-permute-done((bf16[2,2,256,256]{3,2,1,0:T(8,128)(2,1)S(1)}, bf16[2,2,256,256]{3,2,1,0:T(8,128)(2,1)S(1)}, u32[]{:S(2)}, u32[]{:S(2)}) %collective-permute-start) | collective-permute-done | bytes 524320 | tf_op jit(solution)/shard_map/ppermute | solution.py:261
  5.0 19.8 %shard_map.119 = (f32[5120,128]{1,0:T(8,128)}, bf16[5152,128]{1,0:T(8,128)(2,1)}) custom-call(s32[4]{0:T(128)} %lengths.1, s32[4]{0:T(128)} %labels.1, bf16[2,2,512,256]{3,2,1,0:T(8,128)(2,1)} %pad_maximum_fusion.1.feats, bf16[768,512]{1,0:T(8,128)(2,1)} %bitcast.121, bf16[512,512]{1,0:T(8,128)(2,1)} %wap.1, bf16[768,512]{1,0:T(8,128)(2,1)} %bitcast.122, ...), custom_call_target="tpu_custom_call" | custom-call | tf_op jit(solution)/shard_map/pallas_call | solution.py:234
  25.2 2.9 %collective-permute-done.1 = bf16[5152,128]{1,0:T(8,128)(2,1)S(1)} collective-permute-done((bf16[5152,128]{1,0:T(8,128)(2,1)}, bf16[5152,128]{1,0:T(8,128)(2,1)S(1)}, u32[]{:S(2)}, u32[]{:S(2)}) %collective-permute-start.1) | collective-permute-done | bytes 1318944 | tf_op jit(solution)/shard_map/ppermute | solution.py:261
  28.1 2.0 %convert_add_fusion = f32[5120,128]{1,0:T(8,128)S(1)} fusion(f32[5120,128]{1,0:T(8,128)} %get-tuple-element.12, bf16[5152,128]{1,0:T(8,128)(2,1)S(1)} %collective-permute-done.1), kind=kLoop, calls=%fused_computation | loop fusion | flops 1310720 | bytes 6553600 | tf_op jit(solution)/shard_map/add | solution.py:321
  30.3 2.9 %collective-permute-start.4 = (bf16[1280,128]{1,0:T(8,128)(2,1)S(1)}, bf16[1280,128]{1,0:T(8,128)(2,1)S(1)}, u32[]{:S(2)}, u32[]{:S(2)}) collective-permute-start(bf16[1280,128]{1,0:T(8,128)(2,1)S(1)} %fusion.5), channel_id=1, source_target_pairs={{0,4},{2,6},{4,0},{6,2},{8,12},{10,14},{12,8},{14,10},{16,20},{18,... | collective-permute-start | bytes 983048 | tf_op jit(solution)/shard_map/ppermute | solution.py:261
  34.0 1.6 %collective-permute-start.2 = (bf16[1312,128]{1,0:T(8,128)(2,1)S(1)}, bf16[1312,128]{1,0:T(8,128)(2,1)S(1)}, u32[]{:S(2)}, u32[]{:S(2)}) collective-permute-start(bf16[1312,128]{1,0:T(8,128)(2,1)S(1)} %pad_maximum_fusion.4), channel_id=1, source_target_pairs={{0,2},{2,0},{4,6},{6,4},{8,10},{10,8},{12,14},{14,12},{16,18},{18,... | collective-permute-start | bytes 1007624 | tf_op jit(solution)/shard_map/ppermute | solution.py:261
  35.6 5.7 %collective-permute-done.4 = bf16[1280,128]{1,0:T(8,128)(2,1)S(1)} collective-permute-done((bf16[1280,128]{1,0:T(8,128)(2,1)S(1)}, bf16[1280,128]{1,0:T(8,128)(2,1)S(1)}, u32[]{:S(2)}, u32[]{:S(2)}) %collective-permute-start.4) | collective-permute-done | bytes 327712 | tf_op jit(solution)/shard_map/ppermute | solution.py:261
  41.4 1.8 %collective-permute-start.5 = (bf16[640,128]{1,0:T(8,128)(2,1)S(1)}, bf16[640,128]{1,0:T(8,128)(2,1)S(1)}, u32[]{:S(2)}, u32[]{:S(2)}) collective-permute-start(bf16[640,128]{1,0:T(8,128)(2,1)S(1)} %fusion.7), channel_id=1, source_target_pairs={{0,2},{2,0},{4,6},{6,4},{8,10},{10,8},{12,14},{14,12},{16,18},{18,... | collective-permute-start | bytes 491528 | tf_op jit(solution)/shard_map/ppermute | solution.py:261
  44.9 2.4 %collective-permute-done.5 = bf16[640,128]{1,0:T(8,128)(2,1)S(1)} collective-permute-done((bf16[640,128]{1,0:T(8,128)(2,1)S(1)}, bf16[640,128]{1,0:T(8,128)(2,1)S(1)}, u32[]{:S(2)}, u32[]{:S(2)}) %collective-permute-start.5) | collective-permute-done | bytes 163872 | tf_op jit(solution)/shard_map/ppermute | solution.py:261
  47.3 2.1 %collective-permute-done.3 = bf16[672,128]{1,0:T(8,128)(2,1)S(1)} collective-permute-done((bf16[672,128]{1,0:T(8,128)(2,1)S(1)}, bf16[672,128]{1,0:T(8,128)(2,1)S(1)}, u32[]{:S(2)}, u32[]{:S(2)}) %collective-permute-start.3) | collective-permute-done | bytes 172064 | tf_op jit(solution)/shard_map/ppermute | solution.py:261
  49.5 1.8 %collective-permute-start.6 = (bf16[352,128]{1,0:T(8,128)(2,1)S(1)}, bf16[352,128]{1,0:T(8,128)(2,1)S(1)}, u32[]{:S(2)}, u32[]{:S(2)}) collective-permute-start(bf16[352,128]{1,0:T(8,128)(2,1)S(1)} %get-tuple-element.40), channel_id=1, source_target_pairs={{0,8},{2,10},{4,12},{6,14},{8,0},{10,2},{12,4},{14,6},{16,24},{18,... | collective-permute-start | bytes 270344 | tf_op jit(solution)/shard_map/ppermute | solution.py:261
  51.3 2.6 %collective-permute-start.7 = (bf16[352,128]{1,0:T(8,128)(2,1)S(1)}, bf16[352,128]{1,0:T(8,128)(2,1)S(1)}, u32[]{:S(2)}, u32[]{:S(2)}) collective-permute-start(bf16[352,128]{1,0:T(8,128)(2,1)S(1)} %get-tuple-element.41), channel_id=1, source_target_pairs={{0,16},{2,18},{4,20},{6,22},{8,24},{10,26},{12,28},{14,30},{16,0},... | collective-permute-start | bytes 270344 | tf_op jit(solution)/shard_map/ppermute | solution.py:261
  54.3 4.2 %collective-permute-done.7 = bf16[352,128]{1,0:T(8,128)(2,1)S(1)} collective-permute-done((bf16[352,128]{1,0:T(8,128)(2,1)S(1)}, bf16[352,128]{1,0:T(8,128)(2,1)S(1)}, u32[]{:S(2)}, u32[]{:S(2)}) %collective-permute-start.7) | collective-permute-done | bytes 90144 | tf_op jit(solution)/shard_map/ppermute | solution.py:261
  58.5 1.7 %collective-permute-done.8 = bf16[352,128]{1,0:T(8,128)(2,1)S(1)} collective-permute-done((bf16[352,128]{1,0:T(8,128)(2,1)S(1)}, bf16[352,128]{1,0:T(8,128)(2,1)S(1)}, u32[]{:S(2)}, u32[]{:S(2)}) %collective-permute-start.8) | collective-permute-done | bytes 90144 | tf_op jit(solution)/shard_map/ppermute | solution.py:261
  60.3 1.6 %collective-permute-start.11 = (bf16[320,128]{1,0:T(8,128)(2,1)S(1)}, bf16[320,128]{1,0:T(8,128)(2,1)S(1)}, u32[]{:S(2)}, u32[]{:S(2)}) collective-permute-start(bf16[320,128]{1,0:T(8,128)(2,1)S(1)} %fusion.15), channel_id=1, source_target_pairs={{0,24},{2,26},{4,28},{6,30},{8,16},{10,18},{12,20},{14,22},{16,8},... | collective-permute-start | bytes 245768 | tf_op jit(solution)/shard_map/ppermute | solution.py:261
  62.0 2.6 %collective-permute-start.10 = (bf16[320,128]{1,0:T(8,128)(2,1)S(1)}, bf16[320,128]{1,0:T(8,128)(2,1)S(1)}, u32[]{:S(2)}, u32[]{:S(2)}) collective-permute-start(bf16[320,128]{1,0:T(8,128)(2,1)S(1)} %fusion.15), channel_id=1, source_target_pairs={{0,16},{2,18},{4,20},{6,22},{8,24},{10,26},{12,28},{14,30},{16,0},... | collective-permute-start | bytes 245768 | tf_op jit(solution)/shard_map/ppermute | solution.py:261
  65.0 1.7 %collective-permute-done.11 = bf16[320,128]{1,0:T(8,128)(2,1)S(1)} collective-permute-done((bf16[320,128]{1,0:T(8,128)(2,1)S(1)}, bf16[320,128]{1,0:T(8,128)(2,1)S(1)}, u32[]{:S(2)}, u32[]{:S(2)}) %collective-permute-start.11) | collective-permute-done | bytes 81952 | tf_op jit(solution)/shard_map/ppermute | solution.py:261
  66.7 1.7 %collective-permute-done.10 = bf16[320,128]{1,0:T(8,128)(2,1)S(1)} collective-permute-done((bf16[320,128]{1,0:T(8,128)(2,1)S(1)}, bf16[320,128]{1,0:T(8,128)(2,1)S(1)}, u32[]{:S(2)}, u32[]{:S(2)}) %collective-permute-start.10) | collective-permute-done | bytes 81952 | tf_op jit(solution)/shard_map/ppermute | solution.py:261
  71.6 4.9 %collective-permute-done.12 = bf16[640,128]{1,0:T(8,128)(2,1)S(1)} collective-permute-done((bf16[640,128]{1,0:T(8,128)(2,1)S(1)}, bf16[640,128]{1,0:T(8,128)(2,1)S(1)}, u32[]{:S(2)}, u32[]{:S(2)}) %collective-permute-start.12) | collective-permute-done | bytes 163872 | tf_op jit(solution)/shard_map/ppermute | solution.py:261
  76.5 1.7 %collective-permute-start.13 = (bf16[1280,128]{1,0:T(8,128)(2,1)S(1)}, bf16[1280,128]{1,0:T(8,128)(2,1)S(1)}, u32[]{:S(2)}, u32[]{:S(2)}) collective-permute-start(bf16[1280,128]{1,0:T(8,128)(2,1)S(1)} %bitcast.119), channel_id=1, source_target_pairs={{0,2},{2,0},{4,6},{6,4},{8,10},{10,8},{12,14},{14,12},{16,18},{18,... | collective-permute-start | bytes 983048 | tf_op jit(solution)/shard_map/ppermute | solution.py:261
  78.8 4.8 %collective-permute-done.13 = bf16[1280,128]{1,0:T(8,128)(2,1)S(1)} collective-permute-done((bf16[1280,128]{1,0:T(8,128)(2,1)S(1)}, bf16[1280,128]{1,0:T(8,128)(2,1)S(1)}, u32[]{:S(2)}, u32[]{:S(2)}) %collective-permute-start.13) | collective-permute-done | bytes 327712 | tf_op jit(solution)/shard_map/ppermute | solution.py:261
  83.8 1.6 %collective-permute-done.15 = bf16[1280,128]{1,0:T(8,128)(2,1)S(1)} collective-permute-done((bf16[1280,128]{1,0:T(8,128)(2,1)S(1)}, bf16[1280,128]{1,0:T(8,128)(2,1)S(1)}, u32[]{:S(2)}, u32[]{:S(2)}) %collective-permute-start.15) | collective-permute-done | bytes 327712 | tf_op jit(solution)/shard_map/ppermute | solution.py:261
  85.7 3.0 %collective-permute-done.16 = bf16[5120,128]{1,0:T(8,128)(2,1)S(1)} collective-permute-done((bf16[5120,128]{1,0:T(8,128)(2,1)S(1)}, bf16[5120,128]{1,0:T(8,128)(2,1)S(1)}, u32[]{:S(2)}, u32[]{:S(2)}) %collective-permute-start.16) | collective-permute-done | bytes 1310752 | tf_op jit(solution)/shard_map/ppermute | solution.py:261
  88.8 3.5 %shard_map.120 = (f32[8,128]{1,0:T(8,128)S(1)}, f32[768,512]{1,0:T(8,128)}, f32[512,512]{1,0:T(8,128)}, f32[768,512]{1,0:T(8,128)}, f32[512,512]{1,0:T(8,128)}) custom-call(bf16[2,2,1280,128]{3,2,1,0:T(8,128)(2,1)S(1)} %bitcast.97, bf16[2,2,1280,128]{3,2,1,0:T(8,128)(2,1)S(1)} %bitcast.99, bf16[2,2,1280,128]{3,2,1,0:T(8,128)(2,1)S(1)} %bitcast.98, ...), custom_call_target="tpu_custom_call" | custom-call | tf_op jit(solution)/shard_map/pallas_call | solution.py:377
  (54 shorter events, 11.9 us)
Async XLA Ops:
  0.6 3.3 %copy-start.1 = (bf16[4,256,256]{2,1,0:T(8,128)(2,1)S(1)}, bf16[4,256,256]{2,1,0:T(8,128)(2,1)}, u32[]{:S(2)}) copy-start(bf16[4,256,256]{2,1,0:T(8,128)(2,1)} %param.9) | copy-start | bytes 1572868
  0.6 3.2 %copy-start = (bf16[4,256,256]{2,1,0:T(8,128)(2,1)S(1)}, bf16[4,256,256]{2,1,0:T(8,128)(2,1)}, u32[]{:S(2)}) copy-start(bf16[4,256,256]{2,1,0:T(8,128)(2,1)} %param.8) | copy-start | bytes 1572868
  1.8 2.1 %collective-permute-start = (bf16[2,2,256,256]{3,2,1,0:T(8,128)(2,1)S(1)}, bf16[2,2,256,256]{3,2,1,0:T(8,128)(2,1)S(1)}, u32[]{:S(2)}, u32[]{:S(2)}) collective-permute-start(bf16[2,2,256,256]{3,2,1,0:T(8,128)(2,1)S(1)} %fusion.1), channel_id=1, source_target_pairs={{0,1},{1,0},{2,3},{3,2},{4,5},{5,4},{6,7},{7,6},{8,9},{9,8},{10,11... | collective-permute-start | bytes 1572872 | tf_op jit(solution)/shard_map/ppermute | solution.py:261
  24.8 3.3 %collective-permute-start.1 = (bf16[5152,128]{1,0:T(8,128)(2,1)}, bf16[5152,128]{1,0:T(8,128)(2,1)S(1)}, u32[]{:S(2)}, u32[]{:S(2)}) collective-permute-start(bf16[5152,128]{1,0:T(8,128)(2,1)} %get-tuple-element.13), channel_id=1, source_target_pairs={{0,1},{1,0},{2,3},{3,2},{4,5},{5,4},{6,7},{7,6},{8,9},{9,8},{10,11... | collective-permute-start | bytes 3956744 | tf_op jit(solution)/shard_map/ppermute | solution.py:261
  30.3 11.0 %collective-permute-start.4 = (bf16[1280,128]{1,0:T(8,128)(2,1)S(1)}, bf16[1280,128]{1,0:T(8,128)(2,1)S(1)}, u32[]{:S(2)}, u32[]{:S(2)}) collective-permute-start(bf16[1280,128]{1,0:T(8,128)(2,1)S(1)} %fusion.5), channel_id=1, source_target_pairs={{0,4},{2,6},{4,0},{6,2},{8,12},{10,14},{12,8},{14,10},{16,20},{18,... | collective-permute-start | bytes 983048 | tf_op jit(solution)/shard_map/ppermute | solution.py:261
  34.0 9.7 %collective-permute-start.2 = (bf16[1312,128]{1,0:T(8,128)(2,1)S(1)}, bf16[1312,128]{1,0:T(8,128)(2,1)S(1)}, u32[]{:S(2)}, u32[]{:S(2)}) collective-permute-start(bf16[1312,128]{1,0:T(8,128)(2,1)S(1)} %pad_maximum_fusion.4), channel_id=1, source_target_pairs={{0,2},{2,0},{4,6},{6,4},{8,10},{10,8},{12,14},{14,12},{16,18},{18,... | collective-permute-start | bytes 1007624 | tf_op jit(solution)/shard_map/ppermute | solution.py:261
  41.4 5.9 %collective-permute-start.5 = (bf16[640,128]{1,0:T(8,128)(2,1)S(1)}, bf16[640,128]{1,0:T(8,128)(2,1)S(1)}, u32[]{:S(2)}, u32[]{:S(2)}) collective-permute-start(bf16[640,128]{1,0:T(8,128)(2,1)S(1)} %fusion.7), channel_id=1, source_target_pairs={{0,2},{2,0},{4,6},{6,4},{8,10},{10,8},{12,14},{14,12},{16,18},{18,... | collective-permute-start | bytes 491528 | tf_op jit(solution)/shard_map/ppermute | solution.py:261
  43.9 5.5 %collective-permute-start.3 = (bf16[672,128]{1,0:T(8,128)(2,1)S(1)}, bf16[672,128]{1,0:T(8,128)(2,1)S(1)}, u32[]{:S(2)}, u32[]{:S(2)}) collective-permute-start(bf16[672,128]{1,0:T(8,128)(2,1)S(1)} %pad_maximum_fusion.8), channel_id=1, source_target_pairs={{0,4},{2,6},{4,0},{6,2},{8,12},{10,14},{12,8},{14,10},{16,20},{18,... | collective-permute-start | bytes 516104 | tf_op jit(solution)/shard_map/ppermute | solution.py:261
  49.5 4.8 %collective-permute-start.6 = (bf16[352,128]{1,0:T(8,128)(2,1)S(1)}, bf16[352,128]{1,0:T(8,128)(2,1)S(1)}, u32[]{:S(2)}, u32[]{:S(2)}) collective-permute-start(bf16[352,128]{1,0:T(8,128)(2,1)S(1)} %get-tuple-element.40), channel_id=1, source_target_pairs={{0,8},{2,10},{4,12},{6,14},{8,0},{10,2},{12,4},{14,6},{16,24},{18,... | collective-permute-start | bytes 270344 | tf_op jit(solution)/shard_map/ppermute | solution.py:261
  51.3 7.2 %collective-permute-start.7 = (bf16[352,128]{1,0:T(8,128)(2,1)S(1)}, bf16[352,128]{1,0:T(8,128)(2,1)S(1)}, u32[]{:S(2)}, u32[]{:S(2)}) collective-permute-start(bf16[352,128]{1,0:T(8,128)(2,1)S(1)} %get-tuple-element.41), channel_id=1, source_target_pairs={{0,16},{2,18},{4,20},{6,22},{8,24},{10,26},{12,28},{14,30},{16,0},... | collective-permute-start | bytes 270344 | tf_op jit(solution)/shard_map/ppermute | solution.py:261
  53.8 6.4 %collective-permute-start.8 = (bf16[352,128]{1,0:T(8,128)(2,1)S(1)}, bf16[352,128]{1,0:T(8,128)(2,1)S(1)}, u32[]{:S(2)}, u32[]{:S(2)}) collective-permute-start(bf16[352,128]{1,0:T(8,128)(2,1)S(1)} %get-tuple-element.42), channel_id=1, source_target_pairs={{0,24},{2,26},{4,28},{6,30},{8,16},{10,18},{12,20},{14,22},{16,8},... | collective-permute-start | bytes 270344 | tf_op jit(solution)/shard_map/ppermute | solution.py:261
  60.3 6.4 %collective-permute-start.11 = (bf16[320,128]{1,0:T(8,128)(2,1)S(1)}, bf16[320,128]{1,0:T(8,128)(2,1)S(1)}, u32[]{:S(2)}, u32[]{:S(2)}) collective-permute-start(bf16[320,128]{1,0:T(8,128)(2,1)S(1)} %fusion.15), channel_id=1, source_target_pairs={{0,24},{2,26},{4,28},{6,30},{8,16},{10,18},{12,20},{14,22},{16,8},... | collective-permute-start | bytes 245768 | tf_op jit(solution)/shard_map/ppermute | solution.py:261
  62.0 6.4 %collective-permute-start.10 = (bf16[320,128]{1,0:T(8,128)(2,1)S(1)}, bf16[320,128]{1,0:T(8,128)(2,1)S(1)}, u32[]{:S(2)}, u32[]{:S(2)}) collective-permute-start(bf16[320,128]{1,0:T(8,128)(2,1)S(1)} %fusion.15), channel_id=1, source_target_pairs={{0,16},{2,18},{4,20},{6,22},{8,24},{10,26},{12,28},{14,30},{16,0},... | collective-permute-start | bytes 245768 | tf_op jit(solution)/shard_map/ppermute | solution.py:261
  64.5 4.7 %collective-permute-start.9 = (bf16[320,128]{1,0:T(8,128)(2,1)S(1)}, bf16[320,128]{1,0:T(8,128)(2,1)S(1)}, u32[]{:S(2)}, u32[]{:S(2)}) collective-permute-start(bf16[320,128]{1,0:T(8,128)(2,1)S(1)} %fusion.15), channel_id=1, source_target_pairs={{0,8},{2,10},{4,12},{6,14},{8,0},{10,2},{12,4},{14,6},{16,24},{18,... | collective-permute-start | bytes 245768 | tf_op jit(solution)/shard_map/ppermute | solution.py:261
  69.4 7.0 %collective-permute-start.12 = (bf16[640,128]{1,0:T(8,128)(2,1)S(1)}, bf16[640,128]{1,0:T(8,128)(2,1)S(1)}, u32[]{:S(2)}, u32[]{:S(2)}) collective-permute-start(bf16[640,128]{1,0:T(8,128)(2,1)S(1)} %bitcast.124), channel_id=1, source_target_pairs={{0,4},{2,6},{4,0},{6,2},{8,12},{10,14},{12,8},{14,10},{16,20},{18,... | collective-permute-start | bytes 491528 | tf_op jit(solution)/shard_map/ppermute | solution.py:261
  70.5 7.7 %collective-permute-start.14 = (bf16[640,128]{1,0:T(8,128)(2,1)S(1)}, bf16[640,128]{1,0:T(8,128)(2,1)S(1)}, u32[]{:S(2)}, u32[]{:S(2)}) collective-permute-start(bf16[640,128]{1,0:T(8,128)(2,1)S(1)} %bitcast.123), channel_id=1, source_target_pairs={{0,2},{2,0},{4,6},{6,4},{8,10},{10,8},{12,14},{14,12},{16,18},{18,... | collective-permute-start | bytes 491528 | tf_op jit(solution)/shard_map/ppermute | solution.py:261
  76.5 7.1 %collective-permute-start.13 = (bf16[1280,128]{1,0:T(8,128)(2,1)S(1)}, bf16[1280,128]{1,0:T(8,128)(2,1)S(1)}, u32[]{:S(2)}, u32[]{:S(2)}) collective-permute-start(bf16[1280,128]{1,0:T(8,128)(2,1)S(1)} %bitcast.119), channel_id=1, source_target_pairs={{0,2},{2,0},{4,6},{6,4},{8,10},{10,8},{12,14},{14,12},{16,18},{18,... | collective-permute-start | bytes 983048 | tf_op jit(solution)/shard_map/ppermute | solution.py:261
  78.3 7.1 %collective-permute-start.15 = (bf16[1280,128]{1,0:T(8,128)(2,1)S(1)}, bf16[1280,128]{1,0:T(8,128)(2,1)S(1)}, u32[]{:S(2)}, u32[]{:S(2)}) collective-permute-start(bf16[1280,128]{1,0:T(8,128)(2,1)S(1)} %bitcast.120), channel_id=1, source_target_pairs={{0,4},{2,6},{4,0},{6,2},{8,12},{10,14},{12,8},{14,10},{16,20},{18,... | collective-permute-start | bytes 983048 | tf_op jit(solution)/shard_map/ppermute | solution.py:261
  85.7 3.1 %collective-permute-start.16 = (bf16[5120,128]{1,0:T(8,128)(2,1)S(1)}, bf16[5120,128]{1,0:T(8,128)(2,1)S(1)}, u32[]{:S(2)}, u32[]{:S(2)}) collective-permute-start(bf16[5120,128]{1,0:T(8,128)(2,1)S(1)} %pad_maximum_fusion), channel_id=1, source_target_pairs={{0,1},{1,0},{2,3},{3,2},{4,5},{5,4},{6,7},{7,6},{8,9},{9,8},{10,11... | collective-permute-start | bytes 3932168 | tf_op jit(solution)/shard_map/ppermute | solution.py:261

commit v3 on v2

--- a/solution.py
+++ b/solution.py
@@ -114,8 +114,8 @@
 
 
 def kernel(
-    frames, clips, halo, lengths, labels, feats, wac, wap, wvc, wvp, keep, send,
-    cols, slope, hid, gemb, gpre, total, emb_a, emb_v, inv_a, inv_v, gacc, giacc,
+    frames, clips, halo, lengths, labels, own_a, own_v, got, wac, wap, wvc, wvp, keep, send,
+    cols, slope, hid, gemb, gpre, total, emb_a, emb_v, inv_a, inv_v, gacc, giacc, feats,
 ):
     me = lax.axis_index("tm")
     half = lax.rem(me, 2)
@@ -124,6 +124,19 @@
     first_clip = 0 if halo else me * clips
     block = 256 if frames % 256 == 0 else TILE
     per_clip = frames // block
+
+    if halo:
+        feats[0] = own_a[...]
+        feats[1] = own_v[...]
+    else:
+        seg = own_a.shape[1]
+        mine = pl.ds(pl.multiple_of(me * seg, seg), seg)
+        other = pl.ds(pl.multiple_of((1 - me) * seg, seg), seg)
+        for c in range(clips):
+            feats[0, c, mine, :] = own_a[first_clip + c]
+            feats[1, c, mine, :] = own_v[first_clip + c]
+            feats[0, c, other, :] = got[0, c]
+            feats[1, c, other, :] = got[1, c]
 
     for c in range(clips):
         for lo in (0, PAD + frames):
@@ -220,8 +233,10 @@
     hand_over(total, keep, send, 0, half)
 
 
-def local_grads(halo, lengths, labels, feats, wac, wap, wvc, wvp):
-    _, clips, frames, chan = feats.shape
+def local_grads(halo, lengths, labels, own_a, own_v, got, wac, wap, wvc, wvp):
+    clips, frames, chan = own_a.shape
+    if not halo:
+        clips, frames = clips // 2, frames * 2
     width = wap.shape[0]
     rows = clips * frames
     taps = wac.shape[0]
@@ -237,7 +252,7 @@
             jax.ShapeDtypeStruct((2 * blocks * grad_rows, LANES), F32),
             jax.ShapeDtypeStruct((2 * blocks * grad_rows + 2 * PAD, LANES), BF16),
         ),
-        in_specs=[smem, smem] + [vmem] * 5,
+        in_specs=[smem, smem] + [vmem] * 7,
         out_specs=(vmem, vmem),
         scratch_shapes=[
             pltpu.VMEM((2, rows, taps * chan), BF16),
@@ -252,29 +267,35 @@
             pltpu.VMEM((rows, LANES), F32),
             pltpu.VMEM((clips, frames + 2 * PAD, width), F32),
             pltpu.VMEM((clips, frames + 2 * PAD, LANES), F32),
+            pltpu.VMEM((2, clips, frames, chan), BF16),
         ],
         compiler_params=pltpu.CompilerParams(vmem_limit_bytes=60 * 1024 * 1024),
-    )(lengths, labels, feats, wac, wap, wvc, wvp)
+    )(lengths, labels, own_a, own_v, got, wac, wap, wvc, wvp)
 
 
 def swap(value, axis, bit):
     return lax.ppermute(value, axis, [(i, i ^ bit) for i in range(lax.axis_size(axis))])
 
 
+def swap_by_core(value, bits):
+    peers = lax.axis_size("tm")
+    pairs = []
+    for clip in range(lax.axis_size("clip")):
+        for tm in range(peers):
+            pairs.append((clip * peers + tm, (clip ^ bits[tm % 2]) * peers + tm))
+    return lax.ppermute(value, ("clip", "tm"), pairs)
+
+
 def pick(value, index):
     return lax.dynamic_index_in_dim(value, index, 0, keepdims=False)
 
 
-def halve(value, axis, bit, tile=None):
+def halve(value, axis, bit, tile):
     me = (lax.axis_index(axis) // bit) % 2
     parts = value.reshape(2, -1, LANES)
-    out = pick(parts, 1 - me).astype(BF16)
-    if tile is not None:
-        out = jnp.concatenate([out, tile])
-    got = swap(out, axis, bit)
+    got = swap(jnp.concatenate([pick(parts, 1 - me).astype(BF16), tile]), axis, bit).astype(F32)
     rows = parts.shape[1]
-    mine = pick(parts, me).astype(F32) + got[:rows].astype(F32)
-    return mine if tile is None else (mine, (tile.astype(F32) + got[rows:].astype(F32)).astype(BF16))
+    return pick(parts, me).astype(F32) + got[:rows], (tile.astype(F32) + got[rows:]).astype(BF16)
 
 
 def double(value, axis, bit):
@@ -283,26 +304,32 @@
     return jnp.stack([jnp.where(me == 0, value, got), jnp.where(me == 0, got, value)]).reshape(-1, LANES)
 
 
-def quarter(parts, axis, bit, tile):
-    me = (lax.axis_index(axis) // bit) % 4
+def place_of(bits):
+    clip, odd = lax.axis_index("clip"), lax.axis_index("tm") % 2
+    return jnp.where(odd == 0, (clip // bits[0]) % 4, (clip // bits[1]) % 4)
+
+
+def quarter(parts, bits, tile):
+    me = place_of(bits)
     rows = parts.shape[1]
     mine = pick(parts, me).astype(F32)
     whole = tile.astype(F32)
     for k in (1, 2, 3):
-        got = swap(jnp.concatenate([pick(parts, me ^ k).astype(BF16), tile]), axis, k * bit).astype(F32)
+        out = jnp.concatenate([pick(parts, me ^ k).astype(BF16), tile])
+        got = swap_by_core(out, (k * bits[0], k * bits[1])).astype(F32)
         mine = mine + got[:rows]
         whole = whole + got[rows:]
-    return mine, whole
-
-
-def quadruple(value, axis, bit):
-    me = (lax.axis_index(axis) // bit) % 4
-    got = [value] + [swap(value, axis, k * bit) for k in (1, 2, 3)]
+    return mine, whole.astype(BF16)
+
+
+def quadruple(value, bits):
+    me = place_of(bits)
+    got = [value] + [swap_by_core(value, (k * bits[0], k * bits[1])) for k in (1, 2, 3)]
     out = []
     for j in range(4):
         k = me ^ j
         out.append(jnp.where(k == 0, got[0], jnp.where(k == 1, got[1], jnp.where(k == 2, got[2], got[3]))))
-    return jnp.stack(out)
+    return jnp.stack(out).reshape(-1, LANES)
 
 
 def bits_of(axis):
@@ -315,33 +342,19 @@
 
 
 def reduce_all(keep, send):
-    tm_bits, clip_bits = bits_of("tm"), bits_of("clip")
     got = swap(send, "tm", 1)
     rows = keep.shape[0]
     total = keep + got[:rows].astype(F32)
     tile = (send[rows:].astype(F32) + got[rows:].astype(F32)).astype(BF16)
-    first, second = total.reshape(2, -1, LANES)
-    for bit in tm_bits[1:]:
-        first, tile = halve(first, "tm", bit, tile)
-        second = halve(second, "tm", bit)
-    singles, last = clip_bits[:-2], clip_bits[-2]
-    order_1 = singles
-    order_2 = singles[1::-1] + singles[2:]
-    for bit_1, bit_2 in zip(order_1, order_2):
-        first, tile = halve(first, "clip", bit_1, tile)
-        second = halve(second, "clip", bit_2)
-    parts = jnp.concatenate([first.reshape(4, -1, LANES), second.reshape(4, -1, LANES)], axis=1)
-    mine, tile = quarter(parts, "clip", last, tile)
-    parts = quadruple(mine.astype(BF16), "clip", last)
-    n = parts.shape[1] // 2
-    first, second = parts[:, :n].reshape(-1, LANES), parts[:, n:].reshape(-1, LANES)
-    for bit_1, bit_2 in zip(order_1[::-1], order_2[::-1]):
-        first = double(first, "clip", bit_1)
-        second = double(second, "clip", bit_2)
-    for bit in tm_bits[:0:-1]:
-        first = double(first, "tm", bit)
-        second = double(second, "tm", bit)
-    mine = jnp.concatenate([first, second])
+    rest = [("tm", bit) for bit in bits_of("tm")[1:]] + [("clip", bit) for bit in bits_of("clip")[4:]]
+    for axis, bit in rest:
+        total, tile = halve(total, axis, bit, tile)
+    total, tile = quarter(total.reshape(4, -1, LANES), (1, 4), tile)
+    total, tile = quarter(total.reshape(4, -1, LANES), (4, 1), tile)
+    mine = quadruple(total.astype(BF16), (4, 1))
+    mine = quadruple(mine, (1, 4))
+    for axis, bit in rest[::-1]:
+        mine = double(mine, axis, bit)
     return mine, swap(mine, "tm", 1), tile
 
 
@@ -393,22 +406,19 @@
 def shards(
     audio_feats, lip_feats, lengths, labels, w_audio_conv, w_audio_proj, w_lip_conv, w_lip_proj
 ):
-    both = jnp.stack([audio_feats, lip_feats])
     peers = lax.axis_size("tm")
+    clips, frames, chan = audio_feats.shape
     halo = 0
-    if peers == 2 and both.shape[1] % 2 == 0:
-        me = lax.axis_index("tm")
-        parts = both.reshape(2, 2, both.shape[1] // 2, *both.shape[2:])
-        mine = lax.dynamic_index_in_dim(parts, me, 1, keepdims=False)
-        got = swap(lax.dynamic_index_in_dim(parts, 1 - me, 1, keepdims=False), "tm", 1)
-        feats = jnp.concatenate(
-            [jnp.where(me == 0, mine, got), jnp.where(me == 0, got, mine)], axis=2
-        )
+    if peers == 2 and clips % 2 == 0:
+        others = (1 - lax.axis_index("tm")) * (clips // 2)
+        out = jnp.stack([lax.dynamic_slice_in_dim(x, others, clips // 2) for x in (audio_feats, lip_feats)])
+        got = swap(out, "tm", 1)
     else:
         halo = HALO
         after = [(i, i + 1) for i in range(peers - 1)]
         before = [(i + 1, i) for i in range(peers - 1)]
-        feats = jnp.concatenate(
+        both = jnp.stack([audio_feats, lip_feats])
+        audio_feats, lip_feats = jnp.concatenate(
             [
                 lax.ppermute(both[:, :, -HALO:], "tm", after),
                 both,
@@ -416,12 +426,13 @@
             ],
             axis=2,
         )
+        got = lengths.astype(BF16)
     keep, send = local_grads(
-        halo, lengths, labels, feats, w_audio_conv, w_audio_proj, w_lip_conv, w_lip_proj
+        halo, lengths, labels, audio_feats, lip_feats, got, w_audio_conv, w_audio_proj, w_lip_conv, w_lip_proj
     )
     mine, got, tile = reduce_all(keep, send)
     taps, chan, width = w_audio_conv.shape
-    loss, ac, ap, vc, vp = finish(mine, got, tile.astype(BF16), taps * chan, width)
+    loss, ac, ap, vc, vp = finish(mine, got, tile, taps * chan, width)
     return (loss[0, 0], ac.reshape(w_audio_conv.shape), ap, vc.reshape(w_lip_conv.shape), vp)
 
 

time: 93 us -> 90 us (0.968)
  waiting for transfers between devices: 40 us -> 33.4 us
  local copies, waits for them, and re-layouts: 0.84 us -> 3.61 us
  starting transfers between devices: 21.8 us -> 22.8 us
    ppermute x17 -> x3, waiting for transfers between devices: 40 us -> 7.08 us  [swap(): lax.ppermute(value, axis, [(i, i ^ bit) for i in range(lax.axis_size(axis...]
    ppermute x0 -> x12, waiting for transfers between devices: none -> 26.3 us  [swap_by_core(): return lax.ppermute(value, ('clip', 'tm'), pairs)]
    ppermute x0 -> x12, starting transfers between devices: none -> 16.8 us  [swap_by_core(): return lax.ppermute(value, ('clip', 'tm'), pairs)]
    ppermute x17 -> x3, starting transfers between devices: 21.8 us -> 5.93 us  [swap(): lax.ppermute(value, axis, [(i, i ^ bit) for i in range(lax.axis_size(axis...]
    unnamed x4, local copies, waits for them, and re-layouts: 0.01 us -> 1.85 us
    squeeze x1 -> x0, other arithmetic: 1.17 us -> none  [shards(): lax.dynamic_index_in_dim(parts, 1 - me, 1, keepdims=False)]
    convert_element_type x8 -> x9, other arithmetic: 0.15 us -> 1.21 us  [the longest x6 1.15 us: quarter(): got = swap_by_core(out, (k * bits[0], k * bits[1])).astype(F32)]
  transfers between devices with their start and end apart: 17 -> 15, of which waited for: 16 -> 13; matrix products, arithmetic and copies ran while one was open for 1% -> 1% of each run, Pallas kernels for 0% -> 0%
where the time goes in v3:
time: 90 us; the launch traced here: 89.7 us
  waiting for transfers between devices  33.4 us (37%)
  Pallas kernels  23.4 us (26%)
  starting transfers between devices  22.8 us (25%)
  other arithmetic  5.85 us (6%)
  local copies, waits for them, and re-layouts  3.61 us (4%)
    ppermute x12, waiting for transfers between devices, swap_by_core(): return lax.ppermute(value, ('clip', 'tm'), pairs)  26.3 us
    pallas_call x1, Pallas kernels, local_grads(): pl.pallas_call(functools.partial(kernel, frames, clips, halo), out_shape=...  19.9 us
    ppermute x12, starting transfers between devices, swap_by_core(): return lax.ppermute(value, ('clip', 'tm'), pairs)  16.8 us
    ppermute x3, waiting for transfers between devices, swap(): lax.ppermute(value, axis, [(i, i ^ bit) for i in range(lax.axis_size(axis...  7.08 us
    ppermute x3, starting transfers between devices, swap(): lax.ppermute(value, axis, [(i, i ^ bit) for i in range(lax.axis_size(axis...  5.93 us
    pallas_call x1, Pallas kernels, finish(): pl.pallas_call(finish_kernel, grid=(steps,), out_shape=(jax.ShapeDtypeStr...  3.47 us
    add x1, other arithmetic, reduce_all(): total = keep + got[:rows].astype(F32)  2.32 us
    unnamed x4, local copies, waits for them, and re-layouts  1.85 us
  transfers between devices with their start and end apart: 15, of which 13 were waited for; matrix products, arithmetic and copies ran while one was open for 1% of the time, Pallas kernels for 0%

profile of v3, /device:TPU:0, one launch (start us, length us, event | category | flops | bytes accessed | tf_op | source)
XLA Modules:
  0.0 89.7 jit_solution(6962326288722796721)
XLA Ops:
  0.6 1.1 %dynamic-slice_bitcast_fusion = (bf16[1,2,256,256]{3,2,1,0:T(8,128)(2,1)S(1)}, bf16[1,2,256,256]{3,2,1,0:T(8,128)(2,1)S(1)}) fusion(bf16[4,256,256]{2,1,0:T(8,128)(2,1)} %own_v.1, s32[]{:T(128)S(6)} %select_n.238, bf16[4,256,256]{2,1,0:T(8,128)(2,1)} %own_a.1), kind=kLoop, calls=%fused_computation.20 | loop fusion | bytes 1048580 | tf_op jit(solution)/shard_map/stack | solution.py:414
  2.3 1.5 %collective-permute-done.got = bf16[2,2,256,256]{3,2,1,0:T(8,128)(2,1)S(1)} collective-permute-done((bf16[2,2,256,256]{3,2,1,0:T(8,128)(2,1)S(1)}, bf16[2,2,256,256]{3,2,1,0:T(8,128)(2,1)S(1)}, u32[]{:S(2)}, u32[]{:S(2)}) %collective-permute-start) | collective-permute-done | bytes 524320 | tf_op jit(solution)/shard_map/ppermute | solution.py:277
  4.6 19.9 %shard_map.119 = (f32[5120,128]{1,0:T(8,128)}, bf16[5152,128]{1,0:T(8,128)(2,1)}) custom-call(s32[4]{0:T(128)} %lengths.1, s32[4]{0:T(128)} %labels.1, bf16[4,256,256]{2,1,0:T(8,128)(2,1)} %own_a.1, bf16[4,256,256]{2,1,0:T(8,128)(2,1)} %own_v.1, bf16[2,2,256,256]{3,2,1,0:T(8,128)(2,1)} %copy-done.1, bf16[768,512]{1,0:T(8,128)(2,1)} %bitcast.63, ...), custom_call_target="tpu_custom_call" | custom-call | tf_op jit(solution)/shard_map/pallas_call | solution.py:249
  24.9 2.9 %collective-permute-done.1 = bf16[5152,128]{1,0:T(8,128)(2,1)S(1)} collective-permute-done((bf16[5152,128]{1,0:T(8,128)(2,1)}, bf16[5152,128]{1,0:T(8,128)(2,1)S(1)}, u32[]{:S(2)}, u32[]{:S(2)}) %collective-permute-start.1) | collective-permute-done | bytes 1318944 | tf_op jit(solution)/shard_map/ppermute | solution.py:277
  27.8 1.1 %copy-done = bf16[5152,128]{1,0:T(8,128)(2,1)} copy-done((bf16[5152,128]{1,0:T(8,128)(2,1)}, bf16[5152,128]{1,0:T(8,128)(2,1)S(1)}, u32[]{:S(2)}) %copy-start) | copy-done | bytes 1318936
  28.9 2.3 %convert_add_fusion = f32[5120,128]{1,0:T(8,128)S(1)} fusion(f32[5120,128]{1,0:T(8,128)} %get-tuple-element.12, bf16[5152,128]{1,0:T(8,128)(2,1)} %copy-done), kind=kLoop, calls=%fused_computation | loop fusion | flops 1310720 | bytes 6553600 | tf_op jit(solution)/shard_map/add | solution.py:347
  33.0 2.8 %collective-permute-start.2 = (bf16[1312,128]{1,0:T(8,128)(2,1)}, bf16[1312,128]{1,0:T(8,128)(2,1)}, u32[]{:S(2)}, u32[]{:S(2)}) collective-permute-start(bf16[1312,128]{1,0:T(8,128)(2,1)} %get-tuple-element.36), channel_id=1, source_target_pairs={{0,2},{1,9},{2,0},{3,11},{4,6},{5,13},{6,4},{7,15},{8,10},{9,1},{1... | collective-permute-start | bytes 1007624 | tf_op jit(solution)/shard_map/ppermute | solution.py:286
  35.8 1.5 %collective-permute-start.3 = (bf16[1312,128]{1,0:T(8,128)(2,1)}, bf16[1312,128]{1,0:T(8,128)(2,1)S(1)}, u32[]{:S(2)}, u32[]{:S(2)}) collective-permute-start(bf16[1312,128]{1,0:T(8,128)(2,1)} %get-tuple-element.37), channel_id=1, source_target_pairs={{0,4},{1,17},{2,6},{3,19},{4,0},{5,21},{6,2},{7,23},{8,12},{9,25},... | collective-permute-start | bytes 1007624 | tf_op jit(solution)/shard_map/ppermute | solution.py:286
  37.4 3.9 %collective-permute-done.2 = bf16[1312,128]{1,0:T(8,128)(2,1)} collective-permute-done((bf16[1312,128]{1,0:T(8,128)(2,1)}, bf16[1312,128]{1,0:T(8,128)(2,1)}, u32[]{:S(2)}, u32[]{:S(2)}) %collective-permute-start.2) | collective-permute-done | bytes 335904 | tf_op jit(solution)/shard_map/ppermute | solution.py:286
  42.3 4.5 %collective-permute-done.3 = bf16[1312,128]{1,0:T(8,128)(2,1)S(1)} collective-permute-done((bf16[1312,128]{1,0:T(8,128)(2,1)}, bf16[1312,128]{1,0:T(8,128)(2,1)S(1)}, u32[]{:S(2)}, u32[]{:S(2)}) %collective-permute-start.3) | collective-permute-done | bytes 335904 | tf_op jit(solution)/shard_map/ppermute | solution.py:286
  47.2 1.6 %collective-permute-start.5 = (bf16[352,128]{1,0:T(8,128)(2,1)S(1)}, bf16[352,128]{1,0:T(8,128)(2,1)S(1)}, u32[]{:S(2)}, u32[]{:S(2)}) collective-permute-start(bf16[352,128]{1,0:T(8,128)(2,1)S(1)} %get-tuple-element.33), channel_id=1, source_target_pairs={{0,8},{1,3},{2,10},{3,1},{4,12},{5,7},{6,14},{7,5},{8,0},{9,11},{1... | collective-permute-start | bytes 270344 | tf_op jit(solution)/shard_map/ppermute | solution.py:286
  48.8 2.6 %collective-permute-start.6 = (bf16[352,128]{1,0:T(8,128)(2,1)S(1)}, bf16[352,128]{1,0:T(8,128)(2,1)S(1)}, u32[]{:S(2)}, u32[]{:S(2)}) collective-permute-start(bf16[352,128]{1,0:T(8,128)(2,1)S(1)} %get-tuple-element.34), channel_id=1, source_target_pairs={{0,16},{1,5},{2,18},{3,7},{4,20},{5,1},{6,22},{7,3},{8,24},{9,13},... | collective-permute-start | bytes 270344 | tf_op jit(solution)/shard_map/ppermute | solution.py:286
  51.8 4.1 %collective-permute-done.6 = bf16[352,128]{1,0:T(8,128)(2,1)S(1)} collective-permute-done((bf16[352,128]{1,0:T(8,128)(2,1)S(1)}, bf16[352,128]{1,0:T(8,128)(2,1)S(1)}, u32[]{:S(2)}, u32[]{:S(2)}) %collective-permute-start.6) | collective-permute-done | bytes 90144 | tf_op jit(solution)/shard_map/ppermute | solution.py:286
  55.9 1.9 %collective-permute-done.7 = bf16[352,128]{1,0:T(8,128)(2,1)S(1)} collective-permute-done((bf16[352,128]{1,0:T(8,128)(2,1)S(1)}, bf16[352,128]{1,0:T(8,128)(2,1)S(1)}, u32[]{:S(2)}, u32[]{:S(2)}) %collective-permute-start.7) | collective-permute-done | bytes 90144 | tf_op jit(solution)/shard_map/ppermute | solution.py:286
  57.9 1.6 %collective-permute-start.10 = (bf16[320,128]{1,0:T(8,128)(2,1)S(1)}, bf16[320,128]{1,0:T(8,128)(2,1)S(1)}, u32[]{:S(2)}, u32[]{:S(2)}) collective-permute-start(bf16[320,128]{1,0:T(8,128)(2,1)S(1)} %fusion.3), channel_id=1, source_target_pairs={{0,24},{1,7},{2,26},{3,5},{4,28},{5,3},{6,30},{7,1},{8,16},{9,15},... | collective-permute-start | bytes 245768 | tf_op jit(solution)/shard_map/ppermute | solution.py:286
  59.6 2.7 %collective-permute-start.8 = (bf16[320,128]{1,0:T(8,128)(2,1)S(1)}, bf16[320,128]{1,0:T(8,128)(2,1)S(1)}, u32[]{:S(2)}, u32[]{:S(2)}) collective-permute-start(bf16[320,128]{1,0:T(8,128)(2,1)S(1)} %fusion.3), channel_id=1, source_target_pairs={{0,8},{1,3},{2,10},{3,1},{4,12},{5,7},{6,14},{7,5},{8,0},{9,11},{1... | collective-permute-start | bytes 245768 | tf_op jit(solution)/shard_map/ppermute | solution.py:286
  62.3 1.9 %collective-permute-done.10 = bf16[320,128]{1,0:T(8,128)(2,1)S(1)} collective-permute-done((bf16[320,128]{1,0:T(8,128)(2,1)S(1)}, bf16[320,128]{1,0:T(8,128)(2,1)S(1)}, u32[]{:S(2)}, u32[]{:S(2)}) %collective-permute-start.10) | collective-permute-done | bytes 81952 | tf_op jit(solution)/shard_map/ppermute | solution.py:286
  64.2 1.7 %collective-permute-done.9 = bf16[320,128]{1,0:T(8,128)(2,1)S(1)} collective-permute-done((bf16[320,128]{1,0:T(8,128)(2,1)S(1)}, bf16[320,128]{1,0:T(8,128)(2,1)S(1)}, u32[]{:S(2)}, u32[]{:S(2)}) %collective-permute-start.9) | collective-permute-done | bytes 81952 | tf_op jit(solution)/shard_map/ppermute | solution.py:286
  66.1 1.7 %collective-permute-start.13 = (bf16[1280,128]{1,0:T(8,128)(2,1)S(1)}, bf16[1280,128]{1,0:T(8,128)(2,1)S(1)}, u32[]{:S(2)}, u32[]{:S(2)}) collective-permute-start(bf16[1280,128]{1,0:T(8,128)(2,1)S(1)} %bitcast.60), channel_id=1, source_target_pairs={{0,6},{1,25},{2,4},{3,27},{4,2},{5,29},{6,0},{7,31},{8,14},{9,17},... | collective-permute-start | bytes 983048 | tf_op jit(solution)/shard_map/ppermute | solution.py:286
  69.6 4.6 %collective-permute-done.13 = bf16[1280,128]{1,0:T(8,128)(2,1)S(1)} collective-permute-done((bf16[1280,128]{1,0:T(8,128)(2,1)S(1)}, bf16[1280,128]{1,0:T(8,128)(2,1)S(1)}, u32[]{:S(2)}, u32[]{:S(2)}) %collective-permute-start.13) | collective-permute-done | bytes 327712 | tf_op jit(solution)/shard_map/ppermute | solution.py:286
  74.2 3.4 %collective-permute-done.12 = bf16[1280,128]{1,0:T(8,128)(2,1)S(1)} collective-permute-done((bf16[1280,128]{1,0:T(8,128)(2,1)S(1)}, bf16[1280,128]{1,0:T(8,128)(2,1)S(1)}, u32[]{:S(2)}, u32[]{:S(2)}) %collective-permute-start.12) | collective-permute-done | bytes 327712 | tf_op jit(solution)/shard_map/ppermute | solution.py:286
  78.0 5.0 %collective-permute-start.14 = (bf16[5120,128]{1,0:T(8,128)(2,1)S(1)}, bf16[5120,128]{1,0:T(8,128)(2,1)S(1)}, u32[]{:S(2)}, u32[]{:S(2)}) collective-permute-start(bf16[5120,128]{1,0:T(8,128)(2,1)S(1)} %bitcast.51), channel_id=1, source_target_pairs={{0,1},{1,0},{2,3},{3,2},{4,5},{5,4},{6,7},{7,6},{8,9},{9,8},{10,11... | collective-permute-start | bytes 3932168 | tf_op jit(solution)/shard_map/ppermute | solution.py:277
  83.1 2.7 %collective-permute-done.14 = bf16[5120,128]{1,0:T(8,128)(2,1)S(1)} collective-permute-done((bf16[5120,128]{1,0:T(8,128)(2,1)S(1)}, bf16[5120,128]{1,0:T(8,128)(2,1)S(1)}, u32[]{:S(2)}, u32[]{:S(2)}) %collective-permute-start.14) | collective-permute-done | bytes 1310752 | tf_op jit(solution)/shard_map/ppermute | solution.py:277
  85.8 3.5 %shard_map.120 = (f32[8,128]{1,0:T(8,128)S(1)}, f32[768,512]{1,0:T(8,128)}, f32[512,512]{1,0:T(8,128)}, f32[768,512]{1,0:T(8,128)}, f32[512,512]{1,0:T(8,128)}) custom-call(bf16[2,2,1280,128]{3,2,1,0:T(8,128)(2,1)S(1)} %bitcast.52, bf16[2,2,1280,128]{3,2,1,0:T(8,128)(2,1)S(1)} %bitcast.54, bf16[2,2,1280,128]{3,2,1,0:T(8,128)(2,1)S(1)} %bitcast.53, ...), custom_call_target="tpu_custom_call" | custom-call | tf_op jit(solution)/shard_map/pallas_call | solution.py:390
  (35 shorter events, 8.3 us)
Async XLA Ops:
  1.8 2.1 %collective-permute-start = (bf16[2,2,256,256]{3,2,1,0:T(8,128)(2,1)S(1)}, bf16[2,2,256,256]{3,2,1,0:T(8,128)(2,1)S(1)}, u32[]{:S(2)}, u32[]{:S(2)}) collective-permute-start(bf16[2,2,256,256]{3,2,1,0:T(8,128)(2,1)S(1)} %pad_maximum_fusion.4), channel_id=1, source_target_pairs={{0,1},{1,0},{2,3},{3,2},{4,5},{5,4},{6,7},{7,6},{8,9},{9,8},{10,11... | collective-permute-start | bytes 1572872 | tf_op jit(solution)/shard_map/ppermute | solution.py:277
  3.8 0.8 copy-start.1
  24.5 3.3 %collective-permute-start.1 = (bf16[5152,128]{1,0:T(8,128)(2,1)}, bf16[5152,128]{1,0:T(8,128)(2,1)S(1)}, u32[]{:S(2)}, u32[]{:S(2)}) collective-permute-start(bf16[5152,128]{1,0:T(8,128)(2,1)} %get-tuple-element.13), channel_id=1, source_target_pairs={{0,1},{1,0},{2,3},{3,2},{4,5},{5,4},{6,7},{7,6},{8,9},{9,8},{10,11... | collective-permute-start | bytes 3956744 | tf_op jit(solution)/shard_map/ppermute | solution.py:277
  27.8 1.1 %copy-start = (bf16[5152,128]{1,0:T(8,128)(2,1)}, bf16[5152,128]{1,0:T(8,128)(2,1)S(1)}, u32[]{:S(2)}) copy-start(bf16[5152,128]{1,0:T(8,128)(2,1)S(1)} %collective-permute-done.1) | copy-start | bytes 3956740
  33.0 8.3 %collective-permute-start.2 = (bf16[1312,128]{1,0:T(8,128)(2,1)}, bf16[1312,128]{1,0:T(8,128)(2,1)}, u32[]{:S(2)}, u32[]{:S(2)}) collective-permute-start(bf16[1312,128]{1,0:T(8,128)(2,1)} %get-tuple-element.36), channel_id=1, source_target_pairs={{0,2},{1,9},{2,0},{3,11},{4,6},{5,13},{6,4},{7,15},{8,10},{9,1},{1... | collective-permute-start | bytes 1007624 | tf_op jit(solution)/shard_map/ppermute | solution.py:286
  35.8 11.0 %collective-permute-start.3 = (bf16[1312,128]{1,0:T(8,128)(2,1)}, bf16[1312,128]{1,0:T(8,128)(2,1)S(1)}, u32[]{:S(2)}, u32[]{:S(2)}) collective-permute-start(bf16[1312,128]{1,0:T(8,128)(2,1)} %get-tuple-element.37), channel_id=1, source_target_pairs={{0,4},{1,17},{2,6},{3,19},{4,0},{5,21},{6,2},{7,23},{8,12},{9,25},... | collective-permute-start | bytes 1007624 | tf_op jit(solution)/shard_map/ppermute | solution.py:286
  37.4 9.5 %collective-permute-start.4 = (bf16[1312,128]{1,0:T(8,128)(2,1)}, bf16[1312,128]{1,0:T(8,128)(2,1)S(1)}, u32[]{:S(2)}, u32[]{:S(2)}) collective-permute-start(bf16[1312,128]{1,0:T(8,128)(2,1)} %get-tuple-element.38), channel_id=1, source_target_pairs={{0,6},{1,25},{2,4},{3,27},{4,2},{5,29},{6,0},{7,31},{8,14},{9,17},... | collective-permute-start | bytes 1007624 | tf_op jit(solution)/shard_map/ppermute | solution.py:286
  47.2 4.6 %collective-permute-start.5 = (bf16[352,128]{1,0:T(8,128)(2,1)S(1)}, bf16[352,128]{1,0:T(8,128)(2,1)S(1)}, u32[]{:S(2)}, u32[]{:S(2)}) collective-permute-start(bf16[352,128]{1,0:T(8,128)(2,1)S(1)} %get-tuple-element.33), channel_id=1, source_target_pairs={{0,8},{1,3},{2,10},{3,1},{4,12},{5,7},{6,14},{7,5},{8,0},{9,11},{1... | collective-permute-start | bytes 270344 | tf_op jit(solution)/shard_map/ppermute | solution.py:286
  48.8 7.1 %collective-permute-start.6 = (bf16[352,128]{1,0:T(8,128)(2,1)S(1)}, bf16[352,128]{1,0:T(8,128)(2,1)S(1)}, u32[]{:S(2)}, u32[]{:S(2)}) collective-permute-start(bf16[352,128]{1,0:T(8,128)(2,1)S(1)} %get-tuple-element.34), channel_id=1, source_target_pairs={{0,16},{1,5},{2,18},{3,7},{4,20},{5,1},{6,22},{7,3},{8,24},{9,13},... | collective-permute-start | bytes 270344 | tf_op jit(solution)/shard_map/ppermute | solution.py:286
  51.4 6.4 %collective-permute-start.7 = (bf16[352,128]{1,0:T(8,128)(2,1)S(1)}, bf16[352,128]{1,0:T(8,128)(2,1)S(1)}, u32[]{:S(2)}, u32[]{:S(2)}) collective-permute-start(bf16[352,128]{1,0:T(8,128)(2,1)S(1)} %get-tuple-element.35), channel_id=1, source_target_pairs={{0,24},{1,7},{2,26},{3,5},{4,28},{5,3},{6,30},{7,1},{8,16},{9,15},... | collective-permute-start | bytes 270344 | tf_op jit(solution)/shard_map/ppermute | solution.py:286
  57.9 6.4 %collective-permute-start.10 = (bf16[320,128]{1,0:T(8,128)(2,1)S(1)}, bf16[320,128]{1,0:T(8,128)(2,1)S(1)}, u32[]{:S(2)}, u32[]{:S(2)}) collective-permute-start(bf16[320,128]{1,0:T(8,128)(2,1)S(1)} %fusion.3), channel_id=1, source_target_pairs={{0,24},{1,7},{2,26},{3,5},{4,28},{5,3},{6,30},{7,1},{8,16},{9,15},... | collective-permute-start | bytes 245768 | tf_op jit(solution)/shard_map/ppermute | solution.py:286
  59.5 6.5 %collective-permute-start.9 = (bf16[320,128]{1,0:T(8,128)(2,1)S(1)}, bf16[320,128]{1,0:T(8,128)(2,1)S(1)}, u32[]{:S(2)}, u32[]{:S(2)}) collective-permute-start(bf16[320,128]{1,0:T(8,128)(2,1)S(1)} %fusion.3), channel_id=1, source_target_pairs={{0,16},{1,5},{2,18},{3,7},{4,20},{5,1},{6,22},{7,3},{8,24},{9,13},... | collective-permute-start | bytes 245768 | tf_op jit(solution)/shard_map/ppermute | solution.py:286
  59.6 6.4 %collective-permute-start.8 = (bf16[320,128]{1,0:T(8,128)(2,1)S(1)}, bf16[320,128]{1,0:T(8,128)(2,1)S(1)}, u32[]{:S(2)}, u32[]{:S(2)}) collective-permute-start(bf16[320,128]{1,0:T(8,128)(2,1)S(1)} %fusion.3), channel_id=1, source_target_pairs={{0,8},{1,3},{2,10},{3,1},{4,12},{5,7},{6,14},{7,5},{8,0},{9,11},{1... | collective-permute-start | bytes 245768 | tf_op jit(solution)/shard_map/ppermute | solution.py:286
  66.1 8.1 %collective-permute-start.13 = (bf16[1280,128]{1,0:T(8,128)(2,1)S(1)}, bf16[1280,128]{1,0:T(8,128)(2,1)S(1)}, u32[]{:S(2)}, u32[]{:S(2)}) collective-permute-start(bf16[1280,128]{1,0:T(8,128)(2,1)S(1)} %bitcast.60), channel_id=1, source_target_pairs={{0,6},{1,25},{2,4},{3,27},{4,2},{5,29},{6,0},{7,31},{8,14},{9,17},... | collective-permute-start | bytes 983048 | tf_op jit(solution)/shard_map/ppermute | solution.py:286
  67.7 9.9 %collective-permute-start.12 = (bf16[1280,128]{1,0:T(8,128)(2,1)S(1)}, bf16[1280,128]{1,0:T(8,128)(2,1)S(1)}, u32[]{:S(2)}, u32[]{:S(2)}) collective-permute-start(bf16[1280,128]{1,0:T(8,128)(2,1)S(1)} %bitcast.61), channel_id=1, source_target_pairs={{0,4},{1,17},{2,6},{3,19},{4,0},{5,21},{6,2},{7,23},{8,12},{9,25},... | collective-permute-start | bytes 983048 | tf_op jit(solution)/shard_map/ppermute | solution.py:286
  68.6 9.1 %collective-permute-start.11 = (bf16[1280,128]{1,0:T(8,128)(2,1)S(1)}, bf16[1280,128]{1,0:T(8,128)(2,1)S(1)}, u32[]{:S(2)}, u32[]{:S(2)}) collective-permute-start(bf16[1280,128]{1,0:T(8,128)(2,1)S(1)} %bitcast.62), channel_id=1, source_target_pairs={{0,2},{1,9},{2,0},{3,11},{4,6},{5,13},{6,4},{7,15},{8,10},{9,1},{1... | collective-permute-start | bytes 983048 | tf_op jit(solution)/shard_map/ppermute | solution.py:286
  78.0 7.7 %collective-permute-start.14 = (bf16[5120,128]{1,0:T(8,128)(2,1)S(1)}, bf16[5120,128]{1,0:T(8,128)(2,1)S(1)}, u32[]{:S(2)}, u32[]{:S(2)}) collective-permute-start(bf16[5120,128]{1,0:T(8,128)(2,1)S(1)} %bitcast.51), channel_id=1, source_target_pairs={{0,1},{1,0},{2,3},{3,2},{4,5},{5,4},{6,7},{7,6},{8,9},{9,8},{10,11... | collective-permute-start | bytes 3932168 | tf_op jit(solution)/shard_map/ppermute | solution.py:277

commit v4 on v3

--- a/solution.py
+++ b/solution.py
@@ -50,8 +50,10 @@
     return jnp.sum(jnp.where(lane < DIGITS, digits * weight, 0.0))
 
 
-def forward(feats, m, w_conv, w_proj, cols, slope, hid, clips, frames, block, put):
+def forward(feats, m, copies, w_conv, w_proj, cols, slope, hid, clips, frames, block, put):
     chan = feats.shape[-1]
+    for copy in copies[0]:
+        copy.wait()
     for c in range(clips):
         x = feats[m, c].astype(F32)
         row = lax.broadcasted_iota(jnp.int32, x.shape, 0)
@@ -61,6 +63,9 @@
         cols[m, base : base + frames, 2 * chan : 3 * chan] = jnp.where(
             row == frames - 1, 0.0, pltpu.roll(x, frames - 1, 0)
         ).astype(BF16)
+
+    for copy in copies[1]:
+        copy.wait()
 
     def step(i, _):
         rows = pl.ds(pl.multiple_of(i * block, block), block)
@@ -114,8 +119,8 @@
 
 
 def kernel(
-    frames, clips, halo, lengths, labels, own_a, own_v, got, wac, wap, wvc, wvp, keep, send,
-    cols, slope, hid, gemb, gpre, total, emb_a, emb_v, inv_a, inv_v, gacc, giacc, feats,
+    frames, clips, halo, lengths, labels, own_a, own_v, got, wac_in, wap_in, wvc_in, wvp_in, keep, send,
+    cols, slope, hid, gemb, gpre, total, emb_a, emb_v, inv_a, inv_v, gacc, giacc, feats, wac, wap, wvc, wvp, sems,
 ):
     me = lax.axis_index("tm")
     half = lax.rem(me, 2)
@@ -125,18 +130,32 @@
     block = 256 if frames % 256 == 0 else TILE
     per_clip = frames // block
 
-    if halo:
-        feats[0] = own_a[...]
-        feats[1] = own_v[...]
-    else:
-        seg = own_a.shape[1]
+    copies = []
+
+    def fetch(source, target):
+        copy = pltpu.make_async_copy(source, target, sems.at[len(copies)])
+        copy.start()
+        copies.append(copy)
+        return copy
+
+    def fetch_feats(m, own):
+        if halo:
+            return [fetch(own, feats.at[m])]
+        seg = own.shape[1]
         mine = pl.ds(pl.multiple_of(me * seg, seg), seg)
         other = pl.ds(pl.multiple_of((1 - me) * seg, seg), seg)
+        started = []
         for c in range(clips):
-            feats[0, c, mine, :] = own_a[first_clip + c]
-            feats[1, c, mine, :] = own_v[first_clip + c]
-            feats[0, c, other, :] = got[0, c]
-            feats[1, c, other, :] = got[1, c]
+            started.append(fetch(own.at[first_clip + c], feats.at[m, c, mine, :]))
+            started.append(fetch(got.at[m, c], feats.at[m, c, other, :]))
+        return started
+
+    feats_v = fetch_feats(1, own_v)
+    weights_v = [fetch(wvc_in, wvc), fetch(wvp_in, wvp)]
+    feats_a = fetch_feats(0, own_a)
+    weights_a = [fetch(wac_in, wac), fetch(wap_in, wap)]
+    gacc[...] = jnp.zeros(gacc.shape, F32)
+    giacc[...] = jnp.zeros(giacc.shape, F32)
 
     for c in range(clips):
         for lo in (0, PAD + frames):
@@ -154,11 +173,9 @@
         emb_v[pl.ds(at, block), :] = emb
         inv_v[pl.ds(at, block), :] = inv
 
-    forward(feats, 1, wvc, wvp, cols, slope, hid, clips, frames, block, put_v)
-    forward(feats, 0, wac, wap, cols, slope, hid, clips, frames, block, put_a)
-
-    gacc[...] = jnp.zeros(gacc.shape, F32)
-    giacc[...] = jnp.zeros(giacc.shape, F32)
+    forward(feats, 1, (feats_v, weights_v), wvc, wvp, cols, slope, hid, clips, frames, block, put_v)
+    forward(feats, 0, (feats_a, weights_a), wac, wap, cols, slope, hid, clips, frames, block, put_a)
+
     tiles = frames // TILE
     row = lax.broadcasted_iota(jnp.int32, (TILE, WIN), 0)
     col = lax.broadcasted_iota(jnp.int32, (TILE, WIN), 1)
@@ -224,8 +241,10 @@
     if halo:
         count = jnp.where(me == 0, count, 0.0)
     send_rows = send.shape[0] - 2 * PAD
-    send[send_rows : send_rows + PAD, :] = jnp.broadcast_to(digits_of(loss), (PAD, LANES)).astype(BF16)
-    send[send_rows + PAD :, :] = jnp.broadcast_to(digits_of(count), (PAD, LANES)).astype(BF16)
+    for at, value in ((send_rows, loss), (send_rows + PAD, count)):
+        digits = jnp.broadcast_to(digits_of(value), (PAD, LANES))
+        keep[at : at + PAD, :] = digits
+        send[at : at + PAD, :] = digits.astype(BF16)
 
     backward(1, wvp, cols, slope, hid, gemb, gpre, total, block, rows_total)
     hand_over(total, keep, send, 1, half)
@@ -249,10 +268,10 @@
     return pl.pallas_call(
         functools.partial(kernel, frames, clips, halo),
         out_shape=(
-            jax.ShapeDtypeStruct((2 * blocks * grad_rows, LANES), F32),
-            jax.ShapeDtypeStruct((2 * blocks * grad_rows + 2 * PAD, LANES), BF16),
+            pltpu.VMEM((2 * blocks * grad_rows + 2 * PAD, LANES), F32),
+            pltpu.VMEM((2 * blocks * grad_rows + 2 * PAD, LANES), BF16),
         ),
-        in_specs=[smem, smem] + [vmem] * 7,
+        in_specs=[smem, smem] + [pl.BlockSpec(memory_space=pl.ANY)] * 7,
         out_specs=(vmem, vmem),
         scratch_shapes=[
             pltpu.VMEM((2, rows, taps * chan), BF16),
@@ -268,8 +287,13 @@
             pltpu.VMEM((clips, frames + 2 * PAD, width), F32),
             pltpu.VMEM((clips, frames + 2 * PAD, LANES), F32),
             pltpu.VMEM((2, clips, frames, chan), BF16),
+            pltpu.VMEM((taps * chan, width), BF16),
+            pltpu.VMEM((width, width), BF16),
+            pltpu.VMEM((taps * chan, width), BF16),
+            pltpu.VMEM((width, width), BF16),
+            pltpu.SemaphoreType.DMA((4 * clips + 4,)),
         ],
-        compiler_params=pltpu.CompilerParams(vmem_limit_bytes=60 * 1024 * 1024),
+        compiler_params=pltpu.CompilerParams(vmem_limit_bytes=56 * 1024 * 1024),
     )(lengths, labels, own_a, own_v, got, wac, wap, wvc, wvp)
 
 
@@ -341,66 +365,130 @@
     return bits
 
 
+def place_in_kernel(bits):
+    clip, odd = lax.axis_index("clip"), lax.rem(lax.axis_index("tm"), 2)
+    return jnp.where(odd == 0, lax.rem(clip // bits[0], 4), lax.rem(clip // bits[1], 4))
+
+
+def sum_kernel(bits, count, base, *refs):
+    got, mine, outs = refs[:count], refs[count], refs[count + 1 :]
+    me = place_in_kernel(bits)
+    part = mine.shape[0] - 2 * PAD
+
+    def total(rows):
+        value = base[rows, :]
+        for ref in got:
+            value = value + ref[rows, :].astype(F32)
+        return value
+
+    tile = total(pl.ds(4 * part, 2 * PAD))
+    mine[part:, :] = tile
+    for k, out in enumerate(outs):
+        out[0:part, :] = total(pl.ds(pl.multiple_of((me ^ (k + 1)) * part, PAD), part)).astype(BF16)
+        out[part:, :] = tile.astype(BF16)
+    mine[0:part, :] = total(pl.ds(pl.multiple_of(me * part, PAD), part))
+
+
+def sum_and_deal(base, got, bits):
+    part = (base.shape[0] - 2 * PAD) // 4 + 2 * PAD
+    vmem = pl.BlockSpec(memory_space=pltpu.VMEM)
+    return pl.pallas_call(
+        functools.partial(sum_kernel, bits, len(got)),
+        out_shape=[pltpu.VMEM((part, LANES), F32)] + [pltpu.VMEM((part, LANES), BF16)] * 3,
+        in_specs=[vmem] * (1 + len(got)),
+        out_specs=[vmem] * 4,
+        compiler_params=pltpu.CompilerParams(vmem_limit_bytes=16 * 1024 * 1024),
+    )(base, *got)
+
+
 def reduce_all(keep, send):
     got = swap(send, "tm", 1)
-    rows = keep.shape[0]
-    total = keep + got[:rows].astype(F32)
-    tile = (send[rows:].astype(F32) + got[rows:].astype(F32)).astype(BF16)
     rest = [("tm", bit) for bit in bits_of("tm")[1:]] + [("clip", bit) for bit in bits_of("clip")[4:]]
-    for axis, bit in rest:
-        total, tile = halve(total, axis, bit, tile)
-    total, tile = quarter(total.reshape(4, -1, LANES), (1, 4), tile)
-    total, tile = quarter(total.reshape(4, -1, LANES), (4, 1), tile)
-    mine = quadruple(total.astype(BF16), (4, 1))
-    mine = quadruple(mine, (1, 4))
+    rounds = ((1, 4), (4, 1))
+    if rest:
+        total = keep + got.astype(F32)
+        total, tile = total[: -2 * PAD], total[-2 * PAD :].astype(BF16)
+        for axis, bit in rest:
+            total, tile = halve(total, axis, bit, tile)
+        for bits in rounds:
+            total, tile = quarter(total.reshape(4, -1, LANES), bits, tile)
+    else:
+        total, got = keep, [got]
+        for bits in rounds:
+            total, *outs = sum_and_deal(total, got, bits)
+            got = [swap_by_core(out, ((k + 1) * bits[0], (k + 1) * bits[1])) for k, out in enumerate(outs)]
+        for value in got:
+            total = total + value.astype(F32)
+        total, tile = total[: -2 * PAD], total[-2 * PAD :].astype(BF16)
+    mine = total.astype(BF16)
+    for bits in rounds[::-1]:
+        mine = quadruple(mine, bits)
     for axis, bit in rest[::-1]:
         mine = double(mine, axis, bit)
-    return mine, swap(mine, "tm", 1), tile
-
-
-def finish_kernel(mine_c, got_c, mine_p, got_p, tile, loss, ac, ap, vc, vp):
+    return mine, tile
+
+
+def finish_kernel(own, *refs):
+    if own:
+        mine, tile, loss, scale_out, *outs = refs[:8]
+        digits = tile[...].astype(F32)
+        count = value_of(digits[PAD : PAD + 1])
+        scale = 1.0 / count
+        loss[0, 0] = value_of(digits[0:1]) / count
+        scale_out[0, 0] = scale
+    else:
+        mine, scale_in, *outs = refs[:2] + refs[6:10]
+        scale = scale_in[0, 0]
+    staged, sems = refs[-2:]
+    blocks, width = mine.shape[1], mine.shape[1] * LANES
     half = lax.rem(lax.axis_index("tm"), 2)
-    digits = tile[...].astype(F32)
-    count = value_of(digits[PAD : PAD + 1])
-    scale = 1.0 / count
-    loss[...] = jnp.broadcast_to(value_of(digits[0:1]) / count, loss.shape)
-    for mine, got, outs in ((mine_c, got_c, (ac, vc)), (mine_p, got_p, (ap, vp))):
-        for m, out in enumerate(outs):
-            blocks = mine.shape[1]
-            for j in range(blocks):
-                at = pl.multiple_of((half * blocks + j) * LANES, LANES)
-                out[:, pl.ds(at, LANES)] = mine[m, j].astype(F32) * scale
-                at = pl.multiple_of(((1 - half) * blocks + j) * LANES, LANES)
-                out[:, pl.ds(at, LANES)] = got[m, j].astype(F32) * scale
-
-
-def finish(mine, got, tile, conv_rows, width):
-    blocks = width // 2 // LANES
+    half = half if own else 1 - half
+    columns = pl.ds(pl.multiple_of(half * width, width), width)
+    copies = []
+    at = 0
+    for n, out in enumerate(outs):
+        m, rows = n // 2, out.shape[0]
+        at = at if n % 2 else 0
+        for j in range(blocks):
+            staged[m, at : at + rows, j * LANES : (j + 1) * LANES] = mine[m, j, at : at + rows, :].astype(F32) * scale
+        copy = pltpu.make_async_copy(staged.at[m, at : at + rows, :], out.at[:, columns], sems.at[n])
+        copy.start()
+        copies.append(copy)
+        at += rows
+    for copy in copies:
+        copy.wait()
+
+
+def finish(mine, tile, conv_rows, width):
     rows = conv_rows + width
-    mine = mine.reshape(2, blocks, rows, LANES)
-    got = got.reshape(2, blocks, rows, LANES)
-    steps = 4
-    conv, proj = conv_rows // steps, width // steps
-    skip = conv_rows // proj
-    conv_spec = pl.BlockSpec((2, blocks, conv, LANES), lambda i: (0, 0, i, 0))
-    proj_spec = pl.BlockSpec((2, blocks, proj, LANES), lambda i: (0, 0, skip + i, 0))
-    conv_out = pl.BlockSpec((conv, width), lambda i: (i, 0))
-    proj_out = pl.BlockSpec((proj, width), lambda i: (i, 0))
-    one = pl.BlockSpec((8, LANES), lambda i: (0, 0))
-    return pl.pallas_call(
-        finish_kernel,
-        grid=(steps,),
-        out_shape=(
-            jax.ShapeDtypeStruct((8, LANES), F32),
-            jax.ShapeDtypeStruct((conv_rows, width), F32),
-            jax.ShapeDtypeStruct((width, width), F32),
-            jax.ShapeDtypeStruct((conv_rows, width), F32),
-            jax.ShapeDtypeStruct((width, width), F32),
-        ),
-        in_specs=[conv_spec, conv_spec, proj_spec, proj_spec, pl.BlockSpec((2 * PAD, LANES), lambda i: (0, 0))],
-        out_specs=(one, conv_out, proj_out, conv_out, proj_out),
-        compiler_params=pltpu.CompilerParams(vmem_limit_bytes=32 * 1024 * 1024),
-    )(mine, got, mine, got, tile)
+    shape = (2, width // 2 // LANES, rows, LANES)
+    got = swap(mine, "tm", 1)
+    smem, vmem, hbm = (pl.BlockSpec(memory_space=space) for space in (pltpu.SMEM, pltpu.VMEM, pl.ANY))
+    grads = [jax.ShapeDtypeStruct((n, width), F32) for n in (conv_rows, width) * 2]
+    one = jax.ShapeDtypeStruct((1, 1), F32)
+    scratch = [pltpu.VMEM((2, rows, width // 2), F32), pltpu.SemaphoreType.DMA((4,))]
+    params = pltpu.CompilerParams(vmem_limit_bytes=16 * 1024 * 1024)
+    cost = pl.CostEstimate(flops=rows * width, bytes_accessed=rows * width * 6, transcendentals=0)
+    loss, scale, *outs = pl.pallas_call(
+        functools.partial(finish_kernel, True),
+        out_shape=[one, one] + grads,
+        in_specs=[vmem, vmem],
+        out_specs=[smem, smem] + [hbm] * 4,
+        scratch_shapes=scratch,
+        compiler_params=params,
+        cost_estimate=cost,
+    )(mine.reshape(shape), tile)
+    outs = pl.pallas_call(
+        functools.partial(finish_kernel, False),
+        out_shape=grads,
+        in_specs=[vmem, smem] + [hbm] * 4,
+        out_specs=[hbm] * 4,
+        scratch_shapes=scratch,
+        input_output_aliases={n + 2: n for n in range(4)},
+        compiler_params=params,
+        cost_estimate=cost,
+    )(got.reshape(shape), scale, *outs)
+    return loss, outs
 
 
 def shards(
@@ -430,10 +518,10 @@
     keep, send = local_grads(
         halo, lengths, labels, audio_feats, lip_feats, got, w_audio_conv, w_audio_proj, w_lip_conv, w_lip_proj
     )
-    mine, got, tile = reduce_all(keep, send)
+    mine, tile = reduce_all(keep, send)
     taps, chan, width = w_audio_conv.shape
-    loss, ac, ap, vc, vp = finish(mine, got, tile, taps * chan, width)
-    return (loss[0, 0], ac.reshape(w_audio_conv.shape), ap, vc.reshape(w_lip_conv.shape), vp)
+    loss, (ac, ap, vc, vp) = finish(mine, tile, taps * chan, width)
+    return (loss.reshape(()), ac.reshape(w_audio_conv.shape), ap, vc.reshape(w_lip_conv.shape), vp)
 
 
 def solution(mesh):

time: 90 us -> 82 us (0.911)
  other arithmetic: 5.85 us -> 0.54 us
  local copies, waits for them, and re-layouts: 3.61 us -> 1.87 us
  waiting for transfers between devices: 33.4 us -> 31.7 us
    ppermute x3, waiting for transfers between devices: 7.08 us -> 4.61 us  [swap(): lax.ppermute(value, axis, [(i, i ^ bit) for i in range(lax.axis_size(axis...]
    add x2 -> x0, other arithmetic: 2.44 us -> none  [the longest x1 2.32 us: reduce_all(): total = keep + got[:rows].astype(F32)]
    convert_element_type x10 -> x0, other arithmetic: 1.93 us -> none  [the longest x6 1.15 us: quarter(): got = swap_by_core(out, (k * bits[0], k * bits[1])).astype(F32)]
    pallas_call x1 -> x4, Pallas kernels: 3.47 us -> 4.83 us  [the longest x1 2.26 us: finish(): pl.pallas_call(functools.partial(finish_kernel, True), out_shape=[one, on...]
    unnamed x4 -> x2, local copies, waits for them, and re-layouts: 1.85 us -> 0.79 us
    pallas_call x1, Pallas kernels: 19.9 us -> 18.9 us  [local_grads(): pl.pallas_call(functools.partial(kernel, frames, clips, halo), out_shape=...]
    concatenate x2 -> x0, other arithmetic: 0.99 us -> none  [quarter(): out = jnp.concatenate([pick(parts, me ^ k).astype(BF16), tile])]
  transfers between devices with their start and end apart: 15 -> 15, of which waited for: 13 -> 13; matrix products, arithmetic and copies ran while one was open for 1% -> 0% of each run, Pallas kernels for 0% -> 3%
where the time goes in v4:
time: 82 us; the launch traced here: 81.9 us
  waiting for transfers between devices  31.7 us (39%)
  Pallas kernels  23.7 us (29%)
  starting transfers between devices  23.1 us (28%)
  local copies, waits for them, and re-layouts  1.87 us (2%)
  between operations  0.89 us (1%)
    ppermute x12, waiting for transfers between devices, swap_by_core(): return lax.ppermute(value, ('clip', 'tm'), pairs)  27.1 us
    pallas_call x1, Pallas kernels, local_grads(): pl.pallas_call(functools.partial(kernel, frames, clips, halo), out_shape=...  18.9 us
    ppermute x12, starting transfers between devices, swap_by_core(): return lax.ppermute(value, ('clip', 'tm'), pairs)  16.9 us
    ppermute x3, starting transfers between devices, swap(): lax.ppermute(value, axis, [(i, i ^ bit) for i in range(lax.axis_size(axis...  6.19 us
    ppermute x3, waiting for transfers between devices, swap(): lax.ppermute(value, axis, [(i, i ^ bit) for i in range(lax.axis_size(axis...  4.61 us
    pallas_call x1, Pallas kernels, finish(): pl.pallas_call(functools.partial(finish_kernel, True), out_shape=[one, on...  2.26 us
    pallas_call x1, Pallas kernels, finish(): pl.pallas_call(functools.partial(finish_kernel, False), out_shape=grads,...  2.19 us
  transfers between devices with their start and end apart: 15, of which 13 were waited for; matrix products, arithmetic and copies ran while one was open for 0% of the time, Pallas kernels for 3%

profile of v4, /device:TPU:0, one launch (start us, length us, event | category | flops | bytes accessed | tf_op | source)
XLA Modules:
  0.0 81.9 jit_solution(8942070509549300339)
XLA Ops:
  0.6 1.1 %dynamic-slice_bitcast_fusion = (bf16[1,2,256,256]{3,2,1,0:T(8,128)(2,1)S(1)}, bf16[1,2,256,256]{3,2,1,0:T(8,128)(2,1)S(1)}) fusion(bf16[4,256,256]{2,1,0:T(8,128)(2,1)} %own_v.1, s32[]{:T(128)S(6)} %select_n.194, bf16[4,256,256]{2,1,0:T(8,128)(2,1)} %own_a.1), kind=kLoop, calls=%fused_computation.7 | loop fusion | bytes 1048580 | tf_op jit(solution)/shard_map/stack | solution.py:502
  2.3 1.5 %collective-permute-done.got = bf16[2,2,256,256]{3,2,1,0:T(8,128)(2,1)S(1)} collective-permute-done((bf16[2,2,256,256]{3,2,1,0:T(8,128)(2,1)S(1)}, bf16[2,2,256,256]{3,2,1,0:T(8,128)(2,1)S(1)}, u32[]{:S(2)}, u32[]{:S(2)}) %collective-permute-start) | collective-permute-done | bytes 524320 | tf_op jit(solution)/shard_map/ppermute | solution.py:301
  4.6 18.9 %shard_map.119 = (f32[5152,128]{1,0:T(8,128)S(1)}, bf16[5152,128]{1,0:T(8,128)(2,1)S(1)}) custom-call(s32[4]{0:T(128)} %lengths.1, s32[4]{0:T(128)} %labels.1, bf16[4,256,256]{2,1,0:T(8,128)(2,1)} %own_a.1, bf16[4,256,256]{2,1,0:T(8,128)(2,1)} %own_v.1, bf16[2,2,256,256]{3,2,1,0:T(8,128)(2,1)} %copy-done, bf16[768,512]{1,0:T(8,128)(2,1)} %bitcast.41, ...), custom_call_target="tpu_custom_call" | custom-call | tf_op jit(solution)/shard_map/pallas_call | solution.py:268
  24.0 2.7 %collective-permute-done.1.refs_0_ = bf16[5152,128]{1,0:T(8,128)(2,1)S(1)} collective-permute-done((bf16[5152,128]{1,0:T(8,128)(2,1)S(1)}, bf16[5152,128]{1,0:T(8,128)(2,1)S(1)}, u32[]{:S(2)}, u32[]{:S(2)}) %collective-permute-start.1) | collective-permute-done | bytes 1318944 | tf_op jit(solution)/shard_map/ppermute | solution.py:301
  26.9 2.9 %collective-permute-start.2 = (bf16[1312,128]{1,0:T(8,128)(2,1)S(1)}, bf16[1312,128]{1,0:T(8,128)(2,1)S(1)}, u32[]{:S(2)}, u32[]{:S(2)}) collective-permute-start(bf16[1312,128]{1,0:T(8,128)(2,1)S(1)} %get-tuple-element.28), channel_id=1, source_target_pairs={{0,2},{1,9},{2,0},{3,11},{4,6},{5,13},{6,4},{7,15},{8,10},{9,1},{1... | collective-permute-start | bytes 1007624 | tf_op jit(solution)/shard_map/ppermute | solution.py:310
  29.8 1.5 %collective-permute-start.3 = (bf16[1312,128]{1,0:T(8,128)(2,1)S(1)}, bf16[1312,128]{1,0:T(8,128)(2,1)S(1)}, u32[]{:S(2)}, u32[]{:S(2)}) collective-permute-start(bf16[1312,128]{1,0:T(8,128)(2,1)S(1)} %get-tuple-element.29), channel_id=1, source_target_pairs={{0,4},{1,17},{2,6},{3,19},{4,0},{5,21},{6,2},{7,23},{8,12},{9,25},... | collective-permute-start | bytes 1007624 | tf_op jit(solution)/shard_map/ppermute | solution.py:310
  31.3 3.6 %collective-permute-done.2.refs_0_ = bf16[1312,128]{1,0:T(8,128)(2,1)S(1)} collective-permute-done((bf16[1312,128]{1,0:T(8,128)(2,1)S(1)}, bf16[1312,128]{1,0:T(8,128)(2,1)S(1)}, u32[]{:S(2)}, u32[]{:S(2)}) %collective-permute-start.2) | collective-permute-done | bytes 335904 | tf_op jit(solution)/shard_map/ppermute | solution.py:310
  34.9 5.6 %collective-permute-done.3.refs_1_ = bf16[1312,128]{1,0:T(8,128)(2,1)S(1)} collective-permute-done((bf16[1312,128]{1,0:T(8,128)(2,1)S(1)}, bf16[1312,128]{1,0:T(8,128)(2,1)S(1)}, u32[]{:S(2)}, u32[]{:S(2)}) %collective-permute-start.3) | collective-permute-done | bytes 335904 | tf_op jit(solution)/shard_map/ppermute | solution.py:310
  40.7 1.6 %collective-permute-start.5 = (bf16[352,128]{1,0:T(8,128)(2,1)S(1)}, bf16[352,128]{1,0:T(8,128)(2,1)S(1)}, u32[]{:S(2)}, u32[]{:S(2)}) collective-permute-start(bf16[352,128]{1,0:T(8,128)(2,1)S(1)} %get-tuple-element.32), channel_id=1, source_target_pairs={{0,8},{1,3},{2,10},{3,1},{4,12},{5,7},{6,14},{7,5},{8,0},{9,11},{1... | collective-permute-start | bytes 270344 | tf_op jit(solution)/shard_map/ppermute | solution.py:310
  42.3 2.6 %collective-permute-start.6 = (bf16[352,128]{1,0:T(8,128)(2,1)S(1)}, bf16[352,128]{1,0:T(8,128)(2,1)S(1)}, u32[]{:S(2)}, u32[]{:S(2)}) collective-permute-start(bf16[352,128]{1,0:T(8,128)(2,1)S(1)} %get-tuple-element.33), channel_id=1, source_target_pairs={{0,16},{1,5},{2,18},{3,7},{4,20},{5,1},{6,22},{7,3},{8,24},{9,13},... | collective-permute-start | bytes 270344 | tf_op jit(solution)/shard_map/ppermute | solution.py:310
  45.3 4.3 %collective-permute-done.6 = bf16[352,128]{1,0:T(8,128)(2,1)S(1)} collective-permute-done((bf16[352,128]{1,0:T(8,128)(2,1)S(1)}, bf16[352,128]{1,0:T(8,128)(2,1)S(1)}, u32[]{:S(2)}, u32[]{:S(2)}) %collective-permute-start.6) | collective-permute-done | bytes 90144 | tf_op jit(solution)/shard_map/ppermute | solution.py:310
  49.6 1.8 %collective-permute-done.7 = bf16[352,128]{1,0:T(8,128)(2,1)S(1)} collective-permute-done((bf16[352,128]{1,0:T(8,128)(2,1)S(1)}, bf16[352,128]{1,0:T(8,128)(2,1)S(1)}, u32[]{:S(2)}, u32[]{:S(2)}) %collective-permute-start.7) | collective-permute-done | bytes 90144 | tf_op jit(solution)/shard_map/ppermute | solution.py:310
  51.5 1.7 %collective-permute-start.10 = (bf16[320,128]{1,0:T(8,128)(2,1)S(1)}, bf16[320,128]{1,0:T(8,128)(2,1)S(1)}, u32[]{:S(2)}, u32[]{:S(2)}) collective-permute-start(bf16[320,128]{1,0:T(8,128)(2,1)S(1)} %slice.10), channel_id=1, source_target_pairs={{0,24},{1,7},{2,26},{3,5},{4,28},{5,3},{6,30},{7,1},{8,16},{9,15},... | collective-permute-start | bytes 245768 | tf_op jit(solution)/shard_map/ppermute | solution.py:310
  53.7 2.2 %collective-permute-start.8 = (bf16[320,128]{1,0:T(8,128)(2,1)S(1)}, bf16[320,128]{1,0:T(8,128)(2,1)S(1)}, u32[]{:S(2)}, u32[]{:S(2)}) collective-permute-start(bf16[320,128]{1,0:T(8,128)(2,1)S(1)} %slice.10), channel_id=1, source_target_pairs={{0,8},{1,3},{2,10},{3,1},{4,12},{5,7},{6,14},{7,5},{8,0},{9,11},{1... | collective-permute-start | bytes 245768 | tf_op jit(solution)/shard_map/ppermute | solution.py:310
  55.9 1.9 %collective-permute-done.10 = bf16[320,128]{1,0:T(8,128)(2,1)S(1)} collective-permute-done((bf16[320,128]{1,0:T(8,128)(2,1)S(1)}, bf16[320,128]{1,0:T(8,128)(2,1)S(1)}, u32[]{:S(2)}, u32[]{:S(2)}) %collective-permute-start.10) | collective-permute-done | bytes 81952 | tf_op jit(solution)/shard_map/ppermute | solution.py:310
  57.8 1.7 %collective-permute-done.9 = bf16[320,128]{1,0:T(8,128)(2,1)S(1)} collective-permute-done((bf16[320,128]{1,0:T(8,128)(2,1)S(1)}, bf16[320,128]{1,0:T(8,128)(2,1)S(1)}, u32[]{:S(2)}, u32[]{:S(2)}) %collective-permute-start.9) | collective-permute-done | bytes 81952 | tf_op jit(solution)/shard_map/ppermute | solution.py:310
  59.6 1.7 %collective-permute-start.13 = (bf16[1280,128]{1,0:T(8,128)(2,1)S(1)}, bf16[1280,128]{1,0:T(8,128)(2,1)S(1)}, u32[]{:S(2)}, u32[]{:S(2)}) collective-permute-start(bf16[1280,128]{1,0:T(8,128)(2,1)S(1)} %bitcast.38), channel_id=1, source_target_pairs={{0,6},{1,25},{2,4},{3,27},{4,2},{5,29},{6,0},{7,31},{8,14},{9,17},... | collective-permute-start | bytes 983048 | tf_op jit(solution)/shard_map/ppermute | solution.py:310
  61.4 0.8 collective-permute-start.12
  62.1 1.0 %collective-permute-start.11 = (bf16[1280,128]{1,0:T(8,128)(2,1)S(1)}, bf16[1280,128]{1,0:T(8,128)(2,1)S(1)}, u32[]{:S(2)}, u32[]{:S(2)}) collective-permute-start(bf16[1280,128]{1,0:T(8,128)(2,1)S(1)} %bitcast.40), channel_id=1, source_target_pairs={{0,2},{1,9},{2,0},{3,11},{4,6},{5,13},{6,4},{7,15},{8,10},{9,1},{1... | collective-permute-start | bytes 983048 | tf_op jit(solution)/shard_map/ppermute | solution.py:310
  63.2 4.6 %collective-permute-done.13 = bf16[1280,128]{1,0:T(8,128)(2,1)S(1)} collective-permute-done((bf16[1280,128]{1,0:T(8,128)(2,1)S(1)}, bf16[1280,128]{1,0:T(8,128)(2,1)S(1)}, u32[]{:S(2)}, u32[]{:S(2)}) %collective-permute-start.13) | collective-permute-done | bytes 327712 | tf_op jit(solution)/shard_map/ppermute | solution.py:310
  67.8 3.4 %collective-permute-done.12 = bf16[1280,128]{1,0:T(8,128)(2,1)S(1)} collective-permute-done((bf16[1280,128]{1,0:T(8,128)(2,1)S(1)}, bf16[1280,128]{1,0:T(8,128)(2,1)S(1)}, u32[]{:S(2)}, u32[]{:S(2)}) %collective-permute-start.12) | collective-permute-done | bytes 327712 | tf_op jit(solution)/shard_map/ppermute | solution.py:310
  71.6 5.2 %collective-permute-start.14 = (bf16[5120,128]{1,0:T(8,128)(2,1)S(1)}, bf16[5120,128]{1,0:T(8,128)(2,1)S(1)}, u32[]{:S(2)}, u32[]{:S(2)}) collective-permute-start(bf16[5120,128]{1,0:T(8,128)(2,1)S(1)} %bitcast.33), channel_id=1, source_target_pairs={{0,1},{1,0},{2,3},{3,2},{4,5},{5,4},{6,7},{7,6},{8,9},{9,8},{10,11... | collective-permute-start | bytes 3932168 | tf_op jit(solution)/shard_map/ppermute | solution.py:301
  76.9 2.3 %shard_map.122 = (f32[1,1]{1,0:T(1,128)}, f32[1,1]{1,0:T(1,128)}, f32[768,512]{1,0:T(8,128)}, f32[512,512]{1,0:T(8,128)}, f32[768,512]{1,0:T(8,128)}, /*index=5*/f32[512,512]{1,0:T(8,128)}) custom-call(bf16[2,2,1280,128]{3,2,1,0:T(8,128)(2,1)S(1)} %bitcast.34, bf16[32,128]{1,0:T(8,128)(2,1)S(1)} %slice.11.refs_1_), custom_call_target="tpu_custom_call" | custom-call | flops 655360 | bytes 3932160 | tf_op jit(solution)/shard_map/pallas_call | solution.py:472
  79.5 2.2 %shard_map.123 = (f32[768,512]{1,0:T(8,128)}, f32[512,512]{1,0:T(8,128)}, f32[768,512]{1,0:T(8,128)}, f32[512,512]{1,0:T(8,128)}) custom-call(bf16[2,2,1280,128]{3,2,1,0:T(8,128)(2,1)S(1)} %bitcast.35, f32[1,1]{1,0:T(1,128)} %get-tuple-element.36.refs_1_, ...), custom_call_target="tpu_custom_call", output_to_operand_aliasing={{0}: (2, {}), {1}: (3, {}), {2}: (4, {}), {3}: (5, {})} | custom-call | flops 655360 | bytes 3932160 | tf_op jit(solution)/shard_map/pallas_call | solution.py:481
  (22 shorter events, 4.0 us)
Async XLA Ops:
  1.8 2.1 %collective-permute-start = (bf16[2,2,256,256]{3,2,1,0:T(8,128)(2,1)S(1)}, bf16[2,2,256,256]{3,2,1,0:T(8,128)(2,1)S(1)}, u32[]{:S(2)}, u32[]{:S(2)}) collective-permute-start(bf16[2,2,256,256]{3,2,1,0:T(8,128)(2,1)S(1)} %pad_maximum_fusion.1), channel_id=1, source_target_pairs={{0,1},{1,0},{2,3},{3,2},{4,5},{5,4},{6,7},{7,6},{8,9},{9,8},{10,11... | collective-permute-start | bytes 1572872 | tf_op jit(solution)/shard_map/ppermute | solution.py:301
  3.8 0.8 copy-start
  23.5 3.1 %collective-permute-start.1 = (bf16[5152,128]{1,0:T(8,128)(2,1)S(1)}, bf16[5152,128]{1,0:T(8,128)(2,1)S(1)}, u32[]{:S(2)}, u32[]{:S(2)}) collective-permute-start(bf16[5152,128]{1,0:T(8,128)(2,1)S(1)} %get-tuple-element.26), channel_id=1, source_target_pairs={{0,1},{1,0},{2,3},{3,2},{4,5},{5,4},{6,7},{7,6},{8,9},{9,8},{10,11... | collective-permute-start | bytes 3956744 | tf_op jit(solution)/shard_map/ppermute | solution.py:301
  26.9 8.1 %collective-permute-start.2 = (bf16[1312,128]{1,0:T(8,128)(2,1)S(1)}, bf16[1312,128]{1,0:T(8,128)(2,1)S(1)}, u32[]{:S(2)}, u32[]{:S(2)}) collective-permute-start(bf16[1312,128]{1,0:T(8,128)(2,1)S(1)} %get-tuple-element.28), channel_id=1, source_target_pairs={{0,2},{1,9},{2,0},{3,11},{4,6},{5,13},{6,4},{7,15},{8,10},{9,1},{1... | collective-permute-start | bytes 1007624 | tf_op jit(solution)/shard_map/ppermute | solution.py:310
  29.8 10.8 %collective-permute-start.3 = (bf16[1312,128]{1,0:T(8,128)(2,1)S(1)}, bf16[1312,128]{1,0:T(8,128)(2,1)S(1)}, u32[]{:S(2)}, u32[]{:S(2)}) collective-permute-start(bf16[1312,128]{1,0:T(8,128)(2,1)S(1)} %get-tuple-element.29), channel_id=1, source_target_pairs={{0,4},{1,17},{2,6},{3,19},{4,0},{5,21},{6,2},{7,23},{8,12},{9,25},... | collective-permute-start | bytes 1007624 | tf_op jit(solution)/shard_map/ppermute | solution.py:310
  31.3 9.2 %collective-permute-start.4 = (bf16[1312,128]{1,0:T(8,128)(2,1)S(1)}, bf16[1312,128]{1,0:T(8,128)(2,1)S(1)}, u32[]{:S(2)}, u32[]{:S(2)}) collective-permute-start(bf16[1312,128]{1,0:T(8,128)(2,1)S(1)} %get-tuple-element.30), channel_id=1, source_target_pairs={{0,6},{1,25},{2,4},{3,27},{4,2},{5,29},{6,0},{7,31},{8,14},{9,17},... | collective-permute-start | bytes 1007624 | tf_op jit(solution)/shard_map/ppermute | solution.py:310
  40.7 4.6 %collective-permute-start.5 = (bf16[352,128]{1,0:T(8,128)(2,1)S(1)}, bf16[352,128]{1,0:T(8,128)(2,1)S(1)}, u32[]{:S(2)}, u32[]{:S(2)}) collective-permute-start(bf16[352,128]{1,0:T(8,128)(2,1)S(1)} %get-tuple-element.32), channel_id=1, source_target_pairs={{0,8},{1,3},{2,10},{3,1},{4,12},{5,7},{6,14},{7,5},{8,0},{9,11},{1... | collective-permute-start | bytes 270344 | tf_op jit(solution)/shard_map/ppermute | solution.py:310
  42.3 7.3 %collective-permute-start.6 = (bf16[352,128]{1,0:T(8,128)(2,1)S(1)}, bf16[352,128]{1,0:T(8,128)(2,1)S(1)}, u32[]{:S(2)}, u32[]{:S(2)}) collective-permute-start(bf16[352,128]{1,0:T(8,128)(2,1)S(1)} %get-tuple-element.33), channel_id=1, source_target_pairs={{0,16},{1,5},{2,18},{3,7},{4,20},{5,1},{6,22},{7,3},{8,24},{9,13},... | collective-permute-start | bytes 270344 | tf_op jit(solution)/shard_map/ppermute | solution.py:310
  44.9 6.4 %collective-permute-start.7 = (bf16[352,128]{1,0:T(8,128)(2,1)S(1)}, bf16[352,128]{1,0:T(8,128)(2,1)S(1)}, u32[]{:S(2)}, u32[]{:S(2)}) collective-permute-start(bf16[352,128]{1,0:T(8,128)(2,1)S(1)} %get-tuple-element.34), channel_id=1, source_target_pairs={{0,24},{1,7},{2,26},{3,5},{4,28},{5,3},{6,30},{7,1},{8,16},{9,15},... | collective-permute-start | bytes 270344 | tf_op jit(solution)/shard_map/ppermute | solution.py:310
  51.5 6.3 %collective-permute-start.10 = (bf16[320,128]{1,0:T(8,128)(2,1)S(1)}, bf16[320,128]{1,0:T(8,128)(2,1)S(1)}, u32[]{:S(2)}, u32[]{:S(2)}) collective-permute-start(bf16[320,128]{1,0:T(8,128)(2,1)S(1)} %slice.10), channel_id=1, source_target_pairs={{0,24},{1,7},{2,26},{3,5},{4,28},{5,3},{6,30},{7,1},{8,16},{9,15},... | collective-permute-start | bytes 245768 | tf_op jit(solution)/shard_map/ppermute | solution.py:310
  53.2 6.3 %collective-permute-start.9 = (bf16[320,128]{1,0:T(8,128)(2,1)S(1)}, bf16[320,128]{1,0:T(8,128)(2,1)S(1)}, u32[]{:S(2)}, u32[]{:S(2)}) collective-permute-start(bf16[320,128]{1,0:T(8,128)(2,1)S(1)} %slice.10), channel_id=1, source_target_pairs={{0,16},{1,5},{2,18},{3,7},{4,20},{5,1},{6,22},{7,3},{8,24},{9,13},... | collective-permute-start | bytes 245768 | tf_op jit(solution)/shard_map/ppermute | solution.py:310
  53.7 5.8 %collective-permute-start.8 = (bf16[320,128]{1,0:T(8,128)(2,1)S(1)}, bf16[320,128]{1,0:T(8,128)(2,1)S(1)}, u32[]{:S(2)}, u32[]{:S(2)}) collective-permute-start(bf16[320,128]{1,0:T(8,128)(2,1)S(1)} %slice.10), channel_id=1, source_target_pairs={{0,8},{1,3},{2,10},{3,1},{4,12},{5,7},{6,14},{7,5},{8,0},{9,11},{1... | collective-permute-start | bytes 245768 | tf_op jit(solution)/shard_map/ppermute | solution.py:310
  59.6 8.1 %collective-permute-start.13 = (bf16[1280,128]{1,0:T(8,128)(2,1)S(1)}, bf16[1280,128]{1,0:T(8,128)(2,1)S(1)}, u32[]{:S(2)}, u32[]{:S(2)}) collective-permute-start(bf16[1280,128]{1,0:T(8,128)(2,1)S(1)} %bitcast.38), channel_id=1, source_target_pairs={{0,6},{1,25},{2,4},{3,27},{4,2},{5,29},{6,0},{7,31},{8,14},{9,17},... | collective-permute-start | bytes 983048 | tf_op jit(solution)/shard_map/ppermute | solution.py:310
  61.4 9.8 %collective-permute-start.12 = (bf16[1280,128]{1,0:T(8,128)(2,1)S(1)}, bf16[1280,128]{1,0:T(8,128)(2,1)S(1)}, u32[]{:S(2)}, u32[]{:S(2)}) collective-permute-start(bf16[1280,128]{1,0:T(8,128)(2,1)S(1)} %bitcast.39), channel_id=1, source_target_pairs={{0,4},{1,17},{2,6},{3,19},{4,0},{5,21},{6,2},{7,23},{8,12},{9,25},... | collective-permute-start | bytes 983048 | tf_op jit(solution)/shard_map/ppermute | solution.py:310
  62.1 9.1 %collective-permute-start.11 = (bf16[1280,128]{1,0:T(8,128)(2,1)S(1)}, bf16[1280,128]{1,0:T(8,128)(2,1)S(1)}, u32[]{:S(2)}, u32[]{:S(2)}) collective-permute-start(bf16[1280,128]{1,0:T(8,128)(2,1)S(1)} %bitcast.40), channel_id=1, source_target_pairs={{0,2},{1,9},{2,0},{3,11},{4,6},{5,13},{6,4},{7,15},{8,10},{9,1},{1... | collective-permute-start | bytes 983048 | tf_op jit(solution)/shard_map/ppermute | solution.py:310
  71.6 7.9 %collective-permute-start.14 = (bf16[5120,128]{1,0:T(8,128)(2,1)S(1)}, bf16[5120,128]{1,0:T(8,128)(2,1)S(1)}, u32[]{:S(2)}, u32[]{:S(2)}) collective-permute-start(bf16[5120,128]{1,0:T(8,128)(2,1)S(1)} %bitcast.33), channel_id=1, source_target_pairs={{0,1},{1,0},{2,3},{3,2},{4,5},{5,4},{6,7},{7,6},{8,9},{9,8},{10,11... | collective-permute-start | bytes 3932168 | tf_op jit(solution)/shard_map/ppermute | solution.py:301

commit v5 on v4

--- a/solution.py
+++ b/solution.py
@@ -12,6 +12,7 @@
 TILE = 128
 WIN = TILE + 2 * PAD
 HALO = 64
+TILES = 2 * PAD
 LANES = 128
 DIGITS = 48
 FRACTION = 20
@@ -58,22 +59,21 @@
         x = feats[m, c].astype(F32)
         row = lax.broadcasted_iota(jnp.int32, x.shape, 0)
         base = c * frames
-        cols[m, base : base + frames, 0:chan] = jnp.where(row == 0, 0.0, pltpu.roll(x, 1, 0)).astype(BF16)
-        cols[m, base : base + frames, chan : 2 * chan] = feats[m, c]
-        cols[m, base : base + frames, 2 * chan : 3 * chan] = jnp.where(
+        cols[base : base + frames, 0:chan] = jnp.where(row == 0, 0.0, pltpu.roll(x, 1, 0)).astype(BF16)
+        cols[base : base + frames, chan : 2 * chan] = feats[m, c]
+        cols[base : base + frames, 2 * chan : 3 * chan] = jnp.where(
             row == frames - 1, 0.0, pltpu.roll(x, frames - 1, 0)
         ).astype(BF16)
-
     for copy in copies[1]:
         copy.wait()
 
     def step(i, _):
         rows = pl.ds(pl.multiple_of(i * block, block), block)
-        pre = dot(cols[m, rows, :], w_conv[...], NN)
+        pre = dot(cols[rows, :], w_conv[...], NN)
         sigma = 0.5 * jnp.tanh(0.5 * pre) + 0.5
         hidden = (pre * sigma).astype(BF16)
-        hid[m, rows, :] = hidden
-        slope[m, rows, :] = sigma * (1.0 + pre * (1.0 - sigma))
+        hid[rows, :] = hidden
+        slope[rows, :] = sigma * (1.0 + pre * (1.0 - sigma))
         emb = dot(hidden, w_proj[...], NN).astype(BF16)
         values = emb.astype(F32)
         inv = lax.rsqrt(jnp.sum(values * values, axis=1, keepdims=True) + epsilon)
@@ -83,51 +83,37 @@
     lax.fori_loop(0, clips * frames // block, step, 0, unroll=True)
 
 
-def backward(m, w_proj, cols, slope, hid, gemb, gpre, total, block, rows_total):
+def backward(w_proj, cols, slope, hid, gemb, gpre, keep, send, block):
     def step(i, _):
         rows = pl.ds(pl.multiple_of(i * block, block), block)
-        grad = dot(gemb[m, rows, :], w_proj[...], NT) * slope[m, rows, :]
-        gpre[m, rows, :] = grad.astype(BF16)
+        gpre[rows, :] = (dot(gemb[rows, :], w_proj[...], NT) * slope[rows, :]).astype(BF16)
         return 0
 
-    lax.fori_loop(0, rows_total // block, step, 0, unroll=True)
-    conv_rows = cols.shape[-1]
-
-    def conv_step(i, _):
-        at = pl.multiple_of(i * 256, 256)
-        total[pl.ds(at, 256), :] = dot(cols[m, :, pl.ds(at, 256)], gpre[m], TN)
-        return 0
-
-    lax.fori_loop(0, conv_rows // 256, conv_step, 0)
-
-    def proj_step(i, _):
-        at = pl.multiple_of(i * 256, 256)
-        total[pl.ds(conv_rows + at, 256), :] = dot(hid[m, :, pl.ds(at, 256)], gemb[m], TN)
-        return 0
-
-    lax.fori_loop(0, hid.shape[-1] // 256, proj_step, 0)
-
-
-def hand_over(total, keep, send, m, half):
-    width = total.shape[1] // 2
-    for j in range(width // LANES):
-        mine = pl.ds(pl.multiple_of(half * width + j * LANES, LANES), LANES)
-        other = pl.ds(pl.multiple_of((1 - half) * width + j * LANES, LANES), LANES)
-        at = (m * (width // LANES) + j) * total.shape[0]
-        keep[at : at + total.shape[0], :] = total[:, mine]
-        send[at : at + total.shape[0], :] = total[:, other].astype(BF16)
+    lax.fori_loop(0, hid.shape[0] // block, step, 0, unroll=True)
+    even = lax.rem(lax.axis_index("tm"), 2) == 0
+    height = cols.shape[1] + hid.shape[1]
+    start = 0
+    for left, right in ((cols, gpre), (hid, gemb)):
+        grad = dot(left[...], right[...], TN)
+        rows, width = grad.shape[0], grad.shape[1] // 2
+        mine = jnp.where(even, grad[:, :width], grad[:, width:])
+        other = jnp.where(even, grad[:, width:], grad[:, :width])
+        for j in range(width // LANES):
+            at = j * height + start
+            keep[at : at + rows, :] = mine[:, j * LANES : (j + 1) * LANES]
+            send[at : at + rows, :] = other[:, j * LANES : (j + 1) * LANES].astype(BF16)
+        start += rows
 
 
 def kernel(
-    frames, clips, halo, lengths, labels, own_a, own_v, got, wac_in, wap_in, wvc_in, wvp_in, keep, send,
-    cols, slope, hid, gemb, gpre, total, emb_a, emb_v, inv_a, inv_v, gacc, giacc, feats, wac, wap, wvc, wvp, sems,
+    frames, clips, halo, lengths, labels, own_a, own_v, got, wac_in, wap_in, wvc_in, wvp_in,
+    keep, send, cols_a, slope_a, hid_a, gemb_a, cols_v, slope_v, hid_v, gemb_v, gpre, emb_a, emb_v, inv_a, inv_v, gacc, giacc, feats, wac, wap, wvc, wvp, sems,
 ):
     me = lax.axis_index("tm")
-    half = lax.rem(me, 2)
     rows_total = clips * frames
     start = me * (frames - 2 * halo) - halo if halo else 0
     first_clip = 0 if halo else me * clips
-    block = 256 if frames % 256 == 0 else TILE
+    block = block_of(frames)
     per_clip = frames // block
 
     copies = []
@@ -173,8 +159,8 @@
         emb_v[pl.ds(at, block), :] = emb
         inv_v[pl.ds(at, block), :] = inv
 
-    forward(feats, 1, (feats_v, weights_v), wvc, wvp, cols, slope, hid, clips, frames, block, put_v)
-    forward(feats, 0, (feats_a, weights_a), wac, wap, cols, slope, hid, clips, frames, block, put_a)
+    forward(feats, 1, (feats_v, weights_v), wvc, wvp, cols_v, slope_v, hid_v, clips, frames, block, put_v)
+    forward(feats, 0, (feats_a, weights_a), wac, wap, cols_a, slope_a, hid_a, clips, frames, block, put_a)
 
     tiles = frames // TILE
     row = lax.broadcasted_iota(jnp.int32, (TILE, WIN), 0)
@@ -215,7 +201,7 @@
         giv = jnp.sum(by_dots * ia, axis=1, keepdims=True)
         gia = jnp.sum((by_dots * iv).T, axis=1, keepdims=True)
         glip = dot(gd, wa, NN) - (iv * iv * iv * giv) * ev.astype(F32)
-        gemb[1, here, :] = jnp.where(own, glip, 0.0).astype(BF16)
+        gemb_v[here, :] = jnp.where(own, glip, 0.0).astype(BF16)
         gacc[c, window, :] += dot(gd, ev, TN)
         giacc[c, window, :] += jnp.broadcast_to(gia, (WIN, LANES))
         return loss
@@ -230,7 +216,7 @@
         if halo:
             at_row = lax.rem(i, per_clip) * block + lax.broadcasted_iota(jnp.int32, (block, 1), 0)
             grad = jnp.where((at_row >= halo) & (at_row < frames - halo), grad, 0.0)
-        gemb[0, pl.ds(pl.multiple_of(i * block, block), block), :] = grad.astype(BF16)
+        gemb_a[pl.ds(pl.multiple_of(i * block, block), block), :] = grad.astype(BF16)
         return 0
 
     lax.fori_loop(0, rows_total // block, audio_step, 0)
@@ -240,16 +226,23 @@
         count = count + (lengths[first_clip + c] - jnp.abs(labels[first_clip + c])).astype(F32)
     if halo:
         count = jnp.where(me == 0, count, 0.0)
-    send_rows = send.shape[0] - 2 * PAD
+    send_rows = send.shape[0] - TILES
     for at, value in ((send_rows, loss), (send_rows + PAD, count)):
         digits = jnp.broadcast_to(digits_of(value), (PAD, LANES))
         keep[at : at + PAD, :] = digits
         send[at : at + PAD, :] = digits.astype(BF16)
 
-    backward(1, wvp, cols, slope, hid, gemb, gpre, total, block, rows_total)
-    hand_over(total, keep, send, 1, half)
-    backward(0, wap, cols, slope, hid, gemb, gpre, total, block, rows_total)
-    hand_over(total, keep, send, 0, half)
+    backward(wvp, cols_v, slope_v, hid_v, gemb_v, gpre, keep, send, block)
+
+
+def block_of(frames):
+    return next(n for n in (512, 256, TILE) if frames % n == 0)
+
+
+def audio_kernel(block, w_proj, cols, slope, hid, gemb, keep, send, gpre):
+    backward(w_proj, cols, slope, hid, gemb, gpre, keep, send, block)
+    for ref in (keep, send):
+        ref[ref.shape[0] - TILES :, :] = jnp.zeros((TILES, LANES), ref.dtype)
 
 
 def local_grads(halo, lengths, labels, own_a, own_v, got, wac, wap, wvc, wvp):
@@ -265,21 +258,22 @@
     blocks = width // 2 // LANES
     smem = pl.BlockSpec(memory_space=pltpu.SMEM)
     vmem = pl.BlockSpec(memory_space=pltpu.VMEM)
-    return pl.pallas_call(
+    hbm = pl.BlockSpec(memory_space=pl.ANY)
+    sums = [pltpu.VMEM((blocks * grad_rows + TILES, LANES), dtype) for dtype in (F32, BF16)]
+    saved = [
+        pltpu.VMEM((rows, taps * chan), BF16),
+        pltpu.VMEM((rows, width), F32),
+        pltpu.VMEM((rows, width), BF16),
+        pltpu.VMEM((rows, width), BF16),
+    ]
+    keep_v, send_v, *audio = pl.pallas_call(
         functools.partial(kernel, frames, clips, halo),
-        out_shape=(
-            pltpu.VMEM((2 * blocks * grad_rows + 2 * PAD, LANES), F32),
-            pltpu.VMEM((2 * blocks * grad_rows + 2 * PAD, LANES), BF16),
-        ),
-        in_specs=[smem, smem] + [pl.BlockSpec(memory_space=pl.ANY)] * 7,
-        out_specs=(vmem, vmem),
-        scratch_shapes=[
-            pltpu.VMEM((2, rows, taps * chan), BF16),
-            pltpu.VMEM((2, rows, width), F32),
-            pltpu.VMEM((2, rows, width), BF16),
-            pltpu.VMEM((2, rows, width), BF16),
-            pltpu.VMEM((2, rows, width), BF16),
-            pltpu.VMEM((grad_rows, width), F32),
+        out_shape=sums + saved,
+        in_specs=[smem, smem, hbm, hbm, vmem] + [hbm] * 4,
+        out_specs=[vmem] * 6,
+        scratch_shapes=saved
+        + [
+            pltpu.VMEM((rows, width), BF16),
             pltpu.VMEM((clips, frames + 2 * PAD, width), BF16),
             pltpu.VMEM((rows, width), BF16),
             pltpu.VMEM((clips, frames + 2 * PAD, LANES), F32),
@@ -293,8 +287,18 @@
             pltpu.VMEM((width, width), BF16),
             pltpu.SemaphoreType.DMA((4 * clips + 4,)),
         ],
-        compiler_params=pltpu.CompilerParams(vmem_limit_bytes=56 * 1024 * 1024),
+        compiler_params=pltpu.CompilerParams(vmem_limit_bytes=48 * 1024 * 1024),
     )(lengths, labels, own_a, own_v, got, wac, wap, wvc, wvp)
+    keep_a, send_a = pl.pallas_call(
+        functools.partial(audio_kernel, block_of(frames)),
+        out_shape=sums,
+        in_specs=[vmem] * 5,
+        out_specs=[vmem] * 2,
+        scratch_shapes=[pltpu.VMEM((rows, width), BF16)],
+        compiler_params=pltpu.CompilerParams(vmem_limit_bytes=32 * 1024 * 1024),
+        cost_estimate=pl.CostEstimate(flops=2 * rows * width * (grad_rows + width), bytes_accessed=12 * rows * width, transcendentals=0),
+    )(wap, *audio)
+    return (keep_v, keep_a), (send_v, send_a)
 
 
 def swap(value, axis, bit):
@@ -346,9 +350,12 @@
     return mine, whole.astype(BF16)
 
 
-def quadruple(value, bits):
+def spread(value, bits):
+    return [value] + [swap_by_core(value, (k * bits[0], k * bits[1])) for k in (1, 2, 3)]
+
+
+def in_order(got, bits):
     me = place_of(bits)
-    got = [value] + [swap_by_core(value, (k * bits[0], k * bits[1])) for k in (1, 2, 3)]
     out = []
     for j in range(4):
         k = me ^ j
@@ -370,124 +377,170 @@
     return jnp.where(odd == 0, lax.rem(clip // bits[0], 4), lax.rem(clip // bits[1], 4))
 
 
-def sum_kernel(bits, count, base, *refs):
-    got, mine, outs = refs[:count], refs[count], refs[count + 1 :]
+def place_kernel(bits, *refs):
     me = place_in_kernel(bits)
-    part = mine.shape[0] - 2 * PAD
-
-    def total(rows):
-        value = base[rows, :]
-        for ref in got:
+    out = refs[-1]
+    part = out.shape[0] // 4
+    for k in range(4):
+        out[pl.ds(pl.multiple_of((me ^ k) * part, PAD), part), :] = refs[k][...]
+
+
+def place(got, bits):
+    vmem = pl.BlockSpec(memory_space=pltpu.VMEM)
+    return pl.pallas_call(
+        functools.partial(place_kernel, bits),
+        out_shape=pltpu.VMEM((4 * got[0].shape[0], LANES), got[0].dtype),
+        in_specs=[vmem] * 4,
+        out_specs=vmem,
+        compiler_params=pltpu.CompilerParams(vmem_limit_bytes=16 * 1024 * 1024),
+    )(*got)
+
+
+def sum_kernel(bits, counts, last, *refs):
+    groups, at = [], 0
+    for count in counts:
+        groups.append(refs[at : at + 1 + count])
+        at += 1 + count
+    mine, *outs = refs[at:]
+
+    def total(group, rows):
+        value = group[0][rows, :]
+        for ref in group[1:]:
             value = value + ref[rows, :].astype(F32)
         return value
 
-    tile = total(pl.ds(4 * part, 2 * PAD))
-    mine[part:, :] = tile
-    for k, out in enumerate(outs):
-        out[0:part, :] = total(pl.ds(pl.multiple_of((me ^ (k + 1)) * part, PAD), part)).astype(BF16)
-        out[part:, :] = tile.astype(BF16)
-    mine[0:part, :] = total(pl.ds(pl.multiple_of(me * part, PAD), part))
-
-
-def sum_and_deal(base, got, bits):
-    part = (base.shape[0] - 2 * PAD) // 4 + 2 * PAD
+    heights = [group[0].shape[0] - TILES for group in groups]
+    tile = total(groups[0], pl.ds(heights[0], TILES))
+    if last:
+        mine[...] = total(groups[0], pl.ds(0, heights[0])).astype(BF16)
+        outs[0][...] = tile.astype(BF16)
+        return
+    me = place_in_kernel(bits)
+    for k, out in enumerate([mine] + outs):
+        start = 0
+        for group, height in zip(groups, heights):
+            part = height // 4
+            rows = pl.ds(pl.multiple_of((me ^ k) * part, PAD), part)
+            out[start : start + part, :] = total(group, rows).astype(out.dtype)
+            start += part
+        out[start:, :] = tile.astype(out.dtype)
+
+
+def sum_and_deal(groups, bits, last=False):
+    heights = [group[0].shape[0] - TILES for group in groups]
+    if last:
+        shapes = [pltpu.VMEM((heights[0], LANES), BF16), pltpu.VMEM((TILES, LANES), BF16)]
+    else:
+        shapes = [pltpu.VMEM((sum(heights) // 4 + TILES, LANES), dtype) for dtype in (F32, BF16, BF16, BF16)]
+    refs = [ref for group in groups for ref in group]
     vmem = pl.BlockSpec(memory_space=pltpu.VMEM)
     return pl.pallas_call(
-        functools.partial(sum_kernel, bits, len(got)),
-        out_shape=[pltpu.VMEM((part, LANES), F32)] + [pltpu.VMEM((part, LANES), BF16)] * 3,
-        in_specs=[vmem] * (1 + len(got)),
-        out_specs=[vmem] * 4,
+        functools.partial(sum_kernel, bits, [len(group) - 1 for group in groups], last),
+        out_shape=shapes,
+        in_specs=[vmem] * len(refs),
+        out_specs=[vmem] * len(shapes),
         compiler_params=pltpu.CompilerParams(vmem_limit_bytes=16 * 1024 * 1024),
-    )(base, *got)
+    )(*refs)
 
 
 def reduce_all(keep, send):
-    got = swap(send, "tm", 1)
+    gots = [swap(value, "tm", 1) for value in send]
     rest = [("tm", bit) for bit in bits_of("tm")[1:]] + [("clip", bit) for bit in bits_of("clip")[4:]]
     rounds = ((1, 4), (4, 1))
     if rest:
-        total = keep + got.astype(F32)
-        total, tile = total[: -2 * PAD], total[-2 * PAD :].astype(BF16)
-        for axis, bit in rest:
-            total, tile = halve(total, axis, bit, tile)
-        for bits in rounds:
-            total, tile = quarter(total.reshape(4, -1, LANES), bits, tile)
+        mine, tiles = [], []
+        for base, got in zip(keep, gots):
+            total = base + got.astype(F32)
+            total, tile = total[:-TILES], total[-TILES:].astype(BF16)
+            for axis, bit in rest:
+                total, tile = halve(total, axis, bit, tile)
+            for bits in rounds:
+                total, tile = quarter(total.reshape(4, -1, LANES), bits, tile)
+            total = total.astype(BF16)
+            for bits in rounds[::-1]:
+                total = in_order(spread(total, bits), bits)
+            for axis, bit in rest[::-1]:
+                total = double(total, axis, bit)
+            mine.append(total)
+            tiles.append(tile)
+        return mine, tiles[0]
+    groups = []
+    for base, got in zip(keep, gots):
+        base, *outs = sum_and_deal([[base, got]], rounds[0])
+        groups.append([base] + exchange(outs, rounds[0]))
+    base, *outs = sum_and_deal(groups, rounds[1])
+    mine, tile = sum_and_deal([[base] + exchange(outs, rounds[1])], None, last=True)
+    mine = place(spread(mine, rounds[1]), rounds[1]).reshape(4, 2, -1, LANES)
+    gots = [spread(mine[:, m].reshape(-1, LANES), rounds[0]) for m in (0, 1)]
+
+    return [place(got, rounds[0]) for got in gots], tile
+
+
+def exchange(outs, bits):
+    return [swap_by_core(out, ((k + 1) * bits[0], (k + 1) * bits[1])) for k, out in enumerate(outs)]
+
+
+def finish_kernel(own, rows, *refs):
+    staged, sems = refs[-2:]
+    if own:
+        *halves, tile, loss = refs[:4]
     else:
-        total, got = keep, [got]
-        for bits in rounds:
-            total, *outs = sum_and_deal(total, got, bits)
-            got = [swap_by_core(out, ((k + 1) * bits[0], (k + 1) * bits[1])) for k, out in enumerate(outs)]
-        for value in got:
-            total = total + value.astype(F32)
-        total, tile = total[: -2 * PAD], total[-2 * PAD :].astype(BF16)
-    mine = total.astype(BF16)
-    for bits in rounds[::-1]:
-        mine = quadruple(mine, bits)
-    for axis, bit in rest[::-1]:
-        mine = double(mine, axis, bit)
-    return mine, tile
-
-
-def finish_kernel(own, *refs):
+        *halves, tile = refs[:3]
+    outs = refs[-6:-2]
+    digits = tile[...].astype(F32)
+    count = value_of(digits[PAD : PAD + 1])
+    scale = 1.0 / count
     if own:
-        mine, tile, loss, scale_out, *outs = refs[:8]
-        digits = tile[...].astype(F32)
-        count = value_of(digits[PAD : PAD + 1])
-        scale = 1.0 / count
         loss[0, 0] = value_of(digits[0:1]) / count
-        scale_out[0, 0] = scale
-    else:
-        mine, scale_in, *outs = refs[:2] + refs[6:10]
-        scale = scale_in[0, 0]
-    staged, sems = refs[-2:]
-    blocks, width = mine.shape[1], mine.shape[1] * LANES
+    blocks = halves[0].shape[0] // rows
     half = lax.rem(lax.axis_index("tm"), 2)
     half = half if own else 1 - half
-    columns = pl.ds(pl.multiple_of(half * width, width), width)
     copies = []
-    at = 0
-    for n, out in enumerate(outs):
-        m, rows = n // 2, out.shape[0]
-        at = at if n % 2 else 0
+    for m, mine in enumerate(halves):
         for j in range(blocks):
-            staged[m, at : at + rows, j * LANES : (j + 1) * LANES] = mine[m, j, at : at + rows, :].astype(F32) * scale
-        copy = pltpu.make_async_copy(staged.at[m, at : at + rows, :], out.at[:, columns], sems.at[n])
-        copy.start()
-        copies.append(copy)
-        at += rows
+            at = j * rows
+            column = pl.multiple_of((half * blocks + j) * LANES, LANES)
+            for out in outs[2 * m : 2 * m + 2]:
+                size = out.shape[0]
+                staged[m, at : at + size, :] = mine[at : at + size, :].astype(F32) * scale
+                copy = pltpu.make_async_copy(
+                    staged.at[m, at : at + size, :], out.at[:, pl.ds(column, LANES)], sems.at[len(copies)]
+                )
+                copy.start()
+                copies.append(copy)
+                at += size
     for copy in copies:
         copy.wait()
 
 
-def finish(mine, tile, conv_rows, width):
-    rows = conv_rows + width
-    shape = (2, width // 2 // LANES, rows, LANES)
-    got = swap(mine, "tm", 1)
+def finish(halves, tile, conv_rows, width):
+    gots = [swap(half, "tm", 1) for half in halves]
     smem, vmem, hbm = (pl.BlockSpec(memory_space=space) for space in (pltpu.SMEM, pltpu.VMEM, pl.ANY))
     grads = [jax.ShapeDtypeStruct((n, width), F32) for n in (conv_rows, width) * 2]
-    one = jax.ShapeDtypeStruct((1, 1), F32)
-    scratch = [pltpu.VMEM((2, rows, width // 2), F32), pltpu.SemaphoreType.DMA((4,))]
+    rows = conv_rows + width
+    scratch = [pltpu.VMEM((2, *halves[0].shape), F32), pltpu.SemaphoreType.DMA((4 * (halves[0].shape[0] // rows),))]
     params = pltpu.CompilerParams(vmem_limit_bytes=16 * 1024 * 1024)
-    cost = pl.CostEstimate(flops=rows * width, bytes_accessed=rows * width * 6, transcendentals=0)
-    loss, scale, *outs = pl.pallas_call(
-        functools.partial(finish_kernel, True),
-        out_shape=[one, one] + grads,
-        in_specs=[vmem, vmem],
-        out_specs=[smem, smem] + [hbm] * 4,
+    size = 2 * halves[0].size
+    cost = pl.CostEstimate(flops=size, bytes_accessed=6 * size, transcendentals=0)
+    loss, *outs = pl.pallas_call(
+        functools.partial(finish_kernel, True, rows),
+        out_shape=[jax.ShapeDtypeStruct((1, 1), F32)] + grads,
+        in_specs=[vmem] * 3,
+        out_specs=[smem] + [hbm] * 4,
         scratch_shapes=scratch,
         compiler_params=params,
         cost_estimate=cost,
-    )(mine.reshape(shape), tile)
+    )(*halves, tile)
     outs = pl.pallas_call(
-        functools.partial(finish_kernel, False),
+        functools.partial(finish_kernel, False, rows),
         out_shape=grads,
-        in_specs=[vmem, smem] + [hbm] * 4,
+        in_specs=[vmem] * 3 + [hbm] * 4,
         out_specs=[hbm] * 4,
         scratch_shapes=scratch,
-        input_output_aliases={n + 2: n for n in range(4)},
+        input_output_aliases={n + 3: n for n in range(4)},
         compiler_params=params,
         cost_estimate=cost,
-    )(got.reshape(shape), scale, *outs)
+    )(*gots, tile, *outs)
     return loss, outs
 
 
@@ -518,9 +571,9 @@
     keep, send = local_grads(
         halo, lengths, labels, audio_feats, lip_feats, got, w_audio_conv, w_audio_proj, w_lip_conv, w_lip_proj
     )
-    mine, tile = reduce_all(keep, send)
+    halves, tile = reduce_all(keep, send)
     taps, chan, width = w_audio_conv.shape
-    loss, (ac, ap, vc, vp) = finish(mine, tile, taps * chan, width)
+    loss, (vc, vp, ac, ap) = finish(halves, tile, taps * chan, width)
     return (loss.reshape(()), ac.reshape(w_audio_conv.shape), ap, vc.reshape(w_lip_conv.shape), vp)
 
 

time: 82 us -> 77.6 us (0.946)
  waiting for transfers between devices: 31.7 us -> 18.5 us
  starting transfers between devices: 23.1 us -> 35.3 us
  Pallas kernels: 23.7 us -> 20.8 us
    ppermute x12 -> x18, waiting for transfers between devices: 27.1 us -> 16.9 us  [swap_by_core(): return lax.ppermute(value, ('clip', 'tm'), pairs)]
    ppermute x12 -> x18, starting transfers between devices: 16.9 us -> 24.4 us  [swap_by_core(): return lax.ppermute(value, ('clip', 'tm'), pairs)]
    pallas_call x1, Pallas kernels: 18.9 us -> 14 us  [local_grads(): pl.pallas_call(functools.partial(kernel, frames, clips, halo), out_shape=...]
    ppermute x3 -> x5, starting transfers between devices: 6.19 us -> 10.9 us  [swap(): lax.ppermute(value, axis, [(i, i ^ bit) for i in range(lax.axis_size(axis...]
    ppermute x3 -> x5, waiting for transfers between devices: 4.61 us -> 1.55 us  [swap(): lax.ppermute(value, axis, [(i, i ^ bit) for i in range(lax.axis_size(axis...]
    pallas_call x4 -> x10, Pallas kernels: 4.83 us -> 6.78 us  [the longest x1 2.25 us: finish(): pl.pallas_call(functools.partial(finish_kernel, True, rows), out_shape=[j...]
  transfers between devices with their start and end apart: 15 -> 23, of which waited for: 13 -> 13; matrix products, arithmetic and copies ran while one was open for 0% -> 0% of each run, Pallas kernels for 3% -> 6%
where the time goes in v5:
time: 77.6 us; the launch traced here: 77.4 us
  starting transfers between devices  35.3 us (45%)
  Pallas kernels  20.8 us (27%)
  waiting for transfers between devices  18.5 us (24%)
  local copies, waits for them, and re-layouts  1.89 us (2%)
  between operations  0.91 us (1%)
    ppermute x18, starting transfers between devices, swap_by_core(): return lax.ppermute(value, ('clip', 'tm'), pairs)  24.4 us
    ppermute x18, waiting for transfers between devices, swap_by_core(): return lax.ppermute(value, ('clip', 'tm'), pairs)  16.9 us
    pallas_call x1, Pallas kernels, local_grads(): pl.pallas_call(functools.partial(kernel, frames, clips, halo), out_shape=...  14 us
    ppermute x5, starting transfers between devices, swap(): lax.ppermute(value, axis, [(i, i ^ bit) for i in range(lax.axis_size(axis...  10.9 us
    pallas_call x1, Pallas kernels, finish(): pl.pallas_call(functools.partial(finish_kernel, True, rows), out_shape=[j...  2.25 us
    pallas_call x1, Pallas kernels, local_grads(): pl.pallas_call(functools.partial(audio_kernel, block_of(frames)), out_sha...  2.12 us
    pallas_call x1, Pallas kernels, finish(): pl.pallas_call(functools.partial(finish_kernel, False, rows), out_shape=g...  1.74 us
  transfers between devices with their start and end apart: 23, of which 13 were waited for; matrix products, arithmetic and copies ran while one was open for 0% of the time, Pallas kernels for 6%

profile of v5, /device:TPU:0, one launch (start us, length us, event | category | flops | bytes accessed | tf_op | source)
XLA Modules:
  0.0 77.4 jit_solution(13006103578037991839)
XLA Ops:
  2.3 1.5 %collective-permute-done.got = bf16[2,2,256,256]{3,2,1,0:T(8,128)(2,1)S(1)} collective-permute-done((bf16[2,2,256,256]{3,2,1,0:T(8,128)(2,1)S(1)}, bf16[2,2,256,256]{3,2,1,0:T(8,128)(2,1)S(1)}, u32[]{:S(2)}, u32[]{:S(2)}) %collective-permute-start) | collective-permute-done | bytes 524320 | tf_op jit(solution)/shard_map/ppermute | solution.py:305
  4.6 14.0 %shard_map.119 = (f32[2592,128]{1,0:T(8,128)S(1)}, bf16[2592,128]{1,0:T(8,128)(2,1)S(1)}, bf16[1024,768]{1,0:T(8,128)(2,1)S(1)}, f32[1024,512]{1,0:T(8,128)S(1)}...) custom-call(s32[4]{0:T(128)} %lengths.1, s32[4]{0:T(128)} %labels.1, bf16[4,256,256]{2,1,0:T(8,128)(2,1)} %own_a.1, ...), custom_call_target="tpu_custom_call" | custom-call | tf_op jit(solution)/shard_map/pallas_call | solution.py:269
  19.0 2.1 %shard_map.121 = (f32[2592,128]{1,0:T(8,128)S(1)}, bf16[2592,128]{1,0:T(8,128)(2,1)S(1)}) custom-call(bf16[512,512]{1,0:T(8,128)(2,1)S(1)} %copy-done, bf16[1024,768]{1,0:T(8,128)(2,1)S(1)} %get-tuple-element.42.cols, f32[1024,512]{1,0:T(8,128)S(1)} %get-tuple-element.43.slope, bf16[1024,512]{1,0:T(8,128)(2,1)S(1)} %get-tuple-element.44.hid, ...), custom_call_target="tpu_custom_call" | custom-call | flops 1879048192 | bytes 6291456 | tf_op jit(solution)/shard_map/pallas_call | solution.py:292
  21.5 2.9 %collective-permute-start.2 = (bf16[672,128]{1,0:T(8,128)(2,1)S(1)}, bf16[672,128]{1,0:T(8,128)(2,1)S(1)}, u32[]{:S(2)}, u32[]{:S(2)}) collective-permute-start(bf16[672,128]{1,0:T(8,128)(2,1)S(1)} %get-tuple-element.39), channel_id=1, source_target_pairs={{0,2},{1,9},{2,0},{3,11},{4,6},{5,13},{6,4},{7,15},{8,10},{9,1},{1... | collective-permute-start | bytes 516104 | tf_op jit(solution)/shard_map/ppermute | solution.py:314
  24.5 1.5 %collective-permute-start.3 = (bf16[672,128]{1,0:T(8,128)(2,1)S(1)}, bf16[672,128]{1,0:T(8,128)(2,1)S(1)}, u32[]{:S(2)}, u32[]{:S(2)}) collective-permute-start(bf16[672,128]{1,0:T(8,128)(2,1)S(1)} %get-tuple-element.40), channel_id=1, source_target_pairs={{0,4},{1,17},{2,6},{3,19},{4,0},{5,21},{6,2},{7,23},{8,12},{9,25},... | collective-permute-start | bytes 516104 | tf_op jit(solution)/shard_map/ppermute | solution.py:314
  26.1 2.0 %collective-permute-start.6 = (bf16[672,128]{1,0:T(8,128)(2,1)S(1)}, bf16[672,128]{1,0:T(8,128)(2,1)S(1)}, u32[]{:S(2)}, u32[]{:S(2)}) collective-permute-start(bf16[672,128]{1,0:T(8,128)(2,1)S(1)} %get-tuple-element.49), channel_id=1, source_target_pairs={{0,2},{1,9},{2,0},{3,11},{4,6},{5,13},{6,4},{7,15},{8,10},{9,1},{1... | collective-permute-start | bytes 516104 | tf_op jit(solution)/shard_map/ppermute | solution.py:314
  28.1 1.5 %collective-permute-start.7 = (bf16[672,128]{1,0:T(8,128)(2,1)S(1)}, bf16[672,128]{1,0:T(8,128)(2,1)S(1)}, u32[]{:S(2)}, u32[]{:S(2)}) collective-permute-start(bf16[672,128]{1,0:T(8,128)(2,1)S(1)} %get-tuple-element.50), channel_id=1, source_target_pairs={{0,4},{1,17},{2,6},{3,19},{4,0},{5,21},{6,2},{7,23},{8,12},{9,25},... | collective-permute-start | bytes 516104 | tf_op jit(solution)/shard_map/ppermute | solution.py:314
  30.8 1.5 %collective-permute-done.4.refs_3_ = bf16[672,128]{1,0:T(8,128)(2,1)S(1)} collective-permute-done((bf16[672,128]{1,0:T(8,128)(2,1)S(1)}, bf16[672,128]{1,0:T(8,128)(2,1)S(1)}, u32[]{:S(2)}, u32[]{:S(2)}) %collective-permute-start.4) | collective-permute-done | bytes 172064 | tf_op jit(solution)/shard_map/ppermute | solution.py:314
  34.5 1.5 %collective-permute-done.8.refs_7_ = bf16[672,128]{1,0:T(8,128)(2,1)S(1)} collective-permute-done((bf16[672,128]{1,0:T(8,128)(2,1)S(1)}, bf16[672,128]{1,0:T(8,128)(2,1)S(1)}, u32[]{:S(2)}, u32[]{:S(2)}) %collective-permute-start.8) | collective-permute-done | bytes 172064 | tf_op jit(solution)/shard_map/ppermute | solution.py:314
  36.1 1.6 %collective-permute-start.9 = (bf16[352,128]{1,0:T(8,128)(2,1)S(1)}, bf16[352,128]{1,0:T(8,128)(2,1)S(1)}, u32[]{:S(2)}, u32[]{:S(2)}) collective-permute-start(bf16[352,128]{1,0:T(8,128)(2,1)S(1)} %get-tuple-element.53), channel_id=1, source_target_pairs={{0,8},{1,3},{2,10},{3,1},{4,12},{5,7},{6,14},{7,5},{8,0},{9,11},{1... | collective-permute-start | bytes 270344 | tf_op jit(solution)/shard_map/ppermute | solution.py:314
  37.8 2.6 %collective-permute-start.10 = (bf16[352,128]{1,0:T(8,128)(2,1)S(1)}, bf16[352,128]{1,0:T(8,128)(2,1)S(1)}, u32[]{:S(2)}, u32[]{:S(2)}) collective-permute-start(bf16[352,128]{1,0:T(8,128)(2,1)S(1)} %get-tuple-element.54), channel_id=1, source_target_pairs={{0,16},{1,5},{2,18},{3,7},{4,20},{5,1},{6,22},{7,3},{8,24},{9,13},... | collective-permute-start | bytes 270344 | tf_op jit(solution)/shard_map/ppermute | solution.py:314
  41.8 2.8 %collective-permute-done.10.refs_2_ = bf16[352,128]{1,0:T(8,128)(2,1)S(1)} collective-permute-done((bf16[352,128]{1,0:T(8,128)(2,1)S(1)}, bf16[352,128]{1,0:T(8,128)(2,1)S(1)}, u32[]{:S(2)}, u32[]{:S(2)}) %collective-permute-start.10) | collective-permute-done | bytes 90144 | tf_op jit(solution)/shard_map/ppermute | solution.py:314
  44.6 2.2 %collective-permute-done.11.refs_3_ = bf16[352,128]{1,0:T(8,128)(2,1)S(1)} collective-permute-done((bf16[352,128]{1,0:T(8,128)(2,1)S(1)}, bf16[352,128]{1,0:T(8,128)(2,1)S(1)}, u32[]{:S(2)}, u32[]{:S(2)}) %collective-permute-start.11) | collective-permute-done | bytes 90144 | tf_op jit(solution)/shard_map/ppermute | solution.py:314
  46.8 1.4 %collective-permute-start.14 = (bf16[320,128]{1,0:T(8,128)(2,1)S(1)}, bf16[320,128]{1,0:T(8,128)(2,1)S(1)}, u32[]{:S(2)}, u32[]{:S(2)}) collective-permute-start(bf16[320,128]{1,0:T(8,128)(2,1)S(1)} %get-tuple-element.56.refs_0_), channel_id=1, source_target_pairs={{0,24},{1,7},{2,26},{3,5},{4,28},{5,3},{6,30},{7,1},{8,16},{9,15},... | collective-permute-start | bytes 245768 | tf_op jit(solution)/shard_map/ppermute | solution.py:314
  48.4 2.9 %collective-permute-start.12 = (bf16[320,128]{1,0:T(8,128)(2,1)S(1)}, bf16[320,128]{1,0:T(8,128)(2,1)S(1)}, u32[]{:S(2)}, u32[]{:S(2)}) collective-permute-start(bf16[320,128]{1,0:T(8,128)(2,1)S(1)} %get-tuple-element.56.refs_0_), channel_id=1, source_target_pairs={{0,8},{1,3},{2,10},{3,1},{4,12},{5,7},{6,14},{7,5},{8,0},{9,11},{1... | collective-permute-start | bytes 245768 | tf_op jit(solution)/shard_map/ppermute | solution.py:314
  51.2 1.9 %collective-permute-done.14.refs_3_ = bf16[320,128]{1,0:T(8,128)(2,1)S(1)} collective-permute-done((bf16[320,128]{1,0:T(8,128)(2,1)S(1)}, bf16[320,128]{1,0:T(8,128)(2,1)S(1)}, u32[]{:S(2)}, u32[]{:S(2)}) %collective-permute-start.14) | collective-permute-done | bytes 81952 | tf_op jit(solution)/shard_map/ppermute | solution.py:314
  53.1 1.7 %collective-permute-done.13.refs_2_ = bf16[320,128]{1,0:T(8,128)(2,1)S(1)} collective-permute-done((bf16[320,128]{1,0:T(8,128)(2,1)S(1)}, bf16[320,128]{1,0:T(8,128)(2,1)S(1)}, u32[]{:S(2)}, u32[]{:S(2)}) %collective-permute-start.13) | collective-permute-done | bytes 81952 | tf_op jit(solution)/shard_map/ppermute | solution.py:314
  54.9 1.4 %collective-permute-start.20 = (bf16[640,128]{1,0:T(8,128)(2,1)S(1)}, bf16[640,128]{1,0:T(8,128)(2,1)S(1)}, u32[]{:S(2)}, u32[]{:S(2)}) collective-permute-start(bf16[640,128]{1,0:T(8,128)(2,1)S(1)} %bitcast.21), channel_id=1, source_target_pairs={{0,6},{1,25},{2,4},{3,27},{4,2},{5,29},{6,0},{7,31},{8,14},{9,17},... | collective-permute-start | bytes 491528 | tf_op jit(solution)/shard_map/ppermute | solution.py:314
  57.1 1.4 %collective-permute-start.18 = (bf16[640,128]{1,0:T(8,128)(2,1)S(1)}, bf16[640,128]{1,0:T(8,128)(2,1)S(1)}, u32[]{:S(2)}, u32[]{:S(2)}) collective-permute-start(bf16[640,128]{1,0:T(8,128)(2,1)S(1)} %bitcast.23), channel_id=1, source_target_pairs={{0,2},{1,9},{2,0},{3,11},{4,6},{5,13},{6,4},{7,15},{8,10},{9,1},{1... | collective-permute-start | bytes 491528 | tf_op jit(solution)/shard_map/ppermute | solution.py:314
  58.5 1.3 %collective-permute-start.17 = (bf16[640,128]{1,0:T(8,128)(2,1)S(1)}, bf16[640,128]{1,0:T(8,128)(2,1)S(1)}, u32[]{:S(2)}, u32[]{:S(2)}) collective-permute-start(bf16[640,128]{1,0:T(8,128)(2,1)S(1)} %bitcast.17), channel_id=1, source_target_pairs={{0,6},{1,25},{2,4},{3,27},{4,2},{5,29},{6,0},{7,31},{8,14},{9,17},... | collective-permute-start | bytes 491528 | tf_op jit(solution)/shard_map/ppermute | solution.py:314
  63.0 3.3 %collective-permute-start.22 = (bf16[2560,128]{1,0:T(8,128)(2,1)S(1)}, bf16[2560,128]{1,0:T(8,128)(2,1)S(1)}, u32[]{:S(2)}, u32[]{:S(2)}) collective-permute-start(bf16[2560,128]{1,0:T(8,128)(2,1)S(1)} %shard_map.127.refs_1_), channel_id=1, source_target_pairs={{0,1},{1,0},{2,3},{3,2},{4,5},{5,4},{6,7},{7,6},{8,9},{9,8},{10,11... | collective-permute-start | bytes 1966088 | tf_op jit(solution)/shard_map/ppermute | solution.py:305
  66.7 6.5 %collective-permute-start.21 = (bf16[2560,128]{1,0:T(8,128)(2,1)S(1)}, bf16[2560,128]{1,0:T(8,128)(2,1)S(1)}, u32[]{:S(2)}, u32[]{:S(2)}) collective-permute-start(bf16[2560,128]{1,0:T(8,128)(2,1)S(1)} %shard_map.126.refs_0_), channel_id=1, source_target_pairs={{0,1},{1,0},{2,3},{3,2},{4,5},{5,4},{6,7},{7,6},{8,9},{9,8},{10,11... | collective-permute-start | bytes 1966088 | tf_op jit(solution)/shard_map/ppermute | solution.py:305
  73.2 2.3 %shard_map.128 = (f32[1,1]{1,0:T(1,128)}, f32[768,512]{1,0:T(8,128)}, f32[512,512]{1,0:T(8,128)}, f32[768,512]{1,0:T(8,128)}, f32[512,512]{1,0:T(8,128)}) custom-call(bf16[2560,128]{1,0:T(8,128)(2,1)S(1)} %shard_map.126.refs_0_, bf16[2560,128]{1,0:T(8,128)(2,1)S(1)} %shard_map.127.refs_1_, bf16[32,128]{1,0:T(8,128)(2,1)S(1)} %get-tuple-element.57.refs_2_), custom_call_target="tpu_custom_call" | custom-call | flops 655360 | bytes 3932160 | tf_op jit(solution)/shard_map/pallas_call | solution.py:525
  75.5 1.7 %shard_map.129 = (f32[768,512]{1,0:T(8,128)}, f32[512,512]{1,0:T(8,128)}, f32[768,512]{1,0:T(8,128)}, f32[512,512]{1,0:T(8,128)}) custom-call(bf16[2560,128]{1,0:T(8,128)(2,1)S(1)} %collective-permute-done.21.refs_0_, bf16[2560,128]{1,0:T(8,128)(2,1)S(1)} %collective-permute-done.22.refs_1_, ...), custom_call_target="tpu_custom_call", output_to_operand_aliasing={{0}: (3, {}), {1}: (4, {}), {2}: (5, {}), {3}: (6, {})} | custom-call | flops 655360 | bytes 3932160 | tf_op jit(solution)/shard_map/pallas_call | solution.py:534
  (40 shorter events, 12.9 us)
Async XLA Ops:
  1.8 2.1 %collective-permute-start = (bf16[2,2,256,256]{3,2,1,0:T(8,128)(2,1)S(1)}, bf16[2,2,256,256]{3,2,1,0:T(8,128)(2,1)S(1)}, u32[]{:S(2)}, u32[]{:S(2)}) collective-permute-start(bf16[2,2,256,256]{3,2,1,0:T(8,128)(2,1)S(1)} %pad_maximum_fusion), channel_id=1, source_target_pairs={{0,1},{1,0},{2,3},{3,2},{4,5},{5,4},{6,7},{7,6},{8,9},{9,8},{10,11... | collective-permute-start | bytes 1572872 | tf_op jit(solution)/shard_map/ppermute | solution.py:305
  4.6 14.4 %copy-start = (bf16[512,512]{1,0:T(8,128)(2,1)S(1)}, bf16[512,512]{1,0:T(8,128)(2,1)}, u32[]{:S(2)}) copy-start(bf16[512,512]{1,0:T(8,128)(2,1)} %w_proj.1) | copy-start | bytes 1572868
  18.6 2.8 %collective-permute-start.1 = (bf16[2592,128]{1,0:T(8,128)(2,1)S(1)}, bf16[2592,128]{1,0:T(8,128)(2,1)S(1)}, u32[]{:S(2)}, u32[]{:S(2)}) collective-permute-start(bf16[2592,128]{1,0:T(8,128)(2,1)S(1)} %get-tuple-element.37), channel_id=1, source_target_pairs={{0,1},{1,0},{2,3},{3,2},{4,5},{5,4},{6,7},{7,6},{8,9},{9,8},{10,11... | collective-permute-start | bytes 1990664 | tf_op jit(solution)/shard_map/ppermute | solution.py:305
  21.2 4.8 %collective-permute-start.5 = (bf16[2592,128]{1,0:T(8,128)(2,1)S(1)}, bf16[2592,128]{1,0:T(8,128)(2,1)S(1)}, u32[]{:S(2)}, u32[]{:S(2)}) collective-permute-start(bf16[2592,128]{1,0:T(8,128)(2,1)S(1)} %get-tuple-element.47), channel_id=1, source_target_pairs={{0,1},{1,0},{2,3},{3,2},{4,5},{5,4},{6,7},{7,6},{8,9},{9,8},{10,11... | collective-permute-start | bytes 1990664 | tf_op jit(solution)/shard_map/ppermute | solution.py:305
  21.5 8.1 %collective-permute-start.2 = (bf16[672,128]{1,0:T(8,128)(2,1)S(1)}, bf16[672,128]{1,0:T(8,128)(2,1)S(1)}, u32[]{:S(2)}, u32[]{:S(2)}) collective-permute-start(bf16[672,128]{1,0:T(8,128)(2,1)S(1)} %get-tuple-element.39), channel_id=1, source_target_pairs={{0,2},{1,9},{2,0},{3,11},{4,6},{5,13},{6,4},{7,15},{8,10},{9,1},{1... | collective-permute-start | bytes 516104 | tf_op jit(solution)/shard_map/ppermute | solution.py:314
  24.5 6.4 %collective-permute-start.3 = (bf16[672,128]{1,0:T(8,128)(2,1)S(1)}, bf16[672,128]{1,0:T(8,128)(2,1)S(1)}, u32[]{:S(2)}, u32[]{:S(2)}) collective-permute-start(bf16[672,128]{1,0:T(8,128)(2,1)S(1)} %get-tuple-element.40), channel_id=1, source_target_pairs={{0,4},{1,17},{2,6},{3,19},{4,0},{5,21},{6,2},{7,23},{8,12},{9,25},... | collective-permute-start | bytes 516104 | tf_op jit(solution)/shard_map/ppermute | solution.py:314
  26.0 6.4 %collective-permute-start.4 = (bf16[672,128]{1,0:T(8,128)(2,1)S(1)}, bf16[672,128]{1,0:T(8,128)(2,1)S(1)}, u32[]{:S(2)}, u32[]{:S(2)}) collective-permute-start(bf16[672,128]{1,0:T(8,128)(2,1)S(1)} %get-tuple-element.41), channel_id=1, source_target_pairs={{0,6},{1,25},{2,4},{3,27},{4,2},{5,29},{6,0},{7,31},{8,14},{9,17},... | collective-permute-start | bytes 516104 | tf_op jit(solution)/shard_map/ppermute | solution.py:314
  26.1 7.1 %collective-permute-start.6 = (bf16[672,128]{1,0:T(8,128)(2,1)S(1)}, bf16[672,128]{1,0:T(8,128)(2,1)S(1)}, u32[]{:S(2)}, u32[]{:S(2)}) collective-permute-start(bf16[672,128]{1,0:T(8,128)(2,1)S(1)} %get-tuple-element.49), channel_id=1, source_target_pairs={{0,2},{1,9},{2,0},{3,11},{4,6},{5,13},{6,4},{7,15},{8,10},{9,1},{1... | collective-permute-start | bytes 516104 | tf_op jit(solution)/shard_map/ppermute | solution.py:314
  28.1 6.3 %collective-permute-start.7 = (bf16[672,128]{1,0:T(8,128)(2,1)S(1)}, bf16[672,128]{1,0:T(8,128)(2,1)S(1)}, u32[]{:S(2)}, u32[]{:S(2)}) collective-permute-start(bf16[672,128]{1,0:T(8,128)(2,1)S(1)} %get-tuple-element.50), channel_id=1, source_target_pairs={{0,4},{1,17},{2,6},{3,19},{4,0},{5,21},{6,2},{7,23},{8,12},{9,25},... | collective-permute-start | bytes 516104 | tf_op jit(solution)/shard_map/ppermute | solution.py:314
  29.7 6.3 %collective-permute-start.8 = (bf16[672,128]{1,0:T(8,128)(2,1)S(1)}, bf16[672,128]{1,0:T(8,128)(2,1)S(1)}, u32[]{:S(2)}, u32[]{:S(2)}) collective-permute-start(bf16[672,128]{1,0:T(8,128)(2,1)S(1)} %get-tuple-element.51), channel_id=1, source_target_pairs={{0,6},{1,25},{2,4},{3,27},{4,2},{5,29},{6,0},{7,31},{8,14},{9,17},... | collective-permute-start | bytes 516104 | tf_op jit(solution)/shard_map/ppermute | solution.py:314
  36.1 5.6 %collective-permute-start.9 = (bf16[352,128]{1,0:T(8,128)(2,1)S(1)}, bf16[352,128]{1,0:T(8,128)(2,1)S(1)}, u32[]{:S(2)}, u32[]{:S(2)}) collective-permute-start(bf16[352,128]{1,0:T(8,128)(2,1)S(1)} %get-tuple-element.53), channel_id=1, source_target_pairs={{0,8},{1,3},{2,10},{3,1},{4,12},{5,7},{6,14},{7,5},{8,0},{9,11},{1... | collective-permute-start | bytes 270344 | tf_op jit(solution)/shard_map/ppermute | solution.py:314
  37.8 6.8 %collective-permute-start.10 = (bf16[352,128]{1,0:T(8,128)(2,1)S(1)}, bf16[352,128]{1,0:T(8,128)(2,1)S(1)}, u32[]{:S(2)}, u32[]{:S(2)}) collective-permute-start(bf16[352,128]{1,0:T(8,128)(2,1)S(1)} %get-tuple-element.54), channel_id=1, source_target_pairs={{0,16},{1,5},{2,18},{3,7},{4,20},{5,1},{6,22},{7,3},{8,24},{9,13},... | collective-permute-start | bytes 270344 | tf_op jit(solution)/shard_map/ppermute | solution.py:314
  40.4 6.3 %collective-permute-start.11 = (bf16[352,128]{1,0:T(8,128)(2,1)S(1)}, bf16[352,128]{1,0:T(8,128)(2,1)S(1)}, u32[]{:S(2)}, u32[]{:S(2)}) collective-permute-start(bf16[352,128]{1,0:T(8,128)(2,1)S(1)} %get-tuple-element.55), channel_id=1, source_target_pairs={{0,24},{1,7},{2,26},{3,5},{4,28},{5,3},{6,30},{7,1},{8,16},{9,15},... | collective-permute-start | bytes 270344 | tf_op jit(solution)/shard_map/ppermute | solution.py:314
  46.8 6.4 %collective-permute-start.14 = (bf16[320,128]{1,0:T(8,128)(2,1)S(1)}, bf16[320,128]{1,0:T(8,128)(2,1)S(1)}, u32[]{:S(2)}, u32[]{:S(2)}) collective-permute-start(bf16[320,128]{1,0:T(8,128)(2,1)S(1)} %get-tuple-element.56.refs_0_), channel_id=1, source_target_pairs={{0,24},{1,7},{2,26},{3,5},{4,28},{5,3},{6,30},{7,1},{8,16},{9,15},... | collective-permute-start | bytes 245768 | tf_op jit(solution)/shard_map/ppermute | solution.py:314
  48.2 6.6 %collective-permute-start.13 = (bf16[320,128]{1,0:T(8,128)(2,1)S(1)}, bf16[320,128]{1,0:T(8,128)(2,1)S(1)}, u32[]{:S(2)}, u32[]{:S(2)}) collective-permute-start(bf16[320,128]{1,0:T(8,128)(2,1)S(1)} %get-tuple-element.56.refs_0_), channel_id=1, source_target_pairs={{0,16},{1,5},{2,18},{3,7},{4,20},{5,1},{6,22},{7,3},{8,24},{9,13},... | collective-permute-start | bytes 245768 | tf_op jit(solution)/shard_map/ppermute | solution.py:314
  48.4 6.5 %collective-permute-start.12 = (bf16[320,128]{1,0:T(8,128)(2,1)S(1)}, bf16[320,128]{1,0:T(8,128)(2,1)S(1)}, u32[]{:S(2)}, u32[]{:S(2)}) collective-permute-start(bf16[320,128]{1,0:T(8,128)(2,1)S(1)} %get-tuple-element.56.refs_0_), channel_id=1, source_target_pairs={{0,8},{1,3},{2,10},{3,1},{4,12},{5,7},{6,14},{7,5},{8,0},{9,11},{1... | collective-permute-start | bytes 245768 | tf_op jit(solution)/shard_map/ppermute | solution.py:314
  54.9 6.4 %collective-permute-start.20 = (bf16[640,128]{1,0:T(8,128)(2,1)S(1)}, bf16[640,128]{1,0:T(8,128)(2,1)S(1)}, u32[]{:S(2)}, u32[]{:S(2)}) collective-permute-start(bf16[640,128]{1,0:T(8,128)(2,1)S(1)} %bitcast.21), channel_id=1, source_target_pairs={{0,6},{1,25},{2,4},{3,27},{4,2},{5,29},{6,0},{7,31},{8,14},{9,17},... | collective-permute-start | bytes 491528 | tf_op jit(solution)/shard_map/ppermute | solution.py:314
  56.3 6.7 %collective-permute-start.19 = (bf16[640,128]{1,0:T(8,128)(2,1)S(1)}, bf16[640,128]{1,0:T(8,128)(2,1)S(1)}, u32[]{:S(2)}, u32[]{:S(2)}) collective-permute-start(bf16[640,128]{1,0:T(8,128)(2,1)S(1)} %bitcast.22), channel_id=1, source_target_pairs={{0,4},{1,17},{2,6},{3,19},{4,0},{5,21},{6,2},{7,23},{8,12},{9,25},... | collective-permute-start | bytes 491528 | tf_op jit(solution)/shard_map/ppermute | solution.py:314
  57.1 5.9 %collective-permute-start.18 = (bf16[640,128]{1,0:T(8,128)(2,1)S(1)}, bf16[640,128]{1,0:T(8,128)(2,1)S(1)}, u32[]{:S(2)}, u32[]{:S(2)}) collective-permute-start(bf16[640,128]{1,0:T(8,128)(2,1)S(1)} %bitcast.23), channel_id=1, source_target_pairs={{0,2},{1,9},{2,0},{3,11},{4,6},{5,13},{6,4},{7,15},{8,10},{9,1},{1... | collective-permute-start | bytes 491528 | tf_op jit(solution)/shard_map/ppermute | solution.py:314
  58.5 7.8 %collective-permute-start.17 = (bf16[640,128]{1,0:T(8,128)(2,1)S(1)}, bf16[640,128]{1,0:T(8,128)(2,1)S(1)}, u32[]{:S(2)}, u32[]{:S(2)}) collective-permute-start(bf16[640,128]{1,0:T(8,128)(2,1)S(1)} %bitcast.17), channel_id=1, source_target_pairs={{0,6},{1,25},{2,4},{3,27},{4,2},{5,29},{6,0},{7,31},{8,14},{9,17},... | collective-permute-start | bytes 491528 | tf_op jit(solution)/shard_map/ppermute | solution.py:314
  59.8 6.8 %collective-permute-start.16 = (bf16[640,128]{1,0:T(8,128)(2,1)S(1)}, bf16[640,128]{1,0:T(8,128)(2,1)S(1)}, u32[]{:S(2)}, u32[]{:S(2)}) collective-permute-start(bf16[640,128]{1,0:T(8,128)(2,1)S(1)} %bitcast.18), channel_id=1, source_target_pairs={{0,4},{1,17},{2,6},{3,19},{4,0},{5,21},{6,2},{7,23},{8,12},{9,25},... | collective-permute-start | bytes 491528 | tf_op jit(solution)/shard_map/ppermute | solution.py:314
  61.3 5.3 %collective-permute-start.15 = (bf16[640,128]{1,0:T(8,128)(2,1)S(1)}, bf16[640,128]{1,0:T(8,128)(2,1)S(1)}, u32[]{:S(2)}, u32[]{:S(2)}) collective-permute-start(bf16[640,128]{1,0:T(8,128)(2,1)S(1)} %bitcast.19), channel_id=1, source_target_pairs={{0,2},{1,9},{2,0},{3,11},{4,6},{5,13},{6,4},{7,15},{8,10},{9,1},{1... | collective-permute-start | bytes 491528 | tf_op jit(solution)/shard_map/ppermute | solution.py:314
  63.0 12.4 %collective-permute-start.22 = (bf16[2560,128]{1,0:T(8,128)(2,1)S(1)}, bf16[2560,128]{1,0:T(8,128)(2,1)S(1)}, u32[]{:S(2)}, u32[]{:S(2)}) collective-permute-start(bf16[2560,128]{1,0:T(8,128)(2,1)S(1)} %shard_map.127.refs_1_), channel_id=1, source_target_pairs={{0,1},{1,0},{2,3},{3,2},{4,5},{5,4},{6,7},{7,6},{8,9},{9,8},{10,11... | collective-permute-start | bytes 1966088 | tf_op jit(solution)/shard_map/ppermute | solution.py:305
  66.7 8.8 %collective-permute-start.21 = (bf16[2560,128]{1,0:T(8,128)(2,1)S(1)}, bf16[2560,128]{1,0:T(8,128)(2,1)S(1)}, u32[]{:S(2)}, u32[]{:S(2)}) collective-permute-start(bf16[2560,128]{1,0:T(8,128)(2,1)S(1)} %shard_map.126.refs_0_), channel_id=1, source_target_pairs={{0,1},{1,0},{2,3},{3,2},{4,5},{5,4},{6,7},{7,6},{8,9},{9,8},{10,11... | collective-permute-start | bytes 1966088 | tf_op jit(solution)/shard_map/ppermute | solution.py:305
  (1 other events, 0.8 us)

commit v6 on v5

--- a/solution.py
+++ b/solution.py
@@ -13,6 +13,7 @@
 WIN = TILE + 2 * PAD
 HALO = 64
 TILES = 2 * PAD
+PLANS = (((1, 1), (4, 4)), ((1, 4), (4, 1)))
 LANES = 128
 DIGITS = 48
 FRACTION = 20
@@ -287,7 +288,7 @@
             pltpu.VMEM((width, width), BF16),
             pltpu.SemaphoreType.DMA((4 * clips + 4,)),
         ],
-        compiler_params=pltpu.CompilerParams(vmem_limit_bytes=48 * 1024 * 1024),
+        compiler_params=pltpu.CompilerParams(vmem_limit_bytes=44 * 1024 * 1024),
     )(lengths, labels, own_a, own_v, got, wac, wap, wvc, wvp)
     keep_a, send_a = pl.pallas_call(
         functools.partial(audio_kernel, block_of(frames)),
@@ -396,51 +397,44 @@
     )(*got)
 
 
-def sum_kernel(bits, counts, last, *refs):
-    groups, at = [], 0
-    for count in counts:
-        groups.append(refs[at : at + 1 + count])
-        at += 1 + count
-    mine, *outs = refs[at:]
-
-    def total(group, rows):
-        value = group[0][rows, :]
-        for ref in group[1:]:
-            value = value + ref[rows, :].astype(F32)
-        return value
-
-    heights = [group[0].shape[0] - TILES for group in groups]
-    tile = total(groups[0], pl.ds(heights[0], TILES))
-    if last:
-        mine[...] = total(groups[0], pl.ds(0, heights[0])).astype(BF16)
-        outs[0][...] = tile.astype(BF16)
-        return
+def deal_kernel(bits, base, got, mine, *outs):
     me = place_in_kernel(bits)
-    for k, out in enumerate([mine] + outs):
-        start = 0
-        for group, height in zip(groups, heights):
-            part = height // 4
-            rows = pl.ds(pl.multiple_of((me ^ k) * part, PAD), part)
-            out[start : start + part, :] = total(group, rows).astype(out.dtype)
-            start += part
-        out[start:, :] = tile.astype(out.dtype)
-
-
-def sum_and_deal(groups, bits, last=False):
-    heights = [group[0].shape[0] - TILES for group in groups]
-    if last:
-        shapes = [pltpu.VMEM((heights[0], LANES), BF16), pltpu.VMEM((TILES, LANES), BF16)]
-    else:
-        shapes = [pltpu.VMEM((sum(heights) // 4 + TILES, LANES), dtype) for dtype in (F32, BF16, BF16, BF16)]
-    refs = [ref for group in groups for ref in group]
+    part = mine.shape[0] - TILES
+
+    def total(rows):
+        return base[rows, :] + got[rows, :].astype(F32)
+
+    tile = total(pl.ds(4 * part, TILES))
+    for k, out in enumerate((mine, *outs)):
+        rows = pl.ds(pl.multiple_of((me ^ k) * part, PAD), part)
+        out[0:part, :] = total(rows).astype(out.dtype)
+        out[part:, :] = tile.astype(out.dtype)
+
+
+def join_kernel(base, *refs):
+    value = base[...]
+    for ref in refs[:-1]:
+        value = value + ref[...].astype(F32)
+    refs[-1][...] = value.astype(BF16)
+
+
+def split_kernel(one, other, *outs):
+    start = 0
+    for out in outs:
+        rows = pl.ds(start, out.shape[0])
+        out[...] = (one[rows, :].astype(F32) + other[rows, :].astype(F32)).astype(BF16)
+        start += out.shape[0]
+
+
+def on_chip(body, shapes, *args):
     vmem = pl.BlockSpec(memory_space=pltpu.VMEM)
     return pl.pallas_call(
-        functools.partial(sum_kernel, bits, [len(group) - 1 for group in groups], last),
-        out_shape=shapes,
-        in_specs=[vmem] * len(refs),
+        body,
+        out_shape=[pltpu.VMEM((rows, LANES), dtype) for rows, dtype in shapes],
+        in_specs=[vmem] * len(args),
         out_specs=[vmem] * len(shapes),
         compiler_params=pltpu.CompilerParams(vmem_limit_bytes=16 * 1024 * 1024),
-    )(*refs)
+    )(*args)
 
 
 def reduce_all(keep, send):
@@ -464,16 +458,18 @@
             mine.append(total)
             tiles.append(tile)
         return mine, tiles[0]
-    groups = []
-    for base, got in zip(keep, gots):
-        base, *outs = sum_and_deal([[base, got]], rounds[0])
-        groups.append([base] + exchange(outs, rounds[0]))
-    base, *outs = sum_and_deal(groups, rounds[1])
-    mine, tile = sum_and_deal([[base] + exchange(outs, rounds[1])], None, last=True)
-    mine = place(spread(mine, rounds[1]), rounds[1]).reshape(4, 2, -1, LANES)
-    gots = [spread(mine[:, m].reshape(-1, LANES), rounds[0]) for m in (0, 1)]
-
-    return [place(got, rounds[0]) for got in gots], tile
+    mine, tiles = [], []
+    for base, got, (groups, pairs) in zip(keep, gots, PLANS):
+        part = (base.shape[0] - TILES) // 4 + TILES
+        shapes = [(part, F32)] + [(part, BF16)] * 3
+        base, *outs = on_chip(functools.partial(deal_kernel, groups), shapes, base, got)
+        (value,) = on_chip(join_kernel, [(part, BF16)], base, *exchange(outs, groups))
+        twice = tuple(2 * bit for bit in pairs)
+        (value,) = on_chip(split_kernel, [(part, BF16)], value, swap_by_core(value, pairs))
+        value, tile = on_chip(split_kernel, [(part - TILES, BF16), (TILES, BF16)], value, swap_by_core(value, twice))
+        mine.append(value)
+        tiles.append(tile)
+    return [place(spread(value, plan[0]), plan[0]) for value, plan in zip(mine, PLANS)], tiles[0]
 
 
 def exchange(outs, bits):

time: 77.6 us -> 67.9 us (0.88)
  starting transfers between devices: 35.3 us -> 28.5 us
  waiting for transfers between devices: 18.5 us -> 16 us
    ppermute x5, starting transfers between devices: 10.9 us -> 1.3 us  [swap(): lax.ppermute(value, axis, [(i, i ^ bit) for i in range(lax.axis_size(axis...]
    ppermute x18 -> x16, starting transfers between devices: 24.4 us -> 27.2 us  [swap_by_core(): return lax.ppermute(value, ('clip', 'tm'), pairs)]
    ppermute x18 -> x16, waiting for transfers between devices: 16.9 us -> 14.4 us  [swap_by_core(): return lax.ppermute(value, ('clip', 'tm'), pairs)]
  transfers between devices with their start and end apart: 23 -> 21, of which waited for: 13 -> 10; matrix products, arithmetic and copies ran while one was open for 0% -> 0% of each run, Pallas kernels for 6% -> 8%
where the time goes in v6:
time: 67.9 us; the launch traced here: 67.7 us
  starting transfers between devices  28.5 us (42%)
  Pallas kernels  21 us (31%)
  waiting for transfers between devices  16 us (24%)
  local copies, waits for them, and re-layouts  1.23 us (2%)
  between operations  1 us (1%)
    ppermute x16, starting transfers between devices, swap_by_core(): return lax.ppermute(value, ('clip', 'tm'), pairs)  27.2 us
    ppermute x16, waiting for transfers between devices, swap_by_core(): return lax.ppermute(value, ('clip', 'tm'), pairs)  14.4 us
    pallas_call x1, Pallas kernels, local_grads(): pl.pallas_call(functools.partial(kernel, frames, clips, halo), out_shape=...  13.6 us
    pallas_call x1, Pallas kernels, finish(): pl.pallas_call(functools.partial(finish_kernel, True, rows), out_shape=[j...  2.26 us
    pallas_call x1, Pallas kernels, local_grads(): pl.pallas_call(functools.partial(audio_kernel, block_of(frames)), out_sha...  2.11 us
    pallas_call x1, Pallas kernels, finish(): pl.pallas_call(functools.partial(finish_kernel, False, rows), out_shape=g...  1.74 us
    ppermute x5, waiting for transfers between devices, swap(): lax.ppermute(value, axis, [(i, i ^ bit) for i in range(lax.axis_size(axis...  1.55 us
  transfers between devices with their start and end apart: 21, of which 10 were waited for; matrix products, arithmetic and copies ran while one was open for 0% of the time, Pallas kernels for 8%

profile of v6, /device:TPU:0, one launch (start us, length us, event | category | flops | bytes accessed | tf_op | source)
XLA Modules:
  0.0 67.7 jit_solution(2539712826402869622)
XLA Ops:
  0.7 1.2 %dynamic-slice_bitcast_fusion = (bf16[1,2,256,256]{3,2,1,0:T(8,128)(2,1)S(1)}, bf16[1,2,256,256]{3,2,1,0:T(8,128)(2,1)S(1)}) fusion(bf16[4,256,256]{2,1,0:T(8,128)(2,1)} %own_v.1, s32[]{:T(128)S(6)} %select_n.4, bf16[4,256,256]{2,1,0:T(8,128)(2,1)} %own_a.1), kind=kLoop, calls=%fused_computation.1 | loop fusion | bytes 1048580 | tf_op jit(solution)/shard_map/stack | solution.py:551
  2.5 1.5 %collective-permute-done.got = bf16[2,2,256,256]{3,2,1,0:T(8,128)(2,1)S(1)} collective-permute-done((bf16[2,2,256,256]{3,2,1,0:T(8,128)(2,1)S(1)}, bf16[2,2,256,256]{3,2,1,0:T(8,128)(2,1)S(1)}, u32[]{:S(2)}, u32[]{:S(2)}) %collective-permute-start) | collective-permute-done | bytes 524320 | tf_op jit(solution)/shard_map/ppermute | solution.py:306
  4.1 13.6 %shard_map.119 = (f32[2592,128]{1,0:T(8,128)S(1)}, bf16[2592,128]{1,0:T(8,128)(2,1)S(1)}, bf16[1024,768]{1,0:T(8,128)(2,1)S(1)}, f32[1024,512]{1,0:T(8,128)S(1)}...) custom-call(s32[4]{0:T(128)S(1)} %copy-done.4, s32[4]{0:T(128)S(1)} %copy-done.5, ...), custom_call_target="tpu_custom_call" | custom-call | tf_op jit(solution)/shard_map/pallas_call | solution.py:270
  18.1 2.1 %shard_map.125 = (f32[2592,128]{1,0:T(8,128)S(1)}, bf16[2592,128]{1,0:T(8,128)(2,1)S(1)}) custom-call(bf16[512,512]{1,0:T(8,128)(2,1)S(1)} %copy-done.3, bf16[1024,768]{1,0:T(8,128)(2,1)S(1)} %get-tuple-element.40.cols, f32[1024,512]{1,0:T(8,128)S(1)} %get-tuple-element.41.slope, bf16[1024,512]{1,0:T(8,128)(2,1)S(1)} %get-tuple-element.42.hid, ...), custom_call_target="tpu_custom_call" | custom-call | flops 1879048192 | bytes 6291456 | tf_op jit(solution)/shard_map/pallas_call | solution.py:293
  20.5 2.9 %collective-permute-start.2 = (bf16[672,128]{1,0:T(8,128)(2,1)S(1)}, bf16[672,128]{1,0:T(8,128)(2,1)S(1)}, u32[]{:S(2)}, u32[]{:S(2)}) collective-permute-start(bf16[672,128]{1,0:T(8,128)(2,1)S(1)} %get-tuple-element.36), channel_id=1, source_target_pairs={{0,2},{1,3},{2,0},{3,1},{4,6},{5,7},{6,4},{7,5},{8,10},{9,11},{10,... | collective-permute-start | bytes 516104 | tf_op jit(solution)/shard_map/ppermute | solution.py:315
  23.5 1.5 %collective-permute-start.3 = (bf16[672,128]{1,0:T(8,128)(2,1)S(1)}, bf16[672,128]{1,0:T(8,128)(2,1)S(1)}, u32[]{:S(2)}, u32[]{:S(2)}) collective-permute-start(bf16[672,128]{1,0:T(8,128)(2,1)S(1)} %get-tuple-element.37), channel_id=1, source_target_pairs={{0,4},{1,5},{2,6},{3,7},{4,0},{5,1},{6,2},{7,3},{8,12},{9,13},{10,... | collective-permute-start | bytes 516104 | tf_op jit(solution)/shard_map/ppermute | solution.py:315
  25.1 2.0 %collective-permute-start.11 = (bf16[672,128]{1,0:T(8,128)(2,1)S(1)}, bf16[672,128]{1,0:T(8,128)(2,1)S(1)}, u32[]{:S(2)}, u32[]{:S(2)}) collective-permute-start(bf16[672,128]{1,0:T(8,128)(2,1)S(1)} %get-tuple-element.47), channel_id=1, source_target_pairs={{0,2},{1,9},{2,0},{3,11},{4,6},{5,13},{6,4},{7,15},{8,10},{9,1},{1... | collective-permute-start | bytes 516104 | tf_op jit(solution)/shard_map/ppermute | solution.py:315
  27.2 1.5 %collective-permute-start.12 = (bf16[672,128]{1,0:T(8,128)(2,1)S(1)}, bf16[672,128]{1,0:T(8,128)(2,1)S(1)}, u32[]{:S(2)}, u32[]{:S(2)}) collective-permute-start(bf16[672,128]{1,0:T(8,128)(2,1)S(1)} %get-tuple-element.48), channel_id=1, source_target_pairs={{0,4},{1,17},{2,6},{3,19},{4,0},{5,21},{6,2},{7,23},{8,12},{9,25},... | collective-permute-start | bytes 516104 | tf_op jit(solution)/shard_map/ppermute | solution.py:315
  28.7 3.0 %collective-permute-start.13 = (bf16[672,128]{1,0:T(8,128)(2,1)S(1)}, bf16[672,128]{1,0:T(8,128)(2,1)S(1)}, u32[]{:S(2)}, u32[]{:S(2)}) collective-permute-start(bf16[672,128]{1,0:T(8,128)(2,1)S(1)} %get-tuple-element.49), channel_id=1, source_target_pairs={{0,6},{1,25},{2,4},{3,27},{4,2},{5,29},{6,0},{7,31},{8,14},{9,17},... | collective-permute-start | bytes 516104 | tf_op jit(solution)/shard_map/ppermute | solution.py:315
  31.6 1.6 %collective-permute-done.3.refs_1_ = bf16[672,128]{1,0:T(8,128)(2,1)S(1)} collective-permute-done((bf16[672,128]{1,0:T(8,128)(2,1)S(1)}, bf16[672,128]{1,0:T(8,128)(2,1)S(1)}, u32[]{:S(2)}, u32[]{:S(2)}) %collective-permute-start.3) | collective-permute-done | bytes 172064 | tf_op jit(solution)/shard_map/ppermute | solution.py:315
  33.4 1.6 %collective-permute-start.5 = (bf16[672,128]{1,0:T(8,128)(2,1)S(1)}, bf16[672,128]{1,0:T(8,128)(2,1)S(1)}, u32[]{:S(2)}, u32[]{:S(2)}) collective-permute-start(bf16[672,128]{1,0:T(8,128)(2,1)S(1)} %shard_map.121.one), channel_id=1, source_target_pairs={{0,8},{1,9},{2,10},{3,11},{4,12},{5,13},{6,14},{7,15},{8,0},{9,1},... | collective-permute-start | bytes 516104 | tf_op jit(solution)/shard_map/ppermute | solution.py:315
  35.0 2.0 %collective-permute-done.12.refs_1_ = bf16[672,128]{1,0:T(8,128)(2,1)S(1)} collective-permute-done((bf16[672,128]{1,0:T(8,128)(2,1)S(1)}, bf16[672,128]{1,0:T(8,128)(2,1)S(1)}, u32[]{:S(2)}, u32[]{:S(2)}) %collective-permute-start.12) | collective-permute-done | bytes 172064 | tf_op jit(solution)/shard_map/ppermute | solution.py:315
  37.0 1.6 %collective-permute-start.14 = (bf16[672,128]{1,0:T(8,128)(2,1)S(1)}, bf16[672,128]{1,0:T(8,128)(2,1)S(1)}, u32[]{:S(2)}, u32[]{:S(2)}) collective-permute-start(bf16[672,128]{1,0:T(8,128)(2,1)S(1)} %shard_map.127.one), channel_id=1, source_target_pairs={{0,8},{1,3},{2,10},{3,1},{4,12},{5,7},{6,14},{7,5},{8,0},{9,11},{1... | collective-permute-start | bytes 516104 | tf_op jit(solution)/shard_map/ppermute | solution.py:315
  39.0 2.5 %collective-permute-start.6 = (bf16[672,128]{1,0:T(8,128)(2,1)S(1)}, bf16[672,128]{1,0:T(8,128)(2,1)S(1)}, u32[]{:S(2)}, u32[]{:S(2)}) collective-permute-start(bf16[672,128]{1,0:T(8,128)(2,1)S(1)} %shard_map.122.one), channel_id=1, source_target_pairs={{0,16},{1,17},{2,18},{3,19},{4,20},{5,21},{6,22},{7,23},{8,24},{9,... | collective-permute-start | bytes 516104 | tf_op jit(solution)/shard_map/ppermute | solution.py:315
  41.5 2.8 %collective-permute-done.14.other = bf16[672,128]{1,0:T(8,128)(2,1)S(1)} collective-permute-done((bf16[672,128]{1,0:T(8,128)(2,1)S(1)}, bf16[672,128]{1,0:T(8,128)(2,1)S(1)}, u32[]{:S(2)}, u32[]{:S(2)}) %collective-permute-start.14) | collective-permute-done | bytes 172064 | tf_op jit(solution)/shard_map/ppermute | solution.py:315
  44.4 2.1 %collective-permute-start.15 = (bf16[672,128]{1,0:T(8,128)(2,1)S(1)}, bf16[672,128]{1,0:T(8,128)(2,1)S(1)}, u32[]{:S(2)}, u32[]{:S(2)}) collective-permute-start(bf16[672,128]{1,0:T(8,128)(2,1)S(1)} %shard_map.128.one), channel_id=1, source_target_pairs={{0,16},{1,5},{2,18},{3,7},{4,20},{5,1},{6,22},{7,3},{8,24},{9,13},... | collective-permute-start | bytes 516104 | tf_op jit(solution)/shard_map/ppermute | solution.py:315
  46.5 2.0 %collective-permute-done.6.other = bf16[672,128]{1,0:T(8,128)(2,1)S(1)} collective-permute-done((bf16[672,128]{1,0:T(8,128)(2,1)S(1)}, bf16[672,128]{1,0:T(8,128)(2,1)S(1)}, u32[]{:S(2)}, u32[]{:S(2)}) %collective-permute-start.6) | collective-permute-done | bytes 172064 | tf_op jit(solution)/shard_map/ppermute | solution.py:315
  48.6 4.4 %collective-permute-start.9 = (bf16[640,128]{1,0:T(8,128)(2,1)S(1)}, bf16[640,128]{1,0:T(8,128)(2,1)S(1)}, u32[]{:S(2)}, u32[]{:S(2)}) collective-permute-start(bf16[640,128]{1,0:T(8,128)(2,1)S(1)} %get-tuple-element.39.refs_0_), channel_id=1, source_target_pairs={{0,6},{1,7},{2,4},{3,5},{4,2},{5,3},{6,0},{7,1},{8,14},{9,15},{10,... | collective-permute-start | bytes 491528 | tf_op jit(solution)/shard_map/ppermute | solution.py:315
  54.3 2.8 %collective-permute-start.18 = (bf16[640,128]{1,0:T(8,128)(2,1)S(1)}, bf16[640,128]{1,0:T(8,128)(2,1)S(1)}, u32[]{:S(2)}, u32[]{:S(2)}) collective-permute-start(bf16[640,128]{1,0:T(8,128)(2,1)S(1)} %get-tuple-element.50.refs_0_), channel_id=1, source_target_pairs={{0,6},{1,25},{2,4},{3,27},{4,2},{5,29},{6,0},{7,31},{8,14},{9,17},... | collective-permute-start | bytes 491528 | tf_op jit(solution)/shard_map/ppermute | solution.py:315
  57.8 1.3 %collective-permute-done.8.refs_2_ = bf16[640,128]{1,0:T(8,128)(2,1)S(1)} collective-permute-done((bf16[640,128]{1,0:T(8,128)(2,1)S(1)}, bf16[640,128]{1,0:T(8,128)(2,1)S(1)}, u32[]{:S(2)}, u32[]{:S(2)}) %collective-permute-start.8) | collective-permute-done | bytes 163872 | tf_op jit(solution)/shard_map/ppermute | solution.py:315
  59.2 2.4 %collective-permute-done.18.refs_3_ = bf16[640,128]{1,0:T(8,128)(2,1)S(1)} collective-permute-done((bf16[640,128]{1,0:T(8,128)(2,1)S(1)}, bf16[640,128]{1,0:T(8,128)(2,1)S(1)}, u32[]{:S(2)}, u32[]{:S(2)}) %collective-permute-start.18) | collective-permute-done | bytes 163872 | tf_op jit(solution)/shard_map/ppermute | solution.py:315
  61.7 1.7 %collective-permute-done.17.refs_2_ = bf16[640,128]{1,0:T(8,128)(2,1)S(1)} collective-permute-done((bf16[640,128]{1,0:T(8,128)(2,1)S(1)}, bf16[640,128]{1,0:T(8,128)(2,1)S(1)}, u32[]{:S(2)}, u32[]{:S(2)}) %collective-permute-start.17) | collective-permute-done | bytes 163872 | tf_op jit(solution)/shard_map/ppermute | solution.py:315
  63.5 2.3 %shard_map.131 = (f32[1,1]{1,0:T(1,128)}, f32[768,512]{1,0:T(8,128)}, f32[512,512]{1,0:T(8,128)}, f32[768,512]{1,0:T(8,128)}, f32[512,512]{1,0:T(8,128)}) custom-call(bf16[2560,128]{1,0:T(8,128)(2,1)S(1)} %shard_map.124.refs_0_, bf16[2560,128]{1,0:T(8,128)(2,1)S(1)} %shard_map.130.refs_1_, bf16[32,128]{1,0:T(8,128)(2,1)S(1)} %get-tuple-element.51.refs_2_), custom_call_target="tpu_custom_call" | custom-call | flops 655360 | bytes 3932160 | tf_op jit(solution)/shard_map/pallas_call | solution.py:521
  65.8 1.7 %shard_map.132 = (f32[768,512]{1,0:T(8,128)}, f32[512,512]{1,0:T(8,128)}, f32[768,512]{1,0:T(8,128)}, f32[512,512]{1,0:T(8,128)}) custom-call(bf16[2560,128]{1,0:T(8,128)(2,1)S(1)} %collective-permute-done.19.refs_0_, bf16[2560,128]{1,0:T(8,128)(2,1)S(1)} %collective-permute-done.20.refs_1_, ...), custom_call_target="tpu_custom_call", output_to_operand_aliasing={{0}: (3, {}), {1}: (4, {}), {2}: (5, {}), {3}: (6, {})} | custom-call | flops 655360 | bytes 3932160 | tf_op jit(solution)/shard_map/pallas_call | solution.py:530
  (46 shorter events, 4.3 us)
Async XLA Ops:
  0.6 3.4 %copy-start.1 = (bf16[4,256,256]{2,1,0:T(8,128)(2,1)S(1)}, bf16[4,256,256]{2,1,0:T(8,128)(2,1)}, u32[]{:S(2)}) copy-start(bf16[4,256,256]{2,1,0:T(8,128)(2,1)} %own_v.1) | copy-start | bytes 1572868
  0.6 3.4 %copy-start = (bf16[4,256,256]{2,1,0:T(8,128)(2,1)S(1)}, bf16[4,256,256]{2,1,0:T(8,128)(2,1)}, u32[]{:S(2)}) copy-start(bf16[4,256,256]{2,1,0:T(8,128)(2,1)} %own_a.1) | copy-start | bytes 1572868
  0.7 3.4 %copy-start.3 = (bf16[512,512]{1,0:T(8,128)(2,1)S(1)}, bf16[512,512]{1,0:T(8,128)(2,1)}, u32[]{:S(2)}) copy-start(bf16[512,512]{1,0:T(8,128)(2,1)} %w_proj.1) | copy-start | bytes 1572868
  2.0 2.1 %collective-permute-start = (bf16[2,2,256,256]{3,2,1,0:T(8,128)(2,1)S(1)}, bf16[2,2,256,256]{3,2,1,0:T(8,128)(2,1)S(1)}, u32[]{:S(2)}, u32[]{:S(2)}) collective-permute-start(bf16[2,2,256,256]{3,2,1,0:T(8,128)(2,1)S(1)} %pad_maximum_fusion), channel_id=1, source_target_pairs={{0,1},{1,0},{2,3},{3,2},{4,5},{5,4},{6,7},{7,6},{8,9},{9,8},{10,11... | collective-permute-start | bytes 1572872 | tf_op jit(solution)/shard_map/ppermute | solution.py:306
  17.6 2.8 %collective-permute-start.1 = (bf16[2592,128]{1,0:T(8,128)(2,1)S(1)}, bf16[2592,128]{1,0:T(8,128)(2,1)S(1)}, u32[]{:S(2)}, u32[]{:S(2)}) collective-permute-start(bf16[2592,128]{1,0:T(8,128)(2,1)S(1)} %get-tuple-element.34), channel_id=1, source_target_pairs={{0,1},{1,0},{2,3},{3,2},{4,5},{5,4},{6,7},{7,6},{8,9},{9,8},{10,11... | collective-permute-start | bytes 1990664 | tf_op jit(solution)/shard_map/ppermute | solution.py:306
  20.2 4.8 %collective-permute-start.10 = (bf16[2592,128]{1,0:T(8,128)(2,1)S(1)}, bf16[2592,128]{1,0:T(8,128)(2,1)S(1)}, u32[]{:S(2)}, u32[]{:S(2)}) collective-permute-start(bf16[2592,128]{1,0:T(8,128)(2,1)S(1)} %get-tuple-element.45), channel_id=1, source_target_pairs={{0,1},{1,0},{2,3},{3,2},{4,5},{5,4},{6,7},{7,6},{8,9},{9,8},{10,11... | collective-permute-start | bytes 1990664 | tf_op jit(solution)/shard_map/ppermute | solution.py:306
  20.5 8.1 %collective-permute-start.2 = (bf16[672,128]{1,0:T(8,128)(2,1)S(1)}, bf16[672,128]{1,0:T(8,128)(2,1)S(1)}, u32[]{:S(2)}, u32[]{:S(2)}) collective-permute-start(bf16[672,128]{1,0:T(8,128)(2,1)S(1)} %get-tuple-element.36), channel_id=1, source_target_pairs={{0,2},{1,3},{2,0},{3,1},{4,6},{5,7},{6,4},{7,5},{8,10},{9,11},{10,... | collective-permute-start | bytes 516104 | tf_op jit(solution)/shard_map/ppermute | solution.py:315
  23.5 9.8 %collective-permute-start.3 = (bf16[672,128]{1,0:T(8,128)(2,1)S(1)}, bf16[672,128]{1,0:T(8,128)(2,1)S(1)}, u32[]{:S(2)}, u32[]{:S(2)}) collective-permute-start(bf16[672,128]{1,0:T(8,128)(2,1)S(1)} %get-tuple-element.37), channel_id=1, source_target_pairs={{0,4},{1,5},{2,6},{3,7},{4,0},{5,1},{6,2},{7,3},{8,12},{9,13},{10,... | collective-permute-start | bytes 516104 | tf_op jit(solution)/shard_map/ppermute | solution.py:315
  25.0 8.3 %collective-permute-start.4 = (bf16[672,128]{1,0:T(8,128)(2,1)S(1)}, bf16[672,128]{1,0:T(8,128)(2,1)S(1)}, u32[]{:S(2)}, u32[]{:S(2)}) collective-permute-start(bf16[672,128]{1,0:T(8,128)(2,1)S(1)} %get-tuple-element.38), channel_id=1, source_target_pairs={{0,6},{1,7},{2,4},{3,5},{4,2},{5,3},{6,0},{7,1},{8,14},{9,15},{10,... | collective-permute-start | bytes 516104 | tf_op jit(solution)/shard_map/ppermute | solution.py:315
  25.1 9.9 %collective-permute-start.11 = (bf16[672,128]{1,0:T(8,128)(2,1)S(1)}, bf16[672,128]{1,0:T(8,128)(2,1)S(1)}, u32[]{:S(2)}, u32[]{:S(2)}) collective-permute-start(bf16[672,128]{1,0:T(8,128)(2,1)S(1)} %get-tuple-element.47), channel_id=1, source_target_pairs={{0,2},{1,9},{2,0},{3,11},{4,6},{5,13},{6,4},{7,15},{8,10},{9,1},{1... | collective-permute-start | bytes 516104 | tf_op jit(solution)/shard_map/ppermute | solution.py:315
  27.2 9.8 %collective-permute-start.12 = (bf16[672,128]{1,0:T(8,128)(2,1)S(1)}, bf16[672,128]{1,0:T(8,128)(2,1)S(1)}, u32[]{:S(2)}, u32[]{:S(2)}) collective-permute-start(bf16[672,128]{1,0:T(8,128)(2,1)S(1)} %get-tuple-element.48), channel_id=1, source_target_pairs={{0,4},{1,17},{2,6},{3,19},{4,0},{5,21},{6,2},{7,23},{8,12},{9,25},... | collective-permute-start | bytes 516104 | tf_op jit(solution)/shard_map/ppermute | solution.py:315
  28.7 8.3 %collective-permute-start.13 = (bf16[672,128]{1,0:T(8,128)(2,1)S(1)}, bf16[672,128]{1,0:T(8,128)(2,1)S(1)}, u32[]{:S(2)}, u32[]{:S(2)}) collective-permute-start(bf16[672,128]{1,0:T(8,128)(2,1)S(1)} %get-tuple-element.49), channel_id=1, source_target_pairs={{0,6},{1,25},{2,4},{3,27},{4,2},{5,29},{6,0},{7,31},{8,14},{9,17},... | collective-permute-start | bytes 516104 | tf_op jit(solution)/shard_map/ppermute | solution.py:315
  33.4 5.6 %collective-permute-start.5 = (bf16[672,128]{1,0:T(8,128)(2,1)S(1)}, bf16[672,128]{1,0:T(8,128)(2,1)S(1)}, u32[]{:S(2)}, u32[]{:S(2)}) collective-permute-start(bf16[672,128]{1,0:T(8,128)(2,1)S(1)} %shard_map.121.one), channel_id=1, source_target_pairs={{0,8},{1,9},{2,10},{3,11},{4,12},{5,13},{6,14},{7,15},{8,0},{9,1},... | collective-permute-start | bytes 516104 | tf_op jit(solution)/shard_map/ppermute | solution.py:315
  37.0 7.3 %collective-permute-start.14 = (bf16[672,128]{1,0:T(8,128)(2,1)S(1)}, bf16[672,128]{1,0:T(8,128)(2,1)S(1)}, u32[]{:S(2)}, u32[]{:S(2)}) collective-permute-start(bf16[672,128]{1,0:T(8,128)(2,1)S(1)} %shard_map.127.one), channel_id=1, source_target_pairs={{0,8},{1,3},{2,10},{3,1},{4,12},{5,7},{6,14},{7,5},{8,0},{9,11},{1... | collective-permute-start | bytes 516104 | tf_op jit(solution)/shard_map/ppermute | solution.py:315
  39.0 9.6 %collective-permute-start.6 = (bf16[672,128]{1,0:T(8,128)(2,1)S(1)}, bf16[672,128]{1,0:T(8,128)(2,1)S(1)}, u32[]{:S(2)}, u32[]{:S(2)}) collective-permute-start(bf16[672,128]{1,0:T(8,128)(2,1)S(1)} %shard_map.122.one), channel_id=1, source_target_pairs={{0,16},{1,17},{2,18},{3,19},{4,20},{5,21},{6,22},{7,23},{8,24},{9,... | collective-permute-start | bytes 516104 | tf_op jit(solution)/shard_map/ppermute | solution.py:315
  44.4 9.3 %collective-permute-start.15 = (bf16[672,128]{1,0:T(8,128)(2,1)S(1)}, bf16[672,128]{1,0:T(8,128)(2,1)S(1)}, u32[]{:S(2)}, u32[]{:S(2)}) collective-permute-start(bf16[672,128]{1,0:T(8,128)(2,1)S(1)} %shard_map.128.one), channel_id=1, source_target_pairs={{0,16},{1,5},{2,18},{3,7},{4,20},{5,1},{6,22},{7,3},{8,24},{9,13},... | collective-permute-start | bytes 516104 | tf_op jit(solution)/shard_map/ppermute | solution.py:315
  48.6 8.9 %collective-permute-start.9 = (bf16[640,128]{1,0:T(8,128)(2,1)S(1)}, bf16[640,128]{1,0:T(8,128)(2,1)S(1)}, u32[]{:S(2)}, u32[]{:S(2)}) collective-permute-start(bf16[640,128]{1,0:T(8,128)(2,1)S(1)} %get-tuple-element.39.refs_0_), channel_id=1, source_target_pairs={{0,6},{1,7},{2,4},{3,5},{4,2},{5,3},{6,0},{7,1},{8,14},{9,15},{10,... | collective-permute-start | bytes 491528 | tf_op jit(solution)/shard_map/ppermute | solution.py:315
  53.1 6.0 %collective-permute-start.8 = (bf16[640,128]{1,0:T(8,128)(2,1)S(1)}, bf16[640,128]{1,0:T(8,128)(2,1)S(1)}, u32[]{:S(2)}, u32[]{:S(2)}) collective-permute-start(bf16[640,128]{1,0:T(8,128)(2,1)S(1)} %get-tuple-element.39.refs_0_), channel_id=1, source_target_pairs={{0,4},{1,5},{2,6},{3,7},{4,0},{5,1},{6,2},{7,3},{8,12},{9,13},{10,... | collective-permute-start | bytes 491528 | tf_op jit(solution)/shard_map/ppermute | solution.py:315
  53.1 6.0 %collective-permute-start.7 = (bf16[640,128]{1,0:T(8,128)(2,1)S(1)}, bf16[640,128]{1,0:T(8,128)(2,1)S(1)}, u32[]{:S(2)}, u32[]{:S(2)}) collective-permute-start(bf16[640,128]{1,0:T(8,128)(2,1)S(1)} %get-tuple-element.39.refs_0_), channel_id=1, source_target_pairs={{0,2},{1,3},{2,0},{3,1},{4,6},{5,7},{6,4},{7,5},{8,10},{9,11},{10,... | collective-permute-start | bytes 491528 | tf_op jit(solution)/shard_map/ppermute | solution.py:315
  54.3 7.4 %collective-permute-start.18 = (bf16[640,128]{1,0:T(8,128)(2,1)S(1)}, bf16[640,128]{1,0:T(8,128)(2,1)S(1)}, u32[]{:S(2)}, u32[]{:S(2)}) collective-permute-start(bf16[640,128]{1,0:T(8,128)(2,1)S(1)} %get-tuple-element.50.refs_0_), channel_id=1, source_target_pairs={{0,6},{1,25},{2,4},{3,27},{4,2},{5,29},{6,0},{7,31},{8,14},{9,17},... | collective-permute-start | bytes 491528 | tf_op jit(solution)/shard_map/ppermute | solution.py:315
  57.2 6.2 %collective-permute-start.17 = (bf16[640,128]{1,0:T(8,128)(2,1)S(1)}, bf16[640,128]{1,0:T(8,128)(2,1)S(1)}, u32[]{:S(2)}, u32[]{:S(2)}) collective-permute-start(bf16[640,128]{1,0:T(8,128)(2,1)S(1)} %get-tuple-element.50.refs_0_), channel_id=1, source_target_pairs={{0,4},{1,17},{2,6},{3,19},{4,0},{5,21},{6,2},{7,23},{8,12},{9,25},... | collective-permute-start | bytes 491528 | tf_op jit(solution)/shard_map/ppermute | solution.py:315
  57.5 5.9 %collective-permute-start.16 = (bf16[640,128]{1,0:T(8,128)(2,1)S(1)}, bf16[640,128]{1,0:T(8,128)(2,1)S(1)}, u32[]{:S(2)}, u32[]{:S(2)}) collective-permute-start(bf16[640,128]{1,0:T(8,128)(2,1)S(1)} %get-tuple-element.50.refs_0_), channel_id=1, source_target_pairs={{0,2},{1,9},{2,0},{3,11},{4,6},{5,13},{6,4},{7,15},{8,10},{9,1},{1... | collective-permute-start | bytes 491528 | tf_op jit(solution)/shard_map/ppermute | solution.py:315
  59.2 6.6 %collective-permute-start.19 = (bf16[2560,128]{1,0:T(8,128)(2,1)S(1)}, bf16[2560,128]{1,0:T(8,128)(2,1)S(1)}, u32[]{:S(2)}, u32[]{:S(2)}) collective-permute-start(bf16[2560,128]{1,0:T(8,128)(2,1)S(1)} %shard_map.124.refs_0_), channel_id=1, source_target_pairs={{0,1},{1,0},{2,3},{3,2},{4,5},{5,4},{6,7},{7,6},{8,9},{9,8},{10,11... | collective-permute-start | bytes 1966088 | tf_op jit(solution)/shard_map/ppermute | solution.py:306
  63.4 2.4 %collective-permute-start.20 = (bf16[2560,128]{1,0:T(8,128)(2,1)S(1)}, bf16[2560,128]{1,0:T(8,128)(2,1)S(1)}, u32[]{:S(2)}, u32[]{:S(2)}) collective-permute-start(bf16[2560,128]{1,0:T(8,128)(2,1)S(1)} %shard_map.130.refs_1_), channel_id=1, source_target_pairs={{0,1},{1,0},{2,3},{3,2},{4,5},{5,4},{6,7},{7,6},{8,9},{9,8},{10,11... | collective-permute-start | bytes 1966088 | tf_op jit(solution)/shard_map/ppermute | solution.py:306
  (3 other events, 10.1 us)

commit v7 on v6

--- a/solution.py
+++ b/solution.py
@@ -13,7 +13,9 @@
 WIN = TILE + 2 * PAD
 HALO = 64
 TILES = 2 * PAD
-PLANS = (((1, 1), (4, 4)), ((1, 4), (4, 1)))
+SLAB = 256
+GROUPS = (((0, True), (1, True)), ((0, False), (1, False)))
+PLANS = (((1, 1), (4, 8), (8, 4)), ((1, 4), (4, 1), (8, 2)))
 LANES = 128
 DIGITS = 48
 FRACTION = 20
@@ -459,16 +461,16 @@
             tiles.append(tile)
         return mine, tiles[0]
     mine, tiles = [], []
-    for base, got, (groups, pairs) in zip(keep, gots, PLANS):
+    for base, got, (groups, pairs, last_pairs) in zip(keep, gots, PLANS):
         part = (base.shape[0] - TILES) // 4 + TILES
         shapes = [(part, F32)] + [(part, BF16)] * 3
         base, *outs = on_chip(functools.partial(deal_kernel, groups), shapes, base, got)
         (value,) = on_chip(join_kernel, [(part, BF16)], base, *exchange(outs, groups))
-        twice = tuple(2 * bit for bit in pairs)
         (value,) = on_chip(split_kernel, [(part, BF16)], value, swap_by_core(value, pairs))
-        value, tile = on_chip(split_kernel, [(part - TILES, BF16), (TILES, BF16)], value, swap_by_core(value, twice))
+        shapes = [(part - TILES, BF16)] + [(TILES, BF16)] * (not tiles)
+        value, *tile = on_chip(split_kernel, shapes, value, swap_by_core(value, last_pairs))
         mine.append(value)
-        tiles.append(tile)
+        tiles += tile
     return [place(spread(value, plan[0]), plan[0]) for value, plan in zip(mine, PLANS)], tiles[0]
 
 
@@ -476,68 +478,83 @@
     return [swap_by_core(out, ((k + 1) * bits[0], (k + 1) * bits[1])) for k, out in enumerate(outs)]
 
 
-def finish_kernel(own, rows, *refs):
+def finish_kernel(parts, aliased, with_loss, rows, *refs):
     staged, sems = refs[-2:]
-    if own:
-        *halves, tile, loss = refs[:4]
-    else:
-        *halves, tile = refs[:3]
-    outs = refs[-6:-2]
+    sums, scalars = refs[: len(parts)], refs[len(parts)]
+    outs = list(refs[len(parts) + 1 + aliased : -2])
+    scale = scalars[0:1, :]
+    if with_loss:
+        outs.pop(0)[0, 0] = scalars[8, 0]
+    encoders = sorted({m for m, _ in parts})
+    blocks = sums[0].shape[0] // rows
+    odd = lax.rem(lax.axis_index("tm"), 2)
+    copies = []
+    for n, (m, own) in enumerate(parts):
+        half = odd if own else 1 - odd
+        where = encoders.index(m) * 2
+        at = 0
+        columns = pl.ds(pl.multiple_of(half * blocks * LANES, LANES), blocks * LANES)
+        for out in outs[where : where + 2]:
+            for row in range(0, out.shape[0], SLAB):
+                here, there = pl.ds(at + row, SLAB), pl.ds(row, SLAB)
+                for j in range(blocks):
+                    value = sums[n][pl.ds(j * rows + at + row, SLAB), :].astype(F32) * scale
+                    staged[n, here, j * LANES : (j + 1) * LANES] = value
+                copy = pltpu.make_async_copy(staged.at[n, here, :], out.at[there, columns], sems.at[len(copies)])
+                copy.start()
+                copies.append(copy)
+            at += out.shape[0]
+    for copy in copies:
+        copy.wait()
+
+
+def scalars_kernel(tile, out):
     digits = tile[...].astype(F32)
     count = value_of(digits[PAD : PAD + 1])
-    scale = 1.0 / count
-    if own:
-        loss[0, 0] = value_of(digits[0:1]) / count
-    blocks = halves[0].shape[0] // rows
-    half = lax.rem(lax.axis_index("tm"), 2)
-    half = half if own else 1 - half
-    copies = []
-    for m, mine in enumerate(halves):
-        for j in range(blocks):
-            at = j * rows
-            column = pl.multiple_of((half * blocks + j) * LANES, LANES)
-            for out in outs[2 * m : 2 * m + 2]:
-                size = out.shape[0]
-                staged[m, at : at + size, :] = mine[at : at + size, :].astype(F32) * scale
-                copy = pltpu.make_async_copy(
-                    staged.at[m, at : at + size, :], out.at[:, pl.ds(column, LANES)], sems.at[len(copies)]
-                )
-                copy.start()
-                copies.append(copy)
-                at += size
-    for copy in copies:
-        copy.wait()
+    out[0:8, :] = jnp.broadcast_to(1.0 / count, (8, LANES))
+    out[8:16, :] = jnp.broadcast_to(value_of(digits[0:1]) / count, (8, LANES))
+
+
+def finish_some(parts, sums, scalars, earlier, with_loss, conv_rows, width):
+    smem, vmem, hbm = (pl.BlockSpec(memory_space=space) for space in (pltpu.SMEM, pltpu.VMEM, pl.ANY))
+    encoders = sorted({m for m, _ in parts})
+    grads = [jax.ShapeDtypeStruct((n, width), F32) for n in (conv_rows, width) * len(encoders)]
+    known = [(m, array) for m in encoders if m in earlier for array in earlier[m]]
+    places = {(m, n): i for i, (m, n) in enumerate((m, n) for m in encoders for n in (0, 1))}
+    aliases = {
+        len(parts) + 1 + i: with_loss + places[m, i % 2] for i, (m, _) in enumerate(known)
+    }
+    rows = conv_rows + width
+    height = sums[0].shape[0]
+    size = height * LANES * len(parts)
+    outs = pl.pallas_call(
+        functools.partial(finish_kernel, parts, len(known), with_loss, rows),
+        out_shape=[jax.ShapeDtypeStruct((1, 1), F32)] * with_loss + grads,
+        in_specs=[vmem] * (len(parts) + 1) + [hbm] * len(known),
+        out_specs=[smem] * with_loss + [hbm] * len(grads),
+        scratch_shapes=[
+            pltpu.VMEM((len(parts), rows, width // 2), F32),
+            pltpu.SemaphoreType.DMA((len(parts) * rows // SLAB,)),
+        ],
+        input_output_aliases=aliases,
+        compiler_params=pltpu.CompilerParams(vmem_limit_bytes=20 * 1024 * 1024),
+        cost_estimate=pl.CostEstimate(flops=size, bytes_accessed=6 * size, transcendentals=0),
+    )(*sums, scalars, *[array for _, array in known])
+    loss, outs = outs[:with_loss], outs[with_loss:]
+    for i, m in enumerate(encoders):
+        earlier = {**earlier, m: outs[2 * i : 2 * i + 2]}
+    return loss, earlier
 
 
 def finish(halves, tile, conv_rows, width):
     gots = [swap(half, "tm", 1) for half in halves]
-    smem, vmem, hbm = (pl.BlockSpec(memory_space=space) for space in (pltpu.SMEM, pltpu.VMEM, pl.ANY))
-    grads = [jax.ShapeDtypeStruct((n, width), F32) for n in (conv_rows, width) * 2]
-    rows = conv_rows + width
-    scratch = [pltpu.VMEM((2, *halves[0].shape), F32), pltpu.SemaphoreType.DMA((4 * (halves[0].shape[0] // rows),))]
-    params = pltpu.CompilerParams(vmem_limit_bytes=16 * 1024 * 1024)
-    size = 2 * halves[0].size
-    cost = pl.CostEstimate(flops=size, bytes_accessed=6 * size, transcendentals=0)
-    loss, *outs = pl.pallas_call(
-        functools.partial(finish_kernel, True, rows),
-        out_shape=[jax.ShapeDtypeStruct((1, 1), F32)] + grads,
-        in_specs=[vmem] * 3,
-        out_specs=[smem] + [hbm] * 4,
-        scratch_shapes=scratch,
-        compiler_params=params,
-        cost_estimate=cost,
-    )(*halves, tile)
-    outs = pl.pallas_call(
-        functools.partial(finish_kernel, False, rows),
-        out_shape=grads,
-        in_specs=[vmem] * 3 + [hbm] * 4,
-        out_specs=[hbm] * 4,
-        scratch_shapes=scratch,
-        input_output_aliases={n + 3: n for n in range(4)},
-        compiler_params=params,
-        cost_estimate=cost,
-    )(*gots, tile, *outs)
-    return loss, outs
+    sums = {(m, own): (halves if own else gots)[m] for m in (0, 1) for own in (True, False)}
+    (scalars,) = on_chip(scalars_kernel, [(16, F32)], tile)
+    loss, done = [], {}
+    for parts in GROUPS:
+        value, done = finish_some(parts, [sums[part] for part in parts], scalars, done, not loss, conv_rows, width)
+        loss = loss or value
+    return loss[0], [*done[0], *done[1]]
 
 
 def shards(

time: 67.9 us -> 65.5 us (0.965)
  waiting for transfers between devices: 16 us -> 13.9 us
  Pallas kernels: 21 us -> 20.3 us
    ppermute x16, waiting for transfers between devices: 14.4 us -> 12.3 us  [swap_by_core(): return lax.ppermute(value, ('clip', 'tm'), pairs)]
  transfers between devices with their start and end apart: 21 -> 21, of which waited for: 10 -> 12; matrix products, arithmetic and copies ran while one was open for 0% -> 0% of each run, Pallas kernels for 8% -> 8%
where the time goes in v7:
time: 65.5 us; the launch traced here: 65.3 us
  starting transfers between devices  28.9 us (44%)
  Pallas kernels  20.3 us (31%)
  waiting for transfers between devices  13.9 us (21%)
  local copies, waits for them, and re-layouts  1.23 us (2%)
  between operations  1 us (2%)
    ppermute x16, starting transfers between devices, swap_by_core(): return lax.ppermute(value, ('clip', 'tm'), pairs)  27.6 us
    pallas_call x1, Pallas kernels, local_grads(): pl.pallas_call(functools.partial(kernel, frames, clips, halo), out_shape=...  13.6 us
    ppermute x16, waiting for transfers between devices, swap_by_core(): return lax.ppermute(value, ('clip', 'tm'), pairs)  12.3 us
    pallas_call x2, Pallas kernels, finish_some(): pl.pallas_call(functools.partial(finish_kernel, parts, len(known), with_l...  3.69 us
    pallas_call x1, Pallas kernels, local_grads(): pl.pallas_call(functools.partial(audio_kernel, block_of(frames)), out_sha...  2.11 us
    ppermute x5, waiting for transfers between devices, swap(): lax.ppermute(value, axis, [(i, i ^ bit) for i in range(lax.axis_size(axis...  1.55 us
    ppermute x5, starting transfers between devices, swap(): lax.ppermute(value, axis, [(i, i ^ bit) for i in range(lax.axis_size(axis...  1.34 us
  transfers between devices with their start and end apart: 21, of which 12 were waited for; matrix products, arithmetic and copies ran while one was open for 0% of the time, Pallas kernels for 8%

profile of v7, /device:TPU:0, one launch (start us, length us, event | category | flops | bytes accessed | tf_op | source)
XLA Modules:
  0.0 65.3 jit_solution(5322386945847321080)
XLA Ops:
  0.7 1.2 %dynamic-slice_bitcast_fusion = (bf16[1,2,256,256]{3,2,1,0:T(8,128)(2,1)S(1)}, bf16[1,2,256,256]{3,2,1,0:T(8,128)(2,1)S(1)}) fusion(bf16[4,256,256]{2,1,0:T(8,128)(2,1)} %own_v.1, s32[]{:T(128)S(6)} %select_n.4, bf16[4,256,256]{2,1,0:T(8,128)(2,1)} %own_a.1), kind=kLoop, calls=%fused_computation.1 | loop fusion | bytes 1048580 | tf_op jit(solution)/shard_map/stack | solution.py:568
  2.5 1.5 %collective-permute-done.got = bf16[2,2,256,256]{3,2,1,0:T(8,128)(2,1)S(1)} collective-permute-done((bf16[2,2,256,256]{3,2,1,0:T(8,128)(2,1)S(1)}, bf16[2,2,256,256]{3,2,1,0:T(8,128)(2,1)S(1)}, u32[]{:S(2)}, u32[]{:S(2)}) %collective-permute-start) | collective-permute-done | bytes 524320 | tf_op jit(solution)/shard_map/ppermute | solution.py:308
  4.1 13.6 %shard_map.119 = (f32[2592,128]{1,0:T(8,128)S(1)}, bf16[2592,128]{1,0:T(8,128)(2,1)S(1)}, bf16[1024,768]{1,0:T(8,128)(2,1)S(1)}, f32[1024,512]{1,0:T(8,128)S(1)}...) custom-call(s32[4]{0:T(128)S(1)} %copy-done.4, s32[4]{0:T(128)S(1)} %copy-done.5, ...), custom_call_target="tpu_custom_call" | custom-call | tf_op jit(solution)/shard_map/pallas_call | solution.py:272
  18.1 2.1 %shard_map.125 = (f32[2592,128]{1,0:T(8,128)S(1)}, bf16[2592,128]{1,0:T(8,128)(2,1)S(1)}) custom-call(bf16[512,512]{1,0:T(8,128)(2,1)S(1)} %copy-done.3, bf16[1024,768]{1,0:T(8,128)(2,1)S(1)} %get-tuple-element.39.cols, f32[1024,512]{1,0:T(8,128)S(1)} %get-tuple-element.40.slope, bf16[1024,512]{1,0:T(8,128)(2,1)S(1)} %get-tuple-element.41.hid, ...), custom_call_target="tpu_custom_call" | custom-call | flops 1879048192 | bytes 6291456 | tf_op jit(solution)/shard_map/pallas_call | solution.py:295
  20.5 2.9 %collective-permute-start.2 = (bf16[672,128]{1,0:T(8,128)(2,1)S(1)}, bf16[672,128]{1,0:T(8,128)(2,1)S(1)}, u32[]{:S(2)}, u32[]{:S(2)}) collective-permute-start(bf16[672,128]{1,0:T(8,128)(2,1)S(1)} %get-tuple-element.35), channel_id=1, source_target_pairs={{0,2},{1,3},{2,0},{3,1},{4,6},{5,7},{6,4},{7,5},{8,10},{9,11},{10,... | collective-permute-start | bytes 516104 | tf_op jit(solution)/shard_map/ppermute | solution.py:317
  23.5 1.5 %collective-permute-start.3 = (bf16[672,128]{1,0:T(8,128)(2,1)S(1)}, bf16[672,128]{1,0:T(8,128)(2,1)S(1)}, u32[]{:S(2)}, u32[]{:S(2)}) collective-permute-start(bf16[672,128]{1,0:T(8,128)(2,1)S(1)} %get-tuple-element.36), channel_id=1, source_target_pairs={{0,4},{1,5},{2,6},{3,7},{4,0},{5,1},{6,2},{7,3},{8,12},{9,13},{10,... | collective-permute-start | bytes 516104 | tf_op jit(solution)/shard_map/ppermute | solution.py:317
  25.1 2.0 %collective-permute-start.11 = (bf16[672,128]{1,0:T(8,128)(2,1)S(1)}, bf16[672,128]{1,0:T(8,128)(2,1)S(1)}, u32[]{:S(2)}, u32[]{:S(2)}) collective-permute-start(bf16[672,128]{1,0:T(8,128)(2,1)S(1)} %get-tuple-element.46), channel_id=1, source_target_pairs={{0,2},{1,9},{2,0},{3,11},{4,6},{5,13},{6,4},{7,15},{8,10},{9,1},{1... | collective-permute-start | bytes 516104 | tf_op jit(solution)/shard_map/ppermute | solution.py:317
  27.2 1.5 %collective-permute-start.12 = (bf16[672,128]{1,0:T(8,128)(2,1)S(1)}, bf16[672,128]{1,0:T(8,128)(2,1)S(1)}, u32[]{:S(2)}, u32[]{:S(2)}) collective-permute-start(bf16[672,128]{1,0:T(8,128)(2,1)S(1)} %get-tuple-element.47), channel_id=1, source_target_pairs={{0,4},{1,17},{2,6},{3,19},{4,0},{5,21},{6,2},{7,23},{8,12},{9,25},... | collective-permute-start | bytes 516104 | tf_op jit(solution)/shard_map/ppermute | solution.py:317
  28.7 3.0 %collective-permute-start.13 = (bf16[672,128]{1,0:T(8,128)(2,1)S(1)}, bf16[672,128]{1,0:T(8,128)(2,1)S(1)}, u32[]{:S(2)}, u32[]{:S(2)}) collective-permute-start(bf16[672,128]{1,0:T(8,128)(2,1)S(1)} %get-tuple-element.48), channel_id=1, source_target_pairs={{0,6},{1,25},{2,4},{3,27},{4,2},{5,29},{6,0},{7,31},{8,14},{9,17},... | collective-permute-start | bytes 516104 | tf_op jit(solution)/shard_map/ppermute | solution.py:317
  31.6 1.6 %collective-permute-done.3.refs_1_ = bf16[672,128]{1,0:T(8,128)(2,1)S(1)} collective-permute-done((bf16[672,128]{1,0:T(8,128)(2,1)S(1)}, bf16[672,128]{1,0:T(8,128)(2,1)S(1)}, u32[]{:S(2)}, u32[]{:S(2)}) %collective-permute-start.3) | collective-permute-done | bytes 172064 | tf_op jit(solution)/shard_map/ppermute | solution.py:317
  33.4 1.6 %collective-permute-start.5 = (bf16[672,128]{1,0:T(8,128)(2,1)S(1)}, bf16[672,128]{1,0:T(8,128)(2,1)S(1)}, u32[]{:S(2)}, u32[]{:S(2)}) collective-permute-start(bf16[672,128]{1,0:T(8,128)(2,1)S(1)} %shard_map.121.one), channel_id=1, source_target_pairs={{0,8},{1,17},{2,10},{3,19},{4,12},{5,21},{6,14},{7,23},{8,0},{9,25... | collective-permute-start | bytes 516104 | tf_op jit(solution)/shard_map/ppermute | solution.py:317
  35.0 2.0 %collective-permute-done.12.refs_1_ = bf16[672,128]{1,0:T(8,128)(2,1)S(1)} collective-permute-done((bf16[672,128]{1,0:T(8,128)(2,1)S(1)}, bf16[672,128]{1,0:T(8,128)(2,1)S(1)}, u32[]{:S(2)}, u32[]{:S(2)}) %collective-permute-start.12) | collective-permute-done | bytes 172064 | tf_op jit(solution)/shard_map/ppermute | solution.py:317
  37.0 1.6 %collective-permute-start.14 = (bf16[672,128]{1,0:T(8,128)(2,1)S(1)}, bf16[672,128]{1,0:T(8,128)(2,1)S(1)}, u32[]{:S(2)}, u32[]{:S(2)}) collective-permute-start(bf16[672,128]{1,0:T(8,128)(2,1)S(1)} %shard_map.127.one), channel_id=1, source_target_pairs={{0,8},{1,3},{2,10},{3,1},{4,12},{5,7},{6,14},{7,5},{8,0},{9,11},{1... | collective-permute-start | bytes 516104 | tf_op jit(solution)/shard_map/ppermute | solution.py:317
  39.0 3.4 %collective-permute-start.6 = (bf16[672,128]{1,0:T(8,128)(2,1)S(1)}, bf16[672,128]{1,0:T(8,128)(2,1)S(1)}, u32[]{:S(2)}, u32[]{:S(2)}) collective-permute-start(bf16[672,128]{1,0:T(8,128)(2,1)S(1)} %shard_map.122.one), channel_id=1, source_target_pairs={{0,16},{1,9},{2,18},{3,11},{4,20},{5,13},{6,22},{7,15},{8,24},{9,1... | collective-permute-start | bytes 516104 | tf_op jit(solution)/shard_map/ppermute | solution.py:317
  42.7 2.8 %collective-permute-start.15 = (bf16[672,128]{1,0:T(8,128)(2,1)S(1)}, bf16[672,128]{1,0:T(8,128)(2,1)S(1)}, u32[]{:S(2)}, u32[]{:S(2)}) collective-permute-start(bf16[672,128]{1,0:T(8,128)(2,1)S(1)} %shard_map.128.one), channel_id=1, source_target_pairs={{0,16},{1,5},{2,18},{3,7},{4,20},{5,1},{6,22},{7,3},{8,24},{9,13},... | collective-permute-start | bytes 516104 | tf_op jit(solution)/shard_map/ppermute | solution.py:317
  46.0 1.5 %collective-permute-start.9 = (bf16[640,128]{1,0:T(8,128)(2,1)S(1)}, bf16[640,128]{1,0:T(8,128)(2,1)S(1)}, u32[]{:S(2)}, u32[]{:S(2)}) collective-permute-start(bf16[640,128]{1,0:T(8,128)(2,1)S(1)} %get-tuple-element.38.refs_0_), channel_id=1, source_target_pairs={{0,6},{1,7},{2,4},{3,5},{4,2},{5,3},{6,0},{7,1},{8,14},{9,15},{10,... | collective-permute-start | bytes 491528 | tf_op jit(solution)/shard_map/ppermute | solution.py:317
  47.5 1.4 %collective-permute-start.8 = (bf16[640,128]{1,0:T(8,128)(2,1)S(1)}, bf16[640,128]{1,0:T(8,128)(2,1)S(1)}, u32[]{:S(2)}, u32[]{:S(2)}) collective-permute-start(bf16[640,128]{1,0:T(8,128)(2,1)S(1)} %get-tuple-element.38.refs_0_), channel_id=1, source_target_pairs={{0,4},{1,5},{2,6},{3,7},{4,0},{5,1},{6,2},{7,3},{8,12},{9,13},{10,... | collective-permute-start | bytes 491528 | tf_op jit(solution)/shard_map/ppermute | solution.py:317
  49.5 2.4 %collective-permute-done.15.other = bf16[672,128]{1,0:T(8,128)(2,1)S(1)} collective-permute-done((bf16[672,128]{1,0:T(8,128)(2,1)S(1)}, bf16[672,128]{1,0:T(8,128)(2,1)S(1)}, u32[]{:S(2)}, u32[]{:S(2)}) %collective-permute-start.15) | collective-permute-done | bytes 172064 | tf_op jit(solution)/shard_map/ppermute | solution.py:317
  51.9 2.1 %collective-permute-start.18 = (bf16[640,128]{1,0:T(8,128)(2,1)S(1)}, bf16[640,128]{1,0:T(8,128)(2,1)S(1)}, u32[]{:S(2)}, u32[]{:S(2)}) collective-permute-start(bf16[640,128]{1,0:T(8,128)(2,1)S(1)} %shard_map.129.refs_0_), channel_id=1, source_target_pairs={{0,6},{1,25},{2,4},{3,27},{4,2},{5,29},{6,0},{7,31},{8,14},{9,17},... | collective-permute-start | bytes 491528 | tf_op jit(solution)/shard_map/ppermute | solution.py:317
  55.5 2.0 %collective-permute-done.8.refs_2_ = bf16[640,128]{1,0:T(8,128)(2,1)S(1)} collective-permute-done((bf16[640,128]{1,0:T(8,128)(2,1)S(1)}, bf16[640,128]{1,0:T(8,128)(2,1)S(1)}, u32[]{:S(2)}, u32[]{:S(2)}) %collective-permute-start.8) | collective-permute-done | bytes 163872 | tf_op jit(solution)/shard_map/ppermute | solution.py:317
  57.7 1.7 %collective-permute-done.18.refs_3_ = bf16[640,128]{1,0:T(8,128)(2,1)S(1)} collective-permute-done((bf16[640,128]{1,0:T(8,128)(2,1)S(1)}, bf16[640,128]{1,0:T(8,128)(2,1)S(1)}, u32[]{:S(2)}, u32[]{:S(2)}) %collective-permute-start.18) | collective-permute-done | bytes 163872 | tf_op jit(solution)/shard_map/ppermute | solution.py:317
  59.4 1.7 %collective-permute-done.17.refs_2_ = bf16[640,128]{1,0:T(8,128)(2,1)S(1)} collective-permute-done((bf16[640,128]{1,0:T(8,128)(2,1)S(1)}, bf16[640,128]{1,0:T(8,128)(2,1)S(1)}, u32[]{:S(2)}, u32[]{:S(2)}) %collective-permute-start.17) | collective-permute-done | bytes 163872 | tf_op jit(solution)/shard_map/ppermute | solution.py:317
  61.4 2.1 %shard_map.132 = (f32[1,1]{1,0:T(1,128)}, f32[768,512]{1,0:T(8,128)}, f32[512,512]{1,0:T(8,128)}, f32[768,512]{1,0:T(8,128)}, f32[512,512]{1,0:T(8,128)}) custom-call(bf16[2560,128]{1,0:T(8,128)(2,1)S(1)} %shard_map.124.refs_0_, bf16[2560,128]{1,0:T(8,128)(2,1)S(1)} %shard_map.130.refs_1_, f32[16,128]{1,0:T(8,128)S(1)} %shard_map.131.refs_2_), custom_call_target="tpu_custom_call" | custom-call | flops 655360 | bytes 3932160 | tf_op jit(solution)/shard_map/pallas_call | solution.py:530
  63.6 1.6 %shard_map.133 = (f32[768,512]{1,0:T(8,128)}, f32[512,512]{1,0:T(8,128)}, f32[768,512]{1,0:T(8,128)}, f32[512,512]{1,0:T(8,128)}) custom-call(bf16[2560,128]{1,0:T(8,128)(2,1)S(1)} %collective-permute-done.19.refs_0_, bf16[2560,128]{1,0:T(8,128)(2,1)S(1)} %collective-permute-done.20.refs_1_, ...), custom_call_target="tpu_custom_call", output_to_operand_aliasing={{0}: (3, {}), {1}: (4, {}), {2}: (5, {}), {3}: (6, {})} | custom-call | flops 655360 | bytes 3932160 | tf_op jit(solution)/shard_map/pallas_call | solution.py:530
  (47 shorter events, 5.5 us)
Async XLA Ops:
  0.6 3.4 %copy-start.1 = (bf16[4,256,256]{2,1,0:T(8,128)(2,1)S(1)}, bf16[4,256,256]{2,1,0:T(8,128)(2,1)}, u32[]{:S(2)}) copy-start(bf16[4,256,256]{2,1,0:T(8,128)(2,1)} %own_v.1) | copy-start | bytes 1572868
  0.6 3.4 %copy-start = (bf16[4,256,256]{2,1,0:T(8,128)(2,1)S(1)}, bf16[4,256,256]{2,1,0:T(8,128)(2,1)}, u32[]{:S(2)}) copy-start(bf16[4,256,256]{2,1,0:T(8,128)(2,1)} %own_a.1) | copy-start | bytes 1572868
  0.7 3.4 %copy-start.3 = (bf16[512,512]{1,0:T(8,128)(2,1)S(1)}, bf16[512,512]{1,0:T(8,128)(2,1)}, u32[]{:S(2)}) copy-start(bf16[512,512]{1,0:T(8,128)(2,1)} %w_proj.1) | copy-start | bytes 1572868
  2.0 2.1 %collective-permute-start = (bf16[2,2,256,256]{3,2,1,0:T(8,128)(2,1)S(1)}, bf16[2,2,256,256]{3,2,1,0:T(8,128)(2,1)S(1)}, u32[]{:S(2)}, u32[]{:S(2)}) collective-permute-start(bf16[2,2,256,256]{3,2,1,0:T(8,128)(2,1)S(1)} %pad_maximum_fusion), channel_id=1, source_target_pairs={{0,1},{1,0},{2,3},{3,2},{4,5},{5,4},{6,7},{7,6},{8,9},{9,8},{10,11... | collective-permute-start | bytes 1572872 | tf_op jit(solution)/shard_map/ppermute | solution.py:308
  17.6 2.8 %collective-permute-start.1 = (bf16[2592,128]{1,0:T(8,128)(2,1)S(1)}, bf16[2592,128]{1,0:T(8,128)(2,1)S(1)}, u32[]{:S(2)}, u32[]{:S(2)}) collective-permute-start(bf16[2592,128]{1,0:T(8,128)(2,1)S(1)} %get-tuple-element.33), channel_id=1, source_target_pairs={{0,1},{1,0},{2,3},{3,2},{4,5},{5,4},{6,7},{7,6},{8,9},{9,8},{10,11... | collective-permute-start | bytes 1990664 | tf_op jit(solution)/shard_map/ppermute | solution.py:308
  20.2 4.8 %collective-permute-start.10 = (bf16[2592,128]{1,0:T(8,128)(2,1)S(1)}, bf16[2592,128]{1,0:T(8,128)(2,1)S(1)}, u32[]{:S(2)}, u32[]{:S(2)}) collective-permute-start(bf16[2592,128]{1,0:T(8,128)(2,1)S(1)} %get-tuple-element.44), channel_id=1, source_target_pairs={{0,1},{1,0},{2,3},{3,2},{4,5},{5,4},{6,7},{7,6},{8,9},{9,8},{10,11... | collective-permute-start | bytes 1990664 | tf_op jit(solution)/shard_map/ppermute | solution.py:308
  20.5 8.1 %collective-permute-start.2 = (bf16[672,128]{1,0:T(8,128)(2,1)S(1)}, bf16[672,128]{1,0:T(8,128)(2,1)S(1)}, u32[]{:S(2)}, u32[]{:S(2)}) collective-permute-start(bf16[672,128]{1,0:T(8,128)(2,1)S(1)} %get-tuple-element.35), channel_id=1, source_target_pairs={{0,2},{1,3},{2,0},{3,1},{4,6},{5,7},{6,4},{7,5},{8,10},{9,11},{10,... | collective-permute-start | bytes 516104 | tf_op jit(solution)/shard_map/ppermute | solution.py:317
  23.5 9.8 %collective-permute-start.3 = (bf16[672,128]{1,0:T(8,128)(2,1)S(1)}, bf16[672,128]{1,0:T(8,128)(2,1)S(1)}, u32[]{:S(2)}, u32[]{:S(2)}) collective-permute-start(bf16[672,128]{1,0:T(8,128)(2,1)S(1)} %get-tuple-element.36), channel_id=1, source_target_pairs={{0,4},{1,5},{2,6},{3,7},{4,0},{5,1},{6,2},{7,3},{8,12},{9,13},{10,... | collective-permute-start | bytes 516104 | tf_op jit(solution)/shard_map/ppermute | solution.py:317
  25.0 8.3 %collective-permute-start.4 = (bf16[672,128]{1,0:T(8,128)(2,1)S(1)}, bf16[672,128]{1,0:T(8,128)(2,1)S(1)}, u32[]{:S(2)}, u32[]{:S(2)}) collective-permute-start(bf16[672,128]{1,0:T(8,128)(2,1)S(1)} %get-tuple-element.37), channel_id=1, source_target_pairs={{0,6},{1,7},{2,4},{3,5},{4,2},{5,3},{6,0},{7,1},{8,14},{9,15},{10,... | collective-permute-start | bytes 516104 | tf_op jit(solution)/shard_map/ppermute | solution.py:317
  25.1 9.9 %collective-permute-start.11 = (bf16[672,128]{1,0:T(8,128)(2,1)S(1)}, bf16[672,128]{1,0:T(8,128)(2,1)S(1)}, u32[]{:S(2)}, u32[]{:S(2)}) collective-permute-start(bf16[672,128]{1,0:T(8,128)(2,1)S(1)} %get-tuple-element.46), channel_id=1, source_target_pairs={{0,2},{1,9},{2,0},{3,11},{4,6},{5,13},{6,4},{7,15},{8,10},{9,1},{1... | collective-permute-start | bytes 516104 | tf_op jit(solution)/shard_map/ppermute | solution.py:317
  27.2 9.8 %collective-permute-start.12 = (bf16[672,128]{1,0:T(8,128)(2,1)S(1)}, bf16[672,128]{1,0:T(8,128)(2,1)S(1)}, u32[]{:S(2)}, u32[]{:S(2)}) collective-permute-start(bf16[672,128]{1,0:T(8,128)(2,1)S(1)} %get-tuple-element.47), channel_id=1, source_target_pairs={{0,4},{1,17},{2,6},{3,19},{4,0},{5,21},{6,2},{7,23},{8,12},{9,25},... | collective-permute-start | bytes 516104 | tf_op jit(solution)/shard_map/ppermute | solution.py:317
  28.7 8.3 %collective-permute-start.13 = (bf16[672,128]{1,0:T(8,128)(2,1)S(1)}, bf16[672,128]{1,0:T(8,128)(2,1)S(1)}, u32[]{:S(2)}, u32[]{:S(2)}) collective-permute-start(bf16[672,128]{1,0:T(8,128)(2,1)S(1)} %get-tuple-element.48), channel_id=1, source_target_pairs={{0,6},{1,25},{2,4},{3,27},{4,2},{5,29},{6,0},{7,31},{8,14},{9,17},... | collective-permute-start | bytes 516104 | tf_op jit(solution)/shard_map/ppermute | solution.py:317
  33.4 5.6 %collective-permute-start.5 = (bf16[672,128]{1,0:T(8,128)(2,1)S(1)}, bf16[672,128]{1,0:T(8,128)(2,1)S(1)}, u32[]{:S(2)}, u32[]{:S(2)}) collective-permute-start(bf16[672,128]{1,0:T(8,128)(2,1)S(1)} %shard_map.121.one), channel_id=1, source_target_pairs={{0,8},{1,17},{2,10},{3,19},{4,12},{5,21},{6,14},{7,23},{8,0},{9,25... | collective-permute-start | bytes 516104 | tf_op jit(solution)/shard_map/ppermute | solution.py:317
  37.0 5.6 %collective-permute-start.14 = (bf16[672,128]{1,0:T(8,128)(2,1)S(1)}, bf16[672,128]{1,0:T(8,128)(2,1)S(1)}, u32[]{:S(2)}, u32[]{:S(2)}) collective-permute-start(bf16[672,128]{1,0:T(8,128)(2,1)S(1)} %shard_map.127.one), channel_id=1, source_target_pairs={{0,8},{1,3},{2,10},{3,1},{4,12},{5,7},{6,14},{7,5},{8,0},{9,11},{1... | collective-permute-start | bytes 516104 | tf_op jit(solution)/shard_map/ppermute | solution.py:317
  39.0 6.9 %collective-permute-start.6 = (bf16[672,128]{1,0:T(8,128)(2,1)S(1)}, bf16[672,128]{1,0:T(8,128)(2,1)S(1)}, u32[]{:S(2)}, u32[]{:S(2)}) collective-permute-start(bf16[672,128]{1,0:T(8,128)(2,1)S(1)} %shard_map.122.one), channel_id=1, source_target_pairs={{0,16},{1,9},{2,18},{3,11},{4,20},{5,13},{6,22},{7,15},{8,24},{9,1... | collective-permute-start | bytes 516104 | tf_op jit(solution)/shard_map/ppermute | solution.py:317
  42.7 9.2 %collective-permute-start.15 = (bf16[672,128]{1,0:T(8,128)(2,1)S(1)}, bf16[672,128]{1,0:T(8,128)(2,1)S(1)}, u32[]{:S(2)}, u32[]{:S(2)}) collective-permute-start(bf16[672,128]{1,0:T(8,128)(2,1)S(1)} %shard_map.128.one), channel_id=1, source_target_pairs={{0,16},{1,5},{2,18},{3,7},{4,20},{5,1},{6,22},{7,3},{8,24},{9,13},... | collective-permute-start | bytes 516104 | tf_op jit(solution)/shard_map/ppermute | solution.py:317
  46.0 8.8 %collective-permute-start.9 = (bf16[640,128]{1,0:T(8,128)(2,1)S(1)}, bf16[640,128]{1,0:T(8,128)(2,1)S(1)}, u32[]{:S(2)}, u32[]{:S(2)}) collective-permute-start(bf16[640,128]{1,0:T(8,128)(2,1)S(1)} %get-tuple-element.38.refs_0_), channel_id=1, source_target_pairs={{0,6},{1,7},{2,4},{3,5},{4,2},{5,3},{6,0},{7,1},{8,14},{9,15},{10,... | collective-permute-start | bytes 491528 | tf_op jit(solution)/shard_map/ppermute | solution.py:317
  47.5 10.0 %collective-permute-start.8 = (bf16[640,128]{1,0:T(8,128)(2,1)S(1)}, bf16[640,128]{1,0:T(8,128)(2,1)S(1)}, u32[]{:S(2)}, u32[]{:S(2)}) collective-permute-start(bf16[640,128]{1,0:T(8,128)(2,1)S(1)} %get-tuple-element.38.refs_0_), channel_id=1, source_target_pairs={{0,4},{1,5},{2,6},{3,7},{4,0},{5,1},{6,2},{7,3},{8,12},{9,13},{10,... | collective-permute-start | bytes 491528 | tf_op jit(solution)/shard_map/ppermute | solution.py:317
  48.9 8.7 %collective-permute-start.7 = (bf16[640,128]{1,0:T(8,128)(2,1)S(1)}, bf16[640,128]{1,0:T(8,128)(2,1)S(1)}, u32[]{:S(2)}, u32[]{:S(2)}) collective-permute-start(bf16[640,128]{1,0:T(8,128)(2,1)S(1)} %get-tuple-element.38.refs_0_), channel_id=1, source_target_pairs={{0,2},{1,3},{2,0},{3,1},{4,6},{5,7},{6,4},{7,5},{8,10},{9,11},{10,... | collective-permute-start | bytes 491528 | tf_op jit(solution)/shard_map/ppermute | solution.py:317
  51.9 7.4 %collective-permute-start.18 = (bf16[640,128]{1,0:T(8,128)(2,1)S(1)}, bf16[640,128]{1,0:T(8,128)(2,1)S(1)}, u32[]{:S(2)}, u32[]{:S(2)}) collective-permute-start(bf16[640,128]{1,0:T(8,128)(2,1)S(1)} %shard_map.129.refs_0_), channel_id=1, source_target_pairs={{0,6},{1,25},{2,4},{3,27},{4,2},{5,29},{6,0},{7,31},{8,14},{9,17},... | collective-permute-start | bytes 491528 | tf_op jit(solution)/shard_map/ppermute | solution.py:317
  54.0 7.0 %collective-permute-start.17 = (bf16[640,128]{1,0:T(8,128)(2,1)S(1)}, bf16[640,128]{1,0:T(8,128)(2,1)S(1)}, u32[]{:S(2)}, u32[]{:S(2)}) collective-permute-start(bf16[640,128]{1,0:T(8,128)(2,1)S(1)} %shard_map.129.refs_0_), channel_id=1, source_target_pairs={{0,4},{1,17},{2,6},{3,19},{4,0},{5,21},{6,2},{7,23},{8,12},{9,25},... | collective-permute-start | bytes 491528 | tf_op jit(solution)/shard_map/ppermute | solution.py:317
  54.8 6.3 %collective-permute-start.16 = (bf16[640,128]{1,0:T(8,128)(2,1)S(1)}, bf16[640,128]{1,0:T(8,128)(2,1)S(1)}, u32[]{:S(2)}, u32[]{:S(2)}) collective-permute-start(bf16[640,128]{1,0:T(8,128)(2,1)S(1)} %shard_map.129.refs_0_), channel_id=1, source_target_pairs={{0,2},{1,9},{2,0},{3,11},{4,6},{5,13},{6,4},{7,15},{8,10},{9,1},{1... | collective-permute-start | bytes 491528 | tf_op jit(solution)/shard_map/ppermute | solution.py:317
  57.6 5.9 %collective-permute-start.19 = (bf16[2560,128]{1,0:T(8,128)(2,1)S(1)}, bf16[2560,128]{1,0:T(8,128)(2,1)S(1)}, u32[]{:S(2)}, u32[]{:S(2)}) collective-permute-start(bf16[2560,128]{1,0:T(8,128)(2,1)S(1)} %shard_map.124.refs_0_), channel_id=1, source_target_pairs={{0,1},{1,0},{2,3},{3,2},{4,5},{5,4},{6,7},{7,6},{8,9},{9,8},{10,11... | collective-permute-start | bytes 1966088 | tf_op jit(solution)/shard_map/ppermute | solution.py:308
  61.2 2.4 %collective-permute-start.20 = (bf16[2560,128]{1,0:T(8,128)(2,1)S(1)}, bf16[2560,128]{1,0:T(8,128)(2,1)S(1)}, u32[]{:S(2)}, u32[]{:S(2)}) collective-permute-start(bf16[2560,128]{1,0:T(8,128)(2,1)S(1)} %shard_map.130.refs_1_), channel_id=1, source_target_pairs={{0,1},{1,0},{2,3},{3,2},{4,5},{5,4},{6,7},{7,6},{8,9},{9,8},{10,11... | collective-permute-start | bytes 1966088 | tf_op jit(solution)/shard_map/ppermute | solution.py:308
  (3 other events, 10.1 us)

commit v8 on v7

--- a/solution.py
+++ b/solution.py
@@ -54,9 +54,9 @@
     return jnp.sum(jnp.where(lane < DIGITS, digits * weight, 0.0))
 
 
-def forward(feats, m, copies, w_conv, w_proj, cols, slope, hid, clips, frames, block, put):
+def columns(feats, m, copies, cols, clips, frames):
     chan = feats.shape[-1]
-    for copy in copies[0]:
+    for copy in copies:
         copy.wait()
     for c in range(clips):
         x = feats[m, c].astype(F32)
@@ -67,23 +67,31 @@
         cols[base : base + frames, 2 * chan : 3 * chan] = jnp.where(
             row == frames - 1, 0.0, pltpu.roll(x, frames - 1, 0)
         ).astype(BF16)
-    for copy in copies[1]:
-        copy.wait()
-
-    def step(i, _):
-        rows = pl.ds(pl.multiple_of(i * block, block), block)
-        pre = dot(cols[rows, :], w_conv[...], NN)
-        sigma = 0.5 * jnp.tanh(0.5 * pre) + 0.5
-        hidden = (pre * sigma).astype(BF16)
-        hid[rows, :] = hidden
-        slope[rows, :] = sigma * (1.0 + pre * (1.0 - sigma))
-        emb = dot(hidden, w_proj[...], NN).astype(BF16)
-        values = emb.astype(F32)
-        inv = lax.rsqrt(jnp.sum(values * values, axis=1, keepdims=True) + epsilon)
-        put(i, emb, jnp.broadcast_to(inv, (block, LANES)))
-        return 0
-
-    lax.fori_loop(0, clips * frames // block, step, 0, unroll=True)
+
+
+def forward(i, w_conv, w_proj, cols, slope, hid, block, put):
+    rows = pl.ds(i * block, block)
+    pre = dot(cols[rows, :], w_conv[...], NN)
+    yield
+    sigma = 0.5 * jnp.tanh(0.5 * pre) + 0.5
+    hidden = (pre * sigma).astype(BF16)
+    hid[rows, :] = hidden
+    slope[rows, :] = sigma * (1.0 + pre * (1.0 - sigma))
+    yield
+    emb = dot(hidden, w_proj[...], NN).astype(BF16)
+    yield
+    values = emb.astype(F32)
+    inv = lax.rsqrt(jnp.sum(values * values, axis=1, keepdims=True) + epsilon)
+    put(i, emb, jnp.broadcast_to(inv, (block, LANES)))
+    yield
+
+
+def staggered(works):
+    running = []
+    while works or running:
+        running += works[:1]
+        works = works[1:]
+        running = [work for work in running if next(work, running) is not running]
 
 
 def backward(w_proj, cols, slope, hid, gemb, gpre, keep, send, block):
@@ -153,26 +161,35 @@
 
     def put_a(i, emb, inv):
         c = i // per_clip
-        at = pl.multiple_of(PAD + lax.rem(i, per_clip) * block, PAD)
+        at = PAD + i % per_clip * block
         emb_a[c, pl.ds(at, block), :] = emb
         inv_a[c, pl.ds(at, block), :] = inv
 
     def put_v(i, emb, inv):
-        at = pl.multiple_of(i * block, block)
+        at = i * block
         emb_v[pl.ds(at, block), :] = emb
         inv_v[pl.ds(at, block), :] = inv
 
-    forward(feats, 1, (feats_v, weights_v), wvc, wvp, cols_v, slope_v, hid_v, clips, frames, block, put_v)
-    forward(feats, 0, (feats_a, weights_a), wac, wap, cols_a, slope_a, hid_a, clips, frames, block, put_a)
+    columns(feats, 1, feats_v, cols_v, clips, frames)
+    for copy in weights_v:
+        copy.wait()
+    columns(feats, 0, feats_a, cols_a, clips, frames)
+    for copy in weights_a:
+        copy.wait()
+    count = rows_total // block
+    works_v = [forward(i, wvc, wvp, cols_v, slope_v, hid_v, block, put_v) for i in range(count)]
+    works_a = [forward(i, wac, wap, cols_a, slope_a, hid_a, block, put_a) for i in range(count)]
+    staggered(works_v + works_a)
 
     tiles = frames // TILE
+    gang = next(n for n in (4, 2, 1) if clips * tiles % n == 0)
     row = lax.broadcasted_iota(jnp.int32, (TILE, WIN), 0)
     col = lax.broadcasted_iota(jnp.int32, (TILE, WIN), 1)
     shift = col - row - PAD
     in_band = (shift >= -SPAN) & (shift <= SPAN)
     row_1 = lax.broadcasted_iota(jnp.int32, (TILE, 1), 0)
 
-    def tile_step(i, loss):
+    def tile_work(i):
         c = i // tiles
         first = pl.multiple_of(lax.rem(i, tiles) * TILE, TILE)
         length = lengths[first_clip + c]
@@ -181,41 +198,59 @@
         window = pl.ds(first, WIN)
         ev = emb_v[here, :]
         wa = emb_a[c, window, :]
+        dots = dot(ev, wa, NT)
+        yield
         iv = inv_v[here, 0:1]
-        ia = inv_a[c, window, :].T
-        dots = dot(ev, wa, NT)
-        scores = logit_sharpening_divisor * dots * iv * ia
+        both = iv * inv_a[c, window, :].T
+        scores = (logit_sharpening_divisor * dots) * both
+        yield
         t = start + first + row_1
-        u = start + first - PAD + col
+        u = start + first - PAD + col[0:1]
         inside = t < length
-        valid = in_band & inside & (u >= 0) & (u < length)
         target = t + label
         counted = inside & (target >= 0) & (target < length)
         hit = shift == label
-        weights = jnp.where(valid, jnp.exp(scores), 0.0)
-        sums = jnp.where(inside, jnp.sum(weights, axis=1, keepdims=True), 1.0)
+        weights = jnp.where(in_band & ((u >= 0) & (u < length)), jnp.exp(scores), 0.0)
+        yield
+        sums = jnp.where(counted, jnp.sum(weights, axis=1, keepdims=True), 1.0)
         picked = jnp.sum(jnp.where(hit, scores, 0.0), axis=1, keepdims=True)
+        yield
         own = (first + row_1 >= halo) & (first + row_1 < frames - halo)
-        loss = loss + jnp.sum(jnp.where(counted & own, jnp.log(sums) - picked, 0.0))
+        loss = jnp.where(counted & own, jnp.log(sums) - picked, 0.0)
         scale = jnp.where(counted, logit_sharpening_divisor * loss_scale, 0.0)
-        grad = scale * (weights / sums - jnp.where(hit, 1.0, 0.0))
-        gd = (grad * iv * ia).astype(BF16)
+        grad = (weights * (scale / sums) - jnp.where(hit, scale, 0.0)) * both
+        gd = grad.astype(BF16)
+        yield
         by_dots = grad * dots
-        giv = jnp.sum(by_dots * ia, axis=1, keepdims=True)
-        gia = jnp.sum((by_dots * iv).T, axis=1, keepdims=True)
-        glip = dot(gd, wa, NN) - (iv * iv * iv * giv) * ev.astype(F32)
-        gemb_v[here, :] = jnp.where(own, glip, 0.0).astype(BF16)
-        gacc[c, window, :] += dot(gd, ev, TN)
+        lip = dot(gd, wa, NN)
+        yield
+        audio = dot(gd, ev, TN)
+        yield
+        giv = jnp.sum(by_dots, axis=1, keepdims=True)
+        gia = jnp.sum(by_dots.T, axis=1, keepdims=True)
+        yield
+        lip = lip - (iv * iv * giv) * ev.astype(F32)
+        gemb_v[here, :] = jnp.where(own, lip, 0.0).astype(BF16)
+        yield
+        gacc[c, window, :] += audio
         giacc[c, window, :] += jnp.broadcast_to(gia, (WIN, LANES))
-        return loss
-
-    loss = lax.fori_loop(0, clips * tiles, tile_step, jnp.zeros((), F32), unroll=clips * tiles <= 8)
+        yield loss
+
+    def tile_step(i, loss):
+        together = [tile_work(i + k * (clips * tiles // gang)) for k in range(gang)]
+        last = [None]
+        while last[0] is None:
+            last = [next(work) for work in together]
+        return loss + sum(last)
+
+    loss = lax.fori_loop(0, clips * tiles // gang, tile_step, jnp.zeros((TILE, 1), F32), unroll=clips * tiles <= 8)
+    loss = jnp.sum(loss)
 
     def audio_step(i, _):
         c = i // per_clip
         at = pl.ds(pl.multiple_of(PAD + lax.rem(i, per_clip) * block, PAD), block)
         inv = inv_a[c, at, 0:1]
-        grad = gacc[c, at, :] - (inv * inv * inv * giacc[c, at, 0:1]) * emb_a[c, at, :].astype(F32)
+        grad = gacc[c, at, :] - (inv * inv * giacc[c, at, 0:1]) * emb_a[c, at, :].astype(F32)
         if halo:
             at_row = lax.rem(i, per_clip) * block + lax.broadcasted_iota(jnp.int32, (block, 1), 0)
             grad = jnp.where((at_row >= halo) & (at_row < frames - halo), grad, 0.0)

time: 65.5 us -> 63.9 us (0.976)
  Pallas kernels: 20.3 us -> 18.6 us
    pallas_call x1, Pallas kernels: 13.6 us -> 11.9 us  [local_grads(): pl.pallas_call(functools.partial(kernel, frames, clips, halo), out_shape=...]
where the time goes in v8:
time: 63.9 us; the launch traced here: 63.7 us
  starting transfers between devices  29 us (45%)
  Pallas kernels  18.6 us (29%)
  waiting for transfers between devices  13.8 us (22%)
  local copies, waits for them, and re-layouts  1.23 us (2%)
  between operations  1 us (2%)
    ppermute x16, starting transfers between devices, swap_by_core(): return lax.ppermute(value, ('clip', 'tm'), pairs)  27.7 us
    ppermute x16, waiting for transfers between devices, swap_by_core(): return lax.ppermute(value, ('clip', 'tm'), pairs)  12.2 us
    pallas_call x1, Pallas kernels, local_grads(): pl.pallas_call(functools.partial(kernel, frames, clips, halo), out_shape=...  11.9 us
    pallas_call x2, Pallas kernels, finish_some(): pl.pallas_call(functools.partial(finish_kernel, parts, len(known), with_l...  3.69 us
    pallas_call x1, Pallas kernels, local_grads(): pl.pallas_call(functools.partial(audio_kernel, block_of(frames)), out_sha...  2.11 us
    ppermute x5, waiting for transfers between devices, swap(): lax.ppermute(value, axis, [(i, i ^ bit) for i in range(lax.axis_size(axis...  1.55 us
    ppermute x5, starting transfers between devices, swap(): lax.ppermute(value, axis, [(i, i ^ bit) for i in range(lax.axis_size(axis...  1.32 us
  transfers between devices with their start and end apart: 21, of which 12 were waited for; matrix products, arithmetic and copies ran while one was open for 0% of the time, Pallas kernels for 8%

profile of v8, /device:TPU:0, one launch (start us, length us, event | category | flops | bytes accessed | tf_op | source)
XLA Modules:
  0.0 63.7 jit_solution(14394496660762972371)
XLA Ops:
  0.7 1.2 %dynamic-slice_bitcast_fusion = (bf16[1,2,256,256]{3,2,1,0:T(8,128)(2,1)S(1)}, bf16[1,2,256,256]{3,2,1,0:T(8,128)(2,1)S(1)}) fusion(bf16[4,256,256]{2,1,0:T(8,128)(2,1)} %own_v.1, s32[]{:T(128)S(6)} %select_n.4, bf16[4,256,256]{2,1,0:T(8,128)(2,1)} %own_a.1), kind=kLoop, calls=%fused_computation.1 | loop fusion | bytes 1048580 | tf_op jit(solution)/shard_map/stack | solution.py:603
  2.5 1.5 %collective-permute-done.got = bf16[2,2,256,256]{3,2,1,0:T(8,128)(2,1)S(1)} collective-permute-done((bf16[2,2,256,256]{3,2,1,0:T(8,128)(2,1)S(1)}, bf16[2,2,256,256]{3,2,1,0:T(8,128)(2,1)S(1)}, u32[]{:S(2)}, u32[]{:S(2)}) %collective-permute-start) | collective-permute-done | bytes 524320 | tf_op jit(solution)/shard_map/ppermute | solution.py:343
  4.1 11.9 %shard_map.119 = (f32[2592,128]{1,0:T(8,128)S(1)}, bf16[2592,128]{1,0:T(8,128)(2,1)S(1)}, bf16[1024,768]{1,0:T(8,128)(2,1)S(1)}, f32[1024,512]{1,0:T(8,128)S(1)}...) custom-call(s32[4]{0:T(128)S(1)} %copy-done.4, s32[4]{0:T(128)S(1)} %copy-done.5, ...), custom_call_target="tpu_custom_call" | custom-call | tf_op jit(solution)/shard_map/pallas_call | solution.py:307
  16.4 2.1 %shard_map.125 = (f32[2592,128]{1,0:T(8,128)S(1)}, bf16[2592,128]{1,0:T(8,128)(2,1)S(1)}) custom-call(bf16[512,512]{1,0:T(8,128)(2,1)S(1)} %copy-done.3, bf16[1024,768]{1,0:T(8,128)(2,1)S(1)} %get-tuple-element.39.cols, f32[1024,512]{1,0:T(8,128)S(1)} %get-tuple-element.40.slope, bf16[1024,512]{1,0:T(8,128)(2,1)S(1)} %get-tuple-element.41.hid, ...), custom_call_target="tpu_custom_call" | custom-call | flops 1879048192 | bytes 6291456 | tf_op jit(solution)/shard_map/pallas_call | solution.py:330
  18.9 2.9 %collective-permute-start.2 = (bf16[672,128]{1,0:T(8,128)(2,1)S(1)}, bf16[672,128]{1,0:T(8,128)(2,1)S(1)}, u32[]{:S(2)}, u32[]{:S(2)}) collective-permute-start(bf16[672,128]{1,0:T(8,128)(2,1)S(1)} %get-tuple-element.35), channel_id=1, source_target_pairs={{0,2},{1,3},{2,0},{3,1},{4,6},{5,7},{6,4},{7,5},{8,10},{9,11},{10,... | collective-permute-start | bytes 516104 | tf_op jit(solution)/shard_map/ppermute | solution.py:352
  21.8 1.5 %collective-permute-start.3 = (bf16[672,128]{1,0:T(8,128)(2,1)S(1)}, bf16[672,128]{1,0:T(8,128)(2,1)S(1)}, u32[]{:S(2)}, u32[]{:S(2)}) collective-permute-start(bf16[672,128]{1,0:T(8,128)(2,1)S(1)} %get-tuple-element.36), channel_id=1, source_target_pairs={{0,4},{1,5},{2,6},{3,7},{4,0},{5,1},{6,2},{7,3},{8,12},{9,13},{10,... | collective-permute-start | bytes 516104 | tf_op jit(solution)/shard_map/ppermute | solution.py:352
  23.5 2.0 %collective-permute-start.11 = (bf16[672,128]{1,0:T(8,128)(2,1)S(1)}, bf16[672,128]{1,0:T(8,128)(2,1)S(1)}, u32[]{:S(2)}, u32[]{:S(2)}) collective-permute-start(bf16[672,128]{1,0:T(8,128)(2,1)S(1)} %get-tuple-element.46), channel_id=1, source_target_pairs={{0,2},{1,9},{2,0},{3,11},{4,6},{5,13},{6,4},{7,15},{8,10},{9,1},{1... | collective-permute-start | bytes 516104 | tf_op jit(solution)/shard_map/ppermute | solution.py:352
  25.5 1.5 %collective-permute-start.12 = (bf16[672,128]{1,0:T(8,128)(2,1)S(1)}, bf16[672,128]{1,0:T(8,128)(2,1)S(1)}, u32[]{:S(2)}, u32[]{:S(2)}) collective-permute-start(bf16[672,128]{1,0:T(8,128)(2,1)S(1)} %get-tuple-element.47), channel_id=1, source_target_pairs={{0,4},{1,17},{2,6},{3,19},{4,0},{5,21},{6,2},{7,23},{8,12},{9,25},... | collective-permute-start | bytes 516104 | tf_op jit(solution)/shard_map/ppermute | solution.py:352
  27.0 3.0 %collective-permute-start.13 = (bf16[672,128]{1,0:T(8,128)(2,1)S(1)}, bf16[672,128]{1,0:T(8,128)(2,1)S(1)}, u32[]{:S(2)}, u32[]{:S(2)}) collective-permute-start(bf16[672,128]{1,0:T(8,128)(2,1)S(1)} %get-tuple-element.48), channel_id=1, source_target_pairs={{0,6},{1,25},{2,4},{3,27},{4,2},{5,29},{6,0},{7,31},{8,14},{9,17},... | collective-permute-start | bytes 516104 | tf_op jit(solution)/shard_map/ppermute | solution.py:352
  30.0 1.6 %collective-permute-done.3.refs_1_ = bf16[672,128]{1,0:T(8,128)(2,1)S(1)} collective-permute-done((bf16[672,128]{1,0:T(8,128)(2,1)S(1)}, bf16[672,128]{1,0:T(8,128)(2,1)S(1)}, u32[]{:S(2)}, u32[]{:S(2)}) %collective-permute-start.3) | collective-permute-done | bytes 172064 | tf_op jit(solution)/shard_map/ppermute | solution.py:352
  31.7 1.6 %collective-permute-start.5 = (bf16[672,128]{1,0:T(8,128)(2,1)S(1)}, bf16[672,128]{1,0:T(8,128)(2,1)S(1)}, u32[]{:S(2)}, u32[]{:S(2)}) collective-permute-start(bf16[672,128]{1,0:T(8,128)(2,1)S(1)} %shard_map.121.one), channel_id=1, source_target_pairs={{0,8},{1,17},{2,10},{3,19},{4,12},{5,21},{6,14},{7,23},{8,0},{9,25... | collective-permute-start | bytes 516104 | tf_op jit(solution)/shard_map/ppermute | solution.py:352
  33.4 1.9 %collective-permute-done.12.refs_1_ = bf16[672,128]{1,0:T(8,128)(2,1)S(1)} collective-permute-done((bf16[672,128]{1,0:T(8,128)(2,1)S(1)}, bf16[672,128]{1,0:T(8,128)(2,1)S(1)}, u32[]{:S(2)}, u32[]{:S(2)}) %collective-permute-start.12) | collective-permute-done | bytes 172064 | tf_op jit(solution)/shard_map/ppermute | solution.py:352
  35.4 1.6 %collective-permute-start.14 = (bf16[672,128]{1,0:T(8,128)(2,1)S(1)}, bf16[672,128]{1,0:T(8,128)(2,1)S(1)}, u32[]{:S(2)}, u32[]{:S(2)}) collective-permute-start(bf16[672,128]{1,0:T(8,128)(2,1)S(1)} %shard_map.127.one), channel_id=1, source_target_pairs={{0,8},{1,3},{2,10},{3,1},{4,12},{5,7},{6,14},{7,5},{8,0},{9,11},{1... | collective-permute-start | bytes 516104 | tf_op jit(solution)/shard_map/ppermute | solution.py:352
  37.3 3.5 %collective-permute-start.6 = (bf16[672,128]{1,0:T(8,128)(2,1)S(1)}, bf16[672,128]{1,0:T(8,128)(2,1)S(1)}, u32[]{:S(2)}, u32[]{:S(2)}) collective-permute-start(bf16[672,128]{1,0:T(8,128)(2,1)S(1)} %shard_map.122.one), channel_id=1, source_target_pairs={{0,16},{1,9},{2,18},{3,11},{4,20},{5,13},{6,22},{7,15},{8,24},{9,1... | collective-permute-start | bytes 516104 | tf_op jit(solution)/shard_map/ppermute | solution.py:352
  41.0 2.8 %collective-permute-start.15 = (bf16[672,128]{1,0:T(8,128)(2,1)S(1)}, bf16[672,128]{1,0:T(8,128)(2,1)S(1)}, u32[]{:S(2)}, u32[]{:S(2)}) collective-permute-start(bf16[672,128]{1,0:T(8,128)(2,1)S(1)} %shard_map.128.one), channel_id=1, source_target_pairs={{0,16},{1,5},{2,18},{3,7},{4,20},{5,1},{6,22},{7,3},{8,24},{9,13},... | collective-permute-start | bytes 516104 | tf_op jit(solution)/shard_map/ppermute | solution.py:352
  44.4 1.5 %collective-permute-start.9 = (bf16[640,128]{1,0:T(8,128)(2,1)S(1)}, bf16[640,128]{1,0:T(8,128)(2,1)S(1)}, u32[]{:S(2)}, u32[]{:S(2)}) collective-permute-start(bf16[640,128]{1,0:T(8,128)(2,1)S(1)} %get-tuple-element.38.refs_0_), channel_id=1, source_target_pairs={{0,6},{1,7},{2,4},{3,5},{4,2},{5,3},{6,0},{7,1},{8,14},{9,15},{10,... | collective-permute-start | bytes 491528 | tf_op jit(solution)/shard_map/ppermute | solution.py:352
  45.8 1.4 %collective-permute-start.8 = (bf16[640,128]{1,0:T(8,128)(2,1)S(1)}, bf16[640,128]{1,0:T(8,128)(2,1)S(1)}, u32[]{:S(2)}, u32[]{:S(2)}) collective-permute-start(bf16[640,128]{1,0:T(8,128)(2,1)S(1)} %get-tuple-element.38.refs_0_), channel_id=1, source_target_pairs={{0,4},{1,5},{2,6},{3,7},{4,0},{5,1},{6,2},{7,3},{8,12},{9,13},{10,... | collective-permute-start | bytes 491528 | tf_op jit(solution)/shard_map/ppermute | solution.py:352
  47.9 2.3 %collective-permute-done.15.other = bf16[672,128]{1,0:T(8,128)(2,1)S(1)} collective-permute-done((bf16[672,128]{1,0:T(8,128)(2,1)S(1)}, bf16[672,128]{1,0:T(8,128)(2,1)S(1)}, u32[]{:S(2)}, u32[]{:S(2)}) %collective-permute-start.15) | collective-permute-done | bytes 172064 | tf_op jit(solution)/shard_map/ppermute | solution.py:352
  50.3 2.1 %collective-permute-start.18 = (bf16[640,128]{1,0:T(8,128)(2,1)S(1)}, bf16[640,128]{1,0:T(8,128)(2,1)S(1)}, u32[]{:S(2)}, u32[]{:S(2)}) collective-permute-start(bf16[640,128]{1,0:T(8,128)(2,1)S(1)} %shard_map.129.refs_0_), channel_id=1, source_target_pairs={{0,6},{1,25},{2,4},{3,27},{4,2},{5,29},{6,0},{7,31},{8,14},{9,17},... | collective-permute-start | bytes 491528 | tf_op jit(solution)/shard_map/ppermute | solution.py:352
  53.9 1.9 %collective-permute-done.8.refs_2_ = bf16[640,128]{1,0:T(8,128)(2,1)S(1)} collective-permute-done((bf16[640,128]{1,0:T(8,128)(2,1)S(1)}, bf16[640,128]{1,0:T(8,128)(2,1)S(1)}, u32[]{:S(2)}, u32[]{:S(2)}) %collective-permute-start.8) | collective-permute-done | bytes 163872 | tf_op jit(solution)/shard_map/ppermute | solution.py:352
  56.1 1.7 %collective-permute-done.18.refs_3_ = bf16[640,128]{1,0:T(8,128)(2,1)S(1)} collective-permute-done((bf16[640,128]{1,0:T(8,128)(2,1)S(1)}, bf16[640,128]{1,0:T(8,128)(2,1)S(1)}, u32[]{:S(2)}, u32[]{:S(2)}) %collective-permute-start.18) | collective-permute-done | bytes 163872 | tf_op jit(solution)/shard_map/ppermute | solution.py:352
  57.7 1.7 %collective-permute-done.17.refs_2_ = bf16[640,128]{1,0:T(8,128)(2,1)S(1)} collective-permute-done((bf16[640,128]{1,0:T(8,128)(2,1)S(1)}, bf16[640,128]{1,0:T(8,128)(2,1)S(1)}, u32[]{:S(2)}, u32[]{:S(2)}) %collective-permute-start.17) | collective-permute-done | bytes 163872 | tf_op jit(solution)/shard_map/ppermute | solution.py:352
  59.8 2.1 %shard_map.132 = (f32[1,1]{1,0:T(1,128)}, f32[768,512]{1,0:T(8,128)}, f32[512,512]{1,0:T(8,128)}, f32[768,512]{1,0:T(8,128)}, f32[512,512]{1,0:T(8,128)}) custom-call(bf16[2560,128]{1,0:T(8,128)(2,1)S(1)} %shard_map.124.refs_0_, bf16[2560,128]{1,0:T(8,128)(2,1)S(1)} %shard_map.130.refs_1_, f32[16,128]{1,0:T(8,128)S(1)} %shard_map.131.refs_2_), custom_call_target="tpu_custom_call" | custom-call | flops 655360 | bytes 3932160 | tf_op jit(solution)/shard_map/pallas_call | solution.py:565
  61.9 1.6 %shard_map.133 = (f32[768,512]{1,0:T(8,128)}, f32[512,512]{1,0:T(8,128)}, f32[768,512]{1,0:T(8,128)}, f32[512,512]{1,0:T(8,128)}) custom-call(bf16[2560,128]{1,0:T(8,128)(2,1)S(1)} %collective-permute-done.19.refs_0_, bf16[2560,128]{1,0:T(8,128)(2,1)S(1)} %collective-permute-done.20.refs_1_, ...), custom_call_target="tpu_custom_call", output_to_operand_aliasing={{0}: (3, {}), {1}: (4, {}), {2}: (5, {}), {3}: (6, {})} | custom-call | flops 655360 | bytes 3932160 | tf_op jit(solution)/shard_map/pallas_call | solution.py:565
  (47 shorter events, 5.5 us)
Async XLA Ops:
  0.6 3.4 %copy-start.1 = (bf16[4,256,256]{2,1,0:T(8,128)(2,1)S(1)}, bf16[4,256,256]{2,1,0:T(8,128)(2,1)}, u32[]{:S(2)}) copy-start(bf16[4,256,256]{2,1,0:T(8,128)(2,1)} %own_v.1) | copy-start | bytes 1572868
  0.6 3.4 %copy-start = (bf16[4,256,256]{2,1,0:T(8,128)(2,1)S(1)}, bf16[4,256,256]{2,1,0:T(8,128)(2,1)}, u32[]{:S(2)}) copy-start(bf16[4,256,256]{2,1,0:T(8,128)(2,1)} %own_a.1) | copy-start | bytes 1572868
  0.7 3.4 %copy-start.3 = (bf16[512,512]{1,0:T(8,128)(2,1)S(1)}, bf16[512,512]{1,0:T(8,128)(2,1)}, u32[]{:S(2)}) copy-start(bf16[512,512]{1,0:T(8,128)(2,1)} %w_proj.1) | copy-start | bytes 1572868
  2.0 2.1 %collective-permute-start = (bf16[2,2,256,256]{3,2,1,0:T(8,128)(2,1)S(1)}, bf16[2,2,256,256]{3,2,1,0:T(8,128)(2,1)S(1)}, u32[]{:S(2)}, u32[]{:S(2)}) collective-permute-start(bf16[2,2,256,256]{3,2,1,0:T(8,128)(2,1)S(1)} %pad_maximum_fusion), channel_id=1, source_target_pairs={{0,1},{1,0},{2,3},{3,2},{4,5},{5,4},{6,7},{7,6},{8,9},{9,8},{10,11... | collective-permute-start | bytes 1572872 | tf_op jit(solution)/shard_map/ppermute | solution.py:343
  16.0 2.8 %collective-permute-start.1 = (bf16[2592,128]{1,0:T(8,128)(2,1)S(1)}, bf16[2592,128]{1,0:T(8,128)(2,1)S(1)}, u32[]{:S(2)}, u32[]{:S(2)}) collective-permute-start(bf16[2592,128]{1,0:T(8,128)(2,1)S(1)} %get-tuple-element.33), channel_id=1, source_target_pairs={{0,1},{1,0},{2,3},{3,2},{4,5},{5,4},{6,7},{7,6},{8,9},{9,8},{10,11... | collective-permute-start | bytes 1990664 | tf_op jit(solution)/shard_map/ppermute | solution.py:343
  18.6 4.8 %collective-permute-start.10 = (bf16[2592,128]{1,0:T(8,128)(2,1)S(1)}, bf16[2592,128]{1,0:T(8,128)(2,1)S(1)}, u32[]{:S(2)}, u32[]{:S(2)}) collective-permute-start(bf16[2592,128]{1,0:T(8,128)(2,1)S(1)} %get-tuple-element.44), channel_id=1, source_target_pairs={{0,1},{1,0},{2,3},{3,2},{4,5},{5,4},{6,7},{7,6},{8,9},{9,8},{10,11... | collective-permute-start | bytes 1990664 | tf_op jit(solution)/shard_map/ppermute | solution.py:343
  18.9 8.1 %collective-permute-start.2 = (bf16[672,128]{1,0:T(8,128)(2,1)S(1)}, bf16[672,128]{1,0:T(8,128)(2,1)S(1)}, u32[]{:S(2)}, u32[]{:S(2)}) collective-permute-start(bf16[672,128]{1,0:T(8,128)(2,1)S(1)} %get-tuple-element.35), channel_id=1, source_target_pairs={{0,2},{1,3},{2,0},{3,1},{4,6},{5,7},{6,4},{7,5},{8,10},{9,11},{10,... | collective-permute-start | bytes 516104 | tf_op jit(solution)/shard_map/ppermute | solution.py:352
  21.8 9.8 %collective-permute-start.3 = (bf16[672,128]{1,0:T(8,128)(2,1)S(1)}, bf16[672,128]{1,0:T(8,128)(2,1)S(1)}, u32[]{:S(2)}, u32[]{:S(2)}) collective-permute-start(bf16[672,128]{1,0:T(8,128)(2,1)S(1)} %get-tuple-element.36), channel_id=1, source_target_pairs={{0,4},{1,5},{2,6},{3,7},{4,0},{5,1},{6,2},{7,3},{8,12},{9,13},{10,... | collective-permute-start | bytes 516104 | tf_op jit(solution)/shard_map/ppermute | solution.py:352
  23.3 8.3 %collective-permute-start.4 = (bf16[672,128]{1,0:T(8,128)(2,1)S(1)}, bf16[672,128]{1,0:T(8,128)(2,1)S(1)}, u32[]{:S(2)}, u32[]{:S(2)}) collective-permute-start(bf16[672,128]{1,0:T(8,128)(2,1)S(1)} %get-tuple-element.37), channel_id=1, source_target_pairs={{0,6},{1,7},{2,4},{3,5},{4,2},{5,3},{6,0},{7,1},{8,14},{9,15},{10,... | collective-permute-start | bytes 516104 | tf_op jit(solution)/shard_map/ppermute | solution.py:352
  23.5 9.9 %collective-permute-start.11 = (bf16[672,128]{1,0:T(8,128)(2,1)S(1)}, bf16[672,128]{1,0:T(8,128)(2,1)S(1)}, u32[]{:S(2)}, u32[]{:S(2)}) collective-permute-start(bf16[672,128]{1,0:T(8,128)(2,1)S(1)} %get-tuple-element.46), channel_id=1, source_target_pairs={{0,2},{1,9},{2,0},{3,11},{4,6},{5,13},{6,4},{7,15},{8,10},{9,1},{1... | collective-permute-start | bytes 516104 | tf_op jit(solution)/shard_map/ppermute | solution.py:352
  25.5 9.8 %collective-permute-start.12 = (bf16[672,128]{1,0:T(8,128)(2,1)S(1)}, bf16[672,128]{1,0:T(8,128)(2,1)S(1)}, u32[]{:S(2)}, u32[]{:S(2)}) collective-permute-start(bf16[672,128]{1,0:T(8,128)(2,1)S(1)} %get-tuple-element.47), channel_id=1, source_target_pairs={{0,4},{1,17},{2,6},{3,19},{4,0},{5,21},{6,2},{7,23},{8,12},{9,25},... | collective-permute-start | bytes 516104 | tf_op jit(solution)/shard_map/ppermute | solution.py:352
  27.0 8.3 %collective-permute-start.13 = (bf16[672,128]{1,0:T(8,128)(2,1)S(1)}, bf16[672,128]{1,0:T(8,128)(2,1)S(1)}, u32[]{:S(2)}, u32[]{:S(2)}) collective-permute-start(bf16[672,128]{1,0:T(8,128)(2,1)S(1)} %get-tuple-element.48), channel_id=1, source_target_pairs={{0,6},{1,25},{2,4},{3,27},{4,2},{5,29},{6,0},{7,31},{8,14},{9,17},... | collective-permute-start | bytes 516104 | tf_op jit(solution)/shard_map/ppermute | solution.py:352
  31.7 5.5 %collective-permute-start.5 = (bf16[672,128]{1,0:T(8,128)(2,1)S(1)}, bf16[672,128]{1,0:T(8,128)(2,1)S(1)}, u32[]{:S(2)}, u32[]{:S(2)}) collective-permute-start(bf16[672,128]{1,0:T(8,128)(2,1)S(1)} %shard_map.121.one), channel_id=1, source_target_pairs={{0,8},{1,17},{2,10},{3,19},{4,12},{5,21},{6,14},{7,23},{8,0},{9,25... | collective-permute-start | bytes 516104 | tf_op jit(solution)/shard_map/ppermute | solution.py:352
  35.4 5.6 %collective-permute-start.14 = (bf16[672,128]{1,0:T(8,128)(2,1)S(1)}, bf16[672,128]{1,0:T(8,128)(2,1)S(1)}, u32[]{:S(2)}, u32[]{:S(2)}) collective-permute-start(bf16[672,128]{1,0:T(8,128)(2,1)S(1)} %shard_map.127.one), channel_id=1, source_target_pairs={{0,8},{1,3},{2,10},{3,1},{4,12},{5,7},{6,14},{7,5},{8,0},{9,11},{1... | collective-permute-start | bytes 516104 | tf_op jit(solution)/shard_map/ppermute | solution.py:352
  37.3 7.0 %collective-permute-start.6 = (bf16[672,128]{1,0:T(8,128)(2,1)S(1)}, bf16[672,128]{1,0:T(8,128)(2,1)S(1)}, u32[]{:S(2)}, u32[]{:S(2)}) collective-permute-start(bf16[672,128]{1,0:T(8,128)(2,1)S(1)} %shard_map.122.one), channel_id=1, source_target_pairs={{0,16},{1,9},{2,18},{3,11},{4,20},{5,13},{6,22},{7,15},{8,24},{9,1... | collective-permute-start | bytes 516104 | tf_op jit(solution)/shard_map/ppermute | solution.py:352
  41.0 9.2 %collective-permute-start.15 = (bf16[672,128]{1,0:T(8,128)(2,1)S(1)}, bf16[672,128]{1,0:T(8,128)(2,1)S(1)}, u32[]{:S(2)}, u32[]{:S(2)}) collective-permute-start(bf16[672,128]{1,0:T(8,128)(2,1)S(1)} %shard_map.128.one), channel_id=1, source_target_pairs={{0,16},{1,5},{2,18},{3,7},{4,20},{5,1},{6,22},{7,3},{8,24},{9,13},... | collective-permute-start | bytes 516104 | tf_op jit(solution)/shard_map/ppermute | solution.py:352
  44.4 8.8 %collective-permute-start.9 = (bf16[640,128]{1,0:T(8,128)(2,1)S(1)}, bf16[640,128]{1,0:T(8,128)(2,1)S(1)}, u32[]{:S(2)}, u32[]{:S(2)}) collective-permute-start(bf16[640,128]{1,0:T(8,128)(2,1)S(1)} %get-tuple-element.38.refs_0_), channel_id=1, source_target_pairs={{0,6},{1,7},{2,4},{3,5},{4,2},{5,3},{6,0},{7,1},{8,14},{9,15},{10,... | collective-permute-start | bytes 491528 | tf_op jit(solution)/shard_map/ppermute | solution.py:352
  45.8 10.0 %collective-permute-start.8 = (bf16[640,128]{1,0:T(8,128)(2,1)S(1)}, bf16[640,128]{1,0:T(8,128)(2,1)S(1)}, u32[]{:S(2)}, u32[]{:S(2)}) collective-permute-start(bf16[640,128]{1,0:T(8,128)(2,1)S(1)} %get-tuple-element.38.refs_0_), channel_id=1, source_target_pairs={{0,4},{1,5},{2,6},{3,7},{4,0},{5,1},{6,2},{7,3},{8,12},{9,13},{10,... | collective-permute-start | bytes 491528 | tf_op jit(solution)/shard_map/ppermute | solution.py:352
  47.2 8.7 %collective-permute-start.7 = (bf16[640,128]{1,0:T(8,128)(2,1)S(1)}, bf16[640,128]{1,0:T(8,128)(2,1)S(1)}, u32[]{:S(2)}, u32[]{:S(2)}) collective-permute-start(bf16[640,128]{1,0:T(8,128)(2,1)S(1)} %get-tuple-element.38.refs_0_), channel_id=1, source_target_pairs={{0,2},{1,3},{2,0},{3,1},{4,6},{5,7},{6,4},{7,5},{8,10},{9,11},{10,... | collective-permute-start | bytes 491528 | tf_op jit(solution)/shard_map/ppermute | solution.py:352
  50.3 7.4 %collective-permute-start.18 = (bf16[640,128]{1,0:T(8,128)(2,1)S(1)}, bf16[640,128]{1,0:T(8,128)(2,1)S(1)}, u32[]{:S(2)}, u32[]{:S(2)}) collective-permute-start(bf16[640,128]{1,0:T(8,128)(2,1)S(1)} %shard_map.129.refs_0_), channel_id=1, source_target_pairs={{0,6},{1,25},{2,4},{3,27},{4,2},{5,29},{6,0},{7,31},{8,14},{9,17},... | collective-permute-start | bytes 491528 | tf_op jit(solution)/shard_map/ppermute | solution.py:352
  52.4 7.0 %collective-permute-start.17 = (bf16[640,128]{1,0:T(8,128)(2,1)S(1)}, bf16[640,128]{1,0:T(8,128)(2,1)S(1)}, u32[]{:S(2)}, u32[]{:S(2)}) collective-permute-start(bf16[640,128]{1,0:T(8,128)(2,1)S(1)} %shard_map.129.refs_0_), channel_id=1, source_target_pairs={{0,4},{1,17},{2,6},{3,19},{4,0},{5,21},{6,2},{7,23},{8,12},{9,25},... | collective-permute-start | bytes 491528 | tf_op jit(solution)/shard_map/ppermute | solution.py:352
  53.1 6.3 %collective-permute-start.16 = (bf16[640,128]{1,0:T(8,128)(2,1)S(1)}, bf16[640,128]{1,0:T(8,128)(2,1)S(1)}, u32[]{:S(2)}, u32[]{:S(2)}) collective-permute-start(bf16[640,128]{1,0:T(8,128)(2,1)S(1)} %shard_map.129.refs_0_), channel_id=1, source_target_pairs={{0,2},{1,9},{2,0},{3,11},{4,6},{5,13},{6,4},{7,15},{8,10},{9,1},{1... | collective-permute-start | bytes 491528 | tf_op jit(solution)/shard_map/ppermute | solution.py:352
  56.0 5.9 %collective-permute-start.19 = (bf16[2560,128]{1,0:T(8,128)(2,1)S(1)}, bf16[2560,128]{1,0:T(8,128)(2,1)S(1)}, u32[]{:S(2)}, u32[]{:S(2)}) collective-permute-start(bf16[2560,128]{1,0:T(8,128)(2,1)S(1)} %shard_map.124.refs_0_), channel_id=1, source_target_pairs={{0,1},{1,0},{2,3},{3,2},{4,5},{5,4},{6,7},{7,6},{8,9},{9,8},{10,11... | collective-permute-start | bytes 1966088 | tf_op jit(solution)/shard_map/ppermute | solution.py:343
  59.5 2.4 %collective-permute-start.20 = (bf16[2560,128]{1,0:T(8,128)(2,1)S(1)}, bf16[2560,128]{1,0:T(8,128)(2,1)S(1)}, u32[]{:S(2)}, u32[]{:S(2)}) collective-permute-start(bf16[2560,128]{1,0:T(8,128)(2,1)S(1)} %shard_map.130.refs_1_), channel_id=1, source_target_pairs={{0,1},{1,0},{2,3},{3,2},{4,5},{5,4},{6,7},{7,6},{8,9},{9,8},{10,11... | collective-permute-start | bytes 1966088 | tf_op jit(solution)/shard_map/ppermute | solution.py:343
  (3 other events, 10.1 us)

commit v9 on v8

--- a/solution.py
+++ b/solution.py
@@ -206,7 +206,7 @@
         yield
         t = start + first + row_1
         u = start + first - PAD + col[0:1]
-        inside = t < length
+        inside = (t >= 0) & (t < length)
         target = t + label
         counted = inside & (target >= 0) & (target < length)
         hit = shift == label

time: 63.9 us -> 63.9 us (level)
  no operation moved by 1% of the time
where the time goes in v9:
time: 63.9 us; the launch traced here: 63.7 us
  starting transfers between devices  29 us (45%)
  Pallas kernels  18.6 us (29%)
  waiting for transfers between devices  13.8 us (22%)
  local copies, waits for them, and re-layouts  1.23 us (2%)
  between operations  1 us (2%)
    ppermute x16, starting transfers between devices, swap_by_core(): return lax.ppermute(value, ('clip', 'tm'), pairs)  27.7 us
    ppermute x16, waiting for transfers between devices, swap_by_core(): return lax.ppermute(value, ('clip', 'tm'), pairs)  12.2 us
    pallas_call x1, Pallas kernels, local_grads(): pl.pallas_call(functools.partial(kernel, frames, clips, halo), out_shape=...  11.9 us
    pallas_call x2, Pallas kernels, finish_some(): pl.pallas_call(functools.partial(finish_kernel, parts, len(known), with_l...  3.69 us
    pallas_call x1, Pallas kernels, local_grads(): pl.pallas_call(functools.partial(audio_kernel, block_of(frames)), out_sha...  2.11 us
    ppermute x5, waiting for transfers between devices, swap(): lax.ppermute(value, axis, [(i, i ^ bit) for i in range(lax.axis_size(axis...  1.55 us
    ppermute x5, starting transfers between devices, swap(): lax.ppermute(value, axis, [(i, i ^ bit) for i in range(lax.axis_size(axis...  1.32 us
  transfers between devices with their start and end apart: 21, of which 12 were waited for; matrix products, arithmetic and copies ran while one was open for 0% of the time, Pallas kernels for 8%

profile of v9, /device:TPU:0, one launch (start us, length us, event | category | flops | bytes accessed | tf_op | source)
XLA Modules:
  0.0 63.7 jit_solution(14394496660762972371)
XLA Ops:
  0.7 1.2 %dynamic-slice_bitcast_fusion = (bf16[1,2,256,256]{3,2,1,0:T(8,128)(2,1)S(1)}, bf16[1,2,256,256]{3,2,1,0:T(8,128)(2,1)S(1)}) fusion(bf16[4,256,256]{2,1,0:T(8,128)(2,1)} %own_v.1, s32[]{:T(128)S(6)} %select_n.4, bf16[4,256,256]{2,1,0:T(8,128)(2,1)} %own_a.1), kind=kLoop, calls=%fused_computation.1 | loop fusion | bytes 1048580 | tf_op jit(solution)/shard_map/stack | solution.py:603
  2.5 1.5 %collective-permute-done.got = bf16[2,2,256,256]{3,2,1,0:T(8,128)(2,1)S(1)} collective-permute-done((bf16[2,2,256,256]{3,2,1,0:T(8,128)(2,1)S(1)}, bf16[2,2,256,256]{3,2,1,0:T(8,128)(2,1)S(1)}, u32[]{:S(2)}, u32[]{:S(2)}) %collective-permute-start) | collective-permute-done | bytes 524320 | tf_op jit(solution)/shard_map/ppermute | solution.py:343
  4.1 11.9 %shard_map.119 = (f32[2592,128]{1,0:T(8,128)S(1)}, bf16[2592,128]{1,0:T(8,128)(2,1)S(1)}, bf16[1024,768]{1,0:T(8,128)(2,1)S(1)}, f32[1024,512]{1,0:T(8,128)S(1)}...) custom-call(s32[4]{0:T(128)S(1)} %copy-done.4, s32[4]{0:T(128)S(1)} %copy-done.5, ...), custom_call_target="tpu_custom_call" | custom-call | tf_op jit(solution)/shard_map/pallas_call | solution.py:307
  16.4 2.1 %shard_map.125 = (f32[2592,128]{1,0:T(8,128)S(1)}, bf16[2592,128]{1,0:T(8,128)(2,1)S(1)}) custom-call(bf16[512,512]{1,0:T(8,128)(2,1)S(1)} %copy-done.3, bf16[1024,768]{1,0:T(8,128)(2,1)S(1)} %get-tuple-element.39.cols, f32[1024,512]{1,0:T(8,128)S(1)} %get-tuple-element.40.slope, bf16[1024,512]{1,0:T(8,128)(2,1)S(1)} %get-tuple-element.41.hid, ...), custom_call_target="tpu_custom_call" | custom-call | flops 1879048192 | bytes 6291456 | tf_op jit(solution)/shard_map/pallas_call | solution.py:330
  18.9 2.9 %collective-permute-start.2 = (bf16[672,128]{1,0:T(8,128)(2,1)S(1)}, bf16[672,128]{1,0:T(8,128)(2,1)S(1)}, u32[]{:S(2)}, u32[]{:S(2)}) collective-permute-start(bf16[672,128]{1,0:T(8,128)(2,1)S(1)} %get-tuple-element.35), channel_id=1, source_target_pairs={{0,2},{1,3},{2,0},{3,1},{4,6},{5,7},{6,4},{7,5},{8,10},{9,11},{10,... | collective-permute-start | bytes 516104 | tf_op jit(solution)/shard_map/ppermute | solution.py:352
  21.8 1.5 %collective-permute-start.3 = (bf16[672,128]{1,0:T(8,128)(2,1)S(1)}, bf16[672,128]{1,0:T(8,128)(2,1)S(1)}, u32[]{:S(2)}, u32[]{:S(2)}) collective-permute-start(bf16[672,128]{1,0:T(8,128)(2,1)S(1)} %get-tuple-element.36), channel_id=1, source_target_pairs={{0,4},{1,5},{2,6},{3,7},{4,0},{5,1},{6,2},{7,3},{8,12},{9,13},{10,... | collective-permute-start | bytes 516104 | tf_op jit(solution)/shard_map/ppermute | solution.py:352
  23.5 2.0 %collective-permute-start.11 = (bf16[672,128]{1,0:T(8,128)(2,1)S(1)}, bf16[672,128]{1,0:T(8,128)(2,1)S(1)}, u32[]{:S(2)}, u32[]{:S(2)}) collective-permute-start(bf16[672,128]{1,0:T(8,128)(2,1)S(1)} %get-tuple-element.46), channel_id=1, source_target_pairs={{0,2},{1,9},{2,0},{3,11},{4,6},{5,13},{6,4},{7,15},{8,10},{9,1},{1... | collective-permute-start | bytes 516104 | tf_op jit(solution)/shard_map/ppermute | solution.py:352
  25.5 1.5 %collective-permute-start.12 = (bf16[672,128]{1,0:T(8,128)(2,1)S(1)}, bf16[672,128]{1,0:T(8,128)(2,1)S(1)}, u32[]{:S(2)}, u32[]{:S(2)}) collective-permute-start(bf16[672,128]{1,0:T(8,128)(2,1)S(1)} %get-tuple-element.47), channel_id=1, source_target_pairs={{0,4},{1,17},{2,6},{3,19},{4,0},{5,21},{6,2},{7,23},{8,12},{9,25},... | collective-permute-start | bytes 516104 | tf_op jit(solution)/shard_map/ppermute | solution.py:352
  27.0 3.0 %collective-permute-start.13 = (bf16[672,128]{1,0:T(8,128)(2,1)S(1)}, bf16[672,128]{1,0:T(8,128)(2,1)S(1)}, u32[]{:S(2)}, u32[]{:S(2)}) collective-permute-start(bf16[672,128]{1,0:T(8,128)(2,1)S(1)} %get-tuple-element.48), channel_id=1, source_target_pairs={{0,6},{1,25},{2,4},{3,27},{4,2},{5,29},{6,0},{7,31},{8,14},{9,17},... | collective-permute-start | bytes 516104 | tf_op jit(solution)/shard_map/ppermute | solution.py:352
  30.0 1.6 %collective-permute-done.3.refs_1_ = bf16[672,128]{1,0:T(8,128)(2,1)S(1)} collective-permute-done((bf16[672,128]{1,0:T(8,128)(2,1)S(1)}, bf16[672,128]{1,0:T(8,128)(2,1)S(1)}, u32[]{:S(2)}, u32[]{:S(2)}) %collective-permute-start.3) | collective-permute-done | bytes 172064 | tf_op jit(solution)/shard_map/ppermute | solution.py:352
  31.7 1.6 %collective-permute-start.5 = (bf16[672,128]{1,0:T(8,128)(2,1)S(1)}, bf16[672,128]{1,0:T(8,128)(2,1)S(1)}, u32[]{:S(2)}, u32[]{:S(2)}) collective-permute-start(bf16[672,128]{1,0:T(8,128)(2,1)S(1)} %shard_map.121.one), channel_id=1, source_target_pairs={{0,8},{1,17},{2,10},{3,19},{4,12},{5,21},{6,14},{7,23},{8,0},{9,25... | collective-permute-start | bytes 516104 | tf_op jit(solution)/shard_map/ppermute | solution.py:352
  33.4 1.9 %collective-permute-done.12.refs_1_ = bf16[672,128]{1,0:T(8,128)(2,1)S(1)} collective-permute-done((bf16[672,128]{1,0:T(8,128)(2,1)S(1)}, bf16[672,128]{1,0:T(8,128)(2,1)S(1)}, u32[]{:S(2)}, u32[]{:S(2)}) %collective-permute-start.12) | collective-permute-done | bytes 172064 | tf_op jit(solution)/shard_map/ppermute | solution.py:352
  35.4 1.6 %collective-permute-start.14 = (bf16[672,128]{1,0:T(8,128)(2,1)S(1)}, bf16[672,128]{1,0:T(8,128)(2,1)S(1)}, u32[]{:S(2)}, u32[]{:S(2)}) collective-permute-start(bf16[672,128]{1,0:T(8,128)(2,1)S(1)} %shard_map.127.one), channel_id=1, source_target_pairs={{0,8},{1,3},{2,10},{3,1},{4,12},{5,7},{6,14},{7,5},{8,0},{9,11},{1... | collective-permute-start | bytes 516104 | tf_op jit(solution)/shard_map/ppermute | solution.py:352
  37.3 3.5 %collective-permute-start.6 = (bf16[672,128]{1,0:T(8,128)(2,1)S(1)}, bf16[672,128]{1,0:T(8,128)(2,1)S(1)}, u32[]{:S(2)}, u32[]{:S(2)}) collective-permute-start(bf16[672,128]{1,0:T(8,128)(2,1)S(1)} %shard_map.122.one), channel_id=1, source_target_pairs={{0,16},{1,9},{2,18},{3,11},{4,20},{5,13},{6,22},{7,15},{8,24},{9,1... | collective-permute-start | bytes 516104 | tf_op jit(solution)/shard_map/ppermute | solution.py:352
  41.0 2.8 %collective-permute-start.15 = (bf16[672,128]{1,0:T(8,128)(2,1)S(1)}, bf16[672,128]{1,0:T(8,128)(2,1)S(1)}, u32[]{:S(2)}, u32[]{:S(2)}) collective-permute-start(bf16[672,128]{1,0:T(8,128)(2,1)S(1)} %shard_map.128.one), channel_id=1, source_target_pairs={{0,16},{1,5},{2,18},{3,7},{4,20},{5,1},{6,22},{7,3},{8,24},{9,13},... | collective-permute-start | bytes 516104 | tf_op jit(solution)/shard_map/ppermute | solution.py:352
  44.4 1.5 %collective-permute-start.9 = (bf16[640,128]{1,0:T(8,128)(2,1)S(1)}, bf16[640,128]{1,0:T(8,128)(2,1)S(1)}, u32[]{:S(2)}, u32[]{:S(2)}) collective-permute-start(bf16[640,128]{1,0:T(8,128)(2,1)S(1)} %get-tuple-element.38.refs_0_), channel_id=1, source_target_pairs={{0,6},{1,7},{2,4},{3,5},{4,2},{5,3},{6,0},{7,1},{8,14},{9,15},{10,... | collective-permute-start | bytes 491528 | tf_op jit(solution)/shard_map/ppermute | solution.py:352
  45.8 1.4 %collective-permute-start.8 = (bf16[640,128]{1,0:T(8,128)(2,1)S(1)}, bf16[640,128]{1,0:T(8,128)(2,1)S(1)}, u32[]{:S(2)}, u32[]{:S(2)}) collective-permute-start(bf16[640,128]{1,0:T(8,128)(2,1)S(1)} %get-tuple-element.38.refs_0_), channel_id=1, source_target_pairs={{0,4},{1,5},{2,6},{3,7},{4,0},{5,1},{6,2},{7,3},{8,12},{9,13},{10,... | collective-permute-start | bytes 491528 | tf_op jit(solution)/shard_map/ppermute | solution.py:352
  47.9 2.3 %collective-permute-done.15.other = bf16[672,128]{1,0:T(8,128)(2,1)S(1)} collective-permute-done((bf16[672,128]{1,0:T(8,128)(2,1)S(1)}, bf16[672,128]{1,0:T(8,128)(2,1)S(1)}, u32[]{:S(2)}, u32[]{:S(2)}) %collective-permute-start.15) | collective-permute-done | bytes 172064 | tf_op jit(solution)/shard_map/ppermute | solution.py:352
  50.3 2.1 %collective-permute-start.18 = (bf16[640,128]{1,0:T(8,128)(2,1)S(1)}, bf16[640,128]{1,0:T(8,128)(2,1)S(1)}, u32[]{:S(2)}, u32[]{:S(2)}) collective-permute-start(bf16[640,128]{1,0:T(8,128)(2,1)S(1)} %shard_map.129.refs_0_), channel_id=1, source_target_pairs={{0,6},{1,25},{2,4},{3,27},{4,2},{5,29},{6,0},{7,31},{8,14},{9,17},... | collective-permute-start | bytes 491528 | tf_op jit(solution)/shard_map/ppermute | solution.py:352
  53.9 1.9 %collective-permute-done.8.refs_2_ = bf16[640,128]{1,0:T(8,128)(2,1)S(1)} collective-permute-done((bf16[640,128]{1,0:T(8,128)(2,1)S(1)}, bf16[640,128]{1,0:T(8,128)(2,1)S(1)}, u32[]{:S(2)}, u32[]{:S(2)}) %collective-permute-start.8) | collective-permute-done | bytes 163872 | tf_op jit(solution)/shard_map/ppermute | solution.py:352
  56.1 1.7 %collective-permute-done.18.refs_3_ = bf16[640,128]{1,0:T(8,128)(2,1)S(1)} collective-permute-done((bf16[640,128]{1,0:T(8,128)(2,1)S(1)}, bf16[640,128]{1,0:T(8,128)(2,1)S(1)}, u32[]{:S(2)}, u32[]{:S(2)}) %collective-permute-start.18) | collective-permute-done | bytes 163872 | tf_op jit(solution)/shard_map/ppermute | solution.py:352
  57.7 1.7 %collective-permute-done.17.refs_2_ = bf16[640,128]{1,0:T(8,128)(2,1)S(1)} collective-permute-done((bf16[640,128]{1,0:T(8,128)(2,1)S(1)}, bf16[640,128]{1,0:T(8,128)(2,1)S(1)}, u32[]{:S(2)}, u32[]{:S(2)}) %collective-permute-start.17) | collective-permute-done | bytes 163872 | tf_op jit(solution)/shard_map/ppermute | solution.py:352
  59.8 2.1 %shard_map.132 = (f32[1,1]{1,0:T(1,128)}, f32[768,512]{1,0:T(8,128)}, f32[512,512]{1,0:T(8,128)}, f32[768,512]{1,0:T(8,128)}, f32[512,512]{1,0:T(8,128)}) custom-call(bf16[2560,128]{1,0:T(8,128)(2,1)S(1)} %shard_map.124.refs_0_, bf16[2560,128]{1,0:T(8,128)(2,1)S(1)} %shard_map.130.refs_1_, f32[16,128]{1,0:T(8,128)S(1)} %shard_map.131.refs_2_), custom_call_target="tpu_custom_call" | custom-call | flops 655360 | bytes 3932160 | tf_op jit(solution)/shard_map/pallas_call | solution.py:565
  61.9 1.6 %shard_map.133 = (f32[768,512]{1,0:T(8,128)}, f32[512,512]{1,0:T(8,128)}, f32[768,512]{1,0:T(8,128)}, f32[512,512]{1,0:T(8,128)}) custom-call(bf16[2560,128]{1,0:T(8,128)(2,1)S(1)} %collective-permute-done.19.refs_0_, bf16[2560,128]{1,0:T(8,128)(2,1)S(1)} %collective-permute-done.20.refs_1_, ...), custom_call_target="tpu_custom_call", output_to_operand_aliasing={{0}: (3, {}), {1}: (4, {}), {2}: (5, {}), {3}: (6, {})} | custom-call | flops 655360 | bytes 3932160 | tf_op jit(solution)/shard_map/pallas_call | solution.py:565
  (47 shorter events, 5.5 us)
Async XLA Ops:
  0.6 3.4 %copy-start.1 = (bf16[4,256,256]{2,1,0:T(8,128)(2,1)S(1)}, bf16[4,256,256]{2,1,0:T(8,128)(2,1)}, u32[]{:S(2)}) copy-start(bf16[4,256,256]{2,1,0:T(8,128)(2,1)} %own_v.1) | copy-start | bytes 1572868
  0.6 3.4 %copy-start = (bf16[4,256,256]{2,1,0:T(8,128)(2,1)S(1)}, bf16[4,256,256]{2,1,0:T(8,128)(2,1)}, u32[]{:S(2)}) copy-start(bf16[4,256,256]{2,1,0:T(8,128)(2,1)} %own_a.1) | copy-start | bytes 1572868
  0.7 3.4 %copy-start.3 = (bf16[512,512]{1,0:T(8,128)(2,1)S(1)}, bf16[512,512]{1,0:T(8,128)(2,1)}, u32[]{:S(2)}) copy-start(bf16[512,512]{1,0:T(8,128)(2,1)} %w_proj.1) | copy-start | bytes 1572868
  2.0 2.1 %collective-permute-start = (bf16[2,2,256,256]{3,2,1,0:T(8,128)(2,1)S(1)}, bf16[2,2,256,256]{3,2,1,0:T(8,128)(2,1)S(1)}, u32[]{:S(2)}, u32[]{:S(2)}) collective-permute-start(bf16[2,2,256,256]{3,2,1,0:T(8,128)(2,1)S(1)} %pad_maximum_fusion), channel_id=1, source_target_pairs={{0,1},{1,0},{2,3},{3,2},{4,5},{5,4},{6,7},{7,6},{8,9},{9,8},{10,11... | collective-permute-start | bytes 1572872 | tf_op jit(solution)/shard_map/ppermute | solution.py:343
  16.0 2.8 %collective-permute-start.1 = (bf16[2592,128]{1,0:T(8,128)(2,1)S(1)}, bf16[2592,128]{1,0:T(8,128)(2,1)S(1)}, u32[]{:S(2)}, u32[]{:S(2)}) collective-permute-start(bf16[2592,128]{1,0:T(8,128)(2,1)S(1)} %get-tuple-element.33), channel_id=1, source_target_pairs={{0,1},{1,0},{2,3},{3,2},{4,5},{5,4},{6,7},{7,6},{8,9},{9,8},{10,11... | collective-permute-start | bytes 1990664 | tf_op jit(solution)/shard_map/ppermute | solution.py:343
  18.6 4.8 %collective-permute-start.10 = (bf16[2592,128]{1,0:T(8,128)(2,1)S(1)}, bf16[2592,128]{1,0:T(8,128)(2,1)S(1)}, u32[]{:S(2)}, u32[]{:S(2)}) collective-permute-start(bf16[2592,128]{1,0:T(8,128)(2,1)S(1)} %get-tuple-element.44), channel_id=1, source_target_pairs={{0,1},{1,0},{2,3},{3,2},{4,5},{5,4},{6,7},{7,6},{8,9},{9,8},{10,11... | collective-permute-start | bytes 1990664 | tf_op jit(solution)/shard_map/ppermute | solution.py:343
  18.9 8.1 %collective-permute-start.2 = (bf16[672,128]{1,0:T(8,128)(2,1)S(1)}, bf16[672,128]{1,0:T(8,128)(2,1)S(1)}, u32[]{:S(2)}, u32[]{:S(2)}) collective-permute-start(bf16[672,128]{1,0:T(8,128)(2,1)S(1)} %get-tuple-element.35), channel_id=1, source_target_pairs={{0,2},{1,3},{2,0},{3,1},{4,6},{5,7},{6,4},{7,5},{8,10},{9,11},{10,... | collective-permute-start | bytes 516104 | tf_op jit(solution)/shard_map/ppermute | solution.py:352
  21.8 9.8 %collective-permute-start.3 = (bf16[672,128]{1,0:T(8,128)(2,1)S(1)}, bf16[672,128]{1,0:T(8,128)(2,1)S(1)}, u32[]{:S(2)}, u32[]{:S(2)}) collective-permute-start(bf16[672,128]{1,0:T(8,128)(2,1)S(1)} %get-tuple-element.36), channel_id=1, source_target_pairs={{0,4},{1,5},{2,6},{3,7},{4,0},{5,1},{6,2},{7,3},{8,12},{9,13},{10,... | collective-permute-start | bytes 516104 | tf_op jit(solution)/shard_map/ppermute | solution.py:352
  23.3 8.3 %collective-permute-start.4 = (bf16[672,128]{1,0:T(8,128)(2,1)S(1)}, bf16[672,128]{1,0:T(8,128)(2,1)S(1)}, u32[]{:S(2)}, u32[]{:S(2)}) collective-permute-start(bf16[672,128]{1,0:T(8,128)(2,1)S(1)} %get-tuple-element.37), channel_id=1, source_target_pairs={{0,6},{1,7},{2,4},{3,5},{4,2},{5,3},{6,0},{7,1},{8,14},{9,15},{10,... | collective-permute-start | bytes 516104 | tf_op jit(solution)/shard_map/ppermute | solution.py:352
  23.5 9.9 %collective-permute-start.11 = (bf16[672,128]{1,0:T(8,128)(2,1)S(1)}, bf16[672,128]{1,0:T(8,128)(2,1)S(1)}, u32[]{:S(2)}, u32[]{:S(2)}) collective-permute-start(bf16[672,128]{1,0:T(8,128)(2,1)S(1)} %get-tuple-element.46), channel_id=1, source_target_pairs={{0,2},{1,9},{2,0},{3,11},{4,6},{5,13},{6,4},{7,15},{8,10},{9,1},{1... | collective-permute-start | bytes 516104 | tf_op jit(solution)/shard_map/ppermute | solution.py:352
  25.5 9.8 %collective-permute-start.12 = (bf16[672,128]{1,0:T(8,128)(2,1)S(1)}, bf16[672,128]{1,0:T(8,128)(2,1)S(1)}, u32[]{:S(2)}, u32[]{:S(2)}) collective-permute-start(bf16[672,128]{1,0:T(8,128)(2,1)S(1)} %get-tuple-element.47), channel_id=1, source_target_pairs={{0,4},{1,17},{2,6},{3,19},{4,0},{5,21},{6,2},{7,23},{8,12},{9,25},... | collective-permute-start | bytes 516104 | tf_op jit(solution)/shard_map/ppermute | solution.py:352
  27.0 8.3 %collective-permute-start.13 = (bf16[672,128]{1,0:T(8,128)(2,1)S(1)}, bf16[672,128]{1,0:T(8,128)(2,1)S(1)}, u32[]{:S(2)}, u32[]{:S(2)}) collective-permute-start(bf16[672,128]{1,0:T(8,128)(2,1)S(1)} %get-tuple-element.48), channel_id=1, source_target_pairs={{0,6},{1,25},{2,4},{3,27},{4,2},{5,29},{6,0},{7,31},{8,14},{9,17},... | collective-permute-start | bytes 516104 | tf_op jit(solution)/shard_map/ppermute | solution.py:352
  31.7 5.5 %collective-permute-start.5 = (bf16[672,128]{1,0:T(8,128)(2,1)S(1)}, bf16[672,128]{1,0:T(8,128)(2,1)S(1)}, u32[]{:S(2)}, u32[]{:S(2)}) collective-permute-start(bf16[672,128]{1,0:T(8,128)(2,1)S(1)} %shard_map.121.one), channel_id=1, source_target_pairs={{0,8},{1,17},{2,10},{3,19},{4,12},{5,21},{6,14},{7,23},{8,0},{9,25... | collective-permute-start | bytes 516104 | tf_op jit(solution)/shard_map/ppermute | solution.py:352
  35.4 5.6 %collective-permute-start.14 = (bf16[672,128]{1,0:T(8,128)(2,1)S(1)}, bf16[672,128]{1,0:T(8,128)(2,1)S(1)}, u32[]{:S(2)}, u32[]{:S(2)}) collective-permute-start(bf16[672,128]{1,0:T(8,128)(2,1)S(1)} %shard_map.127.one), channel_id=1, source_target_pairs={{0,8},{1,3},{2,10},{3,1},{4,12},{5,7},{6,14},{7,5},{8,0},{9,11},{1... | collective-permute-start | bytes 516104 | tf_op jit(solution)/shard_map/ppermute | solution.py:352
  37.3 7.0 %collective-permute-start.6 = (bf16[672,128]{1,0:T(8,128)(2,1)S(1)}, bf16[672,128]{1,0:T(8,128)(2,1)S(1)}, u32[]{:S(2)}, u32[]{:S(2)}) collective-permute-start(bf16[672,128]{1,0:T(8,128)(2,1)S(1)} %shard_map.122.one), channel_id=1, source_target_pairs={{0,16},{1,9},{2,18},{3,11},{4,20},{5,13},{6,22},{7,15},{8,24},{9,1... | collective-permute-start | bytes 516104 | tf_op jit(solution)/shard_map/ppermute | solution.py:352
  41.0 9.2 %collective-permute-start.15 = (bf16[672,128]{1,0:T(8,128)(2,1)S(1)}, bf16[672,128]{1,0:T(8,128)(2,1)S(1)}, u32[]{:S(2)}, u32[]{:S(2)}) collective-permute-start(bf16[672,128]{1,0:T(8,128)(2,1)S(1)} %shard_map.128.one), channel_id=1, source_target_pairs={{0,16},{1,5},{2,18},{3,7},{4,20},{5,1},{6,22},{7,3},{8,24},{9,13},... | collective-permute-start | bytes 516104 | tf_op jit(solution)/shard_map/ppermute | solution.py:352
  44.4 8.8 %collective-permute-start.9 = (bf16[640,128]{1,0:T(8,128)(2,1)S(1)}, bf16[640,128]{1,0:T(8,128)(2,1)S(1)}, u32[]{:S(2)}, u32[]{:S(2)}) collective-permute-start(bf16[640,128]{1,0:T(8,128)(2,1)S(1)} %get-tuple-element.38.refs_0_), channel_id=1, source_target_pairs={{0,6},{1,7},{2,4},{3,5},{4,2},{5,3},{6,0},{7,1},{8,14},{9,15},{10,... | collective-permute-start | bytes 491528 | tf_op jit(solution)/shard_map/ppermute | solution.py:352
  45.8 10.0 %collective-permute-start.8 = (bf16[640,128]{1,0:T(8,128)(2,1)S(1)}, bf16[640,128]{1,0:T(8,128)(2,1)S(1)}, u32[]{:S(2)}, u32[]{:S(2)}) collective-permute-start(bf16[640,128]{1,0:T(8,128)(2,1)S(1)} %get-tuple-element.38.refs_0_), channel_id=1, source_target_pairs={{0,4},{1,5},{2,6},{3,7},{4,0},{5,1},{6,2},{7,3},{8,12},{9,13},{10,... | collective-permute-start | bytes 491528 | tf_op jit(solution)/shard_map/ppermute | solution.py:352
  47.2 8.7 %collective-permute-start.7 = (bf16[640,128]{1,0:T(8,128)(2,1)S(1)}, bf16[640,128]{1,0:T(8,128)(2,1)S(1)}, u32[]{:S(2)}, u32[]{:S(2)}) collective-permute-start(bf16[640,128]{1,0:T(8,128)(2,1)S(1)} %get-tuple-element.38.refs_0_), channel_id=1, source_target_pairs={{0,2},{1,3},{2,0},{3,1},{4,6},{5,7},{6,4},{7,5},{8,10},{9,11},{10,... | collective-permute-start | bytes 491528 | tf_op jit(solution)/shard_map/ppermute | solution.py:352
  50.3 7.4 %collective-permute-start.18 = (bf16[640,128]{1,0:T(8,128)(2,1)S(1)}, bf16[640,128]{1,0:T(8,128)(2,1)S(1)}, u32[]{:S(2)}, u32[]{:S(2)}) collective-permute-start(bf16[640,128]{1,0:T(8,128)(2,1)S(1)} %shard_map.129.refs_0_), channel_id=1, source_target_pairs={{0,6},{1,25},{2,4},{3,27},{4,2},{5,29},{6,0},{7,31},{8,14},{9,17},... | collective-permute-start | bytes 491528 | tf_op jit(solution)/shard_map/ppermute | solution.py:352
  52.4 7.0 %collective-permute-start.17 = (bf16[640,128]{1,0:T(8,128)(2,1)S(1)}, bf16[640,128]{1,0:T(8,128)(2,1)S(1)}, u32[]{:S(2)}, u32[]{:S(2)}) collective-permute-start(bf16[640,128]{1,0:T(8,128)(2,1)S(1)} %shard_map.129.refs_0_), channel_id=1, source_target_pairs={{0,4},{1,17},{2,6},{3,19},{4,0},{5,21},{6,2},{7,23},{8,12},{9,25},... | collective-permute-start | bytes 491528 | tf_op jit(solution)/shard_map/ppermute | solution.py:352
  53.1 6.3 %collective-permute-start.16 = (bf16[640,128]{1,0:T(8,128)(2,1)S(1)}, bf16[640,128]{1,0:T(8,128)(2,1)S(1)}, u32[]{:S(2)}, u32[]{:S(2)}) collective-permute-start(bf16[640,128]{1,0:T(8,128)(2,1)S(1)} %shard_map.129.refs_0_), channel_id=1, source_target_pairs={{0,2},{1,9},{2,0},{3,11},{4,6},{5,13},{6,4},{7,15},{8,10},{9,1},{1... | collective-permute-start | bytes 491528 | tf_op jit(solution)/shard_map/ppermute | solution.py:352
  56.0 5.9 %collective-permute-start.19 = (bf16[2560,128]{1,0:T(8,128)(2,1)S(1)}, bf16[2560,128]{1,0:T(8,128)(2,1)S(1)}, u32[]{:S(2)}, u32[]{:S(2)}) collective-permute-start(bf16[2560,128]{1,0:T(8,128)(2,1)S(1)} %shard_map.124.refs_0_), channel_id=1, source_target_pairs={{0,1},{1,0},{2,3},{3,2},{4,5},{5,4},{6,7},{7,6},{8,9},{9,8},{10,11... | collective-permute-start | bytes 1966088 | tf_op jit(solution)/shard_map/ppermute | solution.py:343
  59.5 2.4 %collective-permute-start.20 = (bf16[2560,128]{1,0:T(8,128)(2,1)S(1)}, bf16[2560,128]{1,0:T(8,128)(2,1)S(1)}, u32[]{:S(2)}, u32[]{:S(2)}) collective-permute-start(bf16[2560,128]{1,0:T(8,128)(2,1)S(1)} %shard_map.130.refs_1_), channel_id=1, source_target_pairs={{0,1},{1,0},{2,3},{3,2},{4,5},{5,4},{6,7},{7,6},{8,9},{9,8},{10,11... | collective-permute-start | bytes 1966088 | tf_op jit(solution)/shard_map/ppermute | solution.py:343
  (3 other events, 10.1 us)

commit v10 on v9

--- a/solution.py
+++ b/solution.py
@@ -257,7 +257,6 @@
         gemb_a[pl.ds(pl.multiple_of(i * block, block), block), :] = grad.astype(BF16)
         return 0
 
-    lax.fori_loop(0, rows_total // block, audio_step, 0)
 
     count = jnp.zeros((), F32)
     for c in range(clips):
@@ -271,6 +270,7 @@
         send[at : at + PAD, :] = digits.astype(BF16)
 
     backward(wvp, cols_v, slope_v, hid_v, gemb_v, gpre, keep, send, block)
+    lax.fori_loop(0, rows_total // block, audio_step, 0, unroll=True)
 
 
 def block_of(frames):

time: 63.9 us -> 62.3 us (0.975)
  Pallas kernels: 18.6 us -> 17.2 us
    pallas_call x1, Pallas kernels: 11.9 us -> 10.5 us  [local_grads(): pl.pallas_call(functools.partial(kernel, frames, clips, halo), out_shape=...]
where the time goes in v10:
time: 62.3 us; the launch traced here: 62.1 us
  starting transfers between devices  29 us (47%)
  Pallas kernels  17.2 us (28%)
  waiting for transfers between devices  13.8 us (22%)
  local copies, waits for them, and re-layouts  1.23 us (2%)
  between operations  0.84 us (1%)
    ppermute x16, starting transfers between devices, swap_by_core(): return lax.ppermute(value, ('clip', 'tm'), pairs)  27.7 us
    ppermute x16, waiting for transfers between devices, swap_by_core(): return lax.ppermute(value, ('clip', 'tm'), pairs)  12.2 us
    pallas_call x1, Pallas kernels, local_grads(): pl.pallas_call(functools.partial(kernel, frames, clips, halo), out_shape=...  10.5 us
    pallas_call x2, Pallas kernels, finish_some(): pl.pallas_call(functools.partial(finish_kernel, parts, len(known), with_l...  3.69 us
    pallas_call x1, Pallas kernels, local_grads(): pl.pallas_call(functools.partial(audio_kernel, block_of(frames)), out_sha...  2.11 us
    ppermute x5, waiting for transfers between devices, swap(): lax.ppermute(value, axis, [(i, i ^ bit) for i in range(lax.axis_size(axis...  1.55 us
    ppermute x5, starting transfers between devices, swap(): lax.ppermute(value, axis, [(i, i ^ bit) for i in range(lax.axis_size(axis...  1.32 us
  transfers between devices with their start and end apart: 21, of which 12 were waited for; matrix products, arithmetic and copies ran while one was open for 0% of the time, Pallas kernels for 8%

profile of v10, /device:TPU:0, one launch (start us, length us, event | category | flops | bytes accessed | tf_op | source)
XLA Modules:
  0.0 62.1 jit_solution(15984412563882456989)
XLA Ops:
  0.7 1.2 %dynamic-slice_bitcast_fusion = (bf16[1,2,256,256]{3,2,1,0:T(8,128)(2,1)S(1)}, bf16[1,2,256,256]{3,2,1,0:T(8,128)(2,1)S(1)}) fusion(bf16[4,256,256]{2,1,0:T(8,128)(2,1)} %own_v.1, s32[]{:T(128)S(6)} %select_n.4, bf16[4,256,256]{2,1,0:T(8,128)(2,1)} %own_a.1), kind=kLoop, calls=%fused_computation.1 | loop fusion | bytes 1048580 | tf_op jit(solution)/shard_map/stack | solution.py:603
  2.5 1.5 %collective-permute-done.got = bf16[2,2,256,256]{3,2,1,0:T(8,128)(2,1)S(1)} collective-permute-done((bf16[2,2,256,256]{3,2,1,0:T(8,128)(2,1)S(1)}, bf16[2,2,256,256]{3,2,1,0:T(8,128)(2,1)S(1)}, u32[]{:S(2)}, u32[]{:S(2)}) %collective-permute-start) | collective-permute-done | bytes 524320 | tf_op jit(solution)/shard_map/ppermute | solution.py:343
  4.1 10.5 %shard_map.119 = (f32[2592,128]{1,0:T(8,128)S(1)}, bf16[2592,128]{1,0:T(8,128)(2,1)S(1)}, bf16[1024,768]{1,0:T(8,128)(2,1)S(1)}, f32[1024,512]{1,0:T(8,128)S(1)}...) custom-call(s32[4]{0:T(128)S(1)} %copy-done.4, s32[4]{0:T(128)S(1)} %copy-done.5, ...), custom_call_target="tpu_custom_call" | custom-call | tf_op jit(solution)/shard_map/pallas_call | solution.py:307
  15.0 2.1 %shard_map.125 = (f32[2592,128]{1,0:T(8,128)S(1)}, bf16[2592,128]{1,0:T(8,128)(2,1)S(1)}) custom-call(bf16[512,512]{1,0:T(8,128)(2,1)S(1)} %copy-done.3, bf16[1024,768]{1,0:T(8,128)(2,1)S(1)} %get-tuple-element.39.cols, f32[1024,512]{1,0:T(8,128)S(1)} %get-tuple-element.40.slope, bf16[1024,512]{1,0:T(8,128)(2,1)S(1)} %get-tuple-element.41.hid, ...), custom_call_target="tpu_custom_call" | custom-call | flops 1879048192 | bytes 6291456 | tf_op jit(solution)/shard_map/pallas_call | solution.py:330
  17.4 2.9 %collective-permute-start.2 = (bf16[672,128]{1,0:T(8,128)(2,1)S(1)}, bf16[672,128]{1,0:T(8,128)(2,1)S(1)}, u32[]{:S(2)}, u32[]{:S(2)}) collective-permute-start(bf16[672,128]{1,0:T(8,128)(2,1)S(1)} %get-tuple-element.35), channel_id=1, source_target_pairs={{0,2},{1,3},{2,0},{3,1},{4,6},{5,7},{6,4},{7,5},{8,10},{9,11},{10,... | collective-permute-start | bytes 516104 | tf_op jit(solution)/shard_map/ppermute | solution.py:352
  20.4 1.5 %collective-permute-start.3 = (bf16[672,128]{1,0:T(8,128)(2,1)S(1)}, bf16[672,128]{1,0:T(8,128)(2,1)S(1)}, u32[]{:S(2)}, u32[]{:S(2)}) collective-permute-start(bf16[672,128]{1,0:T(8,128)(2,1)S(1)} %get-tuple-element.36), channel_id=1, source_target_pairs={{0,4},{1,5},{2,6},{3,7},{4,0},{5,1},{6,2},{7,3},{8,12},{9,13},{10,... | collective-permute-start | bytes 516104 | tf_op jit(solution)/shard_map/ppermute | solution.py:352
  22.1 2.0 %collective-permute-start.11 = (bf16[672,128]{1,0:T(8,128)(2,1)S(1)}, bf16[672,128]{1,0:T(8,128)(2,1)S(1)}, u32[]{:S(2)}, u32[]{:S(2)}) collective-permute-start(bf16[672,128]{1,0:T(8,128)(2,1)S(1)} %get-tuple-element.46), channel_id=1, source_target_pairs={{0,2},{1,9},{2,0},{3,11},{4,6},{5,13},{6,4},{7,15},{8,10},{9,1},{1... | collective-permute-start | bytes 516104 | tf_op jit(solution)/shard_map/ppermute | solution.py:352
  24.1 1.5 %collective-permute-start.12 = (bf16[672,128]{1,0:T(8,128)(2,1)S(1)}, bf16[672,128]{1,0:T(8,128)(2,1)S(1)}, u32[]{:S(2)}, u32[]{:S(2)}) collective-permute-start(bf16[672,128]{1,0:T(8,128)(2,1)S(1)} %get-tuple-element.47), channel_id=1, source_target_pairs={{0,4},{1,17},{2,6},{3,19},{4,0},{5,21},{6,2},{7,23},{8,12},{9,25},... | collective-permute-start | bytes 516104 | tf_op jit(solution)/shard_map/ppermute | solution.py:352
  25.6 3.0 %collective-permute-start.13 = (bf16[672,128]{1,0:T(8,128)(2,1)S(1)}, bf16[672,128]{1,0:T(8,128)(2,1)S(1)}, u32[]{:S(2)}, u32[]{:S(2)}) collective-permute-start(bf16[672,128]{1,0:T(8,128)(2,1)S(1)} %get-tuple-element.48), channel_id=1, source_target_pairs={{0,6},{1,25},{2,4},{3,27},{4,2},{5,29},{6,0},{7,31},{8,14},{9,17},... | collective-permute-start | bytes 516104 | tf_op jit(solution)/shard_map/ppermute | solution.py:352
  28.6 1.6 %collective-permute-done.3.refs_1_ = bf16[672,128]{1,0:T(8,128)(2,1)S(1)} collective-permute-done((bf16[672,128]{1,0:T(8,128)(2,1)S(1)}, bf16[672,128]{1,0:T(8,128)(2,1)S(1)}, u32[]{:S(2)}, u32[]{:S(2)}) %collective-permute-start.3) | collective-permute-done | bytes 172064 | tf_op jit(solution)/shard_map/ppermute | solution.py:352
  30.3 1.6 %collective-permute-start.5 = (bf16[672,128]{1,0:T(8,128)(2,1)S(1)}, bf16[672,128]{1,0:T(8,128)(2,1)S(1)}, u32[]{:S(2)}, u32[]{:S(2)}) collective-permute-start(bf16[672,128]{1,0:T(8,128)(2,1)S(1)} %shard_map.121.one), channel_id=1, source_target_pairs={{0,8},{1,17},{2,10},{3,19},{4,12},{5,21},{6,14},{7,23},{8,0},{9,25... | collective-permute-start | bytes 516104 | tf_op jit(solution)/shard_map/ppermute | solution.py:352
  31.9 2.0 %collective-permute-done.12.refs_1_ = bf16[672,128]{1,0:T(8,128)(2,1)S(1)} collective-permute-done((bf16[672,128]{1,0:T(8,128)(2,1)S(1)}, bf16[672,128]{1,0:T(8,128)(2,1)S(1)}, u32[]{:S(2)}, u32[]{:S(2)}) %collective-permute-start.12) | collective-permute-done | bytes 172064 | tf_op jit(solution)/shard_map/ppermute | solution.py:352
  34.0 1.6 %collective-permute-start.14 = (bf16[672,128]{1,0:T(8,128)(2,1)S(1)}, bf16[672,128]{1,0:T(8,128)(2,1)S(1)}, u32[]{:S(2)}, u32[]{:S(2)}) collective-permute-start(bf16[672,128]{1,0:T(8,128)(2,1)S(1)} %shard_map.127.one), channel_id=1, source_target_pairs={{0,8},{1,3},{2,10},{3,1},{4,12},{5,7},{6,14},{7,5},{8,0},{9,11},{1... | collective-permute-start | bytes 516104 | tf_op jit(solution)/shard_map/ppermute | solution.py:352
  35.9 3.5 %collective-permute-start.6 = (bf16[672,128]{1,0:T(8,128)(2,1)S(1)}, bf16[672,128]{1,0:T(8,128)(2,1)S(1)}, u32[]{:S(2)}, u32[]{:S(2)}) collective-permute-start(bf16[672,128]{1,0:T(8,128)(2,1)S(1)} %shard_map.122.one), channel_id=1, source_target_pairs={{0,16},{1,9},{2,18},{3,11},{4,20},{5,13},{6,22},{7,15},{8,24},{9,1... | collective-permute-start | bytes 516104 | tf_op jit(solution)/shard_map/ppermute | solution.py:352
  39.6 2.8 %collective-permute-start.15 = (bf16[672,128]{1,0:T(8,128)(2,1)S(1)}, bf16[672,128]{1,0:T(8,128)(2,1)S(1)}, u32[]{:S(2)}, u32[]{:S(2)}) collective-permute-start(bf16[672,128]{1,0:T(8,128)(2,1)S(1)} %shard_map.128.one), channel_id=1, source_target_pairs={{0,16},{1,5},{2,18},{3,7},{4,20},{5,1},{6,22},{7,3},{8,24},{9,13},... | collective-permute-start | bytes 516104 | tf_op jit(solution)/shard_map/ppermute | solution.py:352
  42.9 1.5 %collective-permute-start.9 = (bf16[640,128]{1,0:T(8,128)(2,1)S(1)}, bf16[640,128]{1,0:T(8,128)(2,1)S(1)}, u32[]{:S(2)}, u32[]{:S(2)}) collective-permute-start(bf16[640,128]{1,0:T(8,128)(2,1)S(1)} %get-tuple-element.38.refs_0_), channel_id=1, source_target_pairs={{0,6},{1,7},{2,4},{3,5},{4,2},{5,3},{6,0},{7,1},{8,14},{9,15},{10,... | collective-permute-start | bytes 491528 | tf_op jit(solution)/shard_map/ppermute | solution.py:352
  44.4 1.4 %collective-permute-start.8 = (bf16[640,128]{1,0:T(8,128)(2,1)S(1)}, bf16[640,128]{1,0:T(8,128)(2,1)S(1)}, u32[]{:S(2)}, u32[]{:S(2)}) collective-permute-start(bf16[640,128]{1,0:T(8,128)(2,1)S(1)} %get-tuple-element.38.refs_0_), channel_id=1, source_target_pairs={{0,4},{1,5},{2,6},{3,7},{4,0},{5,1},{6,2},{7,3},{8,12},{9,13},{10,... | collective-permute-start | bytes 491528 | tf_op jit(solution)/shard_map/ppermute | solution.py:352
  46.5 2.3 %collective-permute-done.15.other = bf16[672,128]{1,0:T(8,128)(2,1)S(1)} collective-permute-done((bf16[672,128]{1,0:T(8,128)(2,1)S(1)}, bf16[672,128]{1,0:T(8,128)(2,1)S(1)}, u32[]{:S(2)}, u32[]{:S(2)}) %collective-permute-start.15) | collective-permute-done | bytes 172064 | tf_op jit(solution)/shard_map/ppermute | solution.py:352
  48.9 2.1 %collective-permute-start.18 = (bf16[640,128]{1,0:T(8,128)(2,1)S(1)}, bf16[640,128]{1,0:T(8,128)(2,1)S(1)}, u32[]{:S(2)}, u32[]{:S(2)}) collective-permute-start(bf16[640,128]{1,0:T(8,128)(2,1)S(1)} %shard_map.129.refs_0_), channel_id=1, source_target_pairs={{0,6},{1,25},{2,4},{3,27},{4,2},{5,29},{6,0},{7,31},{8,14},{9,17},... | collective-permute-start | bytes 491528 | tf_op jit(solution)/shard_map/ppermute | solution.py:352
  52.4 1.9 %collective-permute-done.8.refs_2_ = bf16[640,128]{1,0:T(8,128)(2,1)S(1)} collective-permute-done((bf16[640,128]{1,0:T(8,128)(2,1)S(1)}, bf16[640,128]{1,0:T(8,128)(2,1)S(1)}, u32[]{:S(2)}, u32[]{:S(2)}) %collective-permute-start.8) | collective-permute-done | bytes 163872 | tf_op jit(solution)/shard_map/ppermute | solution.py:352
  54.6 1.7 %collective-permute-done.18.refs_3_ = bf16[640,128]{1,0:T(8,128)(2,1)S(1)} collective-permute-done((bf16[640,128]{1,0:T(8,128)(2,1)S(1)}, bf16[640,128]{1,0:T(8,128)(2,1)S(1)}, u32[]{:S(2)}, u32[]{:S(2)}) %collective-permute-start.18) | collective-permute-done | bytes 163872 | tf_op jit(solution)/shard_map/ppermute | solution.py:352
  56.3 1.7 %collective-permute-done.17.refs_2_ = bf16[640,128]{1,0:T(8,128)(2,1)S(1)} collective-permute-done((bf16[640,128]{1,0:T(8,128)(2,1)S(1)}, bf16[640,128]{1,0:T(8,128)(2,1)S(1)}, u32[]{:S(2)}, u32[]{:S(2)}) %collective-permute-start.17) | collective-permute-done | bytes 163872 | tf_op jit(solution)/shard_map/ppermute | solution.py:352
  58.4 2.1 %shard_map.132 = (f32[1,1]{1,0:T(1,128)}, f32[768,512]{1,0:T(8,128)}, f32[512,512]{1,0:T(8,128)}, f32[768,512]{1,0:T(8,128)}, f32[512,512]{1,0:T(8,128)}) custom-call(bf16[2560,128]{1,0:T(8,128)(2,1)S(1)} %shard_map.124.refs_0_, bf16[2560,128]{1,0:T(8,128)(2,1)S(1)} %shard_map.130.refs_1_, f32[16,128]{1,0:T(8,128)S(1)} %shard_map.131.refs_2_), custom_call_target="tpu_custom_call" | custom-call | flops 655360 | bytes 3932160 | tf_op jit(solution)/shard_map/pallas_call | solution.py:565
  60.5 1.6 %shard_map.133 = (f32[768,512]{1,0:T(8,128)}, f32[512,512]{1,0:T(8,128)}, f32[768,512]{1,0:T(8,128)}, f32[512,512]{1,0:T(8,128)}) custom-call(bf16[2560,128]{1,0:T(8,128)(2,1)S(1)} %collective-permute-done.19.refs_0_, bf16[2560,128]{1,0:T(8,128)(2,1)S(1)} %collective-permute-done.20.refs_1_, ...), custom_call_target="tpu_custom_call", output_to_operand_aliasing={{0}: (3, {}), {1}: (4, {}), {2}: (5, {}), {3}: (6, {})} | custom-call | flops 655360 | bytes 3932160 | tf_op jit(solution)/shard_map/pallas_call | solution.py:565
  (47 shorter events, 5.5 us)
Async XLA Ops:
  0.6 3.4 %copy-start.1 = (bf16[4,256,256]{2,1,0:T(8,128)(2,1)S(1)}, bf16[4,256,256]{2,1,0:T(8,128)(2,1)}, u32[]{:S(2)}) copy-start(bf16[4,256,256]{2,1,0:T(8,128)(2,1)} %own_v.1) | copy-start | bytes 1572868
  0.6 3.4 %copy-start = (bf16[4,256,256]{2,1,0:T(8,128)(2,1)S(1)}, bf16[4,256,256]{2,1,0:T(8,128)(2,1)}, u32[]{:S(2)}) copy-start(bf16[4,256,256]{2,1,0:T(8,128)(2,1)} %own_a.1) | copy-start | bytes 1572868
  0.7 3.4 %copy-start.3 = (bf16[512,512]{1,0:T(8,128)(2,1)S(1)}, bf16[512,512]{1,0:T(8,128)(2,1)}, u32[]{:S(2)}) copy-start(bf16[512,512]{1,0:T(8,128)(2,1)} %w_proj.1) | copy-start | bytes 1572868
  2.0 2.1 %collective-permute-start = (bf16[2,2,256,256]{3,2,1,0:T(8,128)(2,1)S(1)}, bf16[2,2,256,256]{3,2,1,0:T(8,128)(2,1)S(1)}, u32[]{:S(2)}, u32[]{:S(2)}) collective-permute-start(bf16[2,2,256,256]{3,2,1,0:T(8,128)(2,1)S(1)} %pad_maximum_fusion), channel_id=1, source_target_pairs={{0,1},{1,0},{2,3},{3,2},{4,5},{5,4},{6,7},{7,6},{8,9},{9,8},{10,11... | collective-permute-start | bytes 1572872 | tf_op jit(solution)/shard_map/ppermute | solution.py:343
  14.5 2.8 %collective-permute-start.1 = (bf16[2592,128]{1,0:T(8,128)(2,1)S(1)}, bf16[2592,128]{1,0:T(8,128)(2,1)S(1)}, u32[]{:S(2)}, u32[]{:S(2)}) collective-permute-start(bf16[2592,128]{1,0:T(8,128)(2,1)S(1)} %get-tuple-element.33), channel_id=1, source_target_pairs={{0,1},{1,0},{2,3},{3,2},{4,5},{5,4},{6,7},{7,6},{8,9},{9,8},{10,11... | collective-permute-start | bytes 1990664 | tf_op jit(solution)/shard_map/ppermute | solution.py:343
  17.1 4.8 %collective-permute-start.10 = (bf16[2592,128]{1,0:T(8,128)(2,1)S(1)}, bf16[2592,128]{1,0:T(8,128)(2,1)S(1)}, u32[]{:S(2)}, u32[]{:S(2)}) collective-permute-start(bf16[2592,128]{1,0:T(8,128)(2,1)S(1)} %get-tuple-element.44), channel_id=1, source_target_pairs={{0,1},{1,0},{2,3},{3,2},{4,5},{5,4},{6,7},{7,6},{8,9},{9,8},{10,11... | collective-permute-start | bytes 1990664 | tf_op jit(solution)/shard_map/ppermute | solution.py:343
  17.4 8.1 %collective-permute-start.2 = (bf16[672,128]{1,0:T(8,128)(2,1)S(1)}, bf16[672,128]{1,0:T(8,128)(2,1)S(1)}, u32[]{:S(2)}, u32[]{:S(2)}) collective-permute-start(bf16[672,128]{1,0:T(8,128)(2,1)S(1)} %get-tuple-element.35), channel_id=1, source_target_pairs={{0,2},{1,3},{2,0},{3,1},{4,6},{5,7},{6,4},{7,5},{8,10},{9,11},{10,... | collective-permute-start | bytes 516104 | tf_op jit(solution)/shard_map/ppermute | solution.py:352
  20.4 9.8 %collective-permute-start.3 = (bf16[672,128]{1,0:T(8,128)(2,1)S(1)}, bf16[672,128]{1,0:T(8,128)(2,1)S(1)}, u32[]{:S(2)}, u32[]{:S(2)}) collective-permute-start(bf16[672,128]{1,0:T(8,128)(2,1)S(1)} %get-tuple-element.36), channel_id=1, source_target_pairs={{0,4},{1,5},{2,6},{3,7},{4,0},{5,1},{6,2},{7,3},{8,12},{9,13},{10,... | collective-permute-start | bytes 516104 | tf_op jit(solution)/shard_map/ppermute | solution.py:352
  21.9 8.3 %collective-permute-start.4 = (bf16[672,128]{1,0:T(8,128)(2,1)S(1)}, bf16[672,128]{1,0:T(8,128)(2,1)S(1)}, u32[]{:S(2)}, u32[]{:S(2)}) collective-permute-start(bf16[672,128]{1,0:T(8,128)(2,1)S(1)} %get-tuple-element.37), channel_id=1, source_target_pairs={{0,6},{1,7},{2,4},{3,5},{4,2},{5,3},{6,0},{7,1},{8,14},{9,15},{10,... | collective-permute-start | bytes 516104 | tf_op jit(solution)/shard_map/ppermute | solution.py:352
  22.1 9.9 %collective-permute-start.11 = (bf16[672,128]{1,0:T(8,128)(2,1)S(1)}, bf16[672,128]{1,0:T(8,128)(2,1)S(1)}, u32[]{:S(2)}, u32[]{:S(2)}) collective-permute-start(bf16[672,128]{1,0:T(8,128)(2,1)S(1)} %get-tuple-element.46), channel_id=1, source_target_pairs={{0,2},{1,9},{2,0},{3,11},{4,6},{5,13},{6,4},{7,15},{8,10},{9,1},{1... | collective-permute-start | bytes 516104 | tf_op jit(solution)/shard_map/ppermute | solution.py:352
  24.1 9.8 %collective-permute-start.12 = (bf16[672,128]{1,0:T(8,128)(2,1)S(1)}, bf16[672,128]{1,0:T(8,128)(2,1)S(1)}, u32[]{:S(2)}, u32[]{:S(2)}) collective-permute-start(bf16[672,128]{1,0:T(8,128)(2,1)S(1)} %get-tuple-element.47), channel_id=1, source_target_pairs={{0,4},{1,17},{2,6},{3,19},{4,0},{5,21},{6,2},{7,23},{8,12},{9,25},... | collective-permute-start | bytes 516104 | tf_op jit(solution)/shard_map/ppermute | solution.py:352
  25.6 8.3 %collective-permute-start.13 = (bf16[672,128]{1,0:T(8,128)(2,1)S(1)}, bf16[672,128]{1,0:T(8,128)(2,1)S(1)}, u32[]{:S(2)}, u32[]{:S(2)}) collective-permute-start(bf16[672,128]{1,0:T(8,128)(2,1)S(1)} %get-tuple-element.48), channel_id=1, source_target_pairs={{0,6},{1,25},{2,4},{3,27},{4,2},{5,29},{6,0},{7,31},{8,14},{9,17},... | collective-permute-start | bytes 516104 | tf_op jit(solution)/shard_map/ppermute | solution.py:352
  30.3 5.5 %collective-permute-start.5 = (bf16[672,128]{1,0:T(8,128)(2,1)S(1)}, bf16[672,128]{1,0:T(8,128)(2,1)S(1)}, u32[]{:S(2)}, u32[]{:S(2)}) collective-permute-start(bf16[672,128]{1,0:T(8,128)(2,1)S(1)} %shard_map.121.one), channel_id=1, source_target_pairs={{0,8},{1,17},{2,10},{3,19},{4,12},{5,21},{6,14},{7,23},{8,0},{9,25... | collective-permute-start | bytes 516104 | tf_op jit(solution)/shard_map/ppermute | solution.py:352
  34.0 5.6 %collective-permute-start.14 = (bf16[672,128]{1,0:T(8,128)(2,1)S(1)}, bf16[672,128]{1,0:T(8,128)(2,1)S(1)}, u32[]{:S(2)}, u32[]{:S(2)}) collective-permute-start(bf16[672,128]{1,0:T(8,128)(2,1)S(1)} %shard_map.127.one), channel_id=1, source_target_pairs={{0,8},{1,3},{2,10},{3,1},{4,12},{5,7},{6,14},{7,5},{8,0},{9,11},{1... | collective-permute-start | bytes 516104 | tf_op jit(solution)/shard_map/ppermute | solution.py:352
  35.9 7.0 %collective-permute-start.6 = (bf16[672,128]{1,0:T(8,128)(2,1)S(1)}, bf16[672,128]{1,0:T(8,128)(2,1)S(1)}, u32[]{:S(2)}, u32[]{:S(2)}) collective-permute-start(bf16[672,128]{1,0:T(8,128)(2,1)S(1)} %shard_map.122.one), channel_id=1, source_target_pairs={{0,16},{1,9},{2,18},{3,11},{4,20},{5,13},{6,22},{7,15},{8,24},{9,1... | collective-permute-start | bytes 516104 | tf_op jit(solution)/shard_map/ppermute | solution.py:352
  39.6 9.2 %collective-permute-start.15 = (bf16[672,128]{1,0:T(8,128)(2,1)S(1)}, bf16[672,128]{1,0:T(8,128)(2,1)S(1)}, u32[]{:S(2)}, u32[]{:S(2)}) collective-permute-start(bf16[672,128]{1,0:T(8,128)(2,1)S(1)} %shard_map.128.one), channel_id=1, source_target_pairs={{0,16},{1,5},{2,18},{3,7},{4,20},{5,1},{6,22},{7,3},{8,24},{9,13},... | collective-permute-start | bytes 516104 | tf_op jit(solution)/shard_map/ppermute | solution.py:352
  42.9 8.8 %collective-permute-start.9 = (bf16[640,128]{1,0:T(8,128)(2,1)S(1)}, bf16[640,128]{1,0:T(8,128)(2,1)S(1)}, u32[]{:S(2)}, u32[]{:S(2)}) collective-permute-start(bf16[640,128]{1,0:T(8,128)(2,1)S(1)} %get-tuple-element.38.refs_0_), channel_id=1, source_target_pairs={{0,6},{1,7},{2,4},{3,5},{4,2},{5,3},{6,0},{7,1},{8,14},{9,15},{10,... | collective-permute-start | bytes 491528 | tf_op jit(solution)/shard_map/ppermute | solution.py:352
  44.4 10.0 %collective-permute-start.8 = (bf16[640,128]{1,0:T(8,128)(2,1)S(1)}, bf16[640,128]{1,0:T(8,128)(2,1)S(1)}, u32[]{:S(2)}, u32[]{:S(2)}) collective-permute-start(bf16[640,128]{1,0:T(8,128)(2,1)S(1)} %get-tuple-element.38.refs_0_), channel_id=1, source_target_pairs={{0,4},{1,5},{2,6},{3,7},{4,0},{5,1},{6,2},{7,3},{8,12},{9,13},{10,... | collective-permute-start | bytes 491528 | tf_op jit(solution)/shard_map/ppermute | solution.py:352
  45.8 8.7 %collective-permute-start.7 = (bf16[640,128]{1,0:T(8,128)(2,1)S(1)}, bf16[640,128]{1,0:T(8,128)(2,1)S(1)}, u32[]{:S(2)}, u32[]{:S(2)}) collective-permute-start(bf16[640,128]{1,0:T(8,128)(2,1)S(1)} %get-tuple-element.38.refs_0_), channel_id=1, source_target_pairs={{0,2},{1,3},{2,0},{3,1},{4,6},{5,7},{6,4},{7,5},{8,10},{9,11},{10,... | collective-permute-start | bytes 491528 | tf_op jit(solution)/shard_map/ppermute | solution.py:352
  48.9 7.4 %collective-permute-start.18 = (bf16[640,128]{1,0:T(8,128)(2,1)S(1)}, bf16[640,128]{1,0:T(8,128)(2,1)S(1)}, u32[]{:S(2)}, u32[]{:S(2)}) collective-permute-start(bf16[640,128]{1,0:T(8,128)(2,1)S(1)} %shard_map.129.refs_0_), channel_id=1, source_target_pairs={{0,6},{1,25},{2,4},{3,27},{4,2},{5,29},{6,0},{7,31},{8,14},{9,17},... | collective-permute-start | bytes 491528 | tf_op jit(solution)/shard_map/ppermute | solution.py:352
  51.0 7.0 %collective-permute-start.17 = (bf16[640,128]{1,0:T(8,128)(2,1)S(1)}, bf16[640,128]{1,0:T(8,128)(2,1)S(1)}, u32[]{:S(2)}, u32[]{:S(2)}) collective-permute-start(bf16[640,128]{1,0:T(8,128)(2,1)S(1)} %shard_map.129.refs_0_), channel_id=1, source_target_pairs={{0,4},{1,17},{2,6},{3,19},{4,0},{5,21},{6,2},{7,23},{8,12},{9,25},... | collective-permute-start | bytes 491528 | tf_op jit(solution)/shard_map/ppermute | solution.py:352
  51.7 6.3 %collective-permute-start.16 = (bf16[640,128]{1,0:T(8,128)(2,1)S(1)}, bf16[640,128]{1,0:T(8,128)(2,1)S(1)}, u32[]{:S(2)}, u32[]{:S(2)}) collective-permute-start(bf16[640,128]{1,0:T(8,128)(2,1)S(1)} %shard_map.129.refs_0_), channel_id=1, source_target_pairs={{0,2},{1,9},{2,0},{3,11},{4,6},{5,13},{6,4},{7,15},{8,10},{9,1},{1... | collective-permute-start | bytes 491528 | tf_op jit(solution)/shard_map/ppermute | solution.py:352
  54.5 5.9 %collective-permute-start.19 = (bf16[2560,128]{1,0:T(8,128)(2,1)S(1)}, bf16[2560,128]{1,0:T(8,128)(2,1)S(1)}, u32[]{:S(2)}, u32[]{:S(2)}) collective-permute-start(bf16[2560,128]{1,0:T(8,128)(2,1)S(1)} %shard_map.124.refs_0_), channel_id=1, source_target_pairs={{0,1},{1,0},{2,3},{3,2},{4,5},{5,4},{6,7},{7,6},{8,9},{9,8},{10,11... | collective-permute-start | bytes 1966088 | tf_op jit(solution)/shard_map/ppermute | solution.py:343
  58.1 2.4 %collective-permute-start.20 = (bf16[2560,128]{1,0:T(8,128)(2,1)S(1)}, bf16[2560,128]{1,0:T(8,128)(2,1)S(1)}, u32[]{:S(2)}, u32[]{:S(2)}) collective-permute-start(bf16[2560,128]{1,0:T(8,128)(2,1)S(1)} %shard_map.130.refs_1_), channel_id=1, source_target_pairs={{0,1},{1,0},{2,3},{3,2},{4,5},{5,4},{6,7},{7,6},{8,9},{9,8},{10,11... | collective-permute-start | bytes 1966088 | tf_op jit(solution)/shard_map/ppermute | solution.py:343
  (3 other events, 10.1 us)
